TPU v7x, 32 devices: a whole 2x2x4 slice. The times are simulated.
32 devices in a mesh: dp: 2 (over core), expert: 16 (over z, y, x).
Axes of the slice: x: 2, y: 2, z: 4, core: 2. Of those that a mesh axis runs over, the one named last changes fastest.
Arguments:
- tokens: bfloat16 [4096, 2048], P(('dp', 'expert')), may hold values from -6 to 6
- expert_ids: int32 [4096, 2], P(('dp', 'expert')), may hold values from 0 to 15, all different within a row; in each aligned block of 128 rows (0 to 127, 128 to 255, ...) at most 32 rows name the same one
- gate_prob: float32 [4096, 2], P(('dp', 'expert')), may hold values from 0.1 to 1
- w_gate: bfloat16 [16, 2048, 704], P('expert'), may hold values from -0.125 to 0.125
- w_up: bfloat16 [16, 2048, 704], P('expert'), may hold values from -0.125 to 0.125
- w_down: bfloat16 [16, 704, 2048], P('expert'), may hold values from -0.21875 to 0.21875
- d_mixed: bfloat16 [4096, 2048], P(('dp', 'expert')), may hold values from -6 to 6
Outputs:
- mixed: bfloat16 [4096, 2048], P(('dp', 'expert'))
- d_tokens: bfloat16 [4096, 2048], P(('dp', 'expert'))
- d_gate: float32 [4096, 2], P(('dp', 'expert'))
- grad_gate: float32 [16, 2048, 704], P('expert', 'dp')
- grad_up: float32 [16, 2048, 704], P('expert', 'dp')
- grad_down: float32 [16, 704, 2048], P('expert', None, 'dp')
Inputs may be any that keep to these rules, and one draw needn't show every extreme that they name: `expert_ids`: each token names 2 different experts; among the 128 tokens of one device (aligned blocks) no expert is named more than 32 times, a bound that some block reaches.
All inputs are finite; a program needn't handle non-finite values.
Results may differ from a plain program's by a relative error of at most 0.0065.
Values may be sent and summed in bfloat16 or wider, within the bound.
No kernel may reach another device: no remote copies, remote signals or barrier semaphores. Data moves between devices by JAX's collectives and lax.ppermute only.
A program may use at most 128 MiB of HBM per device.

v0:
```python
import jax
import jax.numpy as jnp
from jax import lax
from jax.sharding import PartitionSpec as P


def on_device(tokens, expert_ids, gate_prob, w_gate, w_up, w_down, d_mixed):
    tok_dev, feature = tokens.shape
    n_top = expert_ids.shape[1]
    experts = lax.axis_size("expert")
    capacity = max(2, 2 * tok_dev * n_top // experts)
    pair_count = tok_dev * n_top
    slot_count = experts * capacity
    flat_ids = expert_ids.reshape(pair_count)
    onehot = (flat_ids[:, None] == jnp.arange(experts, dtype=jnp.int32)[None, :]).astype(jnp.int32)
    pair_rank = jnp.sum((jnp.cumsum(onehot, 0) - 1) * onehot, 1)
    slot_of_pair = flat_ids * capacity + pair_rank
    pair_of_slot = (
        jnp.full((slot_count,), pair_count, jnp.int32)
        .at[slot_of_pair]
        .set(jnp.arange(pair_count, dtype=jnp.int32))
    )
    padding = jnp.zeros((1, feature), jnp.bfloat16)
    x_pairs = jnp.concatenate([jnp.repeat(tokens, n_top, axis=0), padding], 0)
    dy_scaled = (gate_prob[:, :, None] * d_mixed[:, None, :].astype(jnp.float32)).astype(
        jnp.bfloat16
    )
    dy_pairs = jnp.concatenate([dy_scaled.reshape(pair_count, feature), padding], 0)
    send_x = x_pairs[pair_of_slot].reshape(experts, capacity, feature)
    send_dy = dy_pairs[pair_of_slot].reshape(experts, capacity, feature)
    gate_matrix = w_gate[0]
    up_matrix = w_up[0]
    down_matrix = w_down[0]
    hidden_units = gate_matrix.shape[1]
    contract_rows = (((0,), (0,)), ((), ()))
    contract_cols = (((1,), (1,)), ((), ()))
    recv_x, recv_dy = (
        lax.all_to_all(send_x, "expert", split_axis=0, concat_axis=0, tiled=True),
        lax.all_to_all(send_dy, "expert", split_axis=0, concat_axis=0, tiled=True),
    )
    x_rows = recv_x.reshape(slot_count, feature)
    gate_pre = jnp.dot(x_rows, gate_matrix, preferred_element_type=jnp.float32)
    up_pre = jnp.dot(x_rows, up_matrix, preferred_element_type=jnp.float32)
    sig_gate = jax.nn.sigmoid(gate_pre)
    silu_gate = gate_pre * sig_gate
    hidden = (silu_gate * up_pre).astype(jnp.bfloat16)
    expert_out = jnp.dot(hidden, down_matrix, preferred_element_type=jnp.float32).astype(
        jnp.bfloat16
    )
    out_blocks = expert_out.reshape(experts, capacity, feature)
    back_out = lax.all_to_all(out_blocks, "expert", split_axis=0, concat_axis=0, tiled=True)
    dy_rows = recv_dy.reshape(slot_count, feature)
    back_hidden = lax.dot_general(
        dy_rows, down_matrix, contract_cols, preferred_element_type=jnp.float32
    )
    d_silu = sig_gate * (1.0 + gate_pre * (1.0 - sig_gate))
    grad_pre_gate = (back_hidden * up_pre * d_silu).astype(jnp.bfloat16)
    grad_pre_up = (back_hidden * silu_gate).astype(jnp.bfloat16)
    expert_dx = (
        lax.dot_general(
            grad_pre_gate, gate_matrix, contract_cols, preferred_element_type=jnp.float32
        )
        + lax.dot_general(grad_pre_up, up_matrix, contract_cols, preferred_element_type=jnp.float32)
    ).astype(jnp.bfloat16)
    dx_blocks = expert_dx.reshape(experts, capacity, feature)
    term_gate = lax.dot_general(
        x_rows, grad_pre_gate, contract_rows, preferred_element_type=jnp.float32
    )
    term_up = lax.dot_general(
        x_rows, grad_pre_up, contract_rows, preferred_element_type=jnp.float32
    )
    term_down = lax.dot_general(dy_rows, hidden, contract_rows, preferred_element_type=jnp.float32)
    summed = lax.psum_scatter(
        jnp.concatenate([term_gate, term_up, term_down], 1).astype(jnp.bfloat16),
        "dp",
        scatter_dimension=0,
        tiled=True,
    ).astype(jnp.float32)
    grad_gate = summed[:, :hidden_units][None]
    grad_up = summed[:, hidden_units : 2 * hidden_units][None]
    grad_down = summed[:, 2 * hidden_units :].T[None]
    back_dx = lax.all_to_all(dx_blocks, "expert", split_axis=0, concat_axis=0, tiled=True)
    y_pairs = (
        back_out.reshape(slot_count, feature)[slot_of_pair]
        .reshape(tok_dev, n_top, feature)
        .astype(jnp.float32)
    )
    dx_pairs = (
        back_dx.reshape(slot_count, feature)[slot_of_pair]
        .reshape(tok_dev, n_top, feature)
        .astype(jnp.float32)
    )
    mixed = jnp.sum(gate_prob[:, :, None] * y_pairs, 1).astype(jnp.bfloat16)
    d_gate = jnp.sum(d_mixed[:, None, :].astype(jnp.float32) * y_pairs, 2)
    d_tokens = jnp.sum(dx_pairs, 1).astype(jnp.bfloat16)
    return (mixed, d_tokens, d_gate, grad_gate, grad_up, grad_down)


def solution(mesh):
    in_specs = (
        P(("dp", "expert"), None),
        P(("dp", "expert"), None),
        P(("dp", "expert"), None),
        P("expert", None, None),
        P("expert", None, None),
        P("expert", None, None),
        P(("dp", "expert"), None),
    )
    out_specs = (
        P(("dp", "expert"), None),
        P(("dp", "expert"), None),
        P(("dp", "expert"), None),
        P("expert", "dp", None),
        P("expert", "dp", None),
        P("expert", None, "dp"),
    )
    return jax.shard_map(
        on_device, mesh=mesh, in_specs=in_specs, out_specs=out_specs, check_vma=False
    )
```

profile of v0, /device:TPU:0, one launch (start us, length us, event | category | flops | bytes accessed | tf_op | source)
XLA Modules:
  0.0 291.3 jit_solution(1278788049964706952)
XLA Ops:
  19.0 6.6 %gather_fusion = bf16[512,2048]{1,0:T(8,128)(2,1)} fusion(bf16[257,2048]{1,0:T(8,128)(2,1)} %concatenate.10, s32[1024]{0:T(1024)S(1)} %pad_clamp_fusion.1), kind=kCustom, calls=%fused_computation | custom fusion | bytes 4196352 | tf_op jit(solution)/shard_map/gather | solution.py:29
  25.6 8.5 %all-to-all-start = ((bf16[16,32,2048]{2,1,0:T(8,128)(2,1)}), bf16[16,32,2048]{2,1,0:T(8,128)(2,1)}, u32[]{:S(2)}, u32[]{:S(2)}) async-start(bf16[16,32,2048]{2,1,0:T(8,128)(2,1)} %bitcast.62), calls=%async_computation | async-start | bytes 4194304 | tf_op jit(solution)/shard_map/all_to_all | solution.py:38
  36.4 3.7 %mul.87 = f32[256,2048]{1,0:T(8,128)} reshape(f32[128,2,2048]{2,1,0:T(2,128)} %mul.86) | data formatting | bytes 4194304 | tf_op jit(solution)/shard_map/mul | solution.py:25
  43.2 6.6 %gather_fusion.2 = bf16[512,2048]{1,0:T(8,128)(2,1)} fusion(bf16[257,2048]{1,0:T(8,128)(2,1)} %concatenate.11, s32[1024]{0:T(1024)S(1)} %pad_clamp_fusion.1), kind=kCustom, calls=%fused_computation.2 | custom fusion | bytes 4196352 | tf_op jit(solution)/shard_map/gather | solution.py:30
  49.8 27.4 %all-to-all-done = bf16[16,32,2048]{2,1,0:T(8,128)(2,1)} async-done(((bf16[16,32,2048]{2,1,0:T(8,128)(2,1)}), bf16[16,32,2048]{2,1,0:T(8,128)(2,1)}, u32[]{:S(2)}, u32[]{:S(2)}) %all-to-all-start) | async-done | bytes 2097184 | tf_op jit(solution)/shard_map/all_to_all | solution.py:38
  77.2 10.0 %all-to-all-start.2 = ((bf16[16,32,2048]{2,1,0:T(8,128)(2,1)}), bf16[16,32,2048]{2,1,0:T(8,128)(2,1)}, u32[]{:S(2)}, u32[]{:S(2)}) async-start(bf16[16,32,2048]{2,1,0:T(8,128)(2,1)} %bitcast.63), calls=%async_computation.2 | async-start | bytes 4194304 | tf_op jit(solution)/shard_map/all_to_all | solution.py:39
  87.5 5.4 %fusion.8 = f32[512,704]{0,1:T(8,128)} fusion(bf16[512,2048]{1,0:T(8,128)(2,1)} %bitcast.4, bf16[1,2048,704]{1,2,0:T(8,128)(2,1)} %param.10), kind=kOutput, calls=%fused_computation.22 | convolution fusion | flops 1476395008 | bytes 6422528 | tf_op jit(solution)/shard_map/dot_general | solution.py:42
  92.8 4.4 %fusion.4 = f32[512,704]{0,1:T(8,128)} fusion(bf16[512,2048]{1,0:T(8,128)(2,1)} %bitcast.4, bf16[1,2048,704]{1,2,0:T(8,128)(2,1)S(1)} %copy-done.4), kind=kOutput, calls=%fused_computation.18 | convolution fusion | flops 1476395008 | bytes 6422528 | tf_op jit(solution)/shard_map/dot_general | solution.py:43
  97.2 32.5 %all-to-all-done.2 = bf16[16,32,2048]{2,1,0:T(8,128)(2,1)} async-done(((bf16[16,32,2048]{2,1,0:T(8,128)(2,1)}), bf16[16,32,2048]{2,1,0:T(8,128)(2,1)}, u32[]{:S(2)}, u32[]{:S(2)}) %all-to-all-start.2) | async-done | bytes 2097184 | tf_op jit(solution)/shard_map/all_to_all | solution.py:39
  129.8 4.6 %multiply_convert_fusion.1 = (bf16[512,704]{0,1:T(8,128)(2,1)S(1)}, bf16[512,704]{0,1:T(8,128)(2,1)S(1)}, bf16[512,704]{0,1:T(8,128)(2,1)S(1)}) fusion(f32[512,704]{0,1:T(8,128)} %fusion.8, f32[512,704]{0,1:T(8,128)} %fusion.4, bf16[512,2048]{1,0:T(8,128)(2,1)} %bitcast.11, bf16[1,704,2048]{2,1,0:T(8,128)(2,1)S(1)} %copy-done), kind=kOutput, calls=%fused_computation.27 | convolution fusion | flops 1481801728 | bytes 10027008 | tf_op jit(solution)/shard_map/dot_general | solution.py:53
  134.4 4.1 %convolution_convert_fusion = bf16[2048,704]{0,1:T(8,128)(2,1)S(1)} fusion(bf16[512,704]{0,1:T(8,128)(2,1)S(1)} %get-tuple-element.19, bf16[512,2048]{1,0:T(8,128)(2,1)} %bitcast.11), kind=kOutput, calls=%fused_computation.7 | convolution fusion | flops 1477836800 | bytes 5701632 | tf_op jit(solution)/shard_map/dot_general | solution.py:72
  145.1 4.2 %pad_maximum_fusion = bf16[2048,2112]{0,1:T(8,128)(2,1)} fusion(bf16[2048,704]{0,1:T(8,128)(2,1)S(1)} %convolution_convert_fusion, bf16[2048,704]{0,1:T(8,128)(2,1)S(1)} %convolution_convert_fusion.1, bf16[2048,704]{0,1:T(8,128)(2,1)S(1)} %convolution_convert_fusion.2), kind=kLoop, calls=%fused_computation.5 | loop fusion | flops 25952256 | bytes 17301504 | tf_op jit(solution)/shard_map/concatenate | solution.py:74
  149.3 4.3 %convolution_convert_fusion.3 = bf16[512,2048]{1,0:T(8,128)(2,1)} fusion(bf16[512,704]{0,1:T(8,128)(2,1)} %copy-done.6, bf16[1,704,2048]{2,1,0:T(8,128)(2,1)S(1)} %copy-done), kind=kOutput, calls=%fused_computation.10 | convolution fusion | flops 1477443584 | bytes 5701632 | tf_op jit(solution)/shard_map/dot_general | solution.py:47
  153.6 9.8 %all-to-all-start.1 = ((bf16[16,32,2048]{2,1,0:T(8,128)(2,1)}), bf16[16,32,2048]{2,1,0:T(8,128)(2,1)}, u32[]{:S(2)}, u32[]{:S(2)}) async-start(bf16[16,32,2048]{2,1,0:T(8,128)(2,1)} %bitcast.65), calls=%async_computation.1 | async-start | bytes 4194304 | tf_op jit(solution)/shard_map/all_to_all | solution.py:51
  163.4 4.9 %fusion.6 = f32[512,2048]{1,0:T(8,128)S(1)} fusion(bf16[512,704]{0,1:T(8,128)(2,1)} %copy-done.2, bf16[1,2048,704]{1,2,0:T(8,128)(2,1)} %param.10), kind=kOutput, calls=%fused_computation.20 | convolution fusion | flops 1476395008 | bytes 7798784 | tf_op jit(solution)/shard_map/dot_general | solution.py:60
  171.7 34.3 %all-to-all-done.1 = bf16[16,32,2048]{2,1,0:T(8,128)(2,1)} async-done(((bf16[16,32,2048]{2,1,0:T(8,128)(2,1)}), bf16[16,32,2048]{2,1,0:T(8,128)(2,1)}, u32[]{:S(2)}, u32[]{:S(2)}) %all-to-all-start.1) | async-done | bytes 2097184 | tf_op jit(solution)/shard_map/all_to_all | solution.py:51
  206.0 9.8 %all-to-all-start.3 = ((bf16[16,32,2048]{2,1,0:T(8,128)(2,1)}), bf16[16,32,2048]{2,1,0:T(8,128)(2,1)}, u32[]{:S(2)}, u32[]{:S(2)}) async-start(bf16[16,32,2048]{2,1,0:T(8,128)(2,1)} %bitcast.64), calls=%async_computation.3 | async-start | bytes 4194304 | tf_op jit(solution)/shard_map/all_to_all | solution.py:82
  216.9 5.2 %gather_fusion.1 = bf16[256,2048]{1,0:T(8,128)(2,1)} fusion(bf16[512,2048]{1,0:T(8,128)(2,1)} %bitcast.9, s32[1024]{0:T(1024)S(1)} %pad_clamp_fusion), kind=kCustom, calls=%fused_computation.1 | custom fusion | bytes 2098176 | tf_op jit(solution)/shard_map/gather | solution.py:84
  222.1 3.3 %reshape.120 = f32[128,2,2048]{2,1,0:T(2,128)} reshape(bf16[256,2048]{1,0:T(8,128)(2,1)} %gather_fusion.1) | data formatting | bytes 3145728 | tf_op jit(solution)/shard_map/convert_element_type | solution.py:86
  225.4 32.9 %all-to-all-done.3 = bf16[16,32,2048]{2,1,0:T(8,128)(2,1)} async-done(((bf16[16,32,2048]{2,1,0:T(8,128)(2,1)}), bf16[16,32,2048]{2,1,0:T(8,128)(2,1)}, u32[]{:S(2)}, u32[]{:S(2)}) %all-to-all-start.3) | async-done | bytes 2097184 | tf_op jit(solution)/shard_map/all_to_all | solution.py:82
  258.3 5.2 %gather_fusion.3 = bf16[256,2048]{1,0:T(8,128)(2,1)} fusion(bf16[512,2048]{1,0:T(8,128)(2,1)} %bitcast.13, s32[1024]{0:T(1024)S(1)} %pad_clamp_fusion), kind=kCustom, calls=%fused_computation.3 | custom fusion | bytes 2098176 | tf_op jit(solution)/shard_map/gather | solution.py:89
  266.0 4.6 %reduce_sum.44 = bf16[128,2048]{1,0:T(8,128)(2,1)} reduce(bf16[128,2,2048]{2,1,0:T(2,128)(2,1)} %reshape.119, bf16[]{:T(256)} %constant.9.clone.1), dimensions={1}, to_apply=%region_5.6 | reduce | flops 262144 | bytes 1572866 | tf_op jit(solution)/shard_map/reduce_sum | solution.py:95
  270.6 6.3 %multiply_reduce_fusion = (f32[128,2]{1,0:T(8,128)S(1)}, bf16[128,2048]{1,0:T(8,128)(2,1)}) fusion(f32[128,2,2048]{2,1,0:T(2,128)} %reshape.120, f32[128,2048]{1,0:T(8,128)} %convert_element_type.54, f32[128,2]{1,0:T(8,128)S(1)} %copy.20), kind=kLoop, calls=%fused_computation.24 | loop fusion | flops 1834752 | bytes 3672064 | tf_op jit(solution)/shard_map/reduce_sum | solution.py:94
  280.8 3.7 %slice_bitcast_fusion = (f32[1,704,1024]{2,1,0:T(8,128)}, f32[1,1024,704]{1,2,0:T(8,128)}, f32[1,1024,704]{1,2,0:T(8,128)}) fusion(f32[1024,2112]{0,1:T(8,128)S(1)} %convert_element_type.59), kind=kLoop, calls=%fused_computation.11 | loop fusion | bytes 17301504 | tf_op jit(solution)/shard_map/broadcast_in_dim | solution.py:81
  (54 shorter events, 34.9 us)
Async XLA Ops:
  7.2 122.6 %copy-start = (bf16[1,704,2048]{2,1,0:T(8,128)(2,1)S(1)}, bf16[1,704,2048]{2,1,0:T(8,128)(2,1)}, u32[]{:S(2)}) copy-start(bf16[1,704,2048]{2,1,0:T(8,128)(2,1)} %param.12) | copy-start | bytes 8650756
  25.6 8.5 %copy-start.1 = (bf16[128,2048]{1,0:T(8,128)(2,1)S(1)}, bf16[128,2048]{1,0:T(8,128)(2,1)}, u32[]{:S(2)}) copy-start(bf16[128,2048]{1,0:T(8,128)(2,1)} %param.13) | copy-start | bytes 1572868
  25.6 51.6 %all-to-all-start = ((bf16[16,32,2048]{2,1,0:T(8,128)(2,1)}), bf16[16,32,2048]{2,1,0:T(8,128)(2,1)}, u32[]{:S(2)}, u32[]{:S(2)}) async-start(bf16[16,32,2048]{2,1,0:T(8,128)(2,1)} %bitcast.62), calls=%async_computation | async-start | bytes 4194304 | tf_op jit(solution)/shard_map/all_to_all | solution.py:38
  36.4 3.7 %copy-start.3 = (f32[128,2]{0,1:T(2,128)S(1)}, f32[128,2]{0,1:T(2,128)}, u32[]{:S(2)}) copy-start(f32[128,2]{0,1:T(2,128)} %param.9) | copy-start | bytes 3076
  77.2 52.6 %all-to-all-start.2 = ((bf16[16,32,2048]{2,1,0:T(8,128)(2,1)}), bf16[16,32,2048]{2,1,0:T(8,128)(2,1)}, u32[]{:S(2)}, u32[]{:S(2)}) async-start(bf16[16,32,2048]{2,1,0:T(8,128)(2,1)} %bitcast.63), calls=%async_computation.2 | async-start | bytes 4194304 | tf_op jit(solution)/shard_map/all_to_all | solution.py:39
  87.2 190.3 %reduce-scatter.2.cloned.1.call-start = ((), (), s32[]{:S(2)}) async-start(), calls=%async_computation.5 | async-start | bytes 12976128 | tf_op jit(solution)/shard_map/reduce_scatter | solution.py:73
  87.4 5.4 %copy-start.4 = (bf16[1,2048,704]{1,2,0:T(8,128)(2,1)S(1)}, bf16[1,2048,704]{1,2,0:T(8,128)(2,1)}, u32[]{:S(2)}) copy-start(bf16[1,2048,704]{1,2,0:T(8,128)(2,1)} %param.11) | copy-start | bytes 8650756
  134.4 4.1 %copy-start.6 = (bf16[512,704]{0,1:T(8,128)(2,1)}, bf16[512,704]{0,1:T(8,128)(2,1)S(1)}, u32[]{:S(2)}) copy-start(bf16[512,704]{0,1:T(8,128)(2,1)S(1)} %get-tuple-element.19) | copy-start | bytes 2162692
  134.4 4.1 %copy-start.7 = (bf16[512,704]{0,1:T(8,128)(2,1)}, bf16[512,704]{0,1:T(8,128)(2,1)S(1)}, u32[]{:S(2)}) copy-start(bf16[512,704]{0,1:T(8,128)(2,1)S(1)} %get-tuple-element.17) | copy-start | bytes 2162692
  134.4 7.4 %copy-start.2 = (bf16[512,704]{0,1:T(8,128)(2,1)}, bf16[512,704]{0,1:T(8,128)(2,1)S(1)}, u32[]{:S(2)}) copy-start(bf16[512,704]{0,1:T(8,128)(2,1)S(1)} %get-tuple-element.18) | copy-start | bytes 2162692
  153.6 52.5 %all-to-all-start.1 = ((bf16[16,32,2048]{2,1,0:T(8,128)(2,1)}), bf16[16,32,2048]{2,1,0:T(8,128)(2,1)}, u32[]{:S(2)}, u32[]{:S(2)}) async-start(bf16[16,32,2048]{2,1,0:T(8,128)(2,1)} %bitcast.65), calls=%async_computation.1 | async-start | bytes 4194304 | tf_op jit(solution)/shard_map/all_to_all | solution.py:51
  163.4 5.0 %copy-start.5 = (bf16[1,2048,704]{1,2,0:T(8,128)(2,1)S(1)}, bf16[1,2048,704]{1,2,0:T(8,128)(2,1)}, u32[]{:S(2)}) copy-start(bf16[1,2048,704]{1,2,0:T(8,128)(2,1)} %param.11) | copy-start | bytes 8650756
  163.4 5.0 %copy-start.8 = (bf16[512,704]{0,1:T(8,128)(2,1)S(1)}, bf16[512,704]{0,1:T(8,128)(2,1)}, u32[]{:S(2)}) copy-start(bf16[512,704]{0,1:T(8,128)(2,1)} %copy-done.7) | copy-start | bytes 2162692
  206.0 52.3 %all-to-all-start.3 = ((bf16[16,32,2048]{2,1,0:T(8,128)(2,1)}), bf16[16,32,2048]{2,1,0:T(8,128)(2,1)}, u32[]{:S(2)}, u32[]{:S(2)}) async-start(bf16[16,32,2048]{2,1,0:T(8,128)(2,1)} %bitcast.64), calls=%async_computation.3 | async-start | bytes 4194304 | tf_op jit(solution)/shard_map/all_to_all | solution.py:82
Sparse Core Ops, SparseCore 0:
  149.4 21.1 reduce-scatter.1
where the time goes:
time: 296 us; the launch traced here: 291 us
  waiting for transfers between devices  127 us (43%)
  local copies, waits for them, and re-layouts  51.3 us (17%)
  starting transfers between devices  38.3 us (13%)
  matrix products  37.5 us (13%)
  other arithmetic  22.7 us (8%)
  between operations  14.3 us (5%)
    all_to_all x1, waiting for transfers between devices, on_device(): lax.all_to_all(out_blocks, 'expert', split_axis=0, concat_axis=0, tiled=T...  34.3 us
    all_to_all x1, waiting for transfers between devices, on_device(): lax.all_to_all(dx_blocks, 'expert', split_axis=0, concat_axis=0, tiled=True)  32.9 us
    all_to_all x1, waiting for transfers between devices, on_device(): lax.all_to_all(send_dy, 'expert', split_axis=0, concat_axis=0, tiled=True)  32.5 us
    all_to_all x1, waiting for transfers between devices, on_device(): lax.all_to_all(send_x, 'expert', split_axis=0, concat_axis=0, tiled=True)  27.4 us
    all_to_all x1, starting transfers between devices, on_device(): lax.all_to_all(send_dy, 'expert', split_axis=0, concat_axis=0, tiled=True)  10 us
    all_to_all x1, starting transfers between devices, on_device(): lax.all_to_all(out_blocks, 'expert', split_axis=0, concat_axis=0, tiled=T...  9.82 us
    all_to_all x1, starting transfers between devices, on_device(): lax.all_to_all(dx_blocks, 'expert', split_axis=0, concat_axis=0, tiled=True)  9.76 us
    all_to_all x1, starting transfers between devices, on_device(): lax.all_to_all(send_x, 'expert', split_axis=0, concat_axis=0, tiled=True)  8.5 us
  transfers between devices with their start and end apart: 5, of which 4 were waited for; matrix products, arithmetic and copies ran while one was open for 23% of the time, Pallas kernels for 0%

commit v1 on v0

v1 whole, which is shorter than its diff:
```python
import jax
import jax.numpy as jnp
from jax import lax
from jax.sharding import PartitionSpec as P

BF16 = jnp.bfloat16
F32 = jnp.float32


def slot_table(ids, expert_of_row, capacity):
    tok = ids.shape[-1]
    member = jnp.any(ids[..., None, :, :] == expert_of_row[:, None, None], axis=-2)
    earlier = (jnp.arange(tok)[:, None] < jnp.arange(tok)[None, :]).astype(BF16)
    rank = jnp.dot(member.astype(BF16), earlier, preferred_element_type=F32).astype(jnp.int32)
    place = jnp.arange(capacity, dtype=jnp.int32)
    return member[:, None, :] & (rank[:, None, :] == place[None, :, None])


def on_device(tokens, expert_ids, gate_prob, w_gate, w_up, w_down, d_mixed):
    tok, feature = tokens.shape
    top = expert_ids.shape[1]
    experts = lax.axis_size("expert")
    capacity = max(2, 2 * tok * top // experts)
    planes = max(1, experts * capacity // tok)
    plane = experts // planes
    me = lax.axis_index("expert")
    my_plane, my_col = me // plane, me % plane
    bits = [1 << b for b in range(planes.bit_length() - 1)]

    def hop(value, flip):
        pairs = [(e, e ^ flip) for e in range(experts)]
        return lax.ppermute(value, "expert", pairs)

    def along_z(value):
        held = {0: value}
        for bit in reversed(bits):
            for j in sorted(held):
                held[j ^ bit] = hop(held[j], bit * plane)
        return held

    ids_own = expert_ids.T
    meta = jnp.concatenate([ids_own.astype(F32), gate_prob.T], 0)
    meta_all = lax.all_gather(meta, "expert")
    order = jnp.array(
        [[(j * plane) ^ i for i in range(plane)] for j in range(planes)], jnp.int32
    ).reshape(-1)
    meta_rel = meta_all[me ^ order]
    ids_rel = meta_rel[:, :top].astype(jnp.int32)
    gate_rel = meta_rel[:, top:]
    columns = my_plane * plane + (my_col ^ jnp.arange(plane, dtype=jnp.int32))
    pick = {0: slot_table(ids_own, columns, capacity).astype(BF16)}
    for j in range(1, planes):
        pick[j] = slot_table(ids_rel[j * plane], columns, capacity).astype(BF16)
    mine = jax.vmap(lambda ids: slot_table(ids, me[None], capacity)[0])(ids_rel)
    gate_tok = jnp.sum(jnp.where(ids_rel == me, gate_rel, 0.0), 1)
    gate_slot = jnp.sum(jnp.where(mine, gate_tok[:, None, :], 0.0), 2).reshape(-1, 1)

    def dispatch(held):
        parts = {}
        for j in held:
            rows = jnp.einsum("irt,tf->irf", pick[j], held[j], preferred_element_type=F32).astype(BF16)
            for i in range(plane):
                parts[j, i] = rows[i] if i == 0 else hop(rows[i], i)
        return jnp.concatenate([parts[j, i] for j in range(planes) for i in range(plane)], 0)

    def combine(rows):
        rows = rows.reshape(planes, plane, capacity, feature)
        total = {}
        for j in reversed(range(planes)):
            back = [rows[j, i] if i == 0 else hop(rows[j, i], i) for i in range(plane)]
            total[j] = jnp.einsum(
                "irt,irf->tf", pick[j], jnp.stack(back), preferred_element_type=F32
            )
        for bit in bits:
            for j in sorted(total, reverse=True):
                if j & bit:
                    came = hop(total.pop(j).astype(BF16), bit * plane)
                    total[j ^ bit] = total[j ^ bit] + came.astype(F32)
        return total[0].astype(BF16)

    gate_matrix, up_matrix, down_matrix = w_gate[0], w_up[0], w_down[0]
    hidden_units = gate_matrix.shape[1]
    contract_rows = (((0,), (0,)), ((), ()))
    contract_cols = (((1,), (1,)), ((), ()))

    held_x = along_z(tokens)
    held_d = along_z(d_mixed)
    x_rows = dispatch(held_x)
    gate_pre = jnp.dot(x_rows, gate_matrix, preferred_element_type=F32)
    up_pre = jnp.dot(x_rows, up_matrix, preferred_element_type=F32)
    sig_gate = jax.nn.sigmoid(gate_pre)
    silu_gate = gate_pre * sig_gate
    hidden = (silu_gate * up_pre).astype(BF16)
    expert_out = jnp.dot(hidden, down_matrix, preferred_element_type=F32).astype(BF16)
    y_scaled = (gate_slot * expert_out.astype(F32)).astype(BF16)
    mixed = combine(y_scaled)

    d_rows = dispatch(held_d)
    dy_rows = (gate_slot * d_rows.astype(F32)).astype(BF16)
    back_hidden = lax.dot_general(dy_rows, down_matrix, contract_cols, preferred_element_type=F32)
    d_silu = sig_gate * (1.0 + gate_pre * (1.0 - sig_gate))
    grad_pre_gate = (back_hidden * up_pre * d_silu).astype(BF16)
    grad_pre_up = (back_hidden * silu_gate).astype(BF16)
    expert_dx = (
        lax.dot_general(grad_pre_gate, gate_matrix, contract_cols, preferred_element_type=F32)
        + lax.dot_general(grad_pre_up, up_matrix, contract_cols, preferred_element_type=F32)
    ).astype(BF16)
    d_tokens = combine(expert_dx)

    slot_grad = jnp.sum(d_rows.astype(F32) * expert_out.astype(F32), 1).reshape(experts, capacity)
    slot_grad = slot_grad[me ^ order]
    grad_all = lax.all_gather(slot_grad, "expert")
    grad_own = lax.dynamic_index_in_dim(grad_all, me, 1, keepdims=False)
    table = slot_table(ids_own, jnp.arange(experts, dtype=jnp.int32), capacity)
    grad_tok = jnp.sum(jnp.where(table, grad_own[:, :, None], 0.0), 1)
    named = ids_own[:, None, :] == jnp.arange(experts, dtype=jnp.int32)[None, :, None]
    d_gate = jnp.sum(jnp.where(named, grad_tok[None], 0.0), 1).T

    term_gate = lax.dot_general(x_rows, grad_pre_gate, contract_rows, preferred_element_type=F32)
    term_up = lax.dot_general(x_rows, grad_pre_up, contract_rows, preferred_element_type=F32)
    term_down = lax.dot_general(dy_rows, hidden, contract_rows, preferred_element_type=F32)
    summed = lax.psum_scatter(
        jnp.concatenate([term_gate, term_up, term_down], 1).astype(BF16),
        "dp",
        scatter_dimension=0,
        tiled=True,
    ).astype(F32)
    grad_gate = summed[:, :hidden_units][None]
    grad_up = summed[:, hidden_units : 2 * hidden_units][None]
    grad_down = summed[:, 2 * hidden_units :].T[None]
    return (mixed, d_tokens, d_gate, grad_gate, grad_up, grad_down)


def solution(mesh):
    in_specs = (
        P(("dp", "expert"), None),
        P(("dp", "expert"), None),
        P(("dp", "expert"), None),
        P("expert", None, None),
        P("expert", None, None),
        P("expert", None, None),
        P(("dp", "expert"), None),
    )
    out_specs = (
        P(("dp", "expert"), None),
        P(("dp", "expert"), None),
        P(("dp", "expert"), None),
        P("expert", "dp", None),
        P("expert", "dp", None),
        P("expert", None, "dp"),
    )
    return jax.shard_map(
        on_device, mesh=mesh, in_specs=in_specs, out_specs=out_specs, check_vma=False
    )
```

time: 296 us -> 332 us (1.12); the launches traced: 291 us -> 332 us
  blocking collectives: 0 us -> 114 us
  waiting for transfers between devices: 127 us -> 76.1 us
  local copies, waits for them, and re-layouts: 51.3 us -> 16.5 us
  starting transfers between devices: 38.3 us -> 64.2 us
  other arithmetic: 22.7 us -> 11.9 us
    all_to_all x4 -> x0, waiting for transfers between devices: 127 us -> none  [the longest x1 34.3 us: on_device(): lax.all_to_all(out_blocks, 'expert', split_axis=0, concat_axis=0, tiled=T...]
    all_gather x0 -> x2, blocking collectives: none -> 114 us  [the longest x1 74.7 us: on_device(): meta_all = lax.all_gather(meta, 'expert')]
    ppermute x0 -> x60, waiting for transfers between devices: none -> 76.1 us  [hop(): return lax.ppermute(value, 'expert', pairs)]
    ppermute x0 -> x60, starting transfers between devices: none -> 64.2 us  [hop(): return lax.ppermute(value, 'expert', pairs)]
    all_to_all x4 -> x0, starting transfers between devices: 38.1 us -> none  [the longest x1 10 us: on_device(): lax.all_to_all(send_dy, 'expert', split_axis=0, concat_axis=0, tiled=True)]
    gather x4 -> x2, local copies, waits for them, and re-layouts: 23.6 us -> 1.4 us  [the longest x1 0.82 us: on_device(): slot_grad = slot_grad[me ^ order]]
    reduce_sum x3 -> x4, other arithmetic: 10.9 us -> 0.92 us  [the longest x1 0.58 us: on_device(): d_gate = jnp.sum(jnp.where(named, grad_tok[None], 0.0), 1).T]
    dot_general x4 -> x26, matrix products: 18.1 us -> 24.6 us  [the longest x8 7.54 us: dispatch(): jnp.einsum('irt,tf->irf', pick[j], held[j], preferred_element_type=F32)]
  transfers between devices with their start and end apart: 5 -> 61, of which waited for: 4 -> 25; matrix products, arithmetic and copies ran while one was open for 23% -> 13% of each run, Pallas kernels for 0% -> 0%
where the time goes in v1:
time: 332 us
  blocking collectives  114 us (34%)
  waiting for transfers between devices  76.1 us (23%)
  starting transfers between devices  64.2 us (19%)
  matrix products  34.4 us (10%)
  local copies, waits for them, and re-layouts  16.5 us (5%)
  between operations  15 us (5%)
  other arithmetic  11.9 us (4%)
    ppermute x60, waiting for transfers between devices, hop(): return lax.ppermute(value, 'expert', pairs)  76.1 us
    all_gather x1, blocking collectives, on_device(): meta_all = lax.all_gather(meta, 'expert')  74.7 us
    ppermute x60, starting transfers between devices, hop(): return lax.ppermute(value, 'expert', pairs)  64.2 us
    all_gather x1, blocking collectives, on_device(): grad_all = lax.all_gather(slot_grad, 'expert')  39 us
    dot_general x8, matrix products, dispatch(): jnp.einsum('irt,tf->irf', pick[j], held[j], preferred_element_type=F32)  7.54 us
    unnamed x112, local copies, waits for them, and re-layouts  7.4 us
  transfers between devices with their start and end apart: 61, of which 25 were waited for; matrix products, arithmetic and copies ran while one was open for 13% of the time, Pallas kernels for 0%

profile of v1, /device:TPU:0, one launch (start us, length us, event | category | flops | bytes accessed | tf_op | source)
XLA Modules:
  0.0 331.8 jit_solution(12944030654043699038)
XLA Ops:
  7.2 3.1 collective-permute-start.33
  14.7 74.7 %all-gather.2 = f32[16,4,128]{2,1,0:T(4,128)S(1)} all-gather(f32[1,4,128]{2,1,0:T(4,128)S(1)} %maximum_bitcast_fusion), channel_id=2, replica_groups=mesh['dp'=2,'expert'=16] {'expert'}, dimensions={0}, use_global_device_ids=true | all-gather | bytes 34816 | tf_op jit(solution)/shard_map/all_gather | solution.py:43
  102.1 3.6 %collective-permute-done.31 = bf16[32,2048]{1,0:T(8,128)(2,1)S(1)} collective-permute-done((bf16[32,2048]{1,0:T(8,128)(2,1)}, bf16[32,2048]{1,0:T(8,128)(2,1)S(1)}, u32[]{:S(2)}, u32[]{:S(2)}) %collective-permute-start.31) | collective-permute-done | bytes 131104 | tf_op jit(solution)/shard_map/ppermute | solution.py:32
  106.9 5.1 %collective-permute-done.32 = bf16[32,2048]{1,0:T(8,128)(2,1)S(1)} collective-permute-done((bf16[32,2048]{1,0:T(8,128)(2,1)S(1)}, bf16[32,2048]{1,0:T(8,128)(2,1)S(1)}, u32[]{:S(2)}, u32[]{:S(2)}) %collective-permute-start.32) | collective-permute-done | bytes 131104 | tf_op jit(solution)/shard_map/ppermute | solution.py:32
  113.5 3.5 %collective-permute-done = bf16[32,2048]{1,0:T(8,128)(2,1)S(1)} collective-permute-done((bf16[32,2048]{1,0:T(8,128)(2,1)S(1)}, bf16[32,2048]{1,0:T(8,128)(2,1)S(1)}, u32[]{:S(2)}, u32[]{:S(2)}) %collective-permute-start) | collective-permute-done | bytes 131104 | tf_op jit(solution)/shard_map/ppermute | solution.py:32
  117.7 5.7 %collective-permute-done.1 = bf16[32,2048]{1,0:T(8,128)(2,1)S(1)} collective-permute-done((bf16[32,2048]{1,0:T(8,128)(2,1)S(1)}, bf16[32,2048]{1,0:T(8,128)(2,1)S(1)}, u32[]{:S(2)}, u32[]{:S(2)}) %collective-permute-start.1) | collective-permute-done | bytes 131104 | tf_op jit(solution)/shard_map/ppermute | solution.py:32
  124.8 5.9 %collective-permute-done.2 = bf16[32,2048]{1,0:T(8,128)(2,1)S(1)} collective-permute-done((bf16[32,2048]{1,0:T(8,128)(2,1)S(1)}, bf16[32,2048]{1,0:T(8,128)(2,1)S(1)}, u32[]{:S(2)}, u32[]{:S(2)}) %collective-permute-start.2) | collective-permute-done | bytes 131104 | tf_op jit(solution)/shard_map/ppermute | solution.py:32
  145.8 4.2 %collective-permute-done.4 = bf16[32,2048]{1,0:T(8,128)(2,1)S(1)} collective-permute-done((bf16[32,2048]{1,0:T(8,128)(2,1)S(1)}, bf16[32,2048]{1,0:T(8,128)(2,1)S(1)}, u32[]{:S(2)}, u32[]{:S(2)}) %collective-permute-start.4) | collective-permute-done | bytes 131104 | tf_op jit(solution)/shard_map/ppermute | solution.py:32
  152.6 4.1 %collective-permute-done.6 = bf16[32,2048]{1,0:T(8,128)(2,1)S(1)} collective-permute-done((bf16[32,2048]{1,0:T(8,128)(2,1)S(1)}, bf16[32,2048]{1,0:T(8,128)(2,1)S(1)}, u32[]{:S(2)}, u32[]{:S(2)}) %collective-permute-start.6) | collective-permute-done | bytes 131104 | tf_op jit(solution)/shard_map/ppermute | solution.py:32
  156.7 3.0 collective-permute-start.10
  164.4 4.7 %collective-permute-done.41 = bf16[128,2048]{1,0:T(8,128)(2,1)S(1)} collective-permute-done((bf16[128,2048]{1,0:T(8,128)(2,1)}, bf16[128,2048]{1,0:T(8,128)(2,1)S(1)}, u32[]{:S(2)}, u32[]{:S(2)}) %collective-permute-start.41) | collective-permute-done | bytes 524320 | tf_op jit(solution)/shard_map/ppermute | solution.py:32
  170.1 2.9 collective-permute-start.44
  175.8 4.3 %collective-permute-done.12 = bf16[32,2048]{1,0:T(8,128)(2,1)S(1)} collective-permute-done((bf16[32,2048]{1,0:T(8,128)(2,1)S(1)}, bf16[32,2048]{1,0:T(8,128)(2,1)S(1)}, u32[]{:S(2)}, u32[]{:S(2)}) %collective-permute-start.12) | collective-permute-done | bytes 131104 | tf_op jit(solution)/shard_map/ppermute | solution.py:32
  180.8 5.2 %collective-permute-done.14 = bf16[32,2048]{1,0:T(8,128)(2,1)S(1)} collective-permute-done((bf16[32,2048]{1,0:T(8,128)(2,1)S(1)}, bf16[32,2048]{1,0:T(8,128)(2,1)S(1)}, u32[]{:S(2)}, u32[]{:S(2)}) %collective-permute-start.14) | collective-permute-done | bytes 131104 | tf_op jit(solution)/shard_map/ppermute | solution.py:32
  197.4 4.3 %pad_maximum_fusion = bf16[2048,2112]{0,1:T(8,128)(2,1)} fusion(bf16[2048,704]{0,1:T(8,128)(2,1)S(1)} %convolution_convert_fusion, bf16[2048,704]{0,1:T(8,128)(2,1)S(1)} %convolution_convert_fusion.1, bf16[2048,704]{0,1:T(8,128)(2,1)S(1)} %convolution_convert_fusion.2), kind=kLoop, calls=%fused_computation.2 | loop fusion | flops 25952256 | bytes 17301504 | tf_op jit(solution)/shard_map/concatenate | solution.py:123
  202.6 4.2 %fusion.2 = (f32[512]{0:T(512)S(1)}, bf16[512,2048]{1,0:T(8,128)(2,1)S(1)}) fusion(bf16[512,2048]{1,0:T(8,128)(2,1)} %copy-done.25, f32[512]{0:T(512)S(1)} %copy-done.35, bf16[512,704]{0,1:T(8,128)(2,1)} %copy-done.40, bf16[1,704,2048]{2,1,0:T(8,128)(2,1)S(1)} %copy-done), kind=kOutput, calls=%fused_computation.8 | convolution fusion | flops 1483734528 | bytes 7802880 | tf_op jit(solution)/shard_map/dot_general | solution.py:94
  219.0 39.0 %all-gather.1 = f32[256,32]{1,0:T(8,128)S(1)} all-gather(f32[16,32]{1,0:T(8,128)S(1)} %gather_fusion.1), channel_id=3, replica_groups=mesh['dp'=2,'expert'=16] {'expert'}, dimensions={0}, use_global_device_ids=true | all-gather | bytes 34816 | tf_op jit(solution)/shard_map/all_gather | solution.py:112
  290.1 3.0 collective-permute-start.59
  295.1 3.1 collective-permute-done.15
  299.7 3.2 collective-permute-done.21
  308.1 2.6 collective-permute-done.45
  310.7 6.0 %collective-permute-done.59 = bf16[128,2048]{1,0:T(8,128)(2,1)S(1)} collective-permute-done((bf16[128,2048]{1,0:T(8,128)(2,1)S(1)}, bf16[128,2048]{1,0:T(8,128)(2,1)S(1)}, u32[]{:S(2)}, u32[]{:S(2)}) %collective-permute-start.59) | collective-permute-done | bytes 524320 | tf_op jit(solution)/shard_map/ppermute | solution.py:32
  317.9 3.3 convert_element_type.179
  321.2 3.8 %slice_bitcast_fusion = (f32[1,704,1024]{2,1,0:T(8,128)}, f32[1,1024,704]{1,2,0:T(8,128)}, f32[1,1024,704]{1,2,0:T(8,128)}) fusion(f32[1024,2112]{0,1:T(8,128)S(1)} %convert_element_type.179), kind=kLoop, calls=%fused_computation.14 | loop fusion | bytes 17301504 | tf_op jit(solution)/shard_map/broadcast_in_dim | solution.py:130
  (279 shorter events, 114.2 us)
Async XLA Ops:
  7.2 310.7 %reduce-scatter.2.cloned.1.call-start = ((), (), s32[]{:S(2)}) async-start(), calls=%async_computation.1 | async-start | bytes 12976128 | tf_op jit(solution)/shard_map/reduce_scatter | solution.py:122
  7.2 124.1 %collective-permute-start.33 = (bf16[128,2048]{1,0:T(8,128)(2,1)}, bf16[128,2048]{1,0:T(8,128)(2,1)}, u32[]{:S(2)}, u32[]{:S(2)}) collective-permute-start(bf16[128,2048]{1,0:T(8,128)(2,1)} %param.14), channel_id=1, source_target_pairs={{0,4},{1,5},{2,6},{3,7},{4,0},{5,1},{6,2},{7,3},{8,12},{9,13},{10,... | collective-permute-start | bytes 1572872 | tf_op jit(solution)/shard_map/ppermute | solution.py:32
  10.3 123.8 %collective-permute-start.37 = (bf16[128,2048]{1,0:T(8,128)(2,1)}, bf16[128,2048]{1,0:T(8,128)(2,1)}, u32[]{:S(2)}, u32[]{:S(2)}) collective-permute-start(bf16[128,2048]{1,0:T(8,128)(2,1)} %param.14), channel_id=1, source_target_pairs={{0,8},{1,9},{2,10},{3,11},{4,12},{5,13},{6,14},{7,15},{8,0},{9,1},... | collective-permute-start | bytes 1572872 | tf_op jit(solution)/shard_map/ppermute | solution.py:32
  12.9 124.9 %collective-permute-start.3 = (bf16[128,2048]{1,0:T(8,128)(2,1)}, bf16[128,2048]{1,0:T(8,128)(2,1)}, u32[]{:S(2)}, u32[]{:S(2)}) collective-permute-start(bf16[128,2048]{1,0:T(8,128)(2,1)} %param.8), channel_id=1, source_target_pairs={{0,4},{1,5},{2,6},{3,7},{4,0},{5,1},{6,2},{7,3},{8,12},{9,13},{10,... | collective-permute-start | bytes 1572872 | tf_op jit(solution)/shard_map/ppermute | solution.py:32
  13.4 126.5 %collective-permute-start.7 = (bf16[128,2048]{1,0:T(8,128)(2,1)}, bf16[128,2048]{1,0:T(8,128)(2,1)}, u32[]{:S(2)}, u32[]{:S(2)}) collective-permute-start(bf16[128,2048]{1,0:T(8,128)(2,1)} %param.8), channel_id=1, source_target_pairs={{0,8},{1,9},{2,10},{3,11},{4,12},{5,13},{6,14},{7,15},{8,0},{9,1},... | collective-permute-start | bytes 1572872 | tf_op jit(solution)/shard_map/ppermute | solution.py:32
  137.8 18.9 %collective-permute-start.38 = (bf16[32,2048]{1,0:T(8,128)(2,1)S(1)}, bf16[32,2048]{1,0:T(8,128)(2,1)S(1)}, u32[]{:S(2)}, u32[]{:S(2)}) collective-permute-start(bf16[32,2048]{1,0:T(8,128)(2,1)S(1)} %get-tuple-element.55), channel_id=1, source_target_pairs={{0,1},{1,0},{2,3},{3,2},{4,5},{5,4},{6,7},{7,6},{8,9},{9,8},{10,11... | collective-permute-start | bytes 393224 | tf_op jit(solution)/shard_map/ppermute | solution.py:32
  139.9 19.8 %collective-permute-start.39 = (bf16[32,2048]{1,0:T(8,128)(2,1)S(1)}, bf16[32,2048]{1,0:T(8,128)(2,1)S(1)}, u32[]{:S(2)}, u32[]{:S(2)}) collective-permute-start(bf16[32,2048]{1,0:T(8,128)(2,1)S(1)} %get-tuple-element.54), channel_id=1, source_target_pairs={{0,2},{1,3},{2,0},{3,1},{4,6},{5,7},{6,4},{7,5},{8,10},{9,11},{10,... | collective-permute-start | bytes 393224 | tf_op jit(solution)/shard_map/ppermute | solution.py:32
  142.0 17.7 %collective-permute-start.40 = (bf16[32,2048]{1,0:T(8,128)(2,1)S(1)}, bf16[32,2048]{1,0:T(8,128)(2,1)S(1)}, u32[]{:S(2)}, u32[]{:S(2)}) collective-permute-start(bf16[32,2048]{1,0:T(8,128)(2,1)S(1)} %get-tuple-element.53), channel_id=1, source_target_pairs={{0,3},{1,2},{2,1},{3,0},{4,7},{5,6},{6,5},{7,4},{8,11},{9,10},{10,... | collective-permute-start | bytes 393224 | tf_op jit(solution)/shard_map/ppermute | solution.py:32
  150.7 11.1 %collective-permute-start.8 = (bf16[32,2048]{1,0:T(8,128)(2,1)S(1)}, bf16[32,2048]{1,0:T(8,128)(2,1)S(1)}, u32[]{:S(2)}, u32[]{:S(2)}) collective-permute-start(bf16[32,2048]{1,0:T(8,128)(2,1)S(1)} %get-tuple-element.67), channel_id=1, source_target_pairs={{0,1},{1,0},{2,3},{3,2},{4,5},{5,4},{6,7},{7,6},{8,9},{9,8},{10,11... | collective-permute-start | bytes 393224 | tf_op jit(solution)/shard_map/ppermute | solution.py:32
  159.8 15.0 %collective-permute-start.11 = (bf16[128,2048]{1,0:T(8,128)(2,1)}, bf16[128,2048]{1,0:T(8,128)(2,1)S(1)}, u32[]{:S(2)}, u32[]{:S(2)}) collective-permute-start(bf16[128,2048]{1,0:T(8,128)(2,1)} %collective-permute-done.7), channel_id=1, source_target_pairs={{0,4},{1,5},{2,6},{3,7},{4,0},{5,1},{6,2},{7,3},{8,12},{9,13},{10,... | collective-permute-start | bytes 1572872 | tf_op jit(solution)/shard_map/ppermute | solution.py:32
  169.5 20.0 %collective-permute-start.42 = (bf16[32,2048]{1,0:T(8,128)(2,1)S(1)}, bf16[32,2048]{1,0:T(8,128)(2,1)S(1)}, u32[]{:S(2)}, u32[]{:S(2)}) collective-permute-start(bf16[32,2048]{1,0:T(8,128)(2,1)S(1)} %get-tuple-element.52), channel_id=1, source_target_pairs={{0,1},{1,0},{2,3},{3,2},{4,5},{5,4},{6,7},{7,6},{8,9},{9,8},{10,11... | collective-permute-start | bytes 393224 | tf_op jit(solution)/shard_map/ppermute | solution.py:32
  170.1 19.4 %collective-permute-start.43 = (bf16[32,2048]{1,0:T(8,128)(2,1)S(1)}, bf16[32,2048]{1,0:T(8,128)(2,1)S(1)}, u32[]{:S(2)}, u32[]{:S(2)}) collective-permute-start(bf16[32,2048]{1,0:T(8,128)(2,1)S(1)} %get-tuple-element.51), channel_id=1, source_target_pairs={{0,2},{1,3},{2,0},{3,1},{4,6},{5,7},{6,4},{7,5},{8,10},{9,11},{10,... | collective-permute-start | bytes 393224 | tf_op jit(solution)/shard_map/ppermute | solution.py:32
  170.1 19.5 %collective-permute-start.44 = (bf16[32,2048]{1,0:T(8,128)(2,1)S(1)}, bf16[32,2048]{1,0:T(8,128)(2,1)S(1)}, u32[]{:S(2)}, u32[]{:S(2)}) collective-permute-start(bf16[32,2048]{1,0:T(8,128)(2,1)S(1)} %get-tuple-element.50), channel_id=1, source_target_pairs={{0,3},{1,2},{2,1},{3,0},{4,7},{5,6},{6,5},{7,4},{8,11},{9,10},{10,... | collective-permute-start | bytes 393224 | tf_op jit(solution)/shard_map/ppermute | solution.py:32
  207.9 50.2 %collective-permute-start.27 = (bf16[32,2048]{1,0:T(8,128)(2,1)}, bf16[32,2048]{1,0:T(8,128)(2,1)S(1)}, u32[]{:S(2)}, u32[]{:S(2)}) collective-permute-start(bf16[32,2048]{1,0:T(8,128)(2,1)} %get-tuple-element.35), channel_id=1, source_target_pairs={{0,3},{1,2},{2,1},{3,0},{4,7},{5,6},{6,5},{7,4},{8,11},{9,10},{10,... | collective-permute-start | bytes 393224 | tf_op jit(solution)/shard_map/ppermute | solution.py:32
  207.9 50.2 %collective-permute-start.26 = (bf16[32,2048]{1,0:T(8,128)(2,1)}, bf16[32,2048]{1,0:T(8,128)(2,1)S(1)}, u32[]{:S(2)}, u32[]{:S(2)}) collective-permute-start(bf16[32,2048]{1,0:T(8,128)(2,1)} %get-tuple-element.36), channel_id=1, source_target_pairs={{0,2},{1,3},{2,0},{3,1},{4,6},{5,7},{6,4},{7,5},{8,10},{9,11},{10,... | collective-permute-start | bytes 393224 | tf_op jit(solution)/shard_map/ppermute | solution.py:32
  209.7 50.0 %collective-permute-start.25 = (bf16[32,2048]{1,0:T(8,128)(2,1)}, bf16[32,2048]{1,0:T(8,128)(2,1)}, u32[]{:S(2)}, u32[]{:S(2)}) collective-permute-start(bf16[32,2048]{1,0:T(8,128)(2,1)} %get-tuple-element.37), channel_id=1, source_target_pairs={{0,1},{1,0},{2,3},{3,2},{4,5},{5,4},{6,7},{7,6},{8,9},{9,8},{10,11... | collective-permute-start | bytes 393224 | tf_op jit(solution)/shard_map/ppermute | solution.py:32
  211.4 55.7 %collective-permute-start.20 = (bf16[32,2048]{1,0:T(8,128)(2,1)}, bf16[32,2048]{1,0:T(8,128)(2,1)S(1)}, u32[]{:S(2)}, u32[]{:S(2)}) collective-permute-start(bf16[32,2048]{1,0:T(8,128)(2,1)} %get-tuple-element.43), channel_id=1, source_target_pairs={{0,3},{1,2},{2,1},{3,0},{4,7},{5,6},{6,5},{7,4},{8,11},{9,10},{10,... | collective-permute-start | bytes 393224 | tf_op jit(solution)/shard_map/ppermute | solution.py:32
  211.4 57.4 %collective-permute-start.19 = (bf16[32,2048]{1,0:T(8,128)(2,1)}, bf16[32,2048]{1,0:T(8,128)(2,1)}, u32[]{:S(2)}, u32[]{:S(2)}) collective-permute-start(bf16[32,2048]{1,0:T(8,128)(2,1)} %get-tuple-element.44), channel_id=1, source_target_pairs={{0,2},{1,3},{2,0},{3,1},{4,6},{5,7},{6,4},{7,5},{8,10},{9,11},{10,... | collective-permute-start | bytes 393224 | tf_op jit(solution)/shard_map/ppermute | solution.py:32
  266.7 15.9 %collective-permute-start.28 = (bf16[128,2048]{1,0:T(8,128)(2,1)S(1)}, bf16[128,2048]{1,0:T(8,128)(2,1)S(1)}, u32[]{:S(2)}, u32[]{:S(2)}) collective-permute-start(bf16[128,2048]{1,0:T(8,128)(2,1)S(1)} %fusion.24), channel_id=1, source_target_pairs={{0,4},{1,5},{2,6},{3,7},{4,0},{5,1},{6,2},{7,3},{8,12},{9,13},{10,... | collective-permute-start | bytes 1572872 | tf_op jit(solution)/shard_map/ppermute | solution.py:32
  269.7 20.0 %collective-permute-start.58 = (bf16[128,2048]{1,0:T(8,128)(2,1)S(1)}, bf16[128,2048]{1,0:T(8,128)(2,1)S(1)}, u32[]{:S(2)}, u32[]{:S(2)}) collective-permute-start(bf16[128,2048]{1,0:T(8,128)(2,1)S(1)} %fusion.26), channel_id=1, source_target_pairs={{0,4},{1,5},{2,6},{3,7},{4,0},{5,1},{6,2},{7,3},{8,12},{9,13},{10,... | collective-permute-start | bytes 1572872 | tf_op jit(solution)/shard_map/ppermute | solution.py:32
  287.7 15.2 %collective-permute-start.21 = (bf16[128,2048]{1,0:T(8,128)(2,1)S(1)}, bf16[128,2048]{1,0:T(8,128)(2,1)S(1)}, u32[]{:S(2)}, u32[]{:S(2)}) collective-permute-start(bf16[128,2048]{1,0:T(8,128)(2,1)S(1)} %fusion.23), channel_id=1, source_target_pairs={{0,4},{1,5},{2,6},{3,7},{4,0},{5,1},{6,2},{7,3},{8,12},{9,13},{10,... | collective-permute-start | bytes 1572872 | tf_op jit(solution)/shard_map/ppermute | solution.py:32
  287.7 22.9 %collective-permute-start.51 = (bf16[128,2048]{1,0:T(8,128)(2,1)S(1)}, bf16[128,2048]{1,0:T(8,128)(2,1)S(1)}, u32[]{:S(2)}, u32[]{:S(2)}) collective-permute-start(bf16[128,2048]{1,0:T(8,128)(2,1)S(1)} %fusion.25), channel_id=1, source_target_pairs={{0,4},{1,5},{2,6},{3,7},{4,0},{5,1},{6,2},{7,3},{8,12},{9,13},{10,... | collective-permute-start | bytes 1572872 | tf_op jit(solution)/shard_map/ppermute | solution.py:32
  289.7 16.0 %collective-permute-start.29 = (bf16[128,2048]{1,0:T(8,128)(2,1)S(1)}, bf16[128,2048]{1,0:T(8,128)(2,1)S(1)}, u32[]{:S(2)}, u32[]{:S(2)}) collective-permute-start(bf16[128,2048]{1,0:T(8,128)(2,1)S(1)} %fusion.21), channel_id=1, source_target_pairs={{0,8},{1,9},{2,10},{3,11},{4,12},{5,13},{6,14},{7,15},{8,0},{9,1},... | collective-permute-start | bytes 1572872 | tf_op jit(solution)/shard_map/ppermute | solution.py:32
  290.1 26.6 %collective-permute-start.59 = (bf16[128,2048]{1,0:T(8,128)(2,1)S(1)}, bf16[128,2048]{1,0:T(8,128)(2,1)S(1)}, u32[]{:S(2)}, u32[]{:S(2)}) collective-permute-start(bf16[128,2048]{1,0:T(8,128)(2,1)S(1)} %fusion.19), channel_id=1, source_target_pairs={{0,8},{1,9},{2,10},{3,11},{4,12},{5,13},{6,14},{7,15},{8,0},{9,1},... | collective-permute-start | bytes 1572872 | tf_op jit(solution)/shard_map/ppermute | solution.py:32
  (78 other events, 1179.5 us)
Sparse Core Ops, SparseCore 0:
  201.9 13.3 reduce-scatter.1

commit v2 on v1

v2 whole, which is shorter than its diff:
```python
import functools

import jax
import jax.numpy as jnp
from jax import lax
from jax.experimental import pallas as pl
from jax.experimental.pallas import tpu as pltpu
from jax.sharding import PartitionSpec as P

BF16 = jnp.bfloat16
F32 = jnp.float32
LANES = 128
STRIP = 512
VMEM = pl.BlockSpec(memory_space=pltpu.VMEM)
PARAMS = pltpu.CompilerParams(vmem_limit_bytes=40 * 1024 * 1024)


def pieces(value):
    out = []
    for _ in range(3):
        part = lax.reduce_precision(value, 8, 7)
        out.append(part.astype(BF16))
        value = value - part
    return out


def local_call(kernel, outs, args, flops):
    size = sum(x.size * x.dtype.itemsize for x in (*outs, *args))
    return pl.pallas_call(
        kernel,
        out_shape=outs,
        in_specs=[VMEM] * len(args),
        out_specs=[VMEM] * len(outs),
        compiler_params=PARAMS,
        cost_estimate=pl.CostEstimate(flops=flops, bytes_accessed=size, transcendentals=0),
    )(*args)


def strips(width):
    return [(c, min(c + STRIP, width)) for c in range(0, width, STRIP)]


def table_kernel(plane, capacity, top, count, *refs):
    metas, (me_ref,), tables = refs[:count], refs[count : count + 1], refs[count + 1 :]
    me = me_ref[0]
    tok = metas[0].shape[0]
    span = 2 * capacity
    wide = plane * span
    slot = lax.broadcasted_iota(jnp.int32, (1, wide), 1)
    expert = (me - lax.rem(me, plane)) + slot // span + 1
    member_of = lax.rem(slot, span) // capacity
    place = lax.rem(slot, capacity)
    row = lax.broadcasted_iota(jnp.int32, (tok, tok), 0)
    column = lax.broadcasted_iota(jnp.int32, (tok, tok), 1)
    earlier = jnp.where(row > column, 1.0, 0.0).astype(BF16)
    for b in range(count):
        ids = metas[b][:, :top].astype(F32)
        member = jnp.zeros((tok, wide), F32)
        for k in range(top):
            member += jnp.where(ids[:, k : k + 1] == expert.astype(F32), 1.0, 0.0)
        rank = jnp.dot(earlier, member.astype(BF16), preferred_element_type=F32)
        mine = jnp.where(member_of == b % 2, 1.0, 0.0)
        held = jnp.where(rank == place.astype(F32), member * mine, 0.0)
        tables[b // 2][(b % 2) * tok : (b % 2 + 1) * tok, :] = held.astype(BF16)


def pick_kernel(n_out, with_meta, *refs):
    table_ref, first, second = refs[:3]
    parts = refs[len(refs) - n_out :]
    table = table_ref[...]
    rows = parts[0].shape[0]
    width = first.shape[1]
    sources = [(c, e, (first, second), c) for c, e in strips(width)]
    if with_meta:
        sources.append((0, LANES, (refs[3], refs[4]), width))
    for c, e, (one, two), at in sources:
        block = jnp.concatenate([one[:, c:e], two[:, c:e]], 0)
        got = lax.dot_general(
            table, block, (((0,), (0,)), ((), ())), preferred_element_type=F32
        ).astype(BF16)
        for i in range(n_out):
            parts[i][:, at : at + e - c] = got[i * rows : (i + 1) * rows]


def info_kernel(top, got_ref, me_ref, info_ref):
    number = (me_ref[0] + 1).astype(F32)
    tail = got_ref[...].astype(F32)
    lane = lax.broadcasted_iota(jnp.int32, tail.shape, 1)
    out = jnp.zeros_like(tail)
    total = jnp.zeros((tail.shape[0], 1), F32)
    for k in range(top):
        named = jnp.where(tail[:, k : k + 1] == number, 1.0, 0.0)
        weight = tail[:, top + k : top + k + 1]
        for term in (1, 2):
            weight = weight + tail[:, top + term * top + k : top + term * top + k + 1]
        total += named * weight
        out = jnp.where(lane == k + 1, named, out)
    info_ref[...] = jnp.where(lane == 0, total, out)


def combine_kernel(table_ref, back_ref, out_ref):
    table = table_ref[...]
    for c, e in strips(out_ref.shape[1]):
        got = jnp.dot(table, back_ref[:, c:e], preferred_element_type=F32)
        out_ref[:, c:e] = got.astype(out_ref.dtype)


def on_device(tokens, expert_ids, gate_prob, w_gate, w_up, w_down, d_mixed):
    tok, feature = tokens.shape
    top = expert_ids.shape[1]
    experts = lax.axis_size("expert")
    capacity = max(2, 2 * tok * top // experts)
    planes = experts * capacity // tok
    plane = experts // planes
    me = lax.axis_index("expert")
    me_arr = me[None]
    bits = [1 << b for b in range(planes.bit_length() - 1)]
    groups = [[j, j + planes // 2] for j in range(planes // 2)]
    plane_sets = [[z * plane + p for p in range(plane)] for z in range(planes)]
    rows = 2 * tok

    def hop(value, flip):
        pairs = [(e, e ^ flip) for e in range(experts)]
        return lax.ppermute(value, "expert", pairs)

    def in_plane(value):
        shaped = value.reshape(plane, 2 * capacity, value.shape[1])
        got = lax.all_to_all(
            shaped, "expert", 0, 0, axis_index_groups=plane_sets, tiled=True
        )
        return got.reshape(value.shape)

    def after(value, *earlier):
        return lax.optimization_barrier((value, *earlier))

    shape = jax.ShapeDtypeStruct

    def along_z(value):
        held = {0: value}
        for bit in reversed(bits):
            for j in sorted(held):
                held[j ^ bit] = hop(held[j], bit * plane)
        return held

    blank = jnp.zeros((tok, LANES - 4 * top), BF16)
    meta = jnp.concatenate([(expert_ids + 1).astype(BF16), *pieces(gate_prob), blank], 1)
    held_x, held_m = {0: tokens}, {0: meta}
    for bit in reversed(bits):
        for j in sorted(held_x):
            held_x[j ^ bit] = hop(held_x[j], bit * plane)
        for j in sorted(held_m):
            held_m[j ^ bit] = hop(held_m[j], bit * plane)
        if bit == bits[-1]:
            held_x[bit], held_m[bit] = after(held_x[bit], held_m[bit])
    top_bit = bits[-1]
    d_late, held_x[top_bit] = after(d_mixed, held_x[top_bit])
    held_d = along_z(d_late)

    tables = [
        local_call(
            functools.partial(table_kernel, plane, capacity, top, 2),
            [shape((rows, rows), BF16)],
            [held_m[group[0]], held_m[group[1]], me_arr],
            4 * rows * rows * tok,
        )[0]
        for group in groups
    ]

    def dispatch(g, held, extra):
        group = groups[g]
        args = [tables[g], held[group[0]], held[group[1]]]
        width = feature
        if extra is not None:
            args += [extra[group[0]], extra[group[1]]]
            width += LANES
        (picked,) = local_call(
            functools.partial(pick_kernel, 1, extra is not None),
            [shape((rows, width), BF16)],
            args,
            2 * rows * rows * width,
        )
        return in_plane(picked)

    def combine(g, value):
        back = in_plane(value)
        (both,) = local_call(
            combine_kernel,
            [shape(back.shape, F32 if g == 0 else BF16)],
            [tables[g], back],
            2 * rows * rows * back.shape[1],
        )
        return both

    def back_along_z(total):
        for bit in bits[:-1]:
            for g in sorted(total, reverse=True):
                if g & bit:
                    came = hop(total.pop(g).astype(BF16), bit * plane)
                    total[g ^ bit] = total[g ^ bit] + came.astype(F32)
        came = hop(total[0][tok:].astype(BF16), top_bit * plane)
        return total[0][:tok] + came.astype(F32)

    gate_matrix, up_matrix, down_matrix = w_gate[0], w_up[0], w_down[0]
    hidden_units = gate_matrix.shape[1]
    contract_rows = (((0,), (0,)), ((), ()))
    contract_cols = (((1,), (1,)), ((), ()))
    order = range(len(groups))

    x_rows, info, gate_pre, up_pre, sig_gate, silu_gate, hidden = {}, {}, {}, {}, {}, {}, {}
    for g in order:
        got = dispatch(g, held_x, held_m)
        x_rows[g] = got[:, :feature]
        info[g] = pl.pallas_call(
            functools.partial(info_kernel, top),
            out_shape=shape((rows, LANES), F32),
            grid=(1,),
            in_specs=[
                pl.BlockSpec((rows, LANES), lambda n: (0, feature // LANES)),
                pl.BlockSpec(memory_space=pltpu.SMEM),
            ],
            out_specs=pl.BlockSpec((rows, LANES), lambda n: (0, 0)),
            compiler_params=PARAMS,
        )(got, me_arr)
        gate_pre[g] = jnp.dot(x_rows[g], gate_matrix, preferred_element_type=F32)
        up_pre[g] = jnp.dot(x_rows[g], up_matrix, preferred_element_type=F32)
        sig_gate[g] = jax.nn.sigmoid(gate_pre[g])
        silu_gate[g] = gate_pre[g] * sig_gate[g]
        hidden[g] = (silu_gate[g] * up_pre[g]).astype(BF16)
    expert_out, y_scaled, total = {}, {}, {}
    for g in reversed(order):
        expert_out[g] = jnp.dot(hidden[g], down_matrix, preferred_element_type=F32).astype(BF16)
        y_scaled[g] = (info[g][:, :1] * expert_out[g].astype(F32)).astype(BF16)
    info[0], *held_y = after(info[0], *[y_scaled[g] for g in order])
    for g in reversed(order):
        total[g] = combine(g, held_y[g])
    last = groups[-1][0]
    held_d[last], total[order[-1]] = after(held_d[last], total[order[-1]])
    mixed = back_along_z(total).astype(BF16)

    dy_rows, grad_pre_gate, grad_pre_up, back_rows = {}, {}, {}, {}
    for g in order:
        d_rows = dispatch(g, held_d, None)
        dy_rows[g] = (info[g][:, :1] * d_rows.astype(F32)).astype(BF16)
        back_hidden = lax.dot_general(
            dy_rows[g], down_matrix, contract_cols, preferred_element_type=F32
        )
        d_silu = sig_gate[g] * (1.0 + gate_pre[g] * (1.0 - sig_gate[g]))
        grad_pre_gate[g] = (back_hidden * up_pre[g] * d_silu).astype(BF16)
        grad_pre_up[g] = (back_hidden * silu_gate[g]).astype(BF16)
        expert_dx = (
            lax.dot_general(
                grad_pre_gate[g], gate_matrix, contract_cols, preferred_element_type=F32
            )
            + lax.dot_general(
                grad_pre_up[g], up_matrix, contract_cols, preferred_element_type=F32
            )
        ).astype(BF16)
        slot_grad = jnp.sum(d_rows.astype(F32) * expert_out[g].astype(F32), 1, keepdims=True)
        grad_cols = jnp.concatenate(pieces(info[g][:, 1 : 1 + top] * slot_grad), 1)
        blank = jnp.zeros((rows, LANES - 3 * top), BF16)
        back_rows[g] = jnp.concatenate([expert_dx, grad_cols, blank], 1)
    joined = after(
        back_rows[0],
        back_rows[1],
        *[jnp.concatenate([part[g] for g in order], 0) for part in (grad_pre_gate, grad_pre_up)],
    )
    back_rows[0], back_rows[1], all_gate, all_up = joined
    total = {}
    for g in reversed(order):
        total[g] = combine(g, back_rows[g])
    result = back_along_z(total)
    d_tokens = result[:, :feature].astype(BF16)
    d_gate = functools.reduce(
        lambda a, b: a + b,
        [result[:, feature + n * top : feature + (n + 1) * top] for n in range(3)],
    )

    all_x, all_dy, all_hidden = (
        jnp.concatenate([part[g] for g in order], 0) for part in (x_rows, dy_rows, hidden)
    )
    term_gate = lax.dot_general(all_gate, all_x, contract_rows, preferred_element_type=F32)
    term_up = lax.dot_general(all_up, all_x, contract_rows, preferred_element_type=F32)
    term_down = lax.dot_general(all_hidden, all_dy, contract_rows, preferred_element_type=F32)
    summed = lax.psum_scatter(
        jnp.concatenate([term_gate, term_up, term_down], 0).astype(BF16),
        "dp",
        scatter_dimension=1,
        tiled=True,
    )
    grad_gate = summed[:hidden_units].astype(F32).T[None]
    grad_up = summed[hidden_units : 2 * hidden_units].astype(F32).T[None]
    grad_down = summed[2 * hidden_units :].astype(F32)[None]
    return (mixed, d_tokens, d_gate, grad_gate, grad_up, grad_down)


def solution(mesh):
    in_specs = (
        P(("dp", "expert"), None),
        P(("dp", "expert"), None),
        P(("dp", "expert"), None),
        P("expert", None, None),
        P("expert", None, None),
        P("expert", None, None),
        P(("dp", "expert"), None),
    )
    out_specs = (
        P(("dp", "expert"), None),
        P(("dp", "expert"), None),
        P(("dp", "expert"), None),
        P("expert", "dp", None),
        P("expert", "dp", None),
        P("expert", None, "dp"),
    )
    return jax.shard_map(
        on_device, mesh=mesh, in_specs=in_specs, out_specs=out_specs, check_vma=False
    )
```

time: 332 us -> 301 us (0.907)
  blocking collectives: 114 us -> 0 us
  waiting for transfers between devices: 76.1 us -> 127 us
  other arithmetic: 11.9 us -> 28.8 us
  Pallas kernels: 0 us -> 14.6 us
  starting transfers between devices: 64.2 us -> 51 us
  local copies, waits for them, and re-layouts: 16.5 us -> 28 us
    all_gather x2 -> x0, blocking collectives: 114 us -> none  [the longest x1 74.7 us: on_device(): meta_all = lax.all_gather(meta, 'expert')]
    ppermute x60 -> x13, starting transfers between devices: 64.2 us -> 17.3 us  [hop(): return lax.ppermute(value, 'expert', pairs)]
    all_to_all x0 -> x8, waiting for transfers between devices: none -> 40.7 us  [in_plane(): lax.all_to_all(shaped, 'expert', 0, 0, axis_index_groups=plane_sets, tile...]
    all_to_all x0 -> x8, starting transfers between devices: none -> 33.7 us  [in_plane(): lax.all_to_all(shaped, 'expert', 0, 0, axis_index_groups=plane_sets, tile...]
    pallas_call x0 -> x12, Pallas kernels: none -> 14.6 us  [the longest x10 12.2 us: local_call(): pl.pallas_call(kernel, out_shape=outs, in_specs=[VMEM] * len(args), out_s...]
    ppermute x60 -> x13, waiting for transfers between devices: 76.1 us -> 86.1 us  [hop(): return lax.ppermute(value, 'expert', pairs)]
    convert_element_type x2 -> x9, other arithmetic: 3.96 us -> 13.2 us  [the longest x4 9.04 us: on_device(): dy_rows[g] = (info[g][:, :1] * d_rows.astype(F32)).astype(BF16)]
    concatenate x2 -> x3, local copies, waits for them, and re-layouts: 0.02 us -> 7.01 us  [the longest x2 6.09 us: on_device(): back_rows[g] = jnp.concatenate([expert_dx, grad_cols, blank], 1)]
  transfers between devices with their start and end apart: 61 -> 22, of which waited for: 25 -> 12; matrix products, arithmetic and copies ran while one was open for 13% -> 17% of each run, Pallas kernels for 0% -> 4%
where the time goes in v2:
time: 301 us; the launch traced here: 299 us
  waiting for transfers between devices  127 us (42%)
  starting transfers between devices  51 us (17%)
  matrix products  35.5 us (12%)
  other arithmetic  28.8 us (10%)
  local copies, waits for them, and re-layouts  28 us (9%)
  Pallas kernels  14.6 us (5%)
  between operations  14.6 us (5%)
    ppermute x13, waiting for transfers between devices, hop(): return lax.ppermute(value, 'expert', pairs)  86.1 us
    all_to_all x8, waiting for transfers between devices, in_plane(): lax.all_to_all(shaped, 'expert', 0, 0, axis_index_groups=plane_sets, tile...  40.7 us
    all_to_all x8, starting transfers between devices, in_plane(): lax.all_to_all(shaped, 'expert', 0, 0, axis_index_groups=plane_sets, tile...  33.7 us
    ppermute x13, starting transfers between devices, hop(): return lax.ppermute(value, 'expert', pairs)  17.3 us
    unnamed x78, local copies, waits for them, and re-layouts  13.1 us
    pallas_call x10, Pallas kernels, local_call(): pl.pallas_call(kernel, out_shape=outs, in_specs=[VMEM] * len(args), out_s...  12.2 us
    convert_element_type x4, other arithmetic, on_device(): dy_rows[g] = (info[g][:, :1] * d_rows.astype(F32)).astype(BF16)  9.04 us
    dot_general x2, matrix products, on_device(): gate_pre[g] = jnp.dot(x_rows[g], gate_matrix, preferred_element_type=F32)  6.47 us
  transfers between devices with their start and end apart: 22, of which 12 were waited for; matrix products, arithmetic and copies ran while one was open for 17% of the time, Pallas kernels for 4%

profile of v2, /device:TPU:0, one launch (start us, length us, event | category | flops | bytes accessed | tf_op | source)
XLA Modules:
  0.0 299.4 jit_solution(15044525625459251362)
XLA Ops:
  7.2 4.1 %collective-permute-start = (bf16[128,2048]{1,0:T(8,128)(2,1)}, bf16[128,2048]{1,0:T(8,128)(2,1)S(1)}, u32[]{:S(2)}, u32[]{:S(2)}) collective-permute-start(bf16[128,2048]{1,0:T(8,128)(2,1)} %refs_1_.1), channel_id=1, source_target_pairs={{0,8},{1,9},{2,10},{3,11},{4,12},{5,13},{6,14},{7,15},{8,0},{9,1},... | collective-permute-start | bytes 1572872 | tf_op jit(solution)/shard_map/ppermute | solution.py:124
  16.8 19.2 %collective-permute-done.1.refs_1_.refs_4_ = bf16[128,128]{1,0:T(8,128)(2,1)S(1)} collective-permute-done((bf16[128,128]{1,0:T(8,128)(2,1)S(1)}, bf16[128,128]{1,0:T(8,128)(2,1)S(1)}, u32[]{:S(2)}, u32[]{:S(2)}) %collective-permute-start.1) | collective-permute-done | bytes 32800 | tf_op jit(solution)/shard_map/ppermute | solution.py:124
  40.7 4.2 %all-to-all-start = ((bf16[4,64,2176]{2,1,0:T(8,128)(2,1)}), bf16[4,64,2176]{2,1,0:T(8,128)(2,1)}, u32[]{:S(2)}, u32[]{:S(2)}) async-start(bf16[4,64,2176]{2,1,0:T(8,128)(2,1)} %bitcast.101), calls=%async_computation | async-start | bytes 2228224 | tf_op jit(solution)/shard_map/all_to_all | solution.py:128
  45.1 4.1 %collective-permute-start.4 = (bf16[128,2048]{1,0:T(8,128)(2,1)}, bf16[128,2048]{1,0:T(8,128)(2,1)S(1)}, u32[]{:S(2)}, u32[]{:S(2)}) collective-permute-start(bf16[128,2048]{1,0:T(8,128)(2,1)} %refs_1_.1), channel_id=1, source_target_pairs={{0,4},{1,5},{2,6},{3,7},{4,0},{5,1},{6,2},{7,3},{8,12},{9,13},{10,... | collective-permute-start | bytes 1572872 | tf_op jit(solution)/shard_map/ppermute | solution.py:124
  51.2 31.7 %collective-permute-done.2.refs_0_.refs_3_ = bf16[128,128]{1,0:T(8,128)(2,1)S(1)} collective-permute-done((bf16[128,128]{1,0:T(8,128)(2,1)S(1)}, bf16[128,128]{1,0:T(8,128)(2,1)S(1)}, u32[]{:S(2)}, u32[]{:S(2)}) %collective-permute-start.2) | collective-permute-done | bytes 32800 | tf_op jit(solution)/shard_map/ppermute | solution.py:124
  90.4 4.3 %all-to-all-start.1 = ((bf16[4,64,2176]{2,1,0:T(8,128)(2,1)}), bf16[4,64,2176]{2,1,0:T(8,128)(2,1)}, u32[]{:S(2)}, u32[]{:S(2)}) async-start(bf16[4,64,2176]{2,1,0:T(8,128)(2,1)} %bitcast.102), calls=%async_computation.1 | async-start | bytes 2228224 | tf_op jit(solution)/shard_map/all_to_all | solution.py:128
  95.9 3.2 %fusion.22 = f32[256,704]{0,1:T(8,128)S(1)} fusion(bf16[1,2048,704]{1,2,0:T(8,128)(2,1)} %param.10, bf16[256,2176]{1,0:T(8,128)(2,1)} %bitcast.2.got_ref), kind=kOutput, calls=%fused_computation.26 | convolution fusion | flops 738197504 | bytes 4653056 | tf_op jit(solution)/shard_map/dot_general | solution.py:224
  107.9 4.3 %all-to-all-start.4 = ((bf16[4,64,2048]{2,1,0:T(8,128)(2,1)}), bf16[4,64,2048]{2,1,0:T(8,128)(2,1)}, u32[]{:S(2)}, u32[]{:S(2)}) async-start(bf16[4,64,2048]{2,1,0:T(8,128)(2,1)} %bitcast.104), calls=%async_computation.4 | async-start | bytes 2097152 | tf_op jit(solution)/shard_map/all_to_all | solution.py:128
  113.4 3.2 %fusion.20 = f32[256,704]{0,1:T(8,128)S(1)} fusion(bf16[1,2048,704]{1,2,0:T(8,128)(2,1)} %param.10, bf16[256,2176]{1,0:T(8,128)(2,1)} %bitcast.7.got_ref), kind=kOutput, calls=%fused_computation.24 | convolution fusion | flops 738197504 | bytes 4653056 | tf_op jit(solution)/shard_map/dot_general | solution.py:224
  125.2 4.2 %all-to-all-start.3 = ((bf16[4,64,2048]{2,1,0:T(8,128)(2,1)}), bf16[4,64,2048]{2,1,0:T(8,128)(2,1)}, u32[]{:S(2)}, u32[]{:S(2)}) async-start(bf16[4,64,2048]{2,1,0:T(8,128)(2,1)} %bitcast.107), calls=%async_computation.3 | async-start | bytes 2097152 | tf_op jit(solution)/shard_map/all_to_all | solution.py:128
  135.9 6.7 %all-to-all-done.3 = bf16[4,64,2048]{2,1,0:T(8,128)(2,1)} async-done(((bf16[4,64,2048]{2,1,0:T(8,128)(2,1)}), bf16[4,64,2048]{2,1,0:T(8,128)(2,1)}, u32[]{:S(2)}, u32[]{:S(2)}) %all-to-all-start.3) | async-done | bytes 1048608 | tf_op jit(solution)/shard_map/all_to_all | solution.py:128
  147.9 4.4 %all-to-all-start.5 = ((bf16[4,64,2048]{2,1,0:T(8,128)(2,1)}), bf16[4,64,2048]{2,1,0:T(8,128)(2,1)}, u32[]{:S(2)}, u32[]{:S(2)}) async-start(bf16[4,64,2048]{2,1,0:T(8,128)(2,1)} %bitcast.105), calls=%async_computation.5 | async-start | bytes 2097152 | tf_op jit(solution)/shard_map/all_to_all | solution.py:128
  180.3 3.6 %convolution_convert_fusion.2 = bf16[704,2048]{1,0:T(8,128)(2,1)S(1)} fusion(bf16[512,704]{0,1:T(8,128)(2,1)} %get-tuple-element.30, bf16[256,2048]{1,0:T(8,128)(2,1)} %slice.79, bf16[256,2048]{1,0:T(8,128)(2,1)} %slice.77), kind=kOutput, calls=%fused_computation.3 | convolution fusion | flops 1482031104 | bytes 5701632 | tf_op jit(solution)/shard_map/dot_general | solution.py:281
  187.4 4.3 %pad_maximum_fusion = bf16[2112,2048]{1,0:T(8,128)(2,1)} fusion(bf16[704,2048]{1,0:T(8,128)(2,1)S(1)} %convolution_convert_fusion, bf16[704,2048]{1,0:T(8,128)(2,1)S(1)} %convolution_convert_fusion.1, bf16[704,2048]{1,0:T(8,128)(2,1)S(1)} %convolution_convert_fusion.2), kind=kLoop, calls=%fused_computation | loop fusion | flops 25952256 | bytes 17301504 | tf_op jit(solution)/shard_map/concatenate | solution.py:285
  191.7 3.5 %all-to-all-start.7 = ((bf16[4,64,2176]{2,1,0:T(8,128)(2,1)}), bf16[4,64,2176]{2,1,0:T(8,128)(2,1)S(1)}, u32[]{:S(2)}, u32[]{:S(2)}) async-start(bf16[4,64,2176]{2,1,0:T(8,128)(2,1)} %bitcast.20), calls=%async_computation.7 | async-start | bytes 2228224 | tf_op jit(solution)/shard_map/all_to_all | solution.py:128
  196.3 12.7 %all-to-all-done.7 = bf16[4,64,2176]{2,1,0:T(8,128)(2,1)S(1)} async-done(((bf16[4,64,2176]{2,1,0:T(8,128)(2,1)}), bf16[4,64,2176]{2,1,0:T(8,128)(2,1)S(1)}, u32[]{:S(2)}, u32[]{:S(2)}) %all-to-all-start.7) | async-done | bytes 1114144 | tf_op jit(solution)/shard_map/all_to_all | solution.py:128
  209.0 4.2 %all-to-all-start.2 = ((bf16[4,64,2048]{2,1,0:T(8,128)(2,1)}), bf16[4,64,2048]{2,1,0:T(8,128)(2,1)}, u32[]{:S(2)}, u32[]{:S(2)}) async-start(bf16[4,64,2048]{2,1,0:T(8,128)(2,1)} %bitcast.8), calls=%async_computation.2 | async-start | bytes 2097152 | tf_op jit(solution)/shard_map/all_to_all | solution.py:128
  215.7 10.8 %all-to-all-done.2 = bf16[4,64,2048]{2,1,0:T(8,128)(2,1)} async-done(((bf16[4,64,2048]{2,1,0:T(8,128)(2,1)}), bf16[4,64,2048]{2,1,0:T(8,128)(2,1)}, u32[]{:S(2)}, u32[]{:S(2)}) %all-to-all-start.2) | async-done | bytes 1048608 | tf_op jit(solution)/shard_map/all_to_all | solution.py:128
  226.4 4.5 %all-to-all-start.6 = ((bf16[4,64,2176]{2,1,0:T(8,128)(2,1)}), bf16[4,64,2176]{2,1,0:T(8,128)(2,1)}, u32[]{:S(2)}, u32[]{:S(2)}) async-start(bf16[4,64,2176]{2,1,0:T(8,128)(2,1)} %bitcast.106), calls=%async_computation.6 | async-start | bytes 2228224 | tf_op jit(solution)/shard_map/all_to_all | solution.py:128
  238.4 6.2 %all-to-all-done.6 = bf16[4,64,2176]{2,1,0:T(8,128)(2,1)} async-done(((bf16[4,64,2176]{2,1,0:T(8,128)(2,1)}), bf16[4,64,2176]{2,1,0:T(8,128)(2,1)}, u32[]{:S(2)}, u32[]{:S(2)}) %all-to-all-start.6) | async-done | bytes 1114144 | tf_op jit(solution)/shard_map/all_to_all | solution.py:128
  246.3 4.7 %collective-permute-done.11 = bf16[256,2176]{1,0:T(8,128)(2,1)} collective-permute-done((bf16[256,2176]{1,0:T(8,128)(2,1)}, bf16[256,2176]{1,0:T(8,128)(2,1)}, u32[]{:S(2)}, u32[]{:S(2)}) %collective-permute-start.11) | collective-permute-done | bytes 1114144 | tf_op jit(solution)/shard_map/ppermute | solution.py:124
  252.6 22.0 %collective-permute-done.8 = bf16[128,2048]{1,0:T(8,128)(2,1)} collective-permute-done((bf16[128,2048]{1,0:T(8,128)(2,1)S(1)}, bf16[128,2048]{1,0:T(8,128)(2,1)}, u32[]{:S(2)}, u32[]{:S(2)}) %collective-permute-start.8) | collective-permute-done | bytes 524320 | tf_op jit(solution)/shard_map/ppermute | solution.py:124
  276.6 8.0 %collective-permute-done.12 = bf16[128,2176]{1,0:T(8,128)(2,1)S(1)} collective-permute-done((bf16[128,2176]{1,0:T(8,128)(2,1)S(1)}, bf16[128,2176]{1,0:T(8,128)(2,1)S(1)}, u32[]{:S(2)}, u32[]{:S(2)}) %collective-permute-start.12) | collective-permute-done | bytes 557088 | tf_op jit(solution)/shard_map/ppermute | solution.py:124
  286.4 6.2 %fusion.53 = (f32[1,704,1024]{2,1,0:T(8,128)}, f32[1,1024,704]{1,2,0:T(8,128)}, f32[1,1024,704]{1,2,0:T(8,128)}) fusion(bf16[2112,1024]{1,0:T(8,128)(2,1)} %reduce-scatter.2.cloned.1.call-done), kind=kLoop, calls=%fused_computation.59 | loop fusion | flops 2162688 | bytes 12976128 | tf_op jit(solution)/shard_map/broadcast_in_dim | solution.py:292
  (161 shorter events, 100.3 us)
Async XLA Ops:
  7.2 98.4 %copy-start = (bf16[1,704,2048]{2,1,0:T(8,128)(2,1)S(1)}, bf16[1,704,2048]{2,1,0:T(8,128)(2,1)}, u32[]{:S(2)}) copy-start(bf16[1,704,2048]{2,1,0:T(8,128)(2,1)} %param.12) | copy-start | bytes 8650756
  7.2 28.9 %collective-permute-start = (bf16[128,2048]{1,0:T(8,128)(2,1)}, bf16[128,2048]{1,0:T(8,128)(2,1)S(1)}, u32[]{:S(2)}, u32[]{:S(2)}) collective-permute-start(bf16[128,2048]{1,0:T(8,128)(2,1)} %refs_1_.1), channel_id=1, source_target_pairs={{0,8},{1,9},{2,10},{3,11},{4,12},{5,13},{6,14},{7,15},{8,0},{9,1},... | collective-permute-start | bytes 1572872 | tf_op jit(solution)/shard_map/ppermute | solution.py:124
  16.6 19.5 %collective-permute-start.1 = (bf16[128,128]{1,0:T(8,128)(2,1)S(1)}, bf16[128,128]{1,0:T(8,128)(2,1)S(1)}, u32[]{:S(2)}, u32[]{:S(2)}) collective-permute-start(bf16[128,128]{1,0:T(8,128)(2,1)S(1)} %concatenate.28.refs_0_.refs_3_), channel_id=1, source_target_pairs={{0,8},{1,9},{2,10},{3,11},{4,12},{5,13},{6,14},{7,15},{8,0},{9,1},... | collective-permute-start | bytes 98312 | tf_op jit(solution)/shard_map/ppermute | solution.py:124
  40.7 49.7 %all-to-all-start = ((bf16[4,64,2176]{2,1,0:T(8,128)(2,1)}), bf16[4,64,2176]{2,1,0:T(8,128)(2,1)}, u32[]{:S(2)}, u32[]{:S(2)}) async-start(bf16[4,64,2176]{2,1,0:T(8,128)(2,1)} %bitcast.101), calls=%async_computation | async-start | bytes 2228224 | tf_op jit(solution)/shard_map/all_to_all | solution.py:128
  45.0 38.6 %collective-permute-start.9 = (bf16[128,2048]{1,0:T(8,128)(2,1)}, bf16[128,2048]{1,0:T(8,128)(2,1)}, u32[]{:S(2)}, u32[]{:S(2)}) collective-permute-start(bf16[128,2048]{1,0:T(8,128)(2,1)} %refs_1_.2), channel_id=1, source_target_pairs={{0,8},{1,9},{2,10},{3,11},{4,12},{5,13},{6,14},{7,15},{8,0},{9,1},... | collective-permute-start | bytes 1572872 | tf_op jit(solution)/shard_map/ppermute | solution.py:124
  45.1 43.8 %collective-permute-start.4 = (bf16[128,2048]{1,0:T(8,128)(2,1)}, bf16[128,2048]{1,0:T(8,128)(2,1)S(1)}, u32[]{:S(2)}, u32[]{:S(2)}) collective-permute-start(bf16[128,2048]{1,0:T(8,128)(2,1)} %refs_1_.1), channel_id=1, source_target_pairs={{0,4},{1,5},{2,6},{3,7},{4,0},{5,1},{6,2},{7,3},{8,12},{9,13},{10,... | collective-permute-start | bytes 1572872 | tf_op jit(solution)/shard_map/ppermute | solution.py:124
  49.2 39.7 %collective-permute-start.5 = (bf16[128,2048]{1,0:T(8,128)(2,1)}, bf16[128,2048]{1,0:T(8,128)(2,1)S(1)}, u32[]{:S(2)}, u32[]{:S(2)}) collective-permute-start(bf16[128,2048]{1,0:T(8,128)(2,1)} %copy-done.8), channel_id=1, source_target_pairs={{0,4},{1,5},{2,6},{3,7},{4,0},{5,1},{6,2},{7,3},{8,12},{9,13},{10,... | collective-permute-start | bytes 1572872 | tf_op jit(solution)/shard_map/ppermute | solution.py:124
  49.2 33.8 %collective-permute-start.2 = (bf16[128,128]{1,0:T(8,128)(2,1)S(1)}, bf16[128,128]{1,0:T(8,128)(2,1)S(1)}, u32[]{:S(2)}, u32[]{:S(2)}) collective-permute-start(bf16[128,128]{1,0:T(8,128)(2,1)S(1)} %concatenate.28.refs_0_.refs_3_), channel_id=1, source_target_pairs={{0,4},{1,5},{2,6},{3,7},{4,0},{5,1},{6,2},{7,3},{8,12},{9,13},{10,... | collective-permute-start | bytes 98312 | tf_op jit(solution)/shard_map/ppermute | solution.py:124
  51.2 32.1 %collective-permute-start.3 = (bf16[128,128]{1,0:T(8,128)(2,1)S(1)}, bf16[128,128]{1,0:T(8,128)(2,1)S(1)}, u32[]{:S(2)}, u32[]{:S(2)}) collective-permute-start(bf16[128,128]{1,0:T(8,128)(2,1)S(1)} %collective-permute-done.1.refs_1_.refs_4_), channel_id=1, source_target_pairs={{0,4},{1,5},{2,6},{3,7},{4,0},{5,1},{6,2},{7,3},{8,12},{9,13},{10,... | collective-permute-start | bytes 98312 | tf_op jit(solution)/shard_map/ppermute | solution.py:124
  83.0 62.2 %collective-permute-start.6 = (bf16[128,2048]{1,0:T(8,128)(2,1)}, bf16[128,2048]{1,0:T(8,128)(2,1)}, u32[]{:S(2)}, u32[]{:S(2)}) collective-permute-start(bf16[128,2048]{1,0:T(8,128)(2,1)} %refs_1_.2), channel_id=1, source_target_pairs={{0,4},{1,5},{2,6},{3,7},{4,0},{5,1},{6,2},{7,3},{8,12},{9,13},{10,... | collective-permute-start | bytes 1572872 | tf_op jit(solution)/shard_map/ppermute | solution.py:124
  83.6 61.6 %collective-permute-start.10 = (bf16[128,2048]{1,0:T(8,128)(2,1)}, bf16[128,2048]{1,0:T(8,128)(2,1)}, u32[]{:S(2)}, u32[]{:S(2)}) collective-permute-start(bf16[128,2048]{1,0:T(8,128)(2,1)} %collective-permute-done.9.refs_2_), channel_id=1, source_target_pairs={{0,4},{1,5},{2,6},{3,7},{4,0},{5,1},{6,2},{7,3},{8,12},{9,13},{10,... | collective-permute-start | bytes 1572872 | tf_op jit(solution)/shard_map/ppermute | solution.py:124
  90.4 17.5 %all-to-all-start.1 = ((bf16[4,64,2176]{2,1,0:T(8,128)(2,1)}), bf16[4,64,2176]{2,1,0:T(8,128)(2,1)}, u32[]{:S(2)}, u32[]{:S(2)}) async-start(bf16[4,64,2176]{2,1,0:T(8,128)(2,1)} %bitcast.102), calls=%async_computation.1 | async-start | bytes 2228224 | tf_op jit(solution)/shard_map/all_to_all | solution.py:128
  107.9 17.3 %all-to-all-start.4 = ((bf16[4,64,2048]{2,1,0:T(8,128)(2,1)}), bf16[4,64,2048]{2,1,0:T(8,128)(2,1)}, u32[]{:S(2)}, u32[]{:S(2)}) async-start(bf16[4,64,2048]{2,1,0:T(8,128)(2,1)} %bitcast.104), calls=%async_computation.4 | async-start | bytes 2097152 | tf_op jit(solution)/shard_map/all_to_all | solution.py:128
  125.2 17.4 %all-to-all-start.3 = ((bf16[4,64,2048]{2,1,0:T(8,128)(2,1)}), bf16[4,64,2048]{2,1,0:T(8,128)(2,1)}, u32[]{:S(2)}, u32[]{:S(2)}) async-start(bf16[4,64,2048]{2,1,0:T(8,128)(2,1)} %bitcast.107), calls=%async_computation.3 | async-start | bytes 2097152 | tf_op jit(solution)/shard_map/all_to_all | solution.py:128
  147.9 17.4 %all-to-all-start.5 = ((bf16[4,64,2048]{2,1,0:T(8,128)(2,1)}), bf16[4,64,2048]{2,1,0:T(8,128)(2,1)}, u32[]{:S(2)}, u32[]{:S(2)}) async-start(bf16[4,64,2048]{2,1,0:T(8,128)(2,1)} %bitcast.105), calls=%async_computation.5 | async-start | bytes 2097152 | tf_op jit(solution)/shard_map/all_to_all | solution.py:128
  152.3 134.0 %reduce-scatter.2.cloned.1.call-start = ((), (), s32[]{:S(2)}) async-start(), calls=%async_computation.9 | async-start | bytes 12976128 | tf_op jit(solution)/shard_map/reduce_scatter | solution.py:284
  191.7 17.3 %all-to-all-start.7 = ((bf16[4,64,2176]{2,1,0:T(8,128)(2,1)}), bf16[4,64,2176]{2,1,0:T(8,128)(2,1)S(1)}, u32[]{:S(2)}, u32[]{:S(2)}) async-start(bf16[4,64,2176]{2,1,0:T(8,128)(2,1)} %bitcast.20), calls=%async_computation.7 | async-start | bytes 2228224 | tf_op jit(solution)/shard_map/all_to_all | solution.py:128
  195.2 37.4 %collective-permute-start.7 = (bf16[256,2048]{1,0:T(8,128)(2,1)}, bf16[256,2048]{1,0:T(8,128)(2,1)}, u32[]{:S(2)}, u32[]{:S(2)}) collective-permute-start(bf16[256,2048]{1,0:T(8,128)(2,1)} %shard_map.125), channel_id=1, source_target_pairs={{0,4},{1,5},{2,6},{3,7},{4,0},{5,1},{6,2},{7,3},{8,12},{9,13},{10,... | collective-permute-start | bytes 3145736 | tf_op jit(solution)/shard_map/ppermute | solution.py:124
  209.0 17.5 %all-to-all-start.2 = ((bf16[4,64,2048]{2,1,0:T(8,128)(2,1)}), bf16[4,64,2048]{2,1,0:T(8,128)(2,1)}, u32[]{:S(2)}, u32[]{:S(2)}) async-start(bf16[4,64,2048]{2,1,0:T(8,128)(2,1)} %bitcast.8), calls=%async_computation.2 | async-start | bytes 2097152 | tf_op jit(solution)/shard_map/all_to_all | solution.py:128
  214.7 36.3 %collective-permute-start.11 = (bf16[256,2176]{1,0:T(8,128)(2,1)}, bf16[256,2176]{1,0:T(8,128)(2,1)}, u32[]{:S(2)}, u32[]{:S(2)}) collective-permute-start(bf16[256,2176]{1,0:T(8,128)(2,1)} %shard_map.129), channel_id=1, source_target_pairs={{0,4},{1,5},{2,6},{3,7},{4,0},{5,1},{6,2},{7,3},{8,12},{9,13},{10,... | collective-permute-start | bytes 3342344 | tf_op jit(solution)/shard_map/ppermute | solution.py:124
  226.4 18.1 %all-to-all-start.6 = ((bf16[4,64,2176]{2,1,0:T(8,128)(2,1)}), bf16[4,64,2176]{2,1,0:T(8,128)(2,1)}, u32[]{:S(2)}, u32[]{:S(2)}) async-start(bf16[4,64,2176]{2,1,0:T(8,128)(2,1)} %bitcast.106), calls=%async_computation.6 | async-start | bytes 2228224 | tf_op jit(solution)/shard_map/all_to_all | solution.py:128
  235.5 39.1 %collective-permute-start.8 = (bf16[128,2048]{1,0:T(8,128)(2,1)S(1)}, bf16[128,2048]{1,0:T(8,128)(2,1)}, u32[]{:S(2)}, u32[]{:S(2)}) collective-permute-start(bf16[128,2048]{1,0:T(8,128)(2,1)S(1)} %slice.140), channel_id=1, source_target_pairs={{0,8},{1,9},{2,10},{3,11},{4,12},{5,13},{6,14},{7,15},{8,0},{9,1},... | collective-permute-start | bytes 1572872 | tf_op jit(solution)/shard_map/ppermute | solution.py:124
  246.3 28.3 %copy-start.16 = (f32[256,2048]{1,0:T(8,128)S(1)}, f32[256,2048]{1,0:T(8,128)}, u32[]{:S(2)}) copy-start(f32[256,2048]{1,0:T(8,128)} %copy-done.15) | copy-start | bytes 6291460
  252.5 32.1 %collective-permute-start.12 = (bf16[128,2176]{1,0:T(8,128)(2,1)S(1)}, bf16[128,2176]{1,0:T(8,128)(2,1)S(1)}, u32[]{:S(2)}, u32[]{:S(2)}) collective-permute-start(bf16[128,2176]{1,0:T(8,128)(2,1)S(1)} %slice.138), channel_id=1, source_target_pairs={{0,8},{1,9},{2,10},{3,11},{4,12},{5,13},{6,14},{7,15},{8,0},{9,1},... | collective-permute-start | bytes 1671176 | tf_op jit(solution)/shard_map/ppermute | solution.py:124
  (36 other events, 88.0 us)
Sparse Core Ops, SparseCore 0:
  191.8 16.9 reduce-scatter.1

commit v3 on v1

v3 whole, which is shorter than its diff:
```python
import functools

import jax
import jax.numpy as jnp
from jax import lax
from jax.experimental import pallas as pl
from jax.experimental.pallas import tpu as pltpu
from jax.sharding import PartitionSpec as P

BF16 = jnp.bfloat16
F32 = jnp.float32
LANES = 128
STRIP = 512
VMEM = pl.BlockSpec(memory_space=pltpu.VMEM)
SMEM = pl.BlockSpec(memory_space=pltpu.SMEM)


def local_call(kernel, outs, me, args, flops):
    size = sum(x.size * x.dtype.itemsize for x in (*outs, *args))
    return pl.pallas_call(
        kernel,
        out_shape=outs,
        in_specs=[SMEM] + [VMEM] * len(args),
        out_specs=[VMEM] * len(outs),
        compiler_params=pltpu.CompilerParams(vmem_limit_bytes=16 * 1024 * 1024),
        cost_estimate=pl.CostEstimate(flops=flops, bytes_accessed=size, transcendentals=0),
    )(me, *args)


def strips(width):
    return [(c, min(c + STRIP, width)) for c in range(0, width, STRIP)]


def slot_tables(me, metas, top, side, capacity):
    count = len(metas)
    span = count * capacity
    tok = metas[0].shape[1]
    slot = lax.broadcasted_iota(jnp.int32, (side * span, tok), 0)
    expert = ((me - lax.rem(me, side)) + slot // span).astype(F32)
    block_of = lax.rem(slot, span) // capacity
    place = lax.rem(slot, capacity).astype(F32)
    row = lax.broadcasted_iota(jnp.int32, (tok, tok), 0)
    column = lax.broadcasted_iota(jnp.int32, (tok, tok), 1)
    earlier = jnp.where(row < column, 1.0, 0.0).astype(BF16)
    tables = []
    for b in range(count):
        named = [jnp.where(metas[b][k : k + 1, :] == expert, 1.0, 0.0) for k in range(top)]
        member = functools.reduce(lambda p, q: p + q, named)
        rank = jnp.dot(member.astype(BF16), earlier, preferred_element_type=F32)
        here = rank == place
        if count > 1:
            here = here & (block_of == b)
        tables.append([jnp.where(here, part, 0.0) for part in named])
    return tables


def pick_kernel(top, side, capacity, count, scaled, me_ref, *refs):
    metas, blocks, out = refs[:count], refs[count : 2 * count], refs[2 * count]
    tables = slot_tables(me_ref[0], metas, top, side, capacity)
    held = jnp.concatenate([functools.reduce(lambda p, q: p + q, ks) for ks in tables], 1)
    held = held.astype(BF16)
    if scaled:
        gate = 0.0
        for meta, ks in zip(metas, tables):
            for k, part in enumerate(ks):
                gate += jnp.sum(part * meta[top + k : top + k + 1, :], 1, keepdims=True)
    for c, e in strips(out.shape[1]):
        block = jnp.concatenate([ref[:, c:e] for ref in blocks], 0)
        got = jnp.dot(held, block, preferred_element_type=F32)
        out[:, c:e] = ((gate * got) if scaled else got).astype(BF16)


TRANSPOSED = (((0,), (0,)), ((), ()))


def sum_kernel(top, side, capacity, count, me_ref, *refs):
    metas, back, outs = refs[:count], refs[count], refs[count + 1 :]
    tables = slot_tables(me_ref[0], metas, top, side, capacity)
    for ks, out in zip(tables, outs):
        held = functools.reduce(lambda p, q: p + q, ks).astype(BF16)
        for c, e in strips(out.shape[1]):
            out[:, c:e] = lax.dot_general(
                held, back[:, c:e], TRANSPOSED, preferred_element_type=F32
            ).astype(out.dtype)


def mix_kernel(top, side, capacity, count, me_ref, *refs):
    metas, blocks, back = refs[:count], refs[count : 2 * count], refs[2 * count]
    outs, grads = refs[2 * count + 1 : 3 * count + 1], refs[3 * count + 1 :]
    tables = slot_tables(me_ref[0], metas, top, side, capacity)
    tok = metas[0].shape[1]
    lane = lax.broadcasted_iota(jnp.int32, (tok, LANES), 1)
    for b in range(count):
        held = [part.astype(BF16) for part in tables[b]]
        gates = [metas[b][top + k : top + k + 1, :] for k in range(top)]
        gates = [jnp.transpose(jnp.broadcast_to(g, (8, tok)))[:, :1] for g in gates]
        sums = [jnp.zeros((tok, 1), F32) for _ in range(top)]
        for c, e in strips(outs[b].shape[1]):
            cotangent = blocks[b][:, c:e].astype(F32)
            mixed = 0.0
            for k in range(top):
                got = lax.dot_general(held[k], back[:, c:e], TRANSPOSED, preferred_element_type=F32)
                mixed += gates[k] * got
                sums[k] += jnp.sum(cotangent * got, 1, keepdims=True)
            outs[b][:, c:e] = mixed.astype(outs[b].dtype)
        grad = jnp.zeros((tok, LANES), F32)
        for k in range(top):
            grad = jnp.where(lane == k, sums[k], grad)
        grads[b][...] = grad


def on_device(tokens, expert_ids, gate_prob, w_gate, w_up, w_down, d_mixed):
    tok, feature = tokens.shape
    top = expert_ids.shape[1]
    experts = lax.axis_size("expert")
    capacity = max(2, 2 * tok * top // experts)
    side = experts // 2
    half = side * capacity
    me = lax.axis_index("expert")
    me_arr = me[None]
    sets = [[h * side + p for p in range(side)] for h in range(2)]
    shape = jax.ShapeDtypeStruct

    def across(value):
        return lax.ppermute(value, "expert", [(e, (e + side) % experts) for e in range(experts)])

    def exchange(value):
        shaped = value.reshape(side, value.shape[0] // side, value.shape[1])
        got = lax.all_to_all(shaped, "expert", 0, 0, axis_index_groups=sets, tiled=True)
        return got.reshape(value.shape)

    def after(value, *earlier):
        return lax.optimization_barrier((value, *earlier))

    def pick(metas, blocks, scaled):
        count = len(metas)
        return local_call(
            functools.partial(pick_kernel, top, side, capacity, count, scaled),
            [shape((count * half, feature), BF16)],
            me_arr,
            [*metas, *blocks],
            2 * count * count * half * tok * feature,
        )[0]

    def split(rows):
        parts = rows.reshape(side, 2, capacity, feature)
        return [parts[:, b].reshape(half, feature) for b in range(2)]

    meta = jnp.concatenate([expert_ids.T.astype(F32), gate_prob.T], 0)
    x_far = across(tokens)
    meta_far = across(meta)
    x_own = exchange(pick([meta], [tokens], False))
    x_far, meta_far = after(x_far, meta_far)
    d_mixed, x_far = after(d_mixed, x_far)
    d_far = across(d_mixed)
    x_other = exchange(pick([meta_far], [x_far], False))
    x_rows = jnp.stack(
        [part.reshape(side, capacity, feature) for part in (x_own, x_other)], 1
    ).reshape(2 * half, feature)

    metas = [meta, meta_far]
    dy_rows = exchange(pick(metas, [d_mixed, d_far], True))

    gate_matrix, up_matrix, down_matrix = w_gate[0], w_up[0], w_down[0]
    hidden_units = gate_matrix.shape[1]
    contract_rows = (((0,), (0,)), ((), ()))
    contract_cols = (((1,), (1,)), ((), ()))

    gate_pre = jnp.dot(x_rows, gate_matrix, preferred_element_type=F32)
    up_pre = jnp.dot(x_rows, up_matrix, preferred_element_type=F32)
    sig_gate = jax.nn.sigmoid(gate_pre)
    silu_gate = gate_pre * sig_gate
    hidden = (silu_gate * up_pre).astype(BF16)
    expert_out = jnp.dot(hidden, down_matrix, preferred_element_type=F32).astype(BF16)
    expert_out, dy_rows = after(expert_out, dy_rows)
    y_back = exchange(expert_out)

    back_hidden = lax.dot_general(dy_rows, down_matrix, contract_cols, preferred_element_type=F32)
    d_silu = sig_gate * (1.0 + gate_pre * (1.0 - sig_gate))
    grad_pre_gate = (back_hidden * up_pre * d_silu).astype(BF16)
    grad_pre_up = (back_hidden * silu_gate).astype(BF16)
    expert_dx = (
        lax.dot_general(grad_pre_gate, gate_matrix, contract_cols, preferred_element_type=F32)
        + lax.dot_general(grad_pre_up, up_matrix, contract_cols, preferred_element_type=F32)
    ).astype(BF16)
    expert_dx, grad_pre_gate, grad_pre_up = after(expert_dx, grad_pre_gate, grad_pre_up)

    def reduced(left, right):
        term = lax.dot_general(left, right, contract_rows, preferred_element_type=F32)
        return lax.psum_scatter(term.astype(BF16), "dp", scatter_dimension=1, tiled=True)

    grad_down = reduced(hidden, dy_rows)
    grad_gate = reduced(grad_pre_gate, x_rows)
    grad_up = reduced(grad_pre_up, x_rows)

    mixed_own, mixed_far, grads_own, grads_far = local_call(
        functools.partial(mix_kernel, top, side, capacity, 2),
        [
            shape((tok, feature), F32),
            shape((tok, feature), BF16),
            shape((tok, LANES), F32),
            shape((tok, LANES), F32),
        ],
        me_arr,
        [*metas, d_mixed, d_far, y_back],
        4 * top * half * 2 * tok * feature,
    )
    dx_own, dx_far = split(expert_dx)
    dx_far, y_back = after(dx_far, y_back)
    far_back = exchange(dx_far)
    far_back, dx_own = after(far_back, dx_own)
    own_back = exchange(dx_own)

    def total(metas, back, kind):
        return local_call(
            functools.partial(sum_kernel, top, side, capacity, 1),
            [shape((tok, feature), kind)],
            me_arr,
            [*metas, back],
            2 * half * tok * feature,
        )[0]

    tokens_far = across(total([meta_far], far_back, BF16))
    mixed = (mixed_own + across(mixed_far).astype(F32)).astype(BF16)
    d_gate = (grads_own + across(grads_far))[:, :top]
    tokens_own = total([meta], own_back, F32)
    d_tokens = (tokens_own + tokens_far.astype(F32)).astype(BF16)
    return (
        mixed,
        d_tokens,
        d_gate,
        grad_gate.astype(F32).T[None],
        grad_up.astype(F32).T[None],
        grad_down.astype(F32)[None],
    )


def solution(mesh):
    in_specs = (
        P(("dp", "expert"), None),
        P(("dp", "expert"), None),
        P(("dp", "expert"), None),
        P("expert", None, None),
        P("expert", None, None),
        P("expert", None, None),
        P(("dp", "expert"), None),
    )
    out_specs = (
        P(("dp", "expert"), None),
        P(("dp", "expert"), None),
        P(("dp", "expert"), None),
        P("expert", "dp", None),
        P("expert", "dp", None),
        P("expert", None, "dp"),
    )
    return jax.shard_map(
        on_device, mesh=mesh, in_specs=in_specs, out_specs=out_specs, check_vma=False
    )
```

time: 332 us -> 234 us (0.70)
  blocking collectives: 114 us -> 0 us
  waiting for transfers between devices: 76.1 us -> 106 us
  starting transfers between devices: 64.2 us -> 44.2 us
  Pallas kernels: 0 us -> 6.71 us
  other arithmetic: 11.9 us -> 16.3 us
    all_gather x2 -> x0, blocking collectives: 114 us -> none  [the longest x1 74.7 us: on_device(): meta_all = lax.all_gather(meta, 'expert')]
    ppermute x60 -> x6, starting transfers between devices: 64.2 us -> 10.5 us  [across(): lax.ppermute(value, 'expert', [(e, (e + side) % experts) for e in range(e...]
    all_to_all x0 -> x6, waiting for transfers between devices: none -> 46.1 us  [exchange(): lax.all_to_all(shaped, 'expert', 0, 0, axis_index_groups=sets, tiled=True)]
    all_to_all x0 -> x6, starting transfers between devices: none -> 33.4 us  [exchange(): lax.all_to_all(shaped, 'expert', 0, 0, axis_index_groups=sets, tiled=True)]
    ppermute x60 -> x6, waiting for transfers between devices: 76.1 us -> 59.9 us  [across(): lax.ppermute(value, 'expert', [(e, (e + side) % experts) for e in range(e...]
    broadcast_in_dim x0 -> x3, other arithmetic: none -> 9.91 us  [the longest x1 3.3 us: on_device(): grad_down.astype(F32)[None]]
    dot_general x25 -> x3, matrix products: 20.6 us -> 13.8 us  [reduced(): lax.dot_general(left, right, contract_rows, preferred_element_type=F32)]
    pallas_call x0 -> x6, Pallas kernels: none -> 6.71 us  [local_call(): pl.pallas_call(kernel, out_shape=outs, in_specs=[SMEM] + [VMEM] * len(arg...]
  transfers between devices with their start and end apart: 61 -> 15, of which waited for: 25 -> 8; matrix products, arithmetic and copies ran while one was open for 13% -> 18% of each run, Pallas kernels for 0% -> 3%
where the time goes in v3:
time: 234 us; the launch traced here: 233 us
  waiting for transfers between devices  106 us (45%)
  starting transfers between devices  44.2 us (19%)
  matrix products  31.3 us (13%)
  other arithmetic  16.3 us (7%)
  local copies, waits for them, and re-layouts  14.2 us (6%)
  between operations  14 us (6%)
  Pallas kernels  6.71 us (3%)
    ppermute x6, waiting for transfers between devices, across(): lax.ppermute(value, 'expert', [(e, (e + side) % experts) for e in range(e...  59.9 us
    all_to_all x6, waiting for transfers between devices, exchange(): lax.all_to_all(shaped, 'expert', 0, 0, axis_index_groups=sets, tiled=True)  46.1 us
    all_to_all x6, starting transfers between devices, exchange(): lax.all_to_all(shaped, 'expert', 0, 0, axis_index_groups=sets, tiled=True)  33.4 us
    dot_general x3, matrix products, reduced(): lax.dot_general(left, right, contract_rows, preferred_element_type=F32)  13.8 us
    unnamed x49, local copies, waits for them, and re-layouts  11.1 us
    ppermute x6, starting transfers between devices, across(): lax.ppermute(value, 'expert', [(e, (e + side) % experts) for e in range(e...  10.5 us
    pallas_call x6, Pallas kernels, local_call(): pl.pallas_call(kernel, out_shape=outs, in_specs=[SMEM] + [VMEM] * len(arg...  6.71 us
    dot_general x1, matrix products, on_device(): lax.dot_general(dy_rows, down_matrix, contract_cols, preferred_element_ty...  4.68 us
  transfers between devices with their start and end apart: 15, of which 8 were waited for; matrix products, arithmetic and copies ran while one was open for 18% of the time, Pallas kernels for 3%

profile of v3, /device:TPU:0, one launch (start us, length us, event | category | flops | bytes accessed | tf_op | source)
XLA Modules:
  0.0 232.8 jit_solution(5012355854431299078)
XLA Ops:
  11.3 6.2 %all-to-all-start = ((bf16[8,32,2048]{2,1,0:T(8,128)(2,1)}), bf16[8,32,2048]{2,1,0:T(8,128)(2,1)}, u32[]{:S(2)}, u32[]{:S(2)}) async-start(bf16[8,32,2048]{2,1,0:T(8,128)(2,1)} %bitcast.64), calls=%async_computation | async-start | bytes 2097152 | tf_op jit(solution)/shard_map/all_to_all | solution.py:129
  20.5 19.7 %collective-permute-done.1.refs_0_.refs_1_ = f32[4,128]{1,0:T(4,128)S(1)} collective-permute-done((f32[4,128]{1,0:T(4,128)S(1)}, f32[4,128]{1,0:T(4,128)S(1)}, u32[]{:S(2)}, u32[]{:S(2)}) %collective-permute-start.1) | collective-permute-done | bytes 2080 | tf_op jit(solution)/shard_map/ppermute | solution.py:125
  42.6 7.0 %all-to-all-start.1 = ((bf16[8,32,2048]{2,1,0:T(8,128)(2,1)}), bf16[8,32,2048]{2,1,0:T(8,128)(2,1)}, u32[]{:S(2)}, u32[]{:S(2)}) async-start(bf16[8,32,2048]{2,1,0:T(8,128)(2,1)} %bitcast.65), calls=%async_computation.1 | async-start | bytes 2097152 | tf_op jit(solution)/shard_map/all_to_all | solution.py:129
  52.1 19.2 %collective-permute-done.2.refs_3_ = bf16[128,2048]{1,0:T(8,128)(2,1)S(1)} collective-permute-done((bf16[128,2048]{1,0:T(8,128)(2,1)S(1)}, bf16[128,2048]{1,0:T(8,128)(2,1)S(1)}, u32[]{:S(2)}, u32[]{:S(2)}) %collective-permute-start.2) | collective-permute-done | bytes 524320 | tf_op jit(solution)/shard_map/ppermute | solution.py:125
  74.3 7.6 %all-to-all-start.2 = ((bf16[8,64,2048]{2,1,0:T(8,128)(2,1)}), bf16[8,64,2048]{2,1,0:T(8,128)(2,1)}, u32[]{:S(2)}, u32[]{:S(2)}) async-start(bf16[8,64,2048]{2,1,0:T(8,128)(2,1)} %bitcast.62), calls=%async_computation.2 | async-start | bytes 4194304 | tf_op jit(solution)/shard_map/all_to_all | solution.py:129
  90.1 3.2 %convolution_convert_fusion.3 = bf16[512,2048]{1,0:T(8,128)(2,1)} fusion(bf16[512,704]{0,1:T(8,128)(2,1)S(1)} %get-tuple-element.54, bf16[1,704,2048]{2,1,0:T(8,128)(2,1)S(1)} %copy-done), kind=kOutput, calls=%fused_computation.4 | convolution fusion | flops 1477443584 | bytes 5701632 | tf_op jit(solution)/shard_map/dot_general | solution.py:174
  93.3 12.7 %all-to-all-done.2 = bf16[8,64,2048]{2,1,0:T(8,128)(2,1)} async-done(((bf16[8,64,2048]{2,1,0:T(8,128)(2,1)}), bf16[8,64,2048]{2,1,0:T(8,128)(2,1)}, u32[]{:S(2)}, u32[]{:S(2)}) %all-to-all-start.2) | async-done | bytes 2097184 | tf_op jit(solution)/shard_map/all_to_all | solution.py:129
  106.0 5.1 %convolution_convert_fusion = bf16[704,2048]{1,0:T(8,128)(2,1)} fusion(bf16[512,704]{0,1:T(8,128)(2,1)} %copy-done.22, bf16[512,2048]{1,0:T(8,128)(2,1)} %bitcast.12), kind=kOutput, calls=%fused_computation.1 | convolution fusion | flops 1477836800 | bytes 5701632 | tf_op jit(solution)/shard_map/dot_general | solution.py:189
  111.4 4.7 %multiply_convert_fusion = (bf16[512,704]{0,1:T(8,128)(2,1)S(1)}, bf16[512,704]{0,1:T(8,128)(2,1)S(1)}) fusion(f32[512,704]{0,1:T(8,128)} %copy-done.23, f32[512,704]{0,1:T(8,128)} %get-tuple-element.55, bf16[512,2048]{1,0:T(8,128)(2,1)} %bitcast.12, bf16[1,704,2048]{2,1,0:T(8,128)(2,1)S(1)} %copy-done), kind=kOutput, calls=%fused_computation.19 | convolution fusion | flops 1481080832 | bytes 9306112 | tf_op jit(solution)/shard_map/dot_general | solution.py:178
  118.2 3.3 %add_convert_fusion = bf16[512,2048]{1,0:T(8,128)(2,1)} fusion(f32[512,2048]{1,0:T(8,128)S(1)} %fusion.6, bf16[512,704]{0,1:T(8,128)(2,1)S(1)} %get-tuple-element.37, bf16[1,2048,704]{1,2,0:T(8,128)(2,1)S(1)} %copy-done.21), kind=kOutput, calls=%fused_computation | convolution fusion | flops 1478492160 | bytes 9895936 | tf_op jit(solution)/shard_map/dot_general | solution.py:184
  121.5 3.3 %convolution_convert_fusion.1 = bf16[704,2048]{1,0:T(8,128)(2,1)} fusion(bf16[512,704]{0,1:T(8,128)(2,1)S(1)} %get-tuple-element.37, bf16[512,2048]{1,0:T(8,128)(2,1)S(1)} %bitcast.73), kind=kOutput, calls=%fused_computation.2 | convolution fusion | flops 1477836800 | bytes 5701632 | tf_op jit(solution)/shard_map/dot_general | solution.py:189
  124.9 4.8 %all-to-all-start.3 = ((bf16[8,64,2048]{2,1,0:T(8,128)(2,1)}), bf16[8,64,2048]{2,1,0:T(8,128)(2,1)S(1)}, u32[]{:S(2)}, u32[]{:S(2)}) async-start(bf16[8,64,2048]{2,1,0:T(8,128)(2,1)} %bitcast.69), calls=%async_computation.3 | async-start | bytes 4194304 | tf_op jit(solution)/shard_map/all_to_all | solution.py:129
  129.7 5.4 %convolution_convert_fusion.2 = bf16[704,2048]{1,0:T(8,128)(2,1)} fusion(bf16[512,704]{0,1:T(8,128)(2,1)S(1)} %copy-done.19, bf16[512,2048]{1,0:T(8,128)(2,1)} %bitcast.72), kind=kOutput, calls=%fused_computation.3 | convolution fusion | flops 1477836800 | bytes 5701632 | tf_op jit(solution)/shard_map/dot_general | solution.py:189
  135.2 3.1 %fusion.11 = (bf16[8,1,32,2048]{3,2,1,0:T(8,128)(2,1)}, bf16[8,1,32,2048]{3,2,1,0:T(8,128)(2,1)}) fusion(bf16[8,2,32,2048]{3,2,1,0:T(8,128)(2,1)} %bitcast.74), kind=kLoop, calls=%fused_computation.29 | loop fusion | bytes 4194304 | tf_op jit(solution)/shard_map/slice | solution.py:147
  138.3 17.0 %all-to-all-done.3 = bf16[8,64,2048]{2,1,0:T(8,128)(2,1)S(1)} async-done(((bf16[8,64,2048]{2,1,0:T(8,128)(2,1)}), bf16[8,64,2048]{2,1,0:T(8,128)(2,1)S(1)}, u32[]{:S(2)}, u32[]{:S(2)}) %all-to-all-start.3) | async-done | bytes 2097184 | tf_op jit(solution)/shard_map/all_to_all | solution.py:129
  155.3 4.2 %all-to-all-start.4 = ((bf16[8,32,2048]{2,1,0:T(8,128)(2,1)}), bf16[8,32,2048]{2,1,0:T(8,128)(2,1)}, u32[]{:S(2)}, u32[]{:S(2)}) async-start(bf16[8,32,2048]{2,1,0:T(8,128)(2,1)} %bitcast.68), calls=%async_computation.4 | async-start | bytes 2097152 | tf_op jit(solution)/shard_map/all_to_all | solution.py:129
  163.1 15.5 %all-to-all-done.4 = bf16[8,32,2048]{2,1,0:T(8,128)(2,1)} async-done(((bf16[8,32,2048]{2,1,0:T(8,128)(2,1)}), bf16[8,32,2048]{2,1,0:T(8,128)(2,1)}, u32[]{:S(2)}, u32[]{:S(2)}) %all-to-all-start.4) | async-done | bytes 1048608 | tf_op jit(solution)/shard_map/all_to_all | solution.py:129
  178.6 3.6 %all-to-all-start.5 = ((bf16[8,32,2048]{2,1,0:T(8,128)(2,1)}), bf16[8,32,2048]{2,1,0:T(8,128)(2,1)S(1)}, u32[]{:S(2)}, u32[]{:S(2)}) async-start(bf16[8,32,2048]{2,1,0:T(8,128)(2,1)} %bitcast.67), calls=%async_computation.5 | async-start | bytes 2097152 | tf_op jit(solution)/shard_map/all_to_all | solution.py:129
  183.7 11.4 %collective-permute-done.5 = f32[128,128]{1,0:T(8,128)S(1)} collective-permute-done((f32[128,128]{1,0:T(8,128)S(1)}, f32[128,128]{1,0:T(8,128)S(1)}, u32[]{:S(2)}, u32[]{:S(2)}) %collective-permute-start.5) | collective-permute-done | bytes 65568 | tf_op jit(solution)/shard_map/ppermute | solution.py:125
  198.4 3.4 %collective-permute-start.4 = (bf16[128,2048]{1,0:T(8,128)(2,1)S(1)}, bf16[128,2048]{1,0:T(8,128)(2,1)}, u32[]{:S(2)}, u32[]{:S(2)}) collective-permute-start(bf16[128,2048]{1,0:T(8,128)(2,1)S(1)} %shard_map.123), channel_id=1, source_target_pairs={{0,8},{1,9},{2,10},{3,11},{4,12},{5,13},{6,14},{7,15},{8,0},{9,1},... | collective-permute-start | bytes 1572872 | tf_op jit(solution)/shard_map/ppermute | solution.py:125
  201.8 3.3 %bitcast_convert_fusion = f32[1,704,1024]{2,1,0:T(8,128)} fusion(bf16[704,1024]{1,0:T(8,128)(2,1)} %reduce-scatter.8.cloned.1.call-done), kind=kLoop, calls=%fused_computation.18 | loop fusion | flops 720896 | bytes 4325376 | tf_op jit(solution)/shard_map/broadcast_in_dim | solution.py:234
  205.1 3.3 %convert_bitcast_fusion = f32[1,1024,704]{1,2,0:T(8,128)} fusion(bf16[704,1024]{1,0:T(8,128)(2,1)} %reduce-scatter.6.cloned.1.call-done), kind=kLoop, calls=%fused_computation.15 | loop fusion | flops 720896 | bytes 4325376 | tf_op jit(solution)/shard_map/broadcast_in_dim | solution.py:233
  208.4 3.3 %convert_bitcast_fusion.1 = f32[1,1024,704]{1,2,0:T(8,128)} fusion(bf16[704,1024]{1,0:T(8,128)(2,1)} %reduce-scatter.4.cloned.1.call-done), kind=kLoop, calls=%fused_computation.16 | loop fusion | flops 720896 | bytes 4325376 | tf_op jit(solution)/shard_map/broadcast_in_dim | solution.py:232
  214.6 9.6 %collective-permute-done.4 = bf16[128,2048]{1,0:T(8,128)(2,1)} collective-permute-done((bf16[128,2048]{1,0:T(8,128)(2,1)S(1)}, bf16[128,2048]{1,0:T(8,128)(2,1)}, u32[]{:S(2)}, u32[]{:S(2)}) %collective-permute-start.4) | collective-permute-done | bytes 524320 | tf_op jit(solution)/shard_map/ppermute | solution.py:125
  (83 shorter events, 38.8 us)
Async XLA Ops:
  7.2 83.0 %copy-start = (bf16[1,704,2048]{2,1,0:T(8,128)(2,1)S(1)}, bf16[1,704,2048]{2,1,0:T(8,128)(2,1)}, u32[]{:S(2)}) copy-start(bf16[1,704,2048]{2,1,0:T(8,128)(2,1)} %param.12) | copy-start | bytes 8650756
  9.8 7.7 %copy-start.10 = (bf16[128,2048]{1,0:T(8,128)(2,1)S(1)}, bf16[128,2048]{1,0:T(8,128)(2,1)}, u32[]{:S(2)}) copy-start(bf16[128,2048]{1,0:T(8,128)(2,1)} %refs_1_.1) | copy-start | bytes 1572868
  11.3 31.3 %all-to-all-start = ((bf16[8,32,2048]{2,1,0:T(8,128)(2,1)}), bf16[8,32,2048]{2,1,0:T(8,128)(2,1)}, u32[]{:S(2)}, u32[]{:S(2)}) async-start(bf16[8,32,2048]{2,1,0:T(8,128)(2,1)} %bitcast.64), calls=%async_computation | async-start | bytes 2097152 | tf_op jit(solution)/shard_map/all_to_all | solution.py:129
  17.5 22.7 %collective-permute-start = (bf16[128,2048]{1,0:T(8,128)(2,1)S(1)}, bf16[128,2048]{1,0:T(8,128)(2,1)S(1)}, u32[]{:S(2)}, u32[]{:S(2)}) collective-permute-start(bf16[128,2048]{1,0:T(8,128)(2,1)S(1)} %copy-done.10), channel_id=1, source_target_pairs={{0,8},{1,9},{2,10},{3,11},{4,12},{5,13},{6,14},{7,15},{8,0},{9,1},... | collective-permute-start | bytes 1572872 | tf_op jit(solution)/shard_map/ppermute | solution.py:125
  20.1 20.1 %collective-permute-start.1 = (f32[4,128]{1,0:T(4,128)S(1)}, f32[4,128]{1,0:T(4,128)S(1)}, u32[]{:S(2)}, u32[]{:S(2)}) collective-permute-start(f32[4,128]{1,0:T(4,128)S(1)} %pad_maximum_fusion.1.refs_0_), channel_id=1, source_target_pairs={{0,8},{1,9},{2,10},{3,11},{4,12},{5,13},{6,14},{7,15},{8,0},{9,1},... | collective-permute-start | bytes 6152 | tf_op jit(solution)/shard_map/ppermute | solution.py:125
  40.2 9.4 %copy-start.11 = (bf16[128,2048]{1,0:T(8,128)(2,1)S(1)}, bf16[128,2048]{1,0:T(8,128)(2,1)}, u32[]{:S(2)}) copy-start(bf16[128,2048]{1,0:T(8,128)(2,1)} %refs_2_.1) | copy-start | bytes 1572868
  42.6 31.7 %all-to-all-start.1 = ((bf16[8,32,2048]{2,1,0:T(8,128)(2,1)}), bf16[8,32,2048]{2,1,0:T(8,128)(2,1)}, u32[]{:S(2)}, u32[]{:S(2)}) async-start(bf16[8,32,2048]{2,1,0:T(8,128)(2,1)} %bitcast.65), calls=%async_computation.1 | async-start | bytes 2097152 | tf_op jit(solution)/shard_map/all_to_all | solution.py:129
  49.6 21.7 %collective-permute-start.2 = (bf16[128,2048]{1,0:T(8,128)(2,1)S(1)}, bf16[128,2048]{1,0:T(8,128)(2,1)S(1)}, u32[]{:S(2)}, u32[]{:S(2)}) collective-permute-start(bf16[128,2048]{1,0:T(8,128)(2,1)S(1)} %copy-done.11), channel_id=1, source_target_pairs={{0,8},{1,9},{2,10},{3,11},{4,12},{5,13},{6,14},{7,15},{8,0},{9,1},... | collective-permute-start | bytes 1572872 | tf_op jit(solution)/shard_map/ppermute | solution.py:125
  74.3 31.7 %all-to-all-start.2 = ((bf16[8,64,2048]{2,1,0:T(8,128)(2,1)}), bf16[8,64,2048]{2,1,0:T(8,128)(2,1)}, u32[]{:S(2)}, u32[]{:S(2)}) async-start(bf16[8,64,2048]{2,1,0:T(8,128)(2,1)} %bitcast.62), calls=%async_computation.2 | async-start | bytes 4194304 | tf_op jit(solution)/shard_map/all_to_all | solution.py:129
  81.9 119.9 %reduce-scatter.8.cloned.1.call-start = ((), (), s32[]{:S(2)}) async-start(), calls=%async_computation.11 | async-start | bytes 4325376 | tf_op jit(solution)/shard_map/reduce_scatter | solution.py:190
  111.1 94.0 %reduce-scatter.6.cloned.1.call-start = ((), (), s32[]{:S(2)}) async-start(), calls=%async_computation.10 | async-start | bytes 4325376 | tf_op jit(solution)/shard_map/reduce_scatter | solution.py:190
  111.3 4.7 %copy-start.15 = (bf16[1,2048,704]{1,2,0:T(8,128)(2,1)S(1)}, bf16[1,2048,704]{1,2,0:T(8,128)(2,1)}, u32[]{:S(2)}) copy-start(bf16[1,2048,704]{1,2,0:T(8,128)(2,1)} %param.10) | copy-start | bytes 8650756
  118.2 3.3 %copy-start.17 = (bf16[8,2,32,2048]{3,2,1,0:T(8,128)(2,1)S(1)}, bf16[8,2,32,2048]{3,2,1,0:T(8,128)(2,1)}, u32[]{:S(2)}) copy-start(bf16[8,2,32,2048]{3,2,1,0:T(8,128)(2,1)} %copy-done.16) | copy-start | bytes 6291460
  124.8 4.9 %copy-start.19 = (bf16[512,704]{0,1:T(8,128)(2,1)S(1)}, bf16[512,704]{0,1:T(8,128)(2,1)}, u32[]{:S(2)}) copy-start(bf16[512,704]{0,1:T(8,128)(2,1)} %copy-done.18) | copy-start | bytes 2162692
  124.9 30.4 %all-to-all-start.3 = ((bf16[8,64,2048]{2,1,0:T(8,128)(2,1)}), bf16[8,64,2048]{2,1,0:T(8,128)(2,1)S(1)}, u32[]{:S(2)}, u32[]{:S(2)}) async-start(bf16[8,64,2048]{2,1,0:T(8,128)(2,1)} %bitcast.69), calls=%async_computation.3 | async-start | bytes 4194304 | tf_op jit(solution)/shard_map/all_to_all | solution.py:129
  129.7 78.7 %reduce-scatter.4.cloned.1.call-start = ((), (), s32[]{:S(2)}) async-start(), calls=%async_computation.9 | async-start | bytes 4325376 | tf_op jit(solution)/shard_map/reduce_scatter | solution.py:190
  138.3 21.2 %copy-start.13 = (bf16[128,2048]{1,0:T(8,128)(2,1)S(1)}, bf16[128,2048]{1,0:T(8,128)(2,1)}, u32[]{:S(2)}) copy-start(bf16[128,2048]{1,0:T(8,128)(2,1)} %copy-done.12) | copy-start | bytes 1572868
  155.3 23.3 %all-to-all-start.4 = ((bf16[8,32,2048]{2,1,0:T(8,128)(2,1)}), bf16[8,32,2048]{2,1,0:T(8,128)(2,1)}, u32[]{:S(2)}, u32[]{:S(2)}) async-start(bf16[8,32,2048]{2,1,0:T(8,128)(2,1)} %bitcast.68), calls=%async_computation.4 | async-start | bytes 2097152 | tf_op jit(solution)/shard_map/all_to_all | solution.py:129
  163.1 32.6 %copy-start.8 = (f32[128,2048]{1,0:T(8,128)S(1)}, f32[128,2048]{1,0:T(8,128)}, u32[]{:S(2)}) copy-start(f32[128,2048]{1,0:T(8,128)} %copy-done.7) | copy-start | bytes 3145732
  163.1 32.6 %collective-permute-start.3 = (bf16[128,2048]{1,0:T(8,128)(2,1)}, bf16[128,2048]{1,0:T(8,128)(2,1)S(1)}, u32[]{:S(2)}, u32[]{:S(2)}) collective-permute-start(bf16[128,2048]{1,0:T(8,128)(2,1)} %get-tuple-element.28), channel_id=1, source_target_pairs={{0,8},{1,9},{2,10},{3,11},{4,12},{5,13},{6,14},{7,15},{8,0},{9,1},... | collective-permute-start | bytes 1572872 | tf_op jit(solution)/shard_map/ppermute | solution.py:125
  178.6 33.1 %all-to-all-start.5 = ((bf16[8,32,2048]{2,1,0:T(8,128)(2,1)}), bf16[8,32,2048]{2,1,0:T(8,128)(2,1)S(1)}, u32[]{:S(2)}, u32[]{:S(2)}) async-start(bf16[8,32,2048]{2,1,0:T(8,128)(2,1)} %bitcast.67), calls=%async_computation.5 | async-start | bytes 2097152 | tf_op jit(solution)/shard_map/all_to_all | solution.py:129
  182.2 12.9 %collective-permute-start.5 = (f32[128,128]{1,0:T(8,128)S(1)}, f32[128,128]{1,0:T(8,128)S(1)}, u32[]{:S(2)}, u32[]{:S(2)}) collective-permute-start(f32[128,128]{1,0:T(8,128)S(1)} %get-tuple-element.35), channel_id=1, source_target_pairs={{0,8},{1,9},{2,10},{3,11},{4,12},{5,13},{6,14},{7,15},{8,0},{9,1},... | collective-permute-start | bytes 196616 | tf_op jit(solution)/shard_map/ppermute | solution.py:125
  198.4 25.9 %collective-permute-start.4 = (bf16[128,2048]{1,0:T(8,128)(2,1)S(1)}, bf16[128,2048]{1,0:T(8,128)(2,1)}, u32[]{:S(2)}, u32[]{:S(2)}) collective-permute-start(bf16[128,2048]{1,0:T(8,128)(2,1)S(1)} %shard_map.123), channel_id=1, source_target_pairs={{0,8},{1,9},{2,10},{3,11},{4,12},{5,13},{6,14},{7,15},{8,0},{9,1},... | collective-permute-start | bytes 1572872 | tf_op jit(solution)/shard_map/ppermute | solution.py:125
  212.8 13.5 %copy-start.1 = (bf16[1,704,2048]{2,1,0:T(8,128)(2,1)S(1)}, bf16[1,704,2048]{2,1,0:T(8,128)(2,1)}, u32[]{:S(2)}) copy-start(bf16[1,704,2048]{2,1,0:T(8,128)(2,1)} %param.12) | copy-start | bytes 8650756
  (15 other events, 22.9 us)
Sparse Core Ops, SparseCore 0:
  111.2 9.3 reduce-scatter.7
  125.0 10.2 reduce-scatter.5
  138.1 11.6 reduce-scatter.3

commit v4 on v3

--- a/solution.py
+++ b/solution.py
@@ -142,23 +142,14 @@
             2 * count * count * half * tok * feature,
         )[0]
 
-    def split(rows):
-        parts = rows.reshape(side, 2, capacity, feature)
-        return [parts[:, b].reshape(half, feature) for b in range(2)]
-
     meta = jnp.concatenate([expert_ids.T.astype(F32), gate_prob.T], 0)
     x_far = across(tokens)
     meta_far = across(meta)
-    x_own = exchange(pick([meta], [tokens], False))
     x_far, meta_far = after(x_far, meta_far)
     d_mixed, x_far = after(d_mixed, x_far)
     d_far = across(d_mixed)
-    x_other = exchange(pick([meta_far], [x_far], False))
-    x_rows = jnp.stack(
-        [part.reshape(side, capacity, feature) for part in (x_own, x_other)], 1
-    ).reshape(2 * half, feature)
-
     metas = [meta, meta_far]
+    x_rows = exchange(pick(metas, [tokens, x_far], False))
     dy_rows = exchange(pick(metas, [d_mixed, d_far], True))
 
     gate_matrix, up_matrix, down_matrix = w_gate[0], w_up[0], w_down[0]
@@ -183,7 +174,9 @@
         lax.dot_general(grad_pre_gate, gate_matrix, contract_cols, preferred_element_type=F32)
         + lax.dot_general(grad_pre_up, up_matrix, contract_cols, preferred_element_type=F32)
     ).astype(BF16)
-    expert_dx, grad_pre_gate, grad_pre_up = after(expert_dx, grad_pre_gate, grad_pre_up)
+    expert_dx, y_back, grad_pre_gate, grad_pre_up, hidden = after(
+        expert_dx, y_back, grad_pre_gate, grad_pre_up, hidden
+    )
 
     def reduced(left, right):
         term = lax.dot_general(left, right, contract_rows, preferred_element_type=F32)
@@ -205,26 +198,17 @@
         [*metas, d_mixed, d_far, y_back],
         4 * top * half * 2 * tok * feature,
     )
-    dx_own, dx_far = split(expert_dx)
-    dx_far, y_back = after(dx_far, y_back)
-    far_back = exchange(dx_far)
-    far_back, dx_own = after(far_back, dx_own)
-    own_back = exchange(dx_own)
-
-    def total(metas, back, kind):
-        return local_call(
-            functools.partial(sum_kernel, top, side, capacity, 1),
-            [shape((tok, feature), kind)],
-            me_arr,
-            [*metas, back],
-            2 * half * tok * feature,
-        )[0]
-
-    tokens_far = across(total([meta_far], far_back, BF16))
+    dx_back = exchange(expert_dx)
+    tokens_own, tokens_far = local_call(
+        functools.partial(sum_kernel, top, side, capacity, 2),
+        [shape((tok, feature), F32), shape((tok, feature), BF16)],
+        me_arr,
+        [*metas, dx_back],
+        4 * half * tok * feature,
+    )
     mixed = (mixed_own + across(mixed_far).astype(F32)).astype(BF16)
     d_gate = (grads_own + across(grads_far))[:, :top]
-    tokens_own = total([meta], own_back, F32)
-    d_tokens = (tokens_own + tokens_far.astype(F32)).astype(BF16)
+    d_tokens = (tokens_own + across(tokens_far).astype(F32)).astype(BF16)
     return (
         mixed,
         d_tokens,

time: 234 us -> 252 us (1.077)
  waiting for transfers between devices: 106 us -> 129 us
  starting transfers between devices: 44.2 us -> 35.7 us
  matrix products: 31.3 us -> 37.8 us
  local copies, waits for them, and re-layouts: 14.2 us -> 9.57 us
    ppermute x6, waiting for transfers between devices: 59.9 us -> 72.8 us  [across(): lax.ppermute(value, 'expert', [(e, (e + side) % experts) for e in range(e...]
    all_to_all x6 -> x4, waiting for transfers between devices: 46.1 us -> 56.3 us  [exchange(): lax.all_to_all(shaped, 'expert', 0, 0, axis_index_groups=sets, tiled=True)]
    all_to_all x6 -> x4, starting transfers between devices: 33.4 us -> 25.2 us  [exchange(): lax.all_to_all(shaped, 'expert', 0, 0, axis_index_groups=sets, tiled=True)]
    slice x1 -> x0, local copies, waits for them, and re-layouts: 3.11 us -> none  [split(): return [parts[:, b].reshape(half, feature) for b in range(2)]]
    dot_general x1, matrix products: 1.68 us -> 4.28 us  [on_device(): gate_pre = jnp.dot(x_rows, gate_matrix, preferred_element_type=F32)]
    pallas_call x6 -> x4, Pallas kernels: 6.71 us -> 8.29 us  [local_call(): pl.pallas_call(kernel, out_shape=outs, in_specs=[SMEM] + [VMEM] * len(arg...]
    unnamed x49 -> x35, local copies, waits for them, and re-layouts: 11.1 us -> 9.57 us
  transfers between devices with their start and end apart: 15 -> 13, of which waited for: 8 -> 6; matrix products, arithmetic and copies ran while one was open for 18% -> 19% of each run, Pallas kernels for 3% -> 3%
where the time goes in v4:
time: 252 us; the launch traced here: 251 us
  waiting for transfers between devices  129 us (51%)
  matrix products  37.8 us (15%)
  starting transfers between devices  35.7 us (14%)
  other arithmetic  16.4 us (7%)
  between operations  14 us (6%)
  local copies, waits for them, and re-layouts  9.57 us (4%)
  Pallas kernels  8.29 us (3%)
    ppermute x6, waiting for transfers between devices, across(): lax.ppermute(value, 'expert', [(e, (e + side) % experts) for e in range(e...  72.8 us
    all_to_all x4, waiting for transfers between devices, exchange(): lax.all_to_all(shaped, 'expert', 0, 0, axis_index_groups=sets, tiled=True)  56.3 us
    all_to_all x4, starting transfers between devices, exchange(): lax.all_to_all(shaped, 'expert', 0, 0, axis_index_groups=sets, tiled=True)  25.2 us
    dot_general x3, matrix products, reduced(): lax.dot_general(left, right, contract_rows, preferred_element_type=F32)  15.6 us
    ppermute x6, starting transfers between devices, across(): lax.ppermute(value, 'expert', [(e, (e + side) % experts) for e in range(e...  10.2 us
    unnamed x35, local copies, waits for them, and re-layouts  9.57 us
    pallas_call x4, Pallas kernels, local_call(): pl.pallas_call(kernel, out_shape=outs, in_specs=[SMEM] + [VMEM] * len(arg...  8.29 us
  transfers between devices with their start and end apart: 13, of which 6 were waited for; matrix products, arithmetic and copies ran while one was open for 19% of the time, Pallas kernels for 3%

profile of v4, /device:TPU:0, one launch (start us, length us, event | category | flops | bytes accessed | tf_op | source)
XLA Modules:
  0.0 251.0 jit_solution(4595341235094651528)
XLA Ops:
  7.2 4.1 %collective-permute-start = (bf16[128,2048]{1,0:T(8,128)(2,1)}, bf16[128,2048]{1,0:T(8,128)(2,1)S(1)}, u32[]{:S(2)}, u32[]{:S(2)}) collective-permute-start(bf16[128,2048]{1,0:T(8,128)(2,1)} %refs_2_.1), channel_id=1, source_target_pairs={{0,8},{1,9},{2,10},{3,11},{4,12},{5,13},{6,14},{7,15},{8,0},{9,1},... | collective-permute-start | bytes 1572872 | tf_op jit(solution)/shard_map/ppermute | solution.py:125
  12.8 21.9 %collective-permute-done.1.refs_1_ = f32[4,128]{1,0:T(4,128)S(1)} collective-permute-done((f32[4,128]{1,0:T(4,128)S(1)}, f32[4,128]{1,0:T(4,128)S(1)}, u32[]{:S(2)}, u32[]{:S(2)}) %collective-permute-start.1) | collective-permute-done | bytes 2080 | tf_op jit(solution)/shard_map/ppermute | solution.py:125
  37.9 4.5 %all-to-all-start = ((bf16[8,64,2048]{2,1,0:T(8,128)(2,1)}), bf16[8,64,2048]{2,1,0:T(8,128)(2,1)}, u32[]{:S(2)}, u32[]{:S(2)}) async-start(bf16[8,64,2048]{2,1,0:T(8,128)(2,1)} %bitcast.55), calls=%async_computation | async-start | bytes 4194304 | tf_op jit(solution)/shard_map/all_to_all | solution.py:129
  42.4 3.0 %collective-permute-start.2 = (bf16[128,2048]{1,0:T(8,128)(2,1)S(1)}, bf16[128,2048]{1,0:T(8,128)(2,1)S(1)}, u32[]{:S(2)}, u32[]{:S(2)}) collective-permute-start(bf16[128,2048]{1,0:T(8,128)(2,1)S(1)} %copy-done.7), channel_id=1, source_target_pairs={{0,8},{1,9},{2,10},{3,11},{4,12},{5,13},{6,14},{7,15},{8,0},{9,1},... | collective-permute-start | bytes 1572872 | tf_op jit(solution)/shard_map/ppermute | solution.py:125
  45.4 30.8 %collective-permute-done.2.refs_3_ = bf16[128,2048]{1,0:T(8,128)(2,1)S(1)} collective-permute-done((bf16[128,2048]{1,0:T(8,128)(2,1)S(1)}, bf16[128,2048]{1,0:T(8,128)(2,1)S(1)}, u32[]{:S(2)}, u32[]{:S(2)}) %collective-permute-start.2) | collective-permute-done | bytes 524320 | tf_op jit(solution)/shard_map/ppermute | solution.py:125
  79.2 11.4 %all-to-all-start.1 = ((bf16[8,64,2048]{2,1,0:T(8,128)(2,1)}), bf16[8,64,2048]{2,1,0:T(8,128)(2,1)}, u32[]{:S(2)}, u32[]{:S(2)}) async-start(bf16[8,64,2048]{2,1,0:T(8,128)(2,1)} %bitcast.54), calls=%async_computation.1 | async-start | bytes 4194304 | tf_op jit(solution)/shard_map/all_to_all | solution.py:129
  90.6 4.3 %fusion.8 = f32[512,704]{0,1:T(8,128)S(1)} fusion(bf16[512,2048]{1,0:T(8,128)(2,1)} %bitcast.4, bf16[1,2048,704]{1,2,0:T(8,128)(2,1)} %param.10), kind=kOutput, calls=%fused_computation.13 | convolution fusion | flops 1476395008 | bytes 6422528 | tf_op jit(solution)/shard_map/dot_general | solution.py:160
  94.9 5.0 %multiply_convert_fusion.2 = (bf16[512,704]{0,1:T(8,128)(2,1)S(1)}, f32[512,704]{0,1:T(8,128)}) fusion(f32[512,704]{0,1:T(8,128)S(1)} %fusion.8, bf16[512,2048]{1,0:T(8,128)(2,1)} %bitcast.4, bf16[1,2048,704]{1,2,0:T(8,128)(2,1)S(1)} %copy-done.12), kind=kOutput, calls=%fused_computation.20 | convolution fusion | flops 1478557696 | bytes 8585216 | tf_op jit(solution)/shard_map/dot_general | solution.py:161
  100.8 3.1 %convolution_convert_fusion.3 = bf16[512,2048]{1,0:T(8,128)(2,1)} fusion(bf16[512,704]{0,1:T(8,128)(2,1)S(1)} %get-tuple-element.39, bf16[1,704,2048]{2,1,0:T(8,128)(2,1)S(1)} %copy-done), kind=kOutput, calls=%fused_computation.4 | convolution fusion | flops 1477443584 | bytes 5701632 | tf_op jit(solution)/shard_map/dot_general | solution.py:165
  103.9 12.2 %all-to-all-done.1 = bf16[8,64,2048]{2,1,0:T(8,128)(2,1)} async-done(((bf16[8,64,2048]{2,1,0:T(8,128)(2,1)}), bf16[8,64,2048]{2,1,0:T(8,128)(2,1)}, u32[]{:S(2)}, u32[]{:S(2)}) %all-to-all-start.1) | async-done | bytes 2097184 | tf_op jit(solution)/shard_map/all_to_all | solution.py:129
  116.1 4.4 %all-to-all-start.2 = ((bf16[8,64,2048]{2,1,0:T(8,128)(2,1)}), bf16[8,64,2048]{2,1,0:T(8,128)(2,1)}, u32[]{:S(2)}, u32[]{:S(2)}) async-start(bf16[8,64,2048]{2,1,0:T(8,128)(2,1)} %bitcast.57), calls=%async_computation.2 | async-start | bytes 4194304 | tf_op jit(solution)/shard_map/all_to_all | solution.py:129
  120.7 4.7 %multiply_convert_fusion = (bf16[512,704]{0,1:T(8,128)(2,1)S(1)}, bf16[512,704]{0,1:T(8,128)(2,1)S(1)}) fusion(f32[512,704]{0,1:T(8,128)} %copy-done.16, f32[512,704]{0,1:T(8,128)} %get-tuple-element.49, bf16[512,2048]{1,0:T(8,128)(2,1)} %bitcast.9, bf16[1,704,2048]{2,1,0:T(8,128)(2,1)S(1)} %copy-done), kind=kOutput, calls=%fused_computation.18 | convolution fusion | flops 1481080832 | bytes 9306112 | tf_op jit(solution)/shard_map/dot_general | solution.py:169
  127.8 3.3 %add_convert_fusion = bf16[512,2048]{1,0:T(8,128)(2,1)} fusion(f32[512,2048]{1,0:T(8,128)S(1)} %fusion.6, bf16[512,704]{0,1:T(8,128)(2,1)S(1)} %get-tuple-element.38, bf16[1,2048,704]{1,2,0:T(8,128)(2,1)S(1)} %copy-done.13), kind=kOutput, calls=%fused_computation | convolution fusion | flops 1478492160 | bytes 9895936 | tf_op jit(solution)/shard_map/dot_general | solution.py:175
  131.1 15.3 %all-to-all-done.2 = bf16[8,64,2048]{2,1,0:T(8,128)(2,1)} async-done(((bf16[8,64,2048]{2,1,0:T(8,128)(2,1)}), bf16[8,64,2048]{2,1,0:T(8,128)(2,1)}, u32[]{:S(2)}, u32[]{:S(2)}) %all-to-all-start.2) | async-done | bytes 2097184 | tf_op jit(solution)/shard_map/all_to_all | solution.py:129
  146.5 5.1 %convolution_convert_fusion = bf16[704,2048]{1,0:T(8,128)(2,1)} fusion(bf16[512,704]{0,1:T(8,128)(2,1)} %copy-done.14, bf16[512,2048]{1,0:T(8,128)(2,1)} %bitcast.9), kind=kOutput, calls=%fused_computation.1 | convolution fusion | flops 1477836800 | bytes 5701632 | tf_op jit(solution)/shard_map/dot_general | solution.py:182
  151.6 5.1 %convolution_convert_fusion.1 = bf16[704,2048]{1,0:T(8,128)(2,1)} fusion(bf16[512,704]{0,1:T(8,128)(2,1)} %copy-done.15, bf16[512,2048]{1,0:T(8,128)(2,1)} %bitcast.4), kind=kOutput, calls=%fused_computation.2 | convolution fusion | flops 1477836800 | bytes 5701632 | tf_op jit(solution)/shard_map/dot_general | solution.py:182
  156.7 5.5 %convolution_convert_fusion.2 = bf16[704,2048]{1,0:T(8,128)(2,1)} fusion(bf16[512,704]{0,1:T(8,128)(2,1)} %copy-done.11, bf16[512,2048]{1,0:T(8,128)(2,1)} %bitcast.4), kind=kOutput, calls=%fused_computation.3 | convolution fusion | flops 1477836800 | bytes 5701632 | tf_op jit(solution)/shard_map/dot_general | solution.py:182
  162.2 5.0 %all-to-all-start.3 = ((bf16[8,64,2048]{2,1,0:T(8,128)(2,1)}), bf16[8,64,2048]{2,1,0:T(8,128)(2,1)}, u32[]{:S(2)}, u32[]{:S(2)}) async-start(bf16[8,64,2048]{2,1,0:T(8,128)(2,1)} %bitcast.56), calls=%async_computation.3 | async-start | bytes 4194304 | tf_op jit(solution)/shard_map/all_to_all | solution.py:129
  168.2 4.1 %shard_map.120 = (f32[128,2048]{1,0:T(8,128)S(1)}, bf16[128,2048]{1,0:T(8,128)(2,1)}, f32[128,128]{1,0:T(8,128)S(1)}, f32[128,128]{1,0:T(8,128)S(1)}) custom-call(s32[1]{0:T(128)} %bitcast.me_ref, f32[4,128]{1,0:T(4,128)S(1)} %pad_maximum_fusion.refs_0_, f32[4,128]{1,0:T(4,128)S(1)} %collective-permute-done.1.refs_1_, bf16[128,2048]{1,0:T(8,128)(2,1)S(1)} %copy-done.7, ...), custom_call_target="tpu_custom_call" | custom-call | flops 1073741824 | bytes 4853760 | tf_op jit(solution)/shard_map/pallas_call | solution.py:20
  176.3 28.8 %all-to-all-done.3 = bf16[8,64,2048]{2,1,0:T(8,128)(2,1)} async-done(((bf16[8,64,2048]{2,1,0:T(8,128)(2,1)}), bf16[8,64,2048]{2,1,0:T(8,128)(2,1)}, u32[]{:S(2)}, u32[]{:S(2)}) %all-to-all-start.3) | async-done | bytes 2097184 | tf_op jit(solution)/shard_map/all_to_all | solution.py:129
  212.4 20.1 %collective-permute-done.4 = bf16[128,2048]{1,0:T(8,128)(2,1)} collective-permute-done((bf16[128,2048]{1,0:T(8,128)(2,1)S(1)}, bf16[128,2048]{1,0:T(8,128)(2,1)}, u32[]{:S(2)}, u32[]{:S(2)}) %collective-permute-start.4) | collective-permute-done | bytes 524320 | tf_op jit(solution)/shard_map/ppermute | solution.py:125
  234.5 3.3 %bitcast_convert_fusion = f32[1,704,1024]{2,1,0:T(8,128)} fusion(bf16[704,1024]{1,0:T(8,128)(2,1)} %reduce-scatter.8.cloned.1.call-done), kind=kLoop, calls=%fused_computation.17 | loop fusion | flops 720896 | bytes 4325376 | tf_op jit(solution)/shard_map/broadcast_in_dim | solution.py:218
  237.8 3.3 %convert_bitcast_fusion = f32[1,1024,704]{1,2,0:T(8,128)} fusion(bf16[704,1024]{1,0:T(8,128)(2,1)} %reduce-scatter.6.cloned.1.call-done), kind=kLoop, calls=%fused_computation.15 | loop fusion | flops 720896 | bytes 4325376 | tf_op jit(solution)/shard_map/broadcast_in_dim | solution.py:217
  241.1 3.3 %convert_bitcast_fusion.1 = f32[1,1024,704]{1,2,0:T(8,128)} fusion(bf16[704,1024]{1,0:T(8,128)(2,1)} %reduce-scatter.4.cloned.1.call-done), kind=kLoop, calls=%fused_computation.16 | loop fusion | flops 720896 | bytes 4325376 | tf_op jit(solution)/shard_map/broadcast_in_dim | solution.py:216
  (61 shorter events, 25.6 us)
Async XLA Ops:
  7.2 93.6 %copy-start = (bf16[1,704,2048]{2,1,0:T(8,128)(2,1)S(1)}, bf16[1,704,2048]{2,1,0:T(8,128)(2,1)}, u32[]{:S(2)}) copy-start(bf16[1,704,2048]{2,1,0:T(8,128)(2,1)} %param.12) | copy-start | bytes 8650756
  7.2 27.6 %collective-permute-start = (bf16[128,2048]{1,0:T(8,128)(2,1)}, bf16[128,2048]{1,0:T(8,128)(2,1)S(1)}, u32[]{:S(2)}, u32[]{:S(2)}) collective-permute-start(bf16[128,2048]{1,0:T(8,128)(2,1)} %refs_2_.1), channel_id=1, source_target_pairs={{0,8},{1,9},{2,10},{3,11},{4,12},{5,13},{6,14},{7,15},{8,0},{9,1},... | collective-permute-start | bytes 1572872 | tf_op jit(solution)/shard_map/ppermute | solution.py:125
  12.7 22.1 %collective-permute-start.1 = (f32[4,128]{1,0:T(4,128)S(1)}, f32[4,128]{1,0:T(4,128)S(1)}, u32[]{:S(2)}, u32[]{:S(2)}) collective-permute-start(f32[4,128]{1,0:T(4,128)S(1)} %pad_maximum_fusion.refs_0_), channel_id=1, source_target_pairs={{0,8},{1,9},{2,10},{3,11},{4,12},{5,13},{6,14},{7,15},{8,0},{9,1},... | collective-permute-start | bytes 6152 | tf_op jit(solution)/shard_map/ppermute | solution.py:125
  36.6 1.3 copy-start.2
  37.9 4.5 %copy-start.7 = (bf16[128,2048]{1,0:T(8,128)(2,1)S(1)}, bf16[128,2048]{1,0:T(8,128)(2,1)}, u32[]{:S(2)}) copy-start(bf16[128,2048]{1,0:T(8,128)(2,1)} %refs_2_.3) | copy-start | bytes 1572868
  37.9 41.2 %all-to-all-start = ((bf16[8,64,2048]{2,1,0:T(8,128)(2,1)}), bf16[8,64,2048]{2,1,0:T(8,128)(2,1)}, u32[]{:S(2)}, u32[]{:S(2)}) async-start(bf16[8,64,2048]{2,1,0:T(8,128)(2,1)} %bitcast.55), calls=%async_computation | async-start | bytes 4194304 | tf_op jit(solution)/shard_map/all_to_all | solution.py:129
  42.4 33.8 %collective-permute-start.2 = (bf16[128,2048]{1,0:T(8,128)(2,1)S(1)}, bf16[128,2048]{1,0:T(8,128)(2,1)S(1)}, u32[]{:S(2)}, u32[]{:S(2)}) collective-permute-start(bf16[128,2048]{1,0:T(8,128)(2,1)S(1)} %copy-done.7), channel_id=1, source_target_pairs={{0,8},{1,9},{2,10},{3,11},{4,12},{5,13},{6,14},{7,15},{8,0},{9,1},... | collective-permute-start | bytes 1572872 | tf_op jit(solution)/shard_map/ppermute | solution.py:125
  77.1 1.3 copy-start.1
  79.2 37.0 %all-to-all-start.1 = ((bf16[8,64,2048]{2,1,0:T(8,128)(2,1)}), bf16[8,64,2048]{2,1,0:T(8,128)(2,1)}, u32[]{:S(2)}, u32[]{:S(2)}) async-start(bf16[8,64,2048]{2,1,0:T(8,128)(2,1)} %bitcast.54), calls=%async_computation.1 | async-start | bytes 4194304 | tf_op jit(solution)/shard_map/all_to_all | solution.py:129
  90.6 4.3 %copy-start.12 = (bf16[1,2048,704]{1,2,0:T(8,128)(2,1)S(1)}, bf16[1,2048,704]{1,2,0:T(8,128)(2,1)}, u32[]{:S(2)}) copy-start(bf16[1,2048,704]{1,2,0:T(8,128)(2,1)} %param.11) | copy-start | bytes 8650756
  94.9 5.0 %copy-start.16 = (f32[512,704]{0,1:T(8,128)}, f32[512,704]{0,1:T(8,128)S(1)}, u32[]{:S(2)}) copy-start(f32[512,704]{0,1:T(8,128)S(1)} %fusion.8) | copy-start | bytes 4325380
  116.1 30.3 %all-to-all-start.2 = ((bf16[8,64,2048]{2,1,0:T(8,128)(2,1)}), bf16[8,64,2048]{2,1,0:T(8,128)(2,1)}, u32[]{:S(2)}, u32[]{:S(2)}) async-start(bf16[8,64,2048]{2,1,0:T(8,128)(2,1)} %bitcast.57), calls=%async_computation.2 | async-start | bytes 4194304 | tf_op jit(solution)/shard_map/all_to_all | solution.py:129
  120.5 114.0 %reduce-scatter.8.cloned.1.call-start = ((), (), s32[]{:S(2)}) async-start(), calls=%async_computation.9 | async-start | bytes 4325376 | tf_op jit(solution)/shard_map/reduce_scatter | solution.py:183
  120.7 4.7 %copy-start.10 = (bf16[1,2048,704]{1,2,0:T(8,128)(2,1)S(1)}, bf16[1,2048,704]{1,2,0:T(8,128)(2,1)}, u32[]{:S(2)}) copy-start(bf16[1,2048,704]{1,2,0:T(8,128)(2,1)} %param.10) | copy-start | bytes 8650756
  125.4 1.9 copy-start.11
  125.4 1.9 copy-start.15
  125.5 2.3 copy-start.13
  151.5 86.3 %reduce-scatter.6.cloned.1.call-start = ((), (), s32[]{:S(2)}) async-start(), calls=%async_computation.8 | async-start | bytes 4325376 | tf_op jit(solution)/shard_map/reduce_scatter | solution.py:183
  156.7 84.5 %reduce-scatter.4.cloned.1.call-start = ((), (), s32[]{:S(2)}) async-start(), calls=%async_computation.7 | async-start | bytes 4325376 | tf_op jit(solution)/shard_map/reduce_scatter | solution.py:183
  162.2 42.8 %all-to-all-start.3 = ((bf16[8,64,2048]{2,1,0:T(8,128)(2,1)}), bf16[8,64,2048]{2,1,0:T(8,128)(2,1)}, u32[]{:S(2)}, u32[]{:S(2)}) async-start(bf16[8,64,2048]{2,1,0:T(8,128)(2,1)} %bitcast.56), calls=%async_computation.3 | async-start | bytes 4194304 | tf_op jit(solution)/shard_map/all_to_all | solution.py:129
  173.4 36.7 %collective-permute-start.3 = (bf16[128,2048]{1,0:T(8,128)(2,1)}, bf16[128,2048]{1,0:T(8,128)(2,1)}, u32[]{:S(2)}, u32[]{:S(2)}) collective-permute-start(bf16[128,2048]{1,0:T(8,128)(2,1)} %get-tuple-element.31), channel_id=1, source_target_pairs={{0,8},{1,9},{2,10},{3,11},{4,12},{5,13},{6,14},{7,15},{8,0},{9,1},... | collective-permute-start | bytes 1572872 | tf_op jit(solution)/shard_map/ppermute | solution.py:125
  173.4 35.2 %collective-permute-start.5 = (f32[128,128]{1,0:T(8,128)S(1)}, f32[128,128]{1,0:T(8,128)}, u32[]{:S(2)}, u32[]{:S(2)}) collective-permute-start(f32[128,128]{1,0:T(8,128)S(1)} %get-tuple-element.36), channel_id=1, source_target_pairs={{0,8},{1,9},{2,10},{3,11},{4,12},{5,13},{6,14},{7,15},{8,0},{9,1},... | collective-permute-start | bytes 196616 | tf_op jit(solution)/shard_map/ppermute | solution.py:125
  208.6 24.0 %collective-permute-start.4 = (bf16[128,2048]{1,0:T(8,128)(2,1)S(1)}, bf16[128,2048]{1,0:T(8,128)(2,1)}, u32[]{:S(2)}, u32[]{:S(2)}) collective-permute-start(bf16[128,2048]{1,0:T(8,128)(2,1)S(1)} %get-tuple-element.34), channel_id=1, source_target_pairs={{0,8},{1,9},{2,10},{3,11},{4,12},{5,13},{6,14},{7,15},{8,0},{9,1},... | collective-permute-start | bytes 1572872 | tf_op jit(solution)/shard_map/ppermute | solution.py:125
  210.1 22.5 %copy-start.5 = (f32[128,2048]{1,0:T(8,128)S(1)}, f32[128,2048]{1,0:T(8,128)}, u32[]{:S(2)}) copy-start(f32[128,2048]{1,0:T(8,128)} %copy-done.4) | copy-start | bytes 3145732
  (6 other events, 5.8 us)
Sparse Core Ops, SparseCore 0:
  151.7 9.9 reduce-scatter.7
  164.6 11.7 reduce-scatter.5
  179.2 11.6 reduce-scatter.3

commit v5 on v3

--- a/solution.py
+++ b/solution.py
@@ -27,8 +27,8 @@
     )(me, *args)
 
 
-def strips(width):
-    return [(c, min(c + STRIP, width)) for c in range(0, width, STRIP)]
+def strips(width, step=STRIP):
+    return [(c, min(c + step, width)) for c in range(0, width, step)]
 
 
 def slot_tables(me, metas, top, side, capacity):
@@ -109,6 +109,32 @@
         grads[b][...] = grad
 
 
+def backward_kernel(
+    dy_ref, x_ref, gate_ref, up_ref, hidden_ref, wg_ref, wu_ref, wd_ref, dx_ref, terms_ref, gg_ref, gu_ref
+):
+    rows, units = gate_ref.shape
+    across_last = (((1,), (1,)), ((), ()))
+    for c, e in strips(units, 256):
+        back = lax.dot_general(
+            dy_ref[...], wd_ref[c:e, :], across_last, preferred_element_type=F32
+        )
+        gate = gate_ref[:, c:e]
+        sig = 1.0 / (1.0 + jnp.exp(-gate))
+        gg_ref[:, c:e] = (back * up_ref[:, c:e] * (sig * (1.0 + gate * (1.0 - sig)))).astype(BF16)
+        gu_ref[:, c:e] = (back * (gate * sig)).astype(BF16)
+    for c, e in strips(dx_ref.shape[1]):
+        got = jnp.dot(gg_ref[...], wg_ref[:, c:e], preferred_element_type=F32)
+        got += jnp.dot(gu_ref[...], wu_ref[:, c:e], preferred_element_type=F32)
+        dx_ref[:, c:e] = got.astype(BF16)
+    pairs = ((gg_ref, x_ref), (gu_ref, x_ref), (hidden_ref, dy_ref))
+    for n, (left, right) in enumerate(pairs):
+        for r, t in strips(units, 256):
+            for c, e in strips(dx_ref.shape[1], 1024):
+                terms_ref[n * units + r : n * units + t, c:e] = lax.dot_general(
+                    left[:, r:t], right[:, c:e], TRANSPOSED, preferred_element_type=F32
+                ).astype(BF16)
+
+
 def on_device(tokens, expert_ids, gate_prob, w_gate, w_up, w_down, d_mixed):
     tok, feature = tokens.shape
     top = expert_ids.shape[1]
@@ -163,8 +189,6 @@
 
     gate_matrix, up_matrix, down_matrix = w_gate[0], w_up[0], w_down[0]
     hidden_units = gate_matrix.shape[1]
-    contract_rows = (((0,), (0,)), ((), ()))
-    contract_cols = (((1,), (1,)), ((), ()))
 
     gate_pre = jnp.dot(x_rows, gate_matrix, preferred_element_type=F32)
     up_pre = jnp.dot(x_rows, up_matrix, preferred_element_type=F32)
@@ -175,23 +199,17 @@
     expert_out, dy_rows = after(expert_out, dy_rows)
     y_back = exchange(expert_out)
 
-    back_hidden = lax.dot_general(dy_rows, down_matrix, contract_cols, preferred_element_type=F32)
-    d_silu = sig_gate * (1.0 + gate_pre * (1.0 - sig_gate))
-    grad_pre_gate = (back_hidden * up_pre * d_silu).astype(BF16)
-    grad_pre_up = (back_hidden * silu_gate).astype(BF16)
-    expert_dx = (
-        lax.dot_general(grad_pre_gate, gate_matrix, contract_cols, preferred_element_type=F32)
-        + lax.dot_general(grad_pre_up, up_matrix, contract_cols, preferred_element_type=F32)
-    ).astype(BF16)
-    expert_dx, grad_pre_gate, grad_pre_up = after(expert_dx, grad_pre_gate, grad_pre_up)
-
-    def reduced(left, right):
-        term = lax.dot_general(left, right, contract_rows, preferred_element_type=F32)
-        return lax.psum_scatter(term.astype(BF16), "dp", scatter_dimension=1, tiled=True)
-
-    grad_down = reduced(hidden, dy_rows)
-    grad_gate = reduced(grad_pre_gate, x_rows)
-    grad_up = reduced(grad_pre_up, x_rows)
+    n_rows = 2 * half
+    expert_dx, terms = pl.pallas_call(
+        backward_kernel,
+        out_shape=[shape((n_rows, feature), BF16), shape((3 * hidden_units, feature), BF16)],
+        in_specs=[VMEM] * 8,
+        out_specs=[VMEM] * 2,
+        scratch_shapes=[pltpu.VMEM((n_rows, hidden_units), BF16)] * 2,
+        compiler_params=pltpu.CompilerParams(vmem_limit_bytes=48 * 1024 * 1024),
+        cost_estimate=pl.CostEstimate(flops=1, bytes_accessed=1, transcendentals=0),
+    )(dy_rows, x_rows, gate_pre, up_pre, hidden, gate_matrix.T, up_matrix.T, down_matrix)
+    summed = lax.psum_scatter(terms, "dp", scatter_dimension=1, tiled=True)
 
     mixed_own, mixed_far, grads_own, grads_far = local_call(
         functools.partial(mix_kernel, top, side, capacity, 2),
@@ -221,17 +239,18 @@
         )[0]
 
     tokens_far = across(total([meta_far], far_back, BF16))
-    mixed = (mixed_own + across(mixed_far).astype(F32)).astype(BF16)
-    d_gate = (grads_own + across(grads_far))[:, :top]
+    mixed_far, grads_far, own_back = after(across(mixed_far), across(grads_far), own_back)
+    mixed = (mixed_own + mixed_far.astype(F32)).astype(BF16)
+    d_gate = (grads_own + grads_far)[:, :top]
     tokens_own = total([meta], own_back, F32)
     d_tokens = (tokens_own + tokens_far.astype(F32)).astype(BF16)
     return (
         mixed,
         d_tokens,
         d_gate,
-        grad_gate.astype(F32).T[None],
-        grad_up.astype(F32).T[None],
-        grad_down.astype(F32)[None],
+        summed[:hidden_units].astype(F32).T[None],
+        summed[hidden_units : 2 * hidden_units].astype(F32).T[None],
+        summed[2 * hidden_units :].astype(F32)[None],
     )
 
 

time: 234 us -> 252 us (1.077)
  matrix products: 31.3 us -> 6.9 us
  Pallas kernels: 6.71 us -> 28.2 us
  blocking collectives: 0 us -> 19.4 us
  waiting for transfers between devices: 106 us -> 117 us
  starting transfers between devices: 44.2 us -> 37.7 us
  other arithmetic: 16.3 us -> 10.5 us
    dot_general x6 -> x0, matrix products: 23.6 us -> none  [the longest x3 13.8 us: reduced(): lax.dot_general(left, right, contract_rows, preferred_element_type=F32)]
    ppermute x6, waiting for transfers between devices: 59.9 us -> 81 us  [across(): lax.ppermute(value, 'expert', [(e, (e + side) % experts) for e in range(e...]
    all_to_all x0 -> x1, blocking collectives: none -> 19.4 us  [exchange(): lax.all_to_all(shaped, 'expert', 0, 0, axis_index_groups=sets, tiled=True)]
    pallas_call x0 -> x1, Pallas kernels: none -> 19.3 us  [on_device(): pl.pallas_call(backward_kernel, out_shape=[shape((n_rows, feature), BF16)...]
    all_to_all x6 -> x5, waiting for transfers between devices: 46.1 us -> 36.4 us  [exchange(): lax.all_to_all(shaped, 'expert', 0, 0, axis_index_groups=sets, tiled=True)]
    all_to_all x6 -> x5, starting transfers between devices: 33.4 us -> 28.8 us  [exchange(): lax.all_to_all(shaped, 'expert', 0, 0, axis_index_groups=sets, tiled=True)]
    broadcast_in_dim x3 -> x1, other arithmetic: 9.91 us -> 6.07 us  [on_device(): summed[2 * hidden_units:].astype(F32)[None]]
    unnamed x49 -> x31, local copies, waits for them, and re-layouts: 11.1 us -> 13.2 us
  transfers between devices with their start and end apart: 15 -> 12, of which waited for: 8 -> 7; matrix products, arithmetic and copies ran while one was open for 18% -> 6% of each run, Pallas kernels for 3% -> 3%
where the time goes in v5:
time: 252 us; the launch traced here: 251 us
  waiting for transfers between devices  117 us (46%)
  starting transfers between devices  37.7 us (15%)
  Pallas kernels  28.2 us (11%)
  blocking collectives  19.4 us (8%)
  local copies, waits for them, and re-layouts  16.6 us (7%)
  between operations  14.2 us (6%)
  other arithmetic  10.5 us (4%)
  matrix products  6.9 us (3%)
    ppermute x6, waiting for transfers between devices, across(): lax.ppermute(value, 'expert', [(e, (e + side) % experts) for e in range(e...  81 us
    all_to_all x5, waiting for transfers between devices, exchange(): lax.all_to_all(shaped, 'expert', 0, 0, axis_index_groups=sets, tiled=True)  36.4 us
    all_to_all x5, starting transfers between devices, exchange(): lax.all_to_all(shaped, 'expert', 0, 0, axis_index_groups=sets, tiled=True)  28.8 us
    all_to_all x1, blocking collectives, exchange(): lax.all_to_all(shaped, 'expert', 0, 0, axis_index_groups=sets, tiled=True)  19.4 us
    pallas_call x1, Pallas kernels, on_device(): pl.pallas_call(backward_kernel, out_shape=[shape((n_rows, feature), BF16)...  19.3 us
    unnamed x31, local copies, waits for them, and re-layouts  13.2 us
    pallas_call x6, Pallas kernels, local_call(): pl.pallas_call(kernel, out_shape=outs, in_specs=[SMEM] + [VMEM] * len(arg...  8.87 us
    ppermute x6, starting transfers between devices, across(): lax.ppermute(value, 'expert', [(e, (e + side) % experts) for e in range(e...  8.66 us
  transfers between devices with their start and end apart: 12, of which 7 were waited for; matrix products, arithmetic and copies ran while one was open for 6% of the time, Pallas kernels for 3%

profile of v5, /device:TPU:0, one launch (start us, length us, event | category | flops | bytes accessed | tf_op | source)
XLA Modules:
  0.0 250.9 jit_solution(5988620475355170604)
XLA Ops:
  11.1 6.2 %all-to-all-start = ((bf16[8,32,2048]{2,1,0:T(8,128)(2,1)}), bf16[8,32,2048]{2,1,0:T(8,128)(2,1)S(1)}, u32[]{:S(2)}, u32[]{:S(2)}) async-start(bf16[8,32,2048]{2,1,0:T(8,128)(2,1)} %bitcast.3), calls=%async_computation | async-start | bytes 2097152 | tf_op jit(solution)/shard_map/all_to_all | solution.py:155
  17.3 2.7 %collective-permute-start = (bf16[128,2048]{1,0:T(8,128)(2,1)S(1)}, bf16[128,2048]{1,0:T(8,128)(2,1)S(1)}, u32[]{:S(2)}, u32[]{:S(2)}) collective-permute-start(bf16[128,2048]{1,0:T(8,128)(2,1)S(1)} %copy-done.6), channel_id=1, source_target_pairs={{0,8},{1,9},{2,10},{3,11},{4,12},{5,13},{6,14},{7,15},{8,0},{9,1},... | collective-permute-start | bytes 1572872 | tf_op jit(solution)/shard_map/ppermute | solution.py:151
  20.3 19.7 %collective-permute-done.1.refs_0_.refs_1_ = f32[4,128]{1,0:T(4,128)S(1)} collective-permute-done((f32[4,128]{1,0:T(4,128)S(1)}, f32[4,128]{1,0:T(4,128)S(1)}, u32[]{:S(2)}, u32[]{:S(2)}) %collective-permute-start.1) | collective-permute-done | bytes 2080 | tf_op jit(solution)/shard_map/ppermute | solution.py:151
  42.3 7.1 %all-to-all-start.1 = ((bf16[8,32,2048]{2,1,0:T(8,128)(2,1)}), bf16[8,32,2048]{2,1,0:T(8,128)(2,1)S(1)}, u32[]{:S(2)}, u32[]{:S(2)}) async-start(bf16[8,32,2048]{2,1,0:T(8,128)(2,1)} %bitcast.5), calls=%async_computation.1 | async-start | bytes 2097152 | tf_op jit(solution)/shard_map/all_to_all | solution.py:155
  49.4 2.6 %collective-permute-start.2 = (bf16[128,2048]{1,0:T(8,128)(2,1)S(1)}, bf16[128,2048]{1,0:T(8,128)(2,1)S(1)}, u32[]{:S(2)}, u32[]{:S(2)}) collective-permute-start(bf16[128,2048]{1,0:T(8,128)(2,1)S(1)} %copy-done.7), channel_id=1, source_target_pairs={{0,8},{1,9},{2,10},{3,11},{4,12},{5,13},{6,14},{7,15},{8,0},{9,1},... | collective-permute-start | bytes 1572872 | tf_op jit(solution)/shard_map/ppermute | solution.py:151
  52.0 19.1 %collective-permute-done.2.refs_3_ = bf16[128,2048]{1,0:T(8,128)(2,1)S(1)} collective-permute-done((bf16[128,2048]{1,0:T(8,128)(2,1)S(1)}, bf16[128,2048]{1,0:T(8,128)(2,1)S(1)}, u32[]{:S(2)}, u32[]{:S(2)}) %collective-permute-start.2) | collective-permute-done | bytes 524320 | tf_op jit(solution)/shard_map/ppermute | solution.py:151
  71.1 2.2 shard_map.120
  74.1 7.7 %all-to-all-start.2 = ((bf16[8,64,2048]{2,1,0:T(8,128)(2,1)}), bf16[8,64,2048]{2,1,0:T(8,128)(2,1)}, u32[]{:S(2)}, u32[]{:S(2)}) async-start(bf16[8,64,2048]{2,1,0:T(8,128)(2,1)} %bitcast.11), calls=%async_computation.2 | async-start | bytes 4194304 | tf_op jit(solution)/shard_map/all_to_all | solution.py:155
  82.2 2.3 copy-done.12
  86.4 1.9 multiply_convert_fusion
  88.4 3.1 %convolution_convert_fusion = bf16[512,2048]{1,0:T(8,128)(2,1)} fusion(bf16[512,704]{1,0:T(8,128)(2,1)S(1)} %get-tuple-element.59.hidden_ref, bf16[1,704,2048]{2,1,0:T(8,128)(2,1)S(1)} %copy-done.14), kind=kOutput, calls=%fused_computation | convolution fusion | flops 1477443584 | bytes 5701632 | tf_op jit(solution)/shard_map/dot_general | solution.py:198
  92.4 13.5 %all-to-all-done.2 = bf16[8,64,2048]{2,1,0:T(8,128)(2,1)} async-done(((bf16[8,64,2048]{2,1,0:T(8,128)(2,1)}), bf16[8,64,2048]{2,1,0:T(8,128)(2,1)}, u32[]{:S(2)}, u32[]{:S(2)}) %all-to-all-start.2) | async-done | bytes 2097184 | tf_op jit(solution)/shard_map/all_to_all | solution.py:155
  107.0 19.3 %shard_map.122 = (bf16[512,2048]{1,0:T(8,128)(2,1)S(1)}, bf16[2112,2048]{1,0:T(8,128)(2,1)}) custom-call(bf16[512,2048]{1,0:T(8,128)(2,1)} %bitcast.12.dy_ref, bf16[512,2048]{1,0:T(8,128)(2,1)} %bitcast.57, f32[512,704]{1,0:T(8,128)S(1)} %fusion.2.gate_ref, f32[512,704]{1,0:T(8,128)S(1)} %get-tuple-element.60.up_ref, bf16[512,704]{1,0:T(8,128)(2,1)S(1)} %copy-done.4, ...), custom_call_target="tpu_custom_call" | custom-call | flops 1 | bytes 1 | tf_op jit(solution)/shard_map/pallas_call | solution.py:203
  127.6 4.4 %all-to-all-start.3 = ((bf16[8,64,2048]{2,1,0:T(8,128)(2,1)}), bf16[8,64,2048]{2,1,0:T(8,128)(2,1)S(1)}, u32[]{:S(2)}, u32[]{:S(2)}) async-start(bf16[8,64,2048]{2,1,0:T(8,128)(2,1)} %bitcast.64), calls=%async_computation.3 | async-start | bytes 4194304 | tf_op jit(solution)/shard_map/all_to_all | solution.py:155
  132.0 3.5 %fusion.6 = (bf16[8,1,32,2048]{3,2,1,0:T(8,128)(2,1)}, bf16[8,1,32,2048]{3,2,1,0:T(8,128)(2,1)}) fusion(bf16[8,2,32,2048]{3,2,1,0:T(8,128)(2,1)} %bitcast.54), kind=kLoop, calls=%fused_computation.17 | loop fusion | bytes 4194304 | tf_op jit(solution)/shard_map/slice | solution.py:173
  135.4 22.1 %all-to-all-done.3 = bf16[8,64,2048]{2,1,0:T(8,128)(2,1)S(1)} async-done(((bf16[8,64,2048]{2,1,0:T(8,128)(2,1)}), bf16[8,64,2048]{2,1,0:T(8,128)(2,1)S(1)}, u32[]{:S(2)}, u32[]{:S(2)}) %all-to-all-start.3) | async-done | bytes 2097184 | tf_op jit(solution)/shard_map/all_to_all | solution.py:155
  158.9 19.4 %all_to_all.30 = bf16[8,32,2048]{2,1,0:T(8,128)(2,1)S(1)} all-to-all(bf16[8,32,2048]{2,1,0:T(8,128)(2,1)} %bitcast.60), channel_id=1, replica_groups={{0,1,2,3,4,5,6,7},{8,9,10,11,12,13,14,15},{16,17,18,19,20,21,22,23},{24..., dimensions={0} | all-to-all | bytes 2097152 | tf_op jit(solution)/shard_map/all_to_all | solution.py:155
  178.3 3.6 %all-to-all-start.5 = ((bf16[8,32,2048]{2,1,0:T(8,128)(2,1)}), bf16[8,32,2048]{2,1,0:T(8,128)(2,1)S(1)}, u32[]{:S(2)}, u32[]{:S(2)}) async-start(bf16[8,32,2048]{2,1,0:T(8,128)(2,1)} %bitcast.22), calls=%async_computation.5 | async-start | bytes 2097152 | tf_op jit(solution)/shard_map/all_to_all | solution.py:155
  185.5 1.9 shard_map.121
  187.5 2.9 %collective-permute-start.4 = (f32[128,128]{1,0:T(8,128)S(1)}, f32[128,128]{1,0:T(8,128)S(1)}, u32[]{:S(2)}, u32[]{:S(2)}) collective-permute-start(f32[128,128]{1,0:T(8,128)S(1)} %get-tuple-element.31), channel_id=1, source_target_pairs={{0,8},{1,9},{2,10},{3,11},{4,12},{5,13},{6,14},{7,15},{8,0},{9,1},... | collective-permute-start | bytes 196616 | tf_op jit(solution)/shard_map/ppermute | solution.py:151
  191.8 36.0 %collective-permute-done.4 = f32[128,128]{1,0:T(8,128)S(1)} collective-permute-done((f32[128,128]{1,0:T(8,128)S(1)}, f32[128,128]{1,0:T(8,128)S(1)}, u32[]{:S(2)}, u32[]{:S(2)}) %collective-permute-start.4) | collective-permute-done | bytes 65568 | tf_op jit(solution)/shard_map/ppermute | solution.py:151
  228.9 2.0 add_convert_fusion.1
  230.9 6.1 %collective-permute-done.5 = bf16[128,2048]{1,0:T(8,128)(2,1)S(1)} collective-permute-done((bf16[128,2048]{1,0:T(8,128)(2,1)}, bf16[128,2048]{1,0:T(8,128)(2,1)S(1)}, u32[]{:S(2)}, u32[]{:S(2)}) %collective-permute-start.5) | collective-permute-done | bytes 524320 | tf_op jit(solution)/shard_map/ppermute | solution.py:151
  237.9 6.1 %fusion.4 = (f32[1,704,1024]{2,1,0:T(8,128)}, f32[1,1024,704]{1,2,0:T(8,128)}, f32[1,1024,704]{1,2,0:T(8,128)}) fusion(bf16[2112,1024]{1,0:T(8,128)(2,1)} %reduce-scatter.2.cloned.1.call-done), kind=kLoop, calls=%fused_computation.10 | loop fusion | flops 2162688 | bytes 12976128 | tf_op jit(solution)/shard_map/broadcast_in_dim | solution.py:253
  (51 shorter events, 21.5 us)
Async XLA Ops:
  8.5 1.0 copy-start.5
  9.6 7.7 %copy-start.6 = (bf16[128,2048]{1,0:T(8,128)(2,1)S(1)}, bf16[128,2048]{1,0:T(8,128)(2,1)}, u32[]{:S(2)}) copy-start(bf16[128,2048]{1,0:T(8,128)(2,1)} %refs_1_.1) | copy-start | bytes 1572868
  11.1 31.2 %all-to-all-start = ((bf16[8,32,2048]{2,1,0:T(8,128)(2,1)}), bf16[8,32,2048]{2,1,0:T(8,128)(2,1)S(1)}, u32[]{:S(2)}, u32[]{:S(2)}) async-start(bf16[8,32,2048]{2,1,0:T(8,128)(2,1)} %bitcast.3), calls=%async_computation | async-start | bytes 2097152 | tf_op jit(solution)/shard_map/all_to_all | solution.py:155
  17.3 32.1 %copy-start.7 = (bf16[128,2048]{1,0:T(8,128)(2,1)S(1)}, bf16[128,2048]{1,0:T(8,128)(2,1)}, u32[]{:S(2)}) copy-start(bf16[128,2048]{1,0:T(8,128)(2,1)} %refs_2_.1) | copy-start | bytes 1572868
  17.3 22.7 %collective-permute-start = (bf16[128,2048]{1,0:T(8,128)(2,1)S(1)}, bf16[128,2048]{1,0:T(8,128)(2,1)S(1)}, u32[]{:S(2)}, u32[]{:S(2)}) collective-permute-start(bf16[128,2048]{1,0:T(8,128)(2,1)S(1)} %copy-done.6), channel_id=1, source_target_pairs={{0,8},{1,9},{2,10},{3,11},{4,12},{5,13},{6,14},{7,15},{8,0},{9,1},... | collective-permute-start | bytes 1572872 | tf_op jit(solution)/shard_map/ppermute | solution.py:151
  19.9 20.0 %collective-permute-start.1 = (f32[4,128]{1,0:T(4,128)S(1)}, f32[4,128]{1,0:T(4,128)S(1)}, u32[]{:S(2)}, u32[]{:S(2)}) collective-permute-start(f32[4,128]{1,0:T(4,128)S(1)} %pad_maximum_fusion.1.refs_0_), channel_id=1, source_target_pairs={{0,8},{1,9},{2,10},{3,11},{4,12},{5,13},{6,14},{7,15},{8,0},{9,1},... | collective-permute-start | bytes 6152 | tf_op jit(solution)/shard_map/ppermute | solution.py:151
  42.3 31.8 %all-to-all-start.1 = ((bf16[8,32,2048]{2,1,0:T(8,128)(2,1)}), bf16[8,32,2048]{2,1,0:T(8,128)(2,1)S(1)}, u32[]{:S(2)}, u32[]{:S(2)}) async-start(bf16[8,32,2048]{2,1,0:T(8,128)(2,1)} %bitcast.5), calls=%async_computation.1 | async-start | bytes 2097152 | tf_op jit(solution)/shard_map/all_to_all | solution.py:155
  49.4 21.7 %collective-permute-start.2 = (bf16[128,2048]{1,0:T(8,128)(2,1)S(1)}, bf16[128,2048]{1,0:T(8,128)(2,1)S(1)}, u32[]{:S(2)}, u32[]{:S(2)}) collective-permute-start(bf16[128,2048]{1,0:T(8,128)(2,1)S(1)} %copy-done.7), channel_id=1, source_target_pairs={{0,8},{1,9},{2,10},{3,11},{4,12},{5,13},{6,14},{7,15},{8,0},{9,1},... | collective-permute-start | bytes 1572872 | tf_op jit(solution)/shard_map/ppermute | solution.py:151
  74.1 31.8 %all-to-all-start.2 = ((bf16[8,64,2048]{2,1,0:T(8,128)(2,1)}), bf16[8,64,2048]{2,1,0:T(8,128)(2,1)}, u32[]{:S(2)}, u32[]{:S(2)}) async-start(bf16[8,64,2048]{2,1,0:T(8,128)(2,1)} %bitcast.11), calls=%async_computation.2 | async-start | bytes 4194304 | tf_op jit(solution)/shard_map/all_to_all | solution.py:155
  81.7 156.2 %reduce-scatter.2.cloned.1.call-start = ((), (), s32[]{:S(2)}) async-start(), calls=%async_computation.7 | async-start | bytes 12976128 | tf_op jit(solution)/shard_map/reduce_scatter | solution.py:212
  82.0 2.6 %copy-start.12 = (bf16[1,2048,704]{1,2,0:T(8,128)(2,1)S(1)}, bf16[1,2048,704]{1,2,0:T(8,128)(2,1)}, u32[]{:S(2)}) copy-start(bf16[1,2048,704]{1,2,0:T(8,128)(2,1)} %param.10) | copy-start | bytes 8650756
  82.2 4.2 %copy-start.11 = (bf16[8,2,32,2048]{3,2,1,0:T(8,128)(2,1)}, bf16[8,2,32,2048]{3,2,1,0:T(8,128)(2,1)S(1)}, u32[]{:S(2)}) copy-start(bf16[8,2,32,2048]{3,2,1,0:T(8,128)(2,1)S(1)} %pad_maximum_fusion) | copy-start | bytes 6291460
  84.5 1.9 copy-start.13
  86.4 2.0 copy-start.14
  105.9 1.1 copy-start.4
  126.3 1.3 copy-start.2
  127.6 29.9 %all-to-all-start.3 = ((bf16[8,64,2048]{2,1,0:T(8,128)(2,1)}), bf16[8,64,2048]{2,1,0:T(8,128)(2,1)S(1)}, u32[]{:S(2)}, u32[]{:S(2)}) async-start(bf16[8,64,2048]{2,1,0:T(8,128)(2,1)} %bitcast.64), calls=%async_computation.3 | async-start | bytes 4194304 | tf_op jit(solution)/shard_map/all_to_all | solution.py:155
  157.5 1.3 copy-start
  178.3 49.5 %all-to-all-start.5 = ((bf16[8,32,2048]{2,1,0:T(8,128)(2,1)}), bf16[8,32,2048]{2,1,0:T(8,128)(2,1)S(1)}, u32[]{:S(2)}, u32[]{:S(2)}) async-start(bf16[8,32,2048]{2,1,0:T(8,128)(2,1)} %bitcast.22), calls=%async_computation.5 | async-start | bytes 2097152 | tf_op jit(solution)/shard_map/all_to_all | solution.py:155
  181.8 1.6 copy-start.1
  183.4 1.0 copy-start.8
  187.4 40.4 %collective-permute-start.3 = (bf16[128,2048]{1,0:T(8,128)(2,1)S(1)}, bf16[128,2048]{1,0:T(8,128)(2,1)}, u32[]{:S(2)}, u32[]{:S(2)}) collective-permute-start(bf16[128,2048]{1,0:T(8,128)(2,1)S(1)} %get-tuple-element.30), channel_id=1, source_target_pairs={{0,8},{1,9},{2,10},{3,11},{4,12},{5,13},{6,14},{7,15},{8,0},{9,1},... | collective-permute-start | bytes 1572872 | tf_op jit(solution)/shard_map/ppermute | solution.py:151
  187.5 40.3 %collective-permute-start.4 = (f32[128,128]{1,0:T(8,128)S(1)}, f32[128,128]{1,0:T(8,128)S(1)}, u32[]{:S(2)}, u32[]{:S(2)}) collective-permute-start(f32[128,128]{1,0:T(8,128)S(1)} %get-tuple-element.31), channel_id=1, source_target_pairs={{0,8},{1,9},{2,10},{3,11},{4,12},{5,13},{6,14},{7,15},{8,0},{9,1},... | collective-permute-start | bytes 196616 | tf_op jit(solution)/shard_map/ppermute | solution.py:151
  191.7 45.3 %collective-permute-start.5 = (bf16[128,2048]{1,0:T(8,128)(2,1)}, bf16[128,2048]{1,0:T(8,128)(2,1)S(1)}, u32[]{:S(2)}, u32[]{:S(2)}) collective-permute-start(bf16[128,2048]{1,0:T(8,128)(2,1)} %shard_map.124), channel_id=1, source_target_pairs={{0,8},{1,9},{2,10},{3,11},{4,12},{5,13},{6,14},{7,15},{8,0},{9,1},... | collective-permute-start | bytes 1572872 | tf_op jit(solution)/shard_map/ppermute | solution.py:151
  (3 other events, 2.7 us)
Sparse Core Ops, SparseCore 0:
  127.7 15.8 reduce-scatter.1

commit v6 on v5

--- a/solution.py
+++ b/solution.py
@@ -73,15 +73,15 @@
 TRANSPOSED = (((0,), (0,)), ((), ()))
 
 
-def sum_kernel(top, side, capacity, count, me_ref, *refs):
-    metas, back, outs = refs[:count], refs[count], refs[count + 1 :]
-    tables = slot_tables(me_ref[0], metas, top, side, capacity)
-    for ks, out in zip(tables, outs):
-        held = functools.reduce(lambda p, q: p + q, ks).astype(BF16)
-        for c, e in strips(out.shape[1]):
-            out[:, c:e] = lax.dot_general(
-                held, back[:, c:e], TRANSPOSED, preferred_element_type=F32
-            ).astype(out.dtype)
+def sum_kernel(top, side, capacity, me_ref, meta, back, *refs):
+    (table,) = slot_tables(me_ref[0], [meta], top, side, capacity)
+    held = functools.reduce(lambda p, q: p + q, table).astype(BF16)
+    out = refs[-1]
+    for c, e in strips(out.shape[1]):
+        got = lax.dot_general(held, back[:, c:e], TRANSPOSED, preferred_element_type=F32)
+        for other in refs[:-1]:
+            got += other[:, c:e].astype(F32)
+        out[:, c:e] = got.astype(BF16)
 
 
 def mix_kernel(top, side, capacity, count, me_ref, *refs):
@@ -110,9 +110,9 @@
 
 
 def backward_kernel(
-    dy_ref, x_ref, gate_ref, up_ref, hidden_ref, wg_ref, wu_ref, wd_ref, dx_ref, terms_ref, gg_ref, gu_ref
+    side, dy_ref, x_ref, gate_ref, up_ref, hidden_ref, wg_ref, wu_ref, wd_ref, own_ref, far_ref, terms_ref, gg_ref, gu_ref
 ):
-    rows, units = gate_ref.shape
+    units, feature = gate_ref.shape[1], x_ref.shape[1]
     across_last = (((1,), (1,)), ((), ()))
     for c, e in strips(units, 256):
         back = lax.dot_general(
@@ -122,14 +122,16 @@
         sig = 1.0 / (1.0 + jnp.exp(-gate))
         gg_ref[:, c:e] = (back * up_ref[:, c:e] * (sig * (1.0 + gate * (1.0 - sig)))).astype(BF16)
         gu_ref[:, c:e] = (back * (gate * sig)).astype(BF16)
-    for c, e in strips(dx_ref.shape[1]):
+    for c, e in strips(feature):
         got = jnp.dot(gg_ref[...], wg_ref[:, c:e], preferred_element_type=F32)
         got += jnp.dot(gu_ref[...], wu_ref[:, c:e], preferred_element_type=F32)
-        dx_ref[:, c:e] = got.astype(BF16)
+        blocks = got.reshape(side, 2, own_ref.shape[0] // side, e - c)
+        for b, out in enumerate((own_ref, far_ref)):
+            out[:, c:e] = blocks[:, b].reshape(out.shape[0], e - c).astype(BF16)
     pairs = ((gg_ref, x_ref), (gu_ref, x_ref), (hidden_ref, dy_ref))
     for n, (left, right) in enumerate(pairs):
         for r, t in strips(units, 256):
-            for c, e in strips(dx_ref.shape[1], 1024):
+            for c, e in strips(feature, 1024):
                 terms_ref[n * units + r : n * units + t, c:e] = lax.dot_general(
                     left[:, r:t], right[:, c:e], TRANSPOSED, preferred_element_type=F32
                 ).astype(BF16)
@@ -168,10 +170,6 @@
             2 * count * count * half * tok * feature,
         )[0]
 
-    def split(rows):
-        parts = rows.reshape(side, 2, capacity, feature)
-        return [parts[:, b].reshape(half, feature) for b in range(2)]
-
     meta = jnp.concatenate([expert_ids.T.astype(F32), gate_prob.T], 0)
     x_far = across(tokens)
     meta_far = across(meta)
@@ -200,15 +198,20 @@
     y_back = exchange(expert_out)
 
     n_rows = 2 * half
-    expert_dx, terms = pl.pallas_call(
-        backward_kernel,
-        out_shape=[shape((n_rows, feature), BF16), shape((3 * hidden_units, feature), BF16)],
+    dx_own, dx_far, terms = pl.pallas_call(
+        functools.partial(backward_kernel, side),
+        out_shape=[
+            shape((half, feature), BF16),
+            shape((half, feature), BF16),
+            shape((3 * hidden_units, feature), BF16),
+        ],
         in_specs=[VMEM] * 8,
-        out_specs=[VMEM] * 2,
+        out_specs=[VMEM] * 3,
         scratch_shapes=[pltpu.VMEM((n_rows, hidden_units), BF16)] * 2,
         compiler_params=pltpu.CompilerParams(vmem_limit_bytes=48 * 1024 * 1024),
         cost_estimate=pl.CostEstimate(flops=1, bytes_accessed=1, transcendentals=0),
     )(dy_rows, x_rows, gate_pre, up_pre, hidden, gate_matrix.T, up_matrix.T, down_matrix)
+    dx_far, dx_own, terms, y_back = after(dx_far, dx_own, terms, y_back)
     summed = lax.psum_scatter(terms, "dp", scatter_dimension=1, tiled=True)
 
     mixed_own, mixed_far, grads_own, grads_far = local_call(
@@ -223,27 +226,26 @@
         [*metas, d_mixed, d_far, y_back],
         4 * top * half * 2 * tok * feature,
     )
-    dx_own, dx_far = split(expert_dx)
-    dx_far, y_back = after(dx_far, y_back)
     far_back = exchange(dx_far)
     far_back, dx_own = after(far_back, dx_own)
     own_back = exchange(dx_own)
 
-    def total(metas, back, kind):
+    def total(meta, back, *other):
         return local_call(
-            functools.partial(sum_kernel, top, side, capacity, 1),
-            [shape((tok, feature), kind)],
+            functools.partial(sum_kernel, top, side, capacity),
+            [shape((tok, feature), BF16)],
             me_arr,
-            [*metas, back],
+            [meta, back, *other],
             2 * half * tok * feature,
         )[0]
 
-    tokens_far = across(total([meta_far], far_back, BF16))
-    mixed_far, grads_far, own_back = after(across(mixed_far), across(grads_far), own_back)
+    tokens_far, mixed_far, grads_far = after(
+        total(meta_far, far_back), across(mixed_far), across(grads_far)
+    )
+    tokens_far = across(tokens_far)
     mixed = (mixed_own + mixed_far.astype(F32)).astype(BF16)
     d_gate = (grads_own + grads_far)[:, :top]
-    tokens_own = total([meta], own_back, F32)
-    d_tokens = (tokens_own + tokens_far.astype(F32)).astype(BF16)
+    d_tokens = total(meta, own_back, tokens_far)
     return (
         mixed,
         d_tokens,

time: 252 us -> 232 us (0.921)
  waiting for transfers between devices: 117 us -> 97.6 us
    all_to_all x5, waiting for transfers between devices: 36.4 us -> 16.1 us  [exchange(): lax.all_to_all(shaped, 'expert', 0, 0, axis_index_groups=sets, tiled=True)]
    slice x1 -> x0, local copies, waits for them, and re-layouts: 3.46 us -> none  [split(): return [parts[:, b].reshape(half, feature) for b in range(2)]]
    unnamed x31 -> x37, local copies, waits for them, and re-layouts: 13.2 us -> 14.3 us
  transfers between devices with their start and end apart: 12 -> 12, of which waited for: 7 -> 7; matrix products, arithmetic and copies ran while one was open for 6% -> 5% of each run, Pallas kernels for 3% -> 12%
where the time goes in v6:
time: 232 us; the launch traced here: 231 us
  waiting for transfers between devices  97.6 us (42%)
  starting transfers between devices  37.8 us (16%)
  Pallas kernels  28.6 us (12%)
  blocking collectives  19.2 us (8%)
  local copies, waits for them, and re-layouts  14.3 us (6%)
  between operations  14.1 us (6%)
  other arithmetic  11 us (5%)
  matrix products  8.01 us (3%)
    ppermute x6, waiting for transfers between devices, across(): lax.ppermute(value, 'expert', [(e, (e + side) % experts) for e in range(e...  81.5 us
    all_to_all x5, starting transfers between devices, exchange(): lax.all_to_all(shaped, 'expert', 0, 0, axis_index_groups=sets, tiled=True)  29 us
    all_to_all x1, blocking collectives, exchange(): lax.all_to_all(shaped, 'expert', 0, 0, axis_index_groups=sets, tiled=True)  19.2 us
    pallas_call x1, Pallas kernels, on_device(): pl.pallas_call(functools.partial(backward_kernel, side), out_shape=[shape...  19 us
    all_to_all x5, waiting for transfers between devices, exchange(): lax.all_to_all(shaped, 'expert', 0, 0, axis_index_groups=sets, tiled=True)  16.1 us
    unnamed x37, local copies, waits for them, and re-layouts  14.3 us
    pallas_call x6, Pallas kernels, local_call(): pl.pallas_call(kernel, out_shape=outs, in_specs=[SMEM] + [VMEM] * len(arg...  9.68 us
    ppermute x6, starting transfers between devices, across(): lax.ppermute(value, 'expert', [(e, (e + side) % experts) for e in range(e...  8.58 us
  transfers between devices with their start and end apart: 12, of which 7 were waited for; matrix products, arithmetic and copies ran while one was open for 5% of the time, Pallas kernels for 12%

profile of v6, /device:TPU:0, one launch (start us, length us, event | category | flops | bytes accessed | tf_op | source)
XLA Modules:
  0.0 230.6 jit_solution(9551036227590009752)
XLA Ops:
  11.1 6.2 %all-to-all-start = ((bf16[8,32,2048]{2,1,0:T(8,128)(2,1)}), bf16[8,32,2048]{2,1,0:T(8,128)(2,1)S(1)}, u32[]{:S(2)}, u32[]{:S(2)}) async-start(bf16[8,32,2048]{2,1,0:T(8,128)(2,1)} %bitcast.3), calls=%async_computation | async-start | bytes 2097152 | tf_op jit(solution)/shard_map/all_to_all | solution.py:157
  17.3 2.7 %collective-permute-start = (bf16[128,2048]{1,0:T(8,128)(2,1)S(1)}, bf16[128,2048]{1,0:T(8,128)(2,1)S(1)}, u32[]{:S(2)}, u32[]{:S(2)}) collective-permute-start(bf16[128,2048]{1,0:T(8,128)(2,1)S(1)} %copy-done.8), channel_id=1, source_target_pairs={{0,8},{1,9},{2,10},{3,11},{4,12},{5,13},{6,14},{7,15},{8,0},{9,1},... | collective-permute-start | bytes 1572872 | tf_op jit(solution)/shard_map/ppermute | solution.py:153
  20.3 19.7 %collective-permute-done.1.refs_0_.refs_1_.meta = f32[4,128]{1,0:T(4,128)S(1)} collective-permute-done((f32[4,128]{1,0:T(4,128)S(1)}, f32[4,128]{1,0:T(4,128)S(1)}, u32[]{:S(2)}, u32[]{:S(2)}) %collective-permute-start.1) | collective-permute-done | bytes 2080 | tf_op jit(solution)/shard_map/ppermute | solution.py:153
  42.3 7.1 %all-to-all-start.1 = ((bf16[8,32,2048]{2,1,0:T(8,128)(2,1)}), bf16[8,32,2048]{2,1,0:T(8,128)(2,1)}, u32[]{:S(2)}, u32[]{:S(2)}) async-start(bf16[8,32,2048]{2,1,0:T(8,128)(2,1)} %bitcast.5), calls=%async_computation.1 | async-start | bytes 2097152 | tf_op jit(solution)/shard_map/all_to_all | solution.py:157
  49.4 2.6 %collective-permute-start.2 = (bf16[128,2048]{1,0:T(8,128)(2,1)S(1)}, bf16[128,2048]{1,0:T(8,128)(2,1)S(1)}, u32[]{:S(2)}, u32[]{:S(2)}) collective-permute-start(bf16[128,2048]{1,0:T(8,128)(2,1)S(1)} %copy-done.9), channel_id=1, source_target_pairs={{0,8},{1,9},{2,10},{3,11},{4,12},{5,13},{6,14},{7,15},{8,0},{9,1},... | collective-permute-start | bytes 1572872 | tf_op jit(solution)/shard_map/ppermute | solution.py:153
  52.0 19.1 %collective-permute-done.2.refs_3_ = bf16[128,2048]{1,0:T(8,128)(2,1)S(1)} collective-permute-done((bf16[128,2048]{1,0:T(8,128)(2,1)S(1)}, bf16[128,2048]{1,0:T(8,128)(2,1)S(1)}, u32[]{:S(2)}, u32[]{:S(2)}) %collective-permute-start.2) | collective-permute-done | bytes 524320 | tf_op jit(solution)/shard_map/ppermute | solution.py:153
  71.1 2.2 shard_map.120
  74.1 7.7 %all-to-all-start.2 = ((bf16[8,64,2048]{2,1,0:T(8,128)(2,1)}), bf16[8,64,2048]{2,1,0:T(8,128)(2,1)S(1)}, u32[]{:S(2)}, u32[]{:S(2)}) async-start(bf16[8,64,2048]{2,1,0:T(8,128)(2,1)} %bitcast.11), calls=%async_computation.2 | async-start | bytes 4194304 | tf_op jit(solution)/shard_map/all_to_all | solution.py:157
  83.9 1.8 fusion.2.gate_ref
  85.9 3.1 %multiply_convert_fusion = (bf16[512,704]{1,0:T(8,128)(2,1)S(1)}, f32[512,704]{1,0:T(8,128)}) fusion(f32[512,704]{1,0:T(8,128)S(1)} %fusion.2.gate_ref, bf16[512,2048]{1,0:T(8,128)(2,1)S(1)} %bitcast.54, bf16[1,2048,704]{1,2,0:T(8,128)(2,1)S(1)} %copy-done.16), kind=kOutput, calls=%fused_computation.8 | convolution fusion | flops 1478557696 | bytes 8585216 | tf_op jit(solution)/shard_map/dot_general | solution.py:192
  88.9 3.1 %convolution_convert_fusion = bf16[512,2048]{1,0:T(8,128)(2,1)} fusion(bf16[512,704]{1,0:T(8,128)(2,1)S(1)} %get-tuple-element.65.hidden_ref, bf16[1,704,2048]{2,1,0:T(8,128)(2,1)S(1)} %copy-done.17), kind=kOutput, calls=%fused_computation | convolution fusion | flops 1477443584 | bytes 5701632 | tf_op jit(solution)/shard_map/dot_general | solution.py:196
  92.9 12.8 %all-to-all-done.2 = bf16[8,64,2048]{2,1,0:T(8,128)(2,1)S(1)} async-done(((bf16[8,64,2048]{2,1,0:T(8,128)(2,1)}), bf16[8,64,2048]{2,1,0:T(8,128)(2,1)S(1)}, u32[]{:S(2)}, u32[]{:S(2)}) %all-to-all-start.2) | async-done | bytes 2097184 | tf_op jit(solution)/shard_map/all_to_all | solution.py:157
  107.1 4.4 %all-to-all-start.3 = ((bf16[8,64,2048]{2,1,0:T(8,128)(2,1)}), bf16[8,64,2048]{2,1,0:T(8,128)(2,1)S(1)}, u32[]{:S(2)}, u32[]{:S(2)}) async-start(bf16[8,64,2048]{2,1,0:T(8,128)(2,1)} %bitcast.60), calls=%async_computation.3 | async-start | bytes 4194304 | tf_op jit(solution)/shard_map/all_to_all | solution.py:157
  115.6 19.0 %shard_map.121 = (bf16[256,2048]{1,0:T(8,128)(2,1)}, bf16[256,2048]{1,0:T(8,128)(2,1)S(1)}, bf16[2112,2048]{1,0:T(8,128)(2,1)}) custom-call(bf16[512,2048]{1,0:T(8,128)(2,1)} %bitcast.52, bf16[512,2048]{1,0:T(8,128)(2,1)} %bitcast.55, f32[512,704]{1,0:T(8,128)S(1)} %copy-done.3, f32[512,704]{1,0:T(8,128)S(1)} %copy-done.4, bf16[512,704]{1,0:T(8,128)(2,1)S(1)} %copy-done.6, ...), custom_call_target="tpu_custom_call" | custom-call | flops 1 | bytes 1 | tf_op jit(solution)/shard_map/pallas_call | solution.py:201
  134.6 2.4 %all-to-all-done.3 = bf16[8,64,2048]{2,1,0:T(8,128)(2,1)S(1)} async-done(((bf16[8,64,2048]{2,1,0:T(8,128)(2,1)}), bf16[8,64,2048]{2,1,0:T(8,128)(2,1)S(1)}, u32[]{:S(2)}, u32[]{:S(2)}) %all-to-all-start.3) | async-done | bytes 2097184 | tf_op jit(solution)/shard_map/all_to_all | solution.py:157
  138.3 19.2 %all_to_all.30 = bf16[8,32,2048]{2,1,0:T(8,128)(2,1)S(1)} all-to-all(bf16[8,32,2048]{2,1,0:T(8,128)(2,1)S(1)} %bitcast.51), channel_id=1, replica_groups={{0,1,2,3,4,5,6,7},{8,9,10,11,12,13,14,15},{16,17,18,19,20,21,22,23},{24..., dimensions={0} | all-to-all | bytes 2097152 | tf_op jit(solution)/shard_map/all_to_all | solution.py:157
  157.5 3.8 %all-to-all-start.5 = ((bf16[8,32,2048]{2,1,0:T(8,128)(2,1)}), bf16[8,32,2048]{2,1,0:T(8,128)(2,1)S(1)}, u32[]{:S(2)}, u32[]{:S(2)}) async-start(bf16[8,32,2048]{2,1,0:T(8,128)(2,1)} %bitcast.19), calls=%async_computation.5 | async-start | bytes 2097152 | tf_op jit(solution)/shard_map/all_to_all | solution.py:157
  161.3 1.6 copy-done.1
  165.0 1.9 shard_map.122
  166.9 2.9 %collective-permute-start.4 = (f32[128,128]{1,0:T(8,128)S(1)}, f32[128,128]{1,0:T(8,128)S(1)}, u32[]{:S(2)}, u32[]{:S(2)}) collective-permute-start(f32[128,128]{1,0:T(8,128)S(1)} %get-tuple-element.43), channel_id=1, source_target_pairs={{0,8},{1,9},{2,10},{3,11},{4,12},{5,13},{6,14},{7,15},{8,0},{9,1},... | collective-permute-start | bytes 196616 | tf_op jit(solution)/shard_map/ppermute | solution.py:153
  171.1 22.8 %collective-permute-done.4 = f32[128,128]{1,0:T(8,128)S(1)} collective-permute-done((f32[128,128]{1,0:T(8,128)S(1)}, f32[128,128]{1,0:T(8,128)S(1)}, u32[]{:S(2)}, u32[]{:S(2)}) %collective-permute-start.4) | collective-permute-done | bytes 65568 | tf_op jit(solution)/shard_map/ppermute | solution.py:153
  194.6 1.9 add_convert_fusion
  196.6 19.9 %collective-permute-done.5.refs_0_ = bf16[128,2048]{1,0:T(8,128)(2,1)S(1)} collective-permute-done((bf16[128,2048]{1,0:T(8,128)(2,1)}, bf16[128,2048]{1,0:T(8,128)(2,1)S(1)}, u32[]{:S(2)}, u32[]{:S(2)}) %collective-permute-start.5) | collective-permute-done | bytes 524320 | tf_op jit(solution)/shard_map/ppermute | solution.py:153
  217.7 6.1 %fusion.4 = (f32[1,704,1024]{2,1,0:T(8,128)}, f32[1,1024,704]{1,2,0:T(8,128)}, f32[1,1024,704]{1,2,0:T(8,128)}) fusion(bf16[2112,1024]{1,0:T(8,128)(2,1)} %reduce-scatter.2.cloned.1.call-done), kind=kLoop, calls=%fused_computation.10 | loop fusion | flops 2162688 | bytes 12976128 | tf_op jit(solution)/shard_map/broadcast_in_dim | solution.py:255
  (55 shorter events, 22.7 us)
Async XLA Ops:
  9.6 7.7 %copy-start.8 = (bf16[128,2048]{1,0:T(8,128)(2,1)S(1)}, bf16[128,2048]{1,0:T(8,128)(2,1)}, u32[]{:S(2)}) copy-start(bf16[128,2048]{1,0:T(8,128)(2,1)} %refs_1_.1) | copy-start | bytes 1572868
  11.1 31.2 %all-to-all-start = ((bf16[8,32,2048]{2,1,0:T(8,128)(2,1)}), bf16[8,32,2048]{2,1,0:T(8,128)(2,1)S(1)}, u32[]{:S(2)}, u32[]{:S(2)}) async-start(bf16[8,32,2048]{2,1,0:T(8,128)(2,1)} %bitcast.3), calls=%async_computation | async-start | bytes 2097152 | tf_op jit(solution)/shard_map/all_to_all | solution.py:157
  17.3 32.1 %copy-start.9 = (bf16[128,2048]{1,0:T(8,128)(2,1)S(1)}, bf16[128,2048]{1,0:T(8,128)(2,1)}, u32[]{:S(2)}) copy-start(bf16[128,2048]{1,0:T(8,128)(2,1)} %refs_2_.1) | copy-start | bytes 1572868
  17.3 22.7 %collective-permute-start = (bf16[128,2048]{1,0:T(8,128)(2,1)S(1)}, bf16[128,2048]{1,0:T(8,128)(2,1)S(1)}, u32[]{:S(2)}, u32[]{:S(2)}) collective-permute-start(bf16[128,2048]{1,0:T(8,128)(2,1)S(1)} %copy-done.8), channel_id=1, source_target_pairs={{0,8},{1,9},{2,10},{3,11},{4,12},{5,13},{6,14},{7,15},{8,0},{9,1},... | collective-permute-start | bytes 1572872 | tf_op jit(solution)/shard_map/ppermute | solution.py:153
  19.9 20.0 %collective-permute-start.1 = (f32[4,128]{1,0:T(4,128)S(1)}, f32[4,128]{1,0:T(4,128)S(1)}, u32[]{:S(2)}, u32[]{:S(2)}) collective-permute-start(f32[4,128]{1,0:T(4,128)S(1)} %pad_maximum_fusion.1.refs_0_.meta), channel_id=1, source_target_pairs={{0,8},{1,9},{2,10},{3,11},{4,12},{5,13},{6,14},{7,15},{8,0},{9,1},... | collective-permute-start | bytes 6152 | tf_op jit(solution)/shard_map/ppermute | solution.py:153
  42.3 31.8 %all-to-all-start.1 = ((bf16[8,32,2048]{2,1,0:T(8,128)(2,1)}), bf16[8,32,2048]{2,1,0:T(8,128)(2,1)}, u32[]{:S(2)}, u32[]{:S(2)}) async-start(bf16[8,32,2048]{2,1,0:T(8,128)(2,1)} %bitcast.5), calls=%async_computation.1 | async-start | bytes 2097152 | tf_op jit(solution)/shard_map/all_to_all | solution.py:157
  49.4 21.7 %collective-permute-start.2 = (bf16[128,2048]{1,0:T(8,128)(2,1)S(1)}, bf16[128,2048]{1,0:T(8,128)(2,1)S(1)}, u32[]{:S(2)}, u32[]{:S(2)}) collective-permute-start(bf16[128,2048]{1,0:T(8,128)(2,1)S(1)} %copy-done.9), channel_id=1, source_target_pairs={{0,8},{1,9},{2,10},{3,11},{4,12},{5,13},{6,14},{7,15},{8,0},{9,1},... | collective-permute-start | bytes 1572872 | tf_op jit(solution)/shard_map/ppermute | solution.py:153
  74.1 31.7 %all-to-all-start.2 = ((bf16[8,64,2048]{2,1,0:T(8,128)(2,1)}), bf16[8,64,2048]{2,1,0:T(8,128)(2,1)S(1)}, u32[]{:S(2)}, u32[]{:S(2)}) async-start(bf16[8,64,2048]{2,1,0:T(8,128)(2,1)} %bitcast.11), calls=%async_computation.2 | async-start | bytes 4194304 | tf_op jit(solution)/shard_map/all_to_all | solution.py:157
  81.7 2.1 copy-start.15
  83.3 2.4 %copy-start.14 = (bf16[8,2,32,2048]{3,2,1,0:T(8,128)(2,1)}, bf16[8,2,32,2048]{3,2,1,0:T(8,128)(2,1)S(1)}, u32[]{:S(2)}) copy-start(bf16[8,2,32,2048]{3,2,1,0:T(8,128)(2,1)S(1)} %pad_maximum_fusion) | copy-start | bytes 6291460
  83.9 2.0 copy-start.16
  85.9 3.1 %copy-start.2 = (f32[512,704]{1,0:T(8,128)}, f32[512,704]{1,0:T(8,128)S(1)}, u32[]{:S(2)}) copy-start(f32[512,704]{1,0:T(8,128)S(1)} %fusion.2.gate_ref) | copy-start | bytes 4325380
  85.9 3.1 %copy-start.17 = (bf16[1,704,2048]{2,1,0:T(8,128)(2,1)S(1)}, bf16[1,704,2048]{2,1,0:T(8,128)(2,1)}, u32[]{:S(2)}) copy-start(bf16[1,704,2048]{2,1,0:T(8,128)(2,1)} %param.12) | copy-start | bytes 8650756
  105.8 1.3 copy-start.13
  107.1 29.9 %all-to-all-start.3 = ((bf16[8,64,2048]{2,1,0:T(8,128)(2,1)}), bf16[8,64,2048]{2,1,0:T(8,128)(2,1)S(1)}, u32[]{:S(2)}, u32[]{:S(2)}) async-start(bf16[8,64,2048]{2,1,0:T(8,128)(2,1)} %bitcast.60), calls=%async_computation.3 | async-start | bytes 4194304 | tf_op jit(solution)/shard_map/all_to_all | solution.py:157
  111.4 106.3 %reduce-scatter.2.cloned.1.call-start = ((), (), s32[]{:S(2)}) async-start(), calls=%async_computation.7 | async-start | bytes 12976128 | tf_op jit(solution)/shard_map/reduce_scatter | solution.py:215
  111.6 1.4 copy-start.3
  113.1 1.4 copy-start.4
  137.0 1.3 copy-start
  157.5 58.9 %all-to-all-start.5 = ((bf16[8,32,2048]{2,1,0:T(8,128)(2,1)}), bf16[8,32,2048]{2,1,0:T(8,128)(2,1)S(1)}, u32[]{:S(2)}, u32[]{:S(2)}) async-start(bf16[8,32,2048]{2,1,0:T(8,128)(2,1)} %bitcast.19), calls=%async_computation.5 | async-start | bytes 2097152 | tf_op jit(solution)/shard_map/all_to_all | solution.py:157
  161.3 1.6 copy-start.1
  166.9 27.1 %collective-permute-start.3 = (bf16[128,2048]{1,0:T(8,128)(2,1)S(1)}, bf16[128,2048]{1,0:T(8,128)(2,1)}, u32[]{:S(2)}, u32[]{:S(2)}) collective-permute-start(bf16[128,2048]{1,0:T(8,128)(2,1)S(1)} %get-tuple-element.42), channel_id=1, source_target_pairs={{0,8},{1,9},{2,10},{3,11},{4,12},{5,13},{6,14},{7,15},{8,0},{9,1},... | collective-permute-start | bytes 1572872 | tf_op jit(solution)/shard_map/ppermute | solution.py:153
  166.9 27.0 %collective-permute-start.4 = (f32[128,128]{1,0:T(8,128)S(1)}, f32[128,128]{1,0:T(8,128)S(1)}, u32[]{:S(2)}, u32[]{:S(2)}) collective-permute-start(f32[128,128]{1,0:T(8,128)S(1)} %get-tuple-element.43), channel_id=1, source_target_pairs={{0,8},{1,9},{2,10},{3,11},{4,12},{5,13},{6,14},{7,15},{8,0},{9,1},... | collective-permute-start | bytes 196616 | tf_op jit(solution)/shard_map/ppermute | solution.py:153
  194.0 22.5 %collective-permute-start.5 = (bf16[128,2048]{1,0:T(8,128)(2,1)}, bf16[128,2048]{1,0:T(8,128)(2,1)S(1)}, u32[]{:S(2)}, u32[]{:S(2)}) collective-permute-start(bf16[128,2048]{1,0:T(8,128)(2,1)} %shard_map.123), channel_id=1, source_target_pairs={{0,8},{1,9},{2,10},{3,11},{4,12},{5,13},{6,14},{7,15},{8,0},{9,1},... | collective-permute-start | bytes 1572872 | tf_op jit(solution)/shard_map/ppermute | solution.py:153
  (6 other events, 5.9 us)
Sparse Core Ops, SparseCore 0:
  137.1 15.6 reduce-scatter.1

commit v7 on v6

v7 whole, which is shorter than its diff:
```python
import functools

import jax
import jax.numpy as jnp
from jax import lax
from jax.experimental import pallas as pl
from jax.experimental.pallas import tpu as pltpu
from jax.sharding import PartitionSpec as P

BF16 = jnp.bfloat16
F32 = jnp.float32
LANES = 128
STRIP = 512
VMEM = pl.BlockSpec(memory_space=pltpu.VMEM)
SMEM = pl.BlockSpec(memory_space=pltpu.SMEM)


def local_call(kernel, outs, me, args, flops):
    size = sum(x.size * x.dtype.itemsize for x in (*outs, *args))
    return pl.pallas_call(
        kernel,
        out_shape=outs,
        in_specs=[SMEM] + [VMEM] * len(args),
        out_specs=[VMEM] * len(outs),
        compiler_params=pltpu.CompilerParams(vmem_limit_bytes=16 * 1024 * 1024),
        cost_estimate=pl.CostEstimate(flops=flops, bytes_accessed=size, transcendentals=0),
    )(me, *args)


def strips(width, step=STRIP):
    return [(c, min(c + step, width)) for c in range(0, width, step)]


def slot_tables(me, metas, top, side, capacity):
    count = len(metas)
    span = count * capacity
    tok = metas[0].shape[1]
    slot = lax.broadcasted_iota(jnp.int32, (side * span, tok), 0)
    expert = ((me - lax.rem(me, side)) + slot // span).astype(F32)
    block_of = lax.rem(slot, span) // capacity
    place = lax.rem(slot, capacity).astype(F32)
    row = lax.broadcasted_iota(jnp.int32, (tok, tok), 0)
    column = lax.broadcasted_iota(jnp.int32, (tok, tok), 1)
    earlier = jnp.where(row < column, 1.0, 0.0).astype(BF16)
    tables = []
    for b in range(count):
        named = [jnp.where(metas[b][k : k + 1, :] == expert, 1.0, 0.0) for k in range(top)]
        member = functools.reduce(lambda p, q: p + q, named)
        rank = jnp.dot(member.astype(BF16), earlier, preferred_element_type=F32)
        here = rank == place
        if count > 1:
            here = here & (block_of == b)
        tables.append([jnp.where(here, part, 0.0) for part in named])
    return tables


def pick_kernel(top, side, capacity, scaled, me_ref, *refs):
    count = len(scaled)
    metas, blocks, out = refs[:count], refs[count : 2 * count], refs[2 * count]
    tables = slot_tables(me_ref[0], metas, top, side, capacity)
    held = jnp.concatenate([functools.reduce(lambda p, q: p + q, ks) for ks in tables], 1)
    held = held.astype(BF16)
    gate = 0.0
    for meta, ks, has in zip(metas, tables, scaled):
        for k, part in enumerate(ks):
            if has:
                part = part * meta[top + k : top + k + 1, :]
            gate += jnp.sum(part, 1, keepdims=True)
    for c, e in strips(out.shape[1]):
        block = jnp.concatenate([ref[:, c:e] for ref in blocks], 0)
        got = jnp.dot(held, block, preferred_element_type=F32)
        out[:, c:e] = ((gate * got) if any(scaled) else got).astype(BF16)


TRANSPOSED = (((0,), (0,)), ((), ()))


def picked_sum(table, back, c, e):
    return lax.dot_general(
        table.astype(BF16), back[:, c:e], TRANSPOSED, preferred_element_type=F32
    )


def sum_kernel(top, side, capacity, me_ref, meta, back, out):
    (table,) = slot_tables(me_ref[0], [meta], top, side, capacity)
    held = functools.reduce(lambda p, q: p + q, table)
    for c, e in strips(out.shape[1]):
        out[:, c:e] = picked_sum(held, back, c, e).astype(BF16)


def mix(top, table, meta, block, back, out, grads, far=None, far_grads=None):
    tok = meta.shape[1]
    gates = [meta[top + k : top + k + 1, :] for k in range(top)]
    gates = [jnp.transpose(jnp.broadcast_to(g, (8, tok)))[:, :1] for g in gates]
    sums = [jnp.zeros((tok, 1), F32) for _ in range(top)]
    for c, e in strips(out.shape[1]):
        cotangent = block[:, c:e].astype(F32)
        mixed = 0.0 if far is None else far[:, c:e].astype(F32)
        for k in range(top):
            got = picked_sum(table[k], back, c, e)
            mixed += gates[k] * got
            sums[k] += jnp.sum(cotangent * got, 1, keepdims=True)
        out[:, c:e] = mixed.astype(BF16)
    lane = lax.broadcasted_iota(jnp.int32, (tok, LANES), 1)
    grad = jnp.zeros((tok, LANES), F32) if far_grads is None else far_grads[...]
    for k in range(top):
        grad += jnp.where(lane == k, sums[k], 0.0)
    grads[...] = grad


def mix_kernel(top, side, capacity, me_ref, meta, block, back, out, grads):
    (table,) = slot_tables(me_ref[0], [meta], top, side, capacity)
    mix(top, table, meta, block, back, out, grads)


def last_kernel(
    top, side, capacity, me_ref, meta, block, back, far, far_grads, far_dx, out, grads, dx
):
    tables = slot_tables(me_ref[0], [meta, meta], top, side, capacity)
    mix(top, tables[0], meta, block, back, out, grads, far, far_grads)
    held = functools.reduce(lambda p, q: p + q, tables[1])
    for c, e in strips(dx.shape[1]):
        dx[:, c:e] = (picked_sum(held, back, c, e) + far_dx[:, c:e].astype(F32)).astype(BF16)


def backward_kernel(
    dy_ref, x_ref, gate_ref, up_ref, hidden_ref, wg_ref, wu_ref, wd_ref, own_ref, far_ref, terms_ref, gg_ref, gu_ref
):
    units, feature = gate_ref.shape[1], x_ref.shape[1]
    across_last = (((1,), (1,)), ((), ()))
    for c, e in strips(units, 256):
        back = lax.dot_general(
            dy_ref[...], wd_ref[c:e, :], across_last, preferred_element_type=F32
        )
        gate = gate_ref[:, c:e]
        sig = 1.0 / (1.0 + jnp.exp(-gate))
        gg_ref[:, c:e] = (back * up_ref[:, c:e] * (sig * (1.0 + gate * (1.0 - sig)))).astype(BF16)
        gu_ref[:, c:e] = (back * (gate * sig)).astype(BF16)
    for c, e in strips(feature):
        got = jnp.dot(gg_ref[...], wg_ref[:, c:e], preferred_element_type=F32)
        got += jnp.dot(gu_ref[...], wu_ref[:, c:e], preferred_element_type=F32)
        own_ref[:, c:e] = got[: own_ref.shape[0]].astype(BF16)
        far_ref[:, c:e] = got[own_ref.shape[0] :].astype(BF16)
    pairs = ((gg_ref, x_ref), (gu_ref, x_ref), (hidden_ref, dy_ref))
    for n, (left, right) in enumerate(pairs):
        for r, t in strips(units, 256):
            for c, e in strips(feature, 1024):
                terms_ref[n * units + r : n * units + t, c:e] = lax.dot_general(
                    left[:, r:t], right[:, c:e], TRANSPOSED, preferred_element_type=F32
                ).astype(BF16)


def on_device(tokens, expert_ids, gate_prob, w_gate, w_up, w_down, d_mixed):
    tok, feature = tokens.shape
    top = expert_ids.shape[1]
    experts = lax.axis_size("expert")
    capacity = max(2, 2 * tok * top // experts)
    side = experts // 2
    half = side * capacity
    me = lax.axis_index("expert")
    me_arr = me[None]
    sets = [[h * side + p for p in range(side)] for h in range(2)]
    shape = jax.ShapeDtypeStruct

    def across(value):
        return lax.ppermute(value, "expert", [(e, (e + side) % experts) for e in range(experts)])

    def exchange(value):
        shaped = value.reshape(side, value.shape[0] // side, value.shape[1])
        got = lax.all_to_all(shaped, "expert", 0, 0, axis_index_groups=sets, tiled=True)
        return got.reshape(value.shape)

    def after(value, *earlier):
        return lax.optimization_barrier((value, *earlier))

    def call(kernel, outs, args, flops):
        return local_call(
            functools.partial(kernel, top, side, capacity),
            [shape(*out) for out in outs],
            me_arr,
            args,
            flops,
        )

    def pick(metas, blocks, scaled):
        count = len(metas)
        return local_call(
            functools.partial(pick_kernel, top, side, capacity, scaled),
            [shape((count * half, feature), BF16)],
            me_arr,
            [*metas, *blocks],
            2 * count * count * half * tok * feature,
        )[0]

    meta = jnp.concatenate([expert_ids.T.astype(F32), gate_prob.T], 0)
    own = exchange(pick([meta, meta], [tokens, d_mixed], (False, True)))
    own = own.reshape(side, 2, capacity, feature)
    x_far, meta_far = after(across(tokens), across(meta))
    d_late, x_far = after(d_mixed, x_far)
    d_far = across(d_late)
    far_rows = exchange(pick([meta_far], [x_far], (False,)))
    x_rows = jnp.concatenate([own[:, 0].reshape(half, feature), far_rows], 0)
    far_rows, d_far = after(far_rows, d_far)
    d_far_rows = exchange(pick([meta_far], [d_far], (True,)))

    gate_matrix, up_matrix, down_matrix = w_gate[0], w_up[0], w_down[0]
    hidden_units = gate_matrix.shape[1]
    gate_pre = jnp.dot(x_rows, gate_matrix, preferred_element_type=F32)
    up_pre = jnp.dot(x_rows, up_matrix, preferred_element_type=F32)
    hidden = (gate_pre * jax.nn.sigmoid(gate_pre) * up_pre).astype(BF16)
    y_far, y_own = (
        jnp.dot(part, down_matrix, preferred_element_type=F32).astype(BF16)
        for part in (hidden[half:], hidden[:half])
    )
    y_far, y_own, d_far_rows = after(y_far, y_own, d_far_rows)
    y_far_back = exchange(y_far)
    dy_rows = jnp.concatenate([own[:, 1].reshape(half, feature), d_far_rows], 0)

    dx_own, dx_far, terms = pl.pallas_call(
        backward_kernel,
        out_shape=[
            shape((half, feature), BF16),
            shape((half, feature), BF16),
            shape((3 * hidden_units, feature), BF16),
        ],
        in_specs=[VMEM] * 8,
        out_specs=[VMEM] * 3,
        scratch_shapes=[pltpu.VMEM((2 * half, hidden_units), BF16)] * 2,
        compiler_params=pltpu.CompilerParams(vmem_limit_bytes=48 * 1024 * 1024),
        cost_estimate=pl.CostEstimate(flops=1, bytes_accessed=1, transcendentals=0),
    )(dy_rows, x_rows, gate_pre, up_pre, hidden, gate_matrix.T, up_matrix.T, down_matrix)
    dx_far, dx_own, terms, y_far_back = after(dx_far, dx_own, terms, y_far_back)
    summed = lax.psum_scatter(terms, "dp", scatter_dimension=1, tiled=True)

    token_rows, grad_rows = ((tok, feature), BF16), ((tok, LANES), F32)
    work = 2 * half * tok * feature
    mixed_far, grads_far = call(
        mix_kernel, [token_rows, grad_rows], [meta_far, d_far, y_far_back], top * work
    )
    dx_far, mixed_far, grads_far = after(dx_far, mixed_far, grads_far)
    far_back = exchange(dx_far)
    both = jnp.stack([part.reshape(side, capacity, feature) for part in (y_own, dx_own)], 1)
    far_back, both = after(far_back, both)
    own_back = exchange(both.reshape(2 * half, feature))

    (tokens_far,) = call(sum_kernel, [token_rows], [meta_far, far_back], work)
    tokens_far, mixed_far, grads_far = after(tokens_far, across(mixed_far), across(grads_far))
    weight_grads = (
        summed[:hidden_units].astype(F32).T[None],
        summed[hidden_units : 2 * hidden_units].astype(F32).T[None],
        summed[2 * hidden_units :].astype(F32)[None],
    )
    own_back, *weight_grads = after(own_back, *weight_grads)
    mixed, grads, d_tokens = call(
        last_kernel,
        [token_rows, grad_rows, token_rows],
        [meta, d_mixed, own_back, mixed_far, grads_far, across(tokens_far)],
        (top + 1) * 2 * work,
    )
    return (mixed, d_tokens, grads[:, :top], *weight_grads)


def solution(mesh):
    in_specs = (
        P(("dp", "expert"), None),
        P(("dp", "expert"), None),
        P(("dp", "expert"), None),
        P("expert", None, None),
        P("expert", None, None),
        P("expert", None, None),
        P(("dp", "expert"), None),
    )
    out_specs = (
        P(("dp", "expert"), None),
        P(("dp", "expert"), None),
        P(("dp", "expert"), None),
        P("expert", "dp", None),
        P("expert", "dp", None),
        P("expert", None, "dp"),
    )
    return jax.shard_map(
        on_device, mesh=mesh, in_specs=in_specs, out_specs=out_specs, check_vma=False
    )
```

time: 232 us -> 249 us (1.073)
  waiting for transfers between devices: 97.6 us -> 125 us
  blocking collectives: 19.2 us -> 0 us
  starting transfers between devices: 37.8 us -> 44.3 us
  other arithmetic: 11 us -> 15.4 us
  local copies, waits for them, and re-layouts: 14.3 us -> 11.2 us
    all_to_all x1 -> x0, blocking collectives: 19.2 us -> none  [exchange(): lax.all_to_all(shaped, 'expert', 0, 0, axis_index_groups=sets, tiled=True)]
    ppermute x6, waiting for transfers between devices: 81.5 us -> 98 us  [across(): lax.ppermute(value, 'expert', [(e, (e + side) % experts) for e in range(e...]
    all_to_all x5 -> x6, waiting for transfers between devices: 16.1 us -> 26.9 us  [exchange(): lax.all_to_all(shaped, 'expert', 0, 0, axis_index_groups=sets, tiled=True)]
    unnamed x37 -> x41, local copies, waits for them, and re-layouts: 14.3 us -> 6.97 us
    concatenate x0 -> x2, other arithmetic: none -> 6.38 us  [the longest x1 3.2 us: on_device(): x_rows = jnp.concatenate([own[:, 0].reshape(half, feature), far_rows], 0)]
    ppermute x6, starting transfers between devices: 8.58 us -> 13.9 us  [across(): lax.ppermute(value, 'expert', [(e, (e + side) % experts) for e in range(e...]
    optimization_barrier x0 -> x1, local copies, waits for them, and re-layouts: none -> 3.14 us  [after(): return lax.optimization_barrier((value, *earlier))]
    all_to_all x5 -> x6, starting transfers between devices: 29 us -> 30.1 us  [exchange(): lax.all_to_all(shaped, 'expert', 0, 0, axis_index_groups=sets, tiled=True)]
  transfers between devices with their start and end apart: 12 -> 13, of which waited for: 7 -> 8; matrix products, arithmetic and copies ran while one was open for 5% -> 11% of each run, Pallas kernels for 12% -> 10%
where the time goes in v7:
time: 249 us; the launch traced here: 248 us
  waiting for transfers between devices  125 us (50%)
  starting transfers between devices  44.3 us (18%)
  Pallas kernels  29.8 us (12%)
  other arithmetic  15.4 us (6%)
  between operations  14.2 us (6%)
  local copies, waits for them, and re-layouts  11.2 us (4%)
  matrix products  8.75 us (4%)
    ppermute x6, waiting for transfers between devices, across(): lax.ppermute(value, 'expert', [(e, (e + side) % experts) for e in range(e...  98 us
    all_to_all x6, starting transfers between devices, exchange(): lax.all_to_all(shaped, 'expert', 0, 0, axis_index_groups=sets, tiled=True)  30.1 us
    all_to_all x6, waiting for transfers between devices, exchange(): lax.all_to_all(shaped, 'expert', 0, 0, axis_index_groups=sets, tiled=True)  26.9 us
    pallas_call x1, Pallas kernels, on_device(): pl.pallas_call(backward_kernel, out_shape=[shape((half, feature), BF16),...  19.1 us
    ppermute x6, starting transfers between devices, across(): lax.ppermute(value, 'expert', [(e, (e + side) % experts) for e in range(e...  13.9 us
    pallas_call x6, Pallas kernels, local_call(): pl.pallas_call(kernel, out_shape=outs, in_specs=[SMEM] + [VMEM] * len(arg...  10.7 us
    unnamed x41, local copies, waits for them, and re-layouts  6.97 us
    broadcast_in_dim x1, other arithmetic, on_device(): summed[2 * hidden_units:].astype(F32)[None]  6.13 us
  transfers between devices with their start and end apart: 13, of which 8 were waited for; matrix products, arithmetic and copies ran while one was open for 11% of the time, Pallas kernels for 10%

profile of v7, /device:TPU:0, one launch (start us, length us, event | category | flops | bytes accessed | tf_op | source)
XLA Modules:
  0.0 248.5 jit_solution(5022746273765828415)
XLA Ops:
  7.2 4.1 %collective-permute-start = (bf16[128,2048]{1,0:T(8,128)(2,1)}, bf16[128,2048]{1,0:T(8,128)(2,1)S(1)}, u32[]{:S(2)}, u32[]{:S(2)}) collective-permute-start(bf16[128,2048]{1,0:T(8,128)(2,1)} %refs_2_.1), channel_id=1, source_target_pairs={{0,8},{1,9},{2,10},{3,11},{4,12},{5,13},{6,14},{7,15},{8,0},{9,1},... | collective-permute-start | bytes 1572872 | tf_op jit(solution)/shard_map/ppermute | solution.py:166
  12.7 22.0 %collective-permute-done.1.refs_0_.meta = f32[4,128]{1,0:T(4,128)S(1)} collective-permute-done((f32[4,128]{1,0:T(4,128)S(1)}, f32[4,128]{1,0:T(4,128)S(1)}, u32[]{:S(2)}, u32[]{:S(2)}) %collective-permute-start.1) | collective-permute-done | bytes 2080 | tf_op jit(solution)/shard_map/ppermute | solution.py:166
  36.3 4.0 %all-to-all-start.1 = ((bf16[8,32,2048]{2,1,0:T(8,128)(2,1)}), bf16[8,32,2048]{2,1,0:T(8,128)(2,1)S(1)}, u32[]{:S(2)}, u32[]{:S(2)}) async-start(bf16[8,32,2048]{2,1,0:T(8,128)(2,1)} %bitcast.7), calls=%async_computation.1 | async-start | bytes 2097152 | tf_op jit(solution)/shard_map/all_to_all | solution.py:170
  40.2 2.2 shard_map.118
  42.4 12.6 %all-to-all-done.1 = bf16[8,32,2048]{2,1,0:T(8,128)(2,1)S(1)} async-done(((bf16[8,32,2048]{2,1,0:T(8,128)(2,1)}), bf16[8,32,2048]{2,1,0:T(8,128)(2,1)S(1)}, u32[]{:S(2)}, u32[]{:S(2)}) %all-to-all-start.1) | async-done | bytes 1048608 | tf_op jit(solution)/shard_map/all_to_all | solution.py:170
  56.0 3.6 %all-to-all-start = ((bf16[8,64,2048]{2,1,0:T(8,128)(2,1)}), bf16[8,64,2048]{2,1,0:T(8,128)(2,1)S(1)}, u32[]{:S(2)}, u32[]{:S(2)}) async-start(bf16[8,64,2048]{2,1,0:T(8,128)(2,1)} %bitcast.3), calls=%async_computation | async-start | bytes 4194304 | tf_op jit(solution)/shard_map/all_to_all | solution.py:170
  59.6 3.4 %collective-permute-start.2 = (bf16[128,2048]{1,0:T(8,128)(2,1)S(1)}, bf16[128,2048]{1,0:T(8,128)(2,1)S(1)}, u32[]{:S(2)}, u32[]{:S(2)}) collective-permute-start(bf16[128,2048]{1,0:T(8,128)(2,1)S(1)} %copy-done), channel_id=1, source_target_pairs={{0,8},{1,9},{2,10},{3,11},{4,12},{5,13},{6,14},{7,15},{8,0},{9,1},... | collective-permute-start | bytes 1572872 | tf_op jit(solution)/shard_map/ppermute | solution.py:166
  63.0 30.5 %collective-permute-done.2.refs_1_.block = bf16[128,2048]{1,0:T(8,128)(2,1)S(1)} collective-permute-done((bf16[128,2048]{1,0:T(8,128)(2,1)S(1)}, bf16[128,2048]{1,0:T(8,128)(2,1)S(1)}, u32[]{:S(2)}, u32[]{:S(2)}) %collective-permute-start.2) | collective-permute-done | bytes 524320 | tf_op jit(solution)/shard_map/ppermute | solution.py:166
  95.7 10.2 %all-to-all-start.2 = ((bf16[8,32,2048]{2,1,0:T(8,128)(2,1)}), bf16[8,32,2048]{2,1,0:T(8,128)(2,1)}, u32[]{:S(2)}, u32[]{:S(2)}) async-start(bf16[8,32,2048]{2,1,0:T(8,128)(2,1)} %bitcast.12), calls=%async_computation.2 | async-start | bytes 2097152 | tf_op jit(solution)/shard_map/all_to_all | solution.py:170
  110.7 3.0 %multiply_convert_fusion = (bf16[512,704]{1,0:T(8,128)(2,1)S(1)}, f32[512,704]{1,0:T(8,128)}) fusion(f32[512,704]{1,0:T(8,128)S(1)} %fusion.2.gate_ref, bf16[1,2048,704]{1,2,0:T(8,128)(2,1)S(1)} %copy-done.17, bf16[256,2048]{1,0:T(8,128)(2,1)S(1)} %bitcast.61, bf16[256,2048]{1,0:T(8,128)(2,1)S(1)} %bitcast.64), kind=kOutput, calls=%fused_computation.11 | convolution fusion | flops 1482752000 | bytes 8585216 | tf_op jit(solution)/shard_map/dot_general | solution.py:209
  119.4 3.6 %all-to-all-start.3 = ((bf16[8,32,2048]{2,1,0:T(8,128)(2,1)}), bf16[8,32,2048]{2,1,0:T(8,128)(2,1)S(1)}, u32[]{:S(2)}, u32[]{:S(2)}) async-start(bf16[8,32,2048]{2,1,0:T(8,128)(2,1)} %bitcast.69), calls=%async_computation.3 | async-start | bytes 2097152 | tf_op jit(solution)/shard_map/all_to_all | solution.py:170
  123.2 3.2 %pad_maximum_fusion.x_ref = bf16[512,2048]{1,0:T(8,128)(2,1)} fusion(bf16[256,2048]{1,0:T(8,128)(2,1)} %bitcast.59, bf16[256,2048]{1,0:T(8,128)(2,1)} %bitcast.65), kind=kLoop, calls=%fused_computation.8 | loop fusion | flops 4194304 | bytes 4194304 | tf_op jit(solution)/shard_map/concatenate | solution.py:202
  126.4 3.2 %pad_maximum_fusion.1.dy_ref = bf16[512,2048]{1,0:T(8,128)(2,1)} fusion(bf16[256,2048]{1,0:T(8,128)(2,1)} %bitcast.13, bf16[256,2048]{1,0:T(8,128)(2,1)S(1)} %bitcast.62), kind=kLoop, calls=%fused_computation.9 | loop fusion | flops 4194304 | bytes 4194304 | tf_op jit(solution)/shard_map/concatenate | solution.py:217
  129.6 19.1 %shard_map.121 = (bf16[256,2048]{1,0:T(8,128)(2,1)S(1)}, bf16[256,2048]{1,0:T(8,128)(2,1)S(1)}, bf16[2112,2048]{1,0:T(8,128)(2,1)}) custom-call(bf16[512,2048]{1,0:T(8,128)(2,1)} %pad_maximum_fusion.1.dy_ref, bf16[512,2048]{1,0:T(8,128)(2,1)} %pad_maximum_fusion.x_ref, f32[512,704]{1,0:T(8,128)S(1)} %fusion.2.gate_ref, f32[512,704]{1,0:T(8,128)S(1)} %copy-done.2, ...), custom_call_target="tpu_custom_call" | custom-call | flops 1 | bytes 1 | tf_op jit(solution)/shard_map/pallas_call | solution.py:219
  152.3 4.9 %all-to-all-start.4 = ((bf16[8,32,2048]{2,1,0:T(8,128)(2,1)}), bf16[8,32,2048]{2,1,0:T(8,128)(2,1)S(1)}, u32[]{:S(2)}, u32[]{:S(2)}) async-start(bf16[8,32,2048]{2,1,0:T(8,128)(2,1)} %bitcast.54), calls=%async_computation.4 | async-start | bytes 2097152 | tf_op jit(solution)/shard_map/all_to_all | solution.py:170
  158.8 11.8 %all-to-all-done.4 = bf16[8,32,2048]{2,1,0:T(8,128)(2,1)S(1)} async-done(((bf16[8,32,2048]{2,1,0:T(8,128)(2,1)}), bf16[8,32,2048]{2,1,0:T(8,128)(2,1)S(1)}, u32[]{:S(2)}, u32[]{:S(2)}) %all-to-all-start.4) | async-done | bytes 1048608 | tf_op jit(solution)/shard_map/all_to_all | solution.py:170
  170.6 3.1 %copy.34 = bf16[8,2,32,2048]{3,2,1,0:T(8,128)(2,1)} copy(bf16[8,2,32,2048]{3,2,0,1:T(8,128)(2,1)} %pad_maximum_fusion.2) | data formatting | bytes 4194304 | tf_op jit(solution)/shard_map/optimization_barrier | solution.py:174
  173.7 3.8 %all-to-all-start.5 = ((bf16[8,64,2048]{2,1,0:T(8,128)(2,1)}), bf16[8,64,2048]{2,1,0:T(8,128)(2,1)S(1)}, u32[]{:S(2)}, u32[]{:S(2)}) async-start(bf16[8,64,2048]{2,1,0:T(8,128)(2,1)} %bitcast.57), calls=%async_computation.5 | async-start | bytes 4194304 | tf_op jit(solution)/shard_map/all_to_all | solution.py:170
  177.6 2.9 %collective-permute-start.4 = (f32[128,128]{1,0:T(8,128)S(1)}, f32[128,128]{1,0:T(8,128)S(1)}, u32[]{:S(2)}, u32[]{:S(2)}) collective-permute-start(f32[128,128]{1,0:T(8,128)S(1)} %get-tuple-element.60), channel_id=1, source_target_pairs={{0,8},{1,9},{2,10},{3,11},{4,12},{5,13},{6,14},{7,15},{8,0},{9,1},... | collective-permute-start | bytes 196616 | tf_op jit(solution)/shard_map/ppermute | solution.py:166
  181.8 30.1 %collective-permute-done.4.far_grads = f32[128,128]{1,0:T(8,128)S(1)} collective-permute-done((f32[128,128]{1,0:T(8,128)S(1)}, f32[128,128]{1,0:T(8,128)S(1)}, u32[]{:S(2)}, u32[]{:S(2)}) %collective-permute-start.4) | collective-permute-done | bytes 65568 | tf_op jit(solution)/shard_map/ppermute | solution.py:166
  212.7 3.4 %collective-permute-start.5 = (bf16[128,2048]{1,0:T(8,128)(2,1)}, bf16[128,2048]{1,0:T(8,128)(2,1)}, u32[]{:S(2)}, u32[]{:S(2)}) collective-permute-start(bf16[128,2048]{1,0:T(8,128)(2,1)} %shard_map.123), channel_id=1, source_target_pairs={{0,8},{1,9},{2,10},{3,11},{4,12},{5,13},{6,14},{7,15},{8,0},{9,1},... | collective-permute-start | bytes 1572872 | tf_op jit(solution)/shard_map/ppermute | solution.py:166
  216.1 6.1 %fusion.4 = (f32[1,704,1024]{2,1,0:T(8,128)}, f32[1,1024,704]{1,2,0:T(8,128)}, f32[1,1024,704]{1,2,0:T(8,128)}) fusion(bf16[2112,1024]{1,0:T(8,128)(2,1)} %reduce-scatter.2.cloned.1.call-done), kind=kLoop, calls=%fused_computation.13 | loop fusion | flops 2162688 | bytes 12976128 | tf_op jit(solution)/shard_map/broadcast_in_dim | solution.py:251
  222.2 15.4 %collective-permute-done.5.far_dx = bf16[128,2048]{1,0:T(8,128)(2,1)} collective-permute-done((bf16[128,2048]{1,0:T(8,128)(2,1)}, bf16[128,2048]{1,0:T(8,128)(2,1)}, u32[]{:S(2)}, u32[]{:S(2)}) %collective-permute-start.5) | collective-permute-done | bytes 524320 | tf_op jit(solution)/shard_map/ppermute | solution.py:166
  237.7 3.3 %shard_map.124 = (bf16[128,2048]{1,0:T(8,128)(2,1)}, f32[128,128]{1,0:T(8,128)S(1)}, bf16[128,2048]{1,0:T(8,128)(2,1)}) custom-call(s32[1]{0:T(128)} %bitcast.me_ref, f32[4,128]{1,0:T(4,128)S(1)} %pad_maximum_fusion.3.refs_0_.refs_1_.meta, bf16[128,2048]{1,0:T(8,128)(2,1)S(1)} %copy-done.1, bf16[512,2048]{1,0:T(8,128)(2,1)S(1)} %bitcast.51, ...), custom_call_target="tpu_custom_call" | custom-call | flops 805306368 | bytes 4851712 | tf_op jit(solution)/shard_map/pallas_call | solution.py:20
  (63 shorter events, 24.7 us)
Async XLA Ops:
  7.2 33.1 %copy-start.10 = (bf16[128,2048]{1,0:T(8,128)(2,1)S(1)}, bf16[128,2048]{1,0:T(8,128)(2,1)}, u32[]{:S(2)}) copy-start(bf16[128,2048]{1,0:T(8,128)(2,1)} %refs_2_.1) | copy-start | bytes 1572868
  7.2 33.1 %copy-start = (bf16[128,2048]{1,0:T(8,128)(2,1)S(1)}, bf16[128,2048]{1,0:T(8,128)(2,1)}, u32[]{:S(2)}) copy-start(bf16[128,2048]{1,0:T(8,128)(2,1)} %block.1) | copy-start | bytes 1572868
  7.2 27.6 %collective-permute-start = (bf16[128,2048]{1,0:T(8,128)(2,1)}, bf16[128,2048]{1,0:T(8,128)(2,1)S(1)}, u32[]{:S(2)}, u32[]{:S(2)}) collective-permute-start(bf16[128,2048]{1,0:T(8,128)(2,1)} %refs_2_.1), channel_id=1, source_target_pairs={{0,8},{1,9},{2,10},{3,11},{4,12},{5,13},{6,14},{7,15},{8,0},{9,1},... | collective-permute-start | bytes 1572872 | tf_op jit(solution)/shard_map/ppermute | solution.py:166
  12.7 22.1 %collective-permute-start.1 = (f32[4,128]{1,0:T(4,128)S(1)}, f32[4,128]{1,0:T(4,128)S(1)}, u32[]{:S(2)}, u32[]{:S(2)}) collective-permute-start(f32[4,128]{1,0:T(4,128)S(1)} %pad_maximum_fusion.3.refs_0_.refs_1_.meta), channel_id=1, source_target_pairs={{0,8},{1,9},{2,10},{3,11},{4,12},{5,13},{6,14},{7,15},{8,0},{9,1},... | collective-permute-start | bytes 6152 | tf_op jit(solution)/shard_map/ppermute | solution.py:166
  36.3 18.8 %all-to-all-start.1 = ((bf16[8,32,2048]{2,1,0:T(8,128)(2,1)}), bf16[8,32,2048]{2,1,0:T(8,128)(2,1)S(1)}, u32[]{:S(2)}, u32[]{:S(2)}) async-start(bf16[8,32,2048]{2,1,0:T(8,128)(2,1)} %bitcast.7), calls=%async_computation.1 | async-start | bytes 2097152 | tf_op jit(solution)/shard_map/all_to_all | solution.py:170
  56.0 39.7 %all-to-all-start = ((bf16[8,64,2048]{2,1,0:T(8,128)(2,1)}), bf16[8,64,2048]{2,1,0:T(8,128)(2,1)S(1)}, u32[]{:S(2)}, u32[]{:S(2)}) async-start(bf16[8,64,2048]{2,1,0:T(8,128)(2,1)} %bitcast.3), calls=%async_computation | async-start | bytes 4194304 | tf_op jit(solution)/shard_map/all_to_all | solution.py:170
  59.6 33.9 %collective-permute-start.2 = (bf16[128,2048]{1,0:T(8,128)(2,1)S(1)}, bf16[128,2048]{1,0:T(8,128)(2,1)S(1)}, u32[]{:S(2)}, u32[]{:S(2)}) collective-permute-start(bf16[128,2048]{1,0:T(8,128)(2,1)S(1)} %copy-done), channel_id=1, source_target_pairs={{0,8},{1,9},{2,10},{3,11},{4,12},{5,13},{6,14},{7,15},{8,0},{9,1},... | collective-permute-start | bytes 1572872 | tf_op jit(solution)/shard_map/ppermute | solution.py:166
  95.7 23.8 %all-to-all-start.2 = ((bf16[8,32,2048]{2,1,0:T(8,128)(2,1)}), bf16[8,32,2048]{2,1,0:T(8,128)(2,1)}, u32[]{:S(2)}, u32[]{:S(2)}) async-start(bf16[8,32,2048]{2,1,0:T(8,128)(2,1)} %bitcast.12), calls=%async_computation.2 | async-start | bytes 2097152 | tf_op jit(solution)/shard_map/all_to_all | solution.py:170
  107.0 3.6 %copy-start.15 = (bf16[8,1,32,2048]{3,2,1,0:T(8,128)(2,1)}, bf16[8,1,32,2048]{3,2,1,0:T(8,128)(2,1)S(1)}, u32[]{:S(2)}) copy-start(bf16[8,1,32,2048]{3,2,1,0:T(8,128)(2,1)S(1)} %get-tuple-element.92) | copy-start | bytes 3145732
  110.7 3.0 %copy-start.18 = (bf16[1,704,2048]{2,1,0:T(8,128)(2,1)S(1)}, bf16[1,704,2048]{2,1,0:T(8,128)(2,1)}, u32[]{:S(2)}) copy-start(bf16[1,704,2048]{2,1,0:T(8,128)(2,1)} %param.12) | copy-start | bytes 8650756
  119.4 31.2 %all-to-all-start.3 = ((bf16[8,32,2048]{2,1,0:T(8,128)(2,1)}), bf16[8,32,2048]{2,1,0:T(8,128)(2,1)S(1)}, u32[]{:S(2)}, u32[]{:S(2)}) async-start(bf16[8,32,2048]{2,1,0:T(8,128)(2,1)} %bitcast.69), calls=%async_computation.3 | async-start | bytes 2097152 | tf_op jit(solution)/shard_map/all_to_all | solution.py:170
  123.0 93.1 %reduce-scatter.2.cloned.1.call-start = ((), (), s32[]{:S(2)}) async-start(), calls=%async_computation.7 | async-start | bytes 12976128 | tf_op jit(solution)/shard_map/reduce_scatter | solution.py:233
  123.2 3.2 %copy-start.14 = (bf16[8,1,32,2048]{3,2,1,0:T(8,128)(2,1)S(1)}, bf16[8,1,32,2048]{3,2,1,0:T(8,128)(2,1)}, u32[]{:S(2)}) copy-start(bf16[8,1,32,2048]{3,2,1,0:T(8,128)(2,1)} %get-tuple-element.91) | copy-start | bytes 3145732
  126.4 3.2 %copy-start.2 = (f32[512,704]{1,0:T(8,128)S(1)}, f32[512,704]{1,0:T(8,128)}, u32[]{:S(2)}) copy-start(f32[512,704]{1,0:T(8,128)} %get-tuple-element.94.up_ref) | copy-start | bytes 4325380
  126.4 3.2 %copy-start.7 = (bf16[512,704]{1,0:T(8,128)(2,1)S(1)}, bf16[512,704]{1,0:T(8,128)(2,1)}, u32[]{:S(2)}) copy-start(bf16[512,704]{1,0:T(8,128)(2,1)} %copy-done.6) | copy-start | bytes 2162692
  152.3 4.9 %copy-start.5 = (bf16[256,2048]{1,0:T(8,128)(2,1)S(1)}, bf16[256,2048]{1,0:T(8,128)(2,1)}, u32[]{:S(2)}) copy-start(bf16[256,2048]{1,0:T(8,128)(2,1)} %copy-done.4) | copy-start | bytes 3145732
  152.3 4.9 %copy-start.19 = (bf16[256,2048]{1,0:T(8,128)(2,1)S(1)}, bf16[256,2048]{1,0:T(8,128)(2,1)}, u32[]{:S(2)}) copy-start(bf16[256,2048]{1,0:T(8,128)(2,1)} %convolution_convert_fusion) | copy-start | bytes 3145732
  152.3 18.3 %all-to-all-start.4 = ((bf16[8,32,2048]{2,1,0:T(8,128)(2,1)}), bf16[8,32,2048]{2,1,0:T(8,128)(2,1)S(1)}, u32[]{:S(2)}, u32[]{:S(2)}) async-start(bf16[8,32,2048]{2,1,0:T(8,128)(2,1)} %bitcast.54), calls=%async_computation.4 | async-start | bytes 2097152 | tf_op jit(solution)/shard_map/all_to_all | solution.py:170
  173.7 48.5 %all-to-all-start.5 = ((bf16[8,64,2048]{2,1,0:T(8,128)(2,1)}), bf16[8,64,2048]{2,1,0:T(8,128)(2,1)S(1)}, u32[]{:S(2)}, u32[]{:S(2)}) async-start(bf16[8,64,2048]{2,1,0:T(8,128)(2,1)} %bitcast.57), calls=%async_computation.5 | async-start | bytes 4194304 | tf_op jit(solution)/shard_map/all_to_all | solution.py:170
  177.5 34.4 %collective-permute-start.3 = (bf16[128,2048]{1,0:T(8,128)(2,1)}, bf16[128,2048]{1,0:T(8,128)(2,1)S(1)}, u32[]{:S(2)}, u32[]{:S(2)}) collective-permute-start(bf16[128,2048]{1,0:T(8,128)(2,1)} %copy-done.11), channel_id=1, source_target_pairs={{0,8},{1,9},{2,10},{3,11},{4,12},{5,13},{6,14},{7,15},{8,0},{9,1},... | collective-permute-start | bytes 1572872 | tf_op jit(solution)/shard_map/ppermute | solution.py:166
  177.6 34.3 %collective-permute-start.4 = (f32[128,128]{1,0:T(8,128)S(1)}, f32[128,128]{1,0:T(8,128)S(1)}, u32[]{:S(2)}, u32[]{:S(2)}) collective-permute-start(f32[128,128]{1,0:T(8,128)S(1)} %get-tuple-element.60), channel_id=1, source_target_pairs={{0,8},{1,9},{2,10},{3,11},{4,12},{5,13},{6,14},{7,15},{8,0},{9,1},... | collective-permute-start | bytes 196616 | tf_op jit(solution)/shard_map/ppermute | solution.py:166
  181.8 55.8 %copy-start.1 = (bf16[128,2048]{1,0:T(8,128)(2,1)S(1)}, bf16[128,2048]{1,0:T(8,128)(2,1)}, u32[]{:S(2)}) copy-start(bf16[128,2048]{1,0:T(8,128)(2,1)} %block.1) | copy-start | bytes 1572868
  212.7 25.0 %collective-permute-start.5 = (bf16[128,2048]{1,0:T(8,128)(2,1)}, bf16[128,2048]{1,0:T(8,128)(2,1)}, u32[]{:S(2)}, u32[]{:S(2)}) collective-permute-start(bf16[128,2048]{1,0:T(8,128)(2,1)} %shard_map.123), channel_id=1, source_target_pairs={{0,8},{1,9},{2,10},{3,11},{4,12},{5,13},{6,14},{7,15},{8,0},{9,1},... | collective-permute-start | bytes 1572872 | tf_op jit(solution)/shard_map/ppermute | solution.py:166
  216.1 21.6 %copy-start.9 = (bf16[128,2048]{1,0:T(8,128)(2,1)S(1)}, bf16[128,2048]{1,0:T(8,128)(2,1)}, u32[]{:S(2)}) copy-start(bf16[128,2048]{1,0:T(8,128)(2,1)} %copy-done.8) | copy-start | bytes 1572868
  (9 other events, 12.8 us)
Sparse Core Ops, SparseCore 0:
  150.8 16.3 reduce-scatter.1

commit v8 on v7

--- a/solution.py
+++ b/solution.py
@@ -123,31 +123,49 @@
         dx[:, c:e] = (picked_sum(held, back, c, e) + far_dx[:, c:e].astype(F32)).astype(BF16)
 
 
-def backward_kernel(
-    dy_ref, x_ref, gate_ref, up_ref, hidden_ref, wg_ref, wu_ref, wd_ref, own_ref, far_ref, terms_ref, gg_ref, gu_ref
+def dx_kernel(
+    side, d_own, d_far, gate_ref, up_ref, y_own, wg_ref, wu_ref, wd_ref, both, far, gg_ref, gu_ref
 ):
-    units, feature = gate_ref.shape[1], x_ref.shape[1]
+    half, feature = far.shape
+    units = gate_ref.shape[1]
     across_last = (((1,), (1,)), ((), ()))
-    for c, e in strips(units, 256):
-        back = lax.dot_general(
-            dy_ref[...], wd_ref[c:e, :], across_last, preferred_element_type=F32
-        )
-        gate = gate_ref[:, c:e]
-        sig = 1.0 / (1.0 + jnp.exp(-gate))
-        gg_ref[:, c:e] = (back * up_ref[:, c:e] * (sig * (1.0 + gate * (1.0 - sig)))).astype(BF16)
-        gu_ref[:, c:e] = (back * (gate * sig)).astype(BF16)
+    for r, d_rows in ((0, d_own), (half, d_far)):
+        at = slice(r, r + half)
+        for c, e in strips(units, 256):
+            back = lax.dot_general(
+                d_rows[...], wd_ref[c:e, :], across_last, preferred_element_type=F32
+            )
+            gate = gate_ref[at, c:e]
+            sig = 1.0 / (1.0 + jnp.exp(-gate))
+            gg_ref[at, c:e] = (
+                back * up_ref[at, c:e] * (sig * (1.0 + gate * (1.0 - sig)))
+            ).astype(BF16)
+            gu_ref[at, c:e] = (back * (gate * sig)).astype(BF16)
     for c, e in strips(feature):
         got = jnp.dot(gg_ref[...], wg_ref[:, c:e], preferred_element_type=F32)
         got += jnp.dot(gu_ref[...], wu_ref[:, c:e], preferred_element_type=F32)
-        own_ref[:, c:e] = got[: own_ref.shape[0]].astype(BF16)
-        far_ref[:, c:e] = got[own_ref.shape[0] :].astype(BF16)
-    pairs = ((gg_ref, x_ref), (gu_ref, x_ref), (hidden_ref, dy_ref))
-    for n, (left, right) in enumerate(pairs):
+        far[:, c:e] = got[half:].astype(BF16)
+        pair = [
+            part.reshape(side, 1, half // side, e - c)
+            for part in (y_own[:, c:e].astype(F32), got[:half])
+        ]
+        both[:, c:e] = jnp.concatenate(pair, 1).reshape(2 * half, e - c).astype(BF16)
+
+
+def terms_kernel(gg, gu, hidden, x_own, x_far, d_own, d_far, out):
+    half, feature = x_own.shape
+    units = gg.shape[1]
+    pairs = ((gg, x_own, x_far), (gu, x_own, x_far), (hidden, d_own, d_far))
+    for n, (left, own, far) in enumerate(pairs):
         for r, t in strips(units, 256):
             for c, e in strips(feature, 1024):
-                terms_ref[n * units + r : n * units + t, c:e] = lax.dot_general(
-                    left[:, r:t], right[:, c:e], TRANSPOSED, preferred_element_type=F32
-                ).astype(BF16)
+                got = lax.dot_general(
+                    left[:half, r:t], own[:, c:e], TRANSPOSED, preferred_element_type=F32
+                )
+                got += lax.dot_general(
+                    left[half:, r:t], far[:, c:e], TRANSPOSED, preferred_element_type=F32
+                )
+                out[n * units + r : n * units + t, c:e] = got.astype(BF16)
 
 
 def on_device(tokens, expert_ids, gate_prob, w_gate, w_up, w_down, d_mixed):
@@ -198,9 +216,11 @@
     x_far, meta_far = after(across(tokens), across(meta))
     d_late, x_far = after(d_mixed, x_far)
     d_far = across(d_late)
-    far_rows = exchange(pick([meta_far], [x_far], (False,)))
-    x_rows = jnp.concatenate([own[:, 0].reshape(half, feature), far_rows], 0)
-    far_rows, d_far = after(far_rows, d_far)
+    x_far, own = after(x_far, own)
+    x_own, d_own = (own[:, n].reshape(half, feature) for n in range(2))
+    x_far_rows = exchange(pick([meta_far], [x_far], (False,)))
+    x_rows = jnp.concatenate([x_own, x_far_rows], 0)
+    x_far_rows, d_far = after(x_far_rows, d_far)
     d_far_rows = exchange(pick([meta_far], [d_far], (True,)))
 
     gate_matrix, up_matrix, down_matrix = w_gate[0], w_up[0], w_down[0]
@@ -214,23 +234,26 @@
     )
     y_far, y_own, d_far_rows = after(y_far, y_own, d_far_rows)
     y_far_back = exchange(y_far)
-    dy_rows = jnp.concatenate([own[:, 1].reshape(half, feature), d_far_rows], 0)
-
-    dx_own, dx_far, terms = pl.pallas_call(
-        backward_kernel,
-        out_shape=[
-            shape((half, feature), BF16),
-            shape((half, feature), BF16),
-            shape((3 * hidden_units, feature), BF16),
-        ],
+
+    n_rows = 2 * half
+    rows, units = shape((half, feature), BF16), shape((n_rows, hidden_units), BF16)
+    both, dx_far, gg, gu = pl.pallas_call(
+        functools.partial(dx_kernel, side),
+        out_shape=[shape((n_rows, feature), BF16), rows, units, units],
         in_specs=[VMEM] * 8,
-        out_specs=[VMEM] * 3,
-        scratch_shapes=[pltpu.VMEM((2 * half, hidden_units), BF16)] * 2,
-        compiler_params=pltpu.CompilerParams(vmem_limit_bytes=48 * 1024 * 1024),
+        out_specs=[VMEM] * 4,
+        compiler_params=pltpu.CompilerParams(vmem_limit_bytes=32 * 1024 * 1024),
         cost_estimate=pl.CostEstimate(flops=1, bytes_accessed=1, transcendentals=0),
-    )(dy_rows, x_rows, gate_pre, up_pre, hidden, gate_matrix.T, up_matrix.T, down_matrix)
-    dx_far, dx_own, terms, y_far_back = after(dx_far, dx_own, terms, y_far_back)
-    summed = lax.psum_scatter(terms, "dp", scatter_dimension=1, tiled=True)
+    )(d_own, d_far_rows, gate_pre, up_pre, y_own, gate_matrix.T, up_matrix.T, down_matrix)
+    (terms,) = pl.pallas_call(
+        terms_kernel,
+        out_shape=[shape((3 * hidden_units, feature), BF16)],
+        in_specs=[VMEM] * 7,
+        out_specs=[VMEM],
+        compiler_params=pltpu.CompilerParams(vmem_limit_bytes=32 * 1024 * 1024),
+        cost_estimate=pl.CostEstimate(flops=1, bytes_accessed=1, transcendentals=0),
+    )(gg, gu, hidden, x_own, x_far_rows, d_own, d_far_rows)
+    dx_far, both, terms, y_far_back = after(dx_far, both, terms, y_far_back)
 
     token_rows, grad_rows = ((tok, feature), BF16), ((tok, LANES), F32)
     work = 2 * half * tok * feature
@@ -239,12 +262,12 @@
     )
     dx_far, mixed_far, grads_far = after(dx_far, mixed_far, grads_far)
     far_back = exchange(dx_far)
-    both = jnp.stack([part.reshape(side, capacity, feature) for part in (y_own, dx_own)], 1)
-    far_back, both = after(far_back, both)
-    own_back = exchange(both.reshape(2 * half, feature))
-
     (tokens_far,) = call(sum_kernel, [token_rows], [meta_far, far_back], work)
-    tokens_far, mixed_far, grads_far = after(tokens_far, across(mixed_far), across(grads_far))
+    summed = lax.psum_scatter(terms, "dp", scatter_dimension=1, tiled=True)
+    tokens_far, both, mixed_far, grads_far = after(
+        tokens_far, both, across(mixed_far), across(grads_far)
+    )
+    own_back = exchange(both)
     weight_grads = (
         summed[:hidden_units].astype(F32).T[None],
         summed[hidden_units : 2 * hidden_units].astype(F32).T[None],

time: 249 us -> 219 us (0.88)
  waiting for transfers between devices: 125 us -> 104 us
  local copies, waits for them, and re-layouts: 11.2 us -> 21.2 us
  Pallas kernels: 29.8 us -> 21.2 us
  other arithmetic: 15.4 us -> 7.44 us
  starting transfers between devices: 44.3 us -> 41.2 us
    ppermute x6, waiting for transfers between devices: 98 us -> 56.6 us  [across(): lax.ppermute(value, 'expert', [(e, (e + side) % experts) for e in range(e...]
    all_to_all x6, waiting for transfers between devices: 26.9 us -> 47.3 us  [exchange(): lax.all_to_all(shaped, 'expert', 0, 0, axis_index_groups=sets, tiled=True)]
    unnamed x41 -> x53, local copies, waits for them, and re-layouts: 6.97 us -> 19.3 us
    pallas_call x1 -> x2, Pallas kernels: 19.1 us -> 11.3 us  [the longest x1 6.66 us: on_device(): pl.pallas_call(functools.partial(dx_kernel, side), out_shape=[shape((n_ro...]
    concatenate x2 -> x0, other arithmetic: 6.38 us -> none  [the longest x1 3.2 us: on_device(): x_rows = jnp.concatenate([own[:, 0].reshape(half, feature), far_rows], 0)]
    ppermute x6, starting transfers between devices: 13.9 us -> 8.89 us  [across(): lax.ppermute(value, 'expert', [(e, (e + side) % experts) for e in range(e...]
    optimization_barrier x1 -> x0, local copies, waits for them, and re-layouts: 3.14 us -> none  [after(): return lax.optimization_barrier((value, *earlier))]
  transfers between devices with their start and end apart: 13 -> 13, of which waited for: 8 -> 7; matrix products, arithmetic and copies ran while one was open for 11% -> 8% of each run, Pallas kernels for 10% -> 6%
where the time goes in v8:
time: 219 us; the launch traced here: 218 us
  waiting for transfers between devices  104 us (47%)
  starting transfers between devices  41.2 us (19%)
  local copies, waits for them, and re-layouts  21.2 us (10%)
  Pallas kernels  21.2 us (10%)
  between operations  14.2 us (6%)
  matrix products  8.77 us (4%)
  other arithmetic  7.44 us (3%)
    ppermute x6, waiting for transfers between devices, across(): lax.ppermute(value, 'expert', [(e, (e + side) % experts) for e in range(e...  56.6 us
    all_to_all x6, waiting for transfers between devices, exchange(): lax.all_to_all(shaped, 'expert', 0, 0, axis_index_groups=sets, tiled=True)  47.3 us
    all_to_all x6, starting transfers between devices, exchange(): lax.all_to_all(shaped, 'expert', 0, 0, axis_index_groups=sets, tiled=True)  32 us
    unnamed x53, local copies, waits for them, and re-layouts  19.3 us
    pallas_call x6, Pallas kernels, local_call(): pl.pallas_call(kernel, out_shape=outs, in_specs=[SMEM] + [VMEM] * len(arg...  9.89 us
    ppermute x6, starting transfers between devices, across(): lax.ppermute(value, 'expert', [(e, (e + side) % experts) for e in range(e...  8.89 us
    pallas_call x1, Pallas kernels, on_device(): pl.pallas_call(functools.partial(dx_kernel, side), out_shape=[shape((n_ro...  6.66 us
    broadcast_in_dim x1, other arithmetic, on_device(): summed[2 * hidden_units:].astype(F32)[None]  6.07 us
  transfers between devices with their start and end apart: 13, of which 7 were waited for; matrix products, arithmetic and copies ran while one was open for 8% of the time, Pallas kernels for 6%

profile of v8, /device:TPU:0, one launch (start us, length us, event | category | flops | bytes accessed | tf_op | source)
XLA Modules:
  0.0 217.8 jit_solution(6435915177773456173)
XLA Ops:
  10.6 2.2 %shard_map.118 = bf16[512,2048]{1,0:T(8,128)(2,1)} custom-call(s32[1]{0:T(128)} %bitcast.me_ref, f32[4,128]{1,0:T(4,128)S(1)} %pad_maximum_fusion.3.refs_0_.refs_1_.meta, f32[4,128]{1,0:T(4,128)S(1)} %pad_maximum_fusion.3.refs_0_.refs_1_.meta, bf16[128,2048]{1,0:T(8,128)(2,1)S(1)} %copy-done.24, bf16[128,2048]{1,0:T(8,128)(2,1)S(1)} %copy-done.14), custom_call_target="tpu_custom_call" | custom-call | flops 536870912 | bytes 3149824 | tf_op jit(solution)/shard_map/pallas_call | solution.py:20
  12.8 6.3 %all-to-all-start = ((bf16[8,64,2048]{2,1,0:T(8,128)(2,1)}), bf16[8,64,2048]{2,1,0:T(8,128)(2,1)}, u32[]{:S(2)}, u32[]{:S(2)}) async-start(bf16[8,64,2048]{2,1,0:T(8,128)(2,1)} %bitcast.3), calls=%async_computation | async-start | bytes 4194304 | tf_op jit(solution)/shard_map/all_to_all | solution.py:188
  19.2 2.7 %collective-permute-start = (bf16[128,2048]{1,0:T(8,128)(2,1)S(1)}, bf16[128,2048]{1,0:T(8,128)(2,1)S(1)}, u32[]{:S(2)}, u32[]{:S(2)}) collective-permute-start(bf16[128,2048]{1,0:T(8,128)(2,1)S(1)} %copy-done.25), channel_id=1, source_target_pairs={{0,8},{1,9},{2,10},{3,11},{4,12},{5,13},{6,14},{7,15},{8,0},{9,1},... | collective-permute-start | bytes 1572872 | tf_op jit(solution)/shard_map/ppermute | solution.py:184
  22.1 31.0 %collective-permute-done.1.refs_0_.meta = f32[4,128]{1,0:T(4,128)S(1)} collective-permute-done((f32[4,128]{1,0:T(4,128)S(1)}, f32[4,128]{1,0:T(4,128)S(1)}, u32[]{:S(2)}, u32[]{:S(2)}) %collective-permute-start.1) | collective-permute-done | bytes 2080 | tf_op jit(solution)/shard_map/ppermute | solution.py:184
  53.2 2.2 all-to-all-done
  56.9 8.1 %all-to-all-start.1 = ((bf16[8,32,2048]{2,1,0:T(8,128)(2,1)}), bf16[8,32,2048]{2,1,0:T(8,128)(2,1)S(1)}, u32[]{:S(2)}, u32[]{:S(2)}) async-start(bf16[8,32,2048]{2,1,0:T(8,128)(2,1)} %bitcast.7), calls=%async_computation.1 | async-start | bytes 2097152 | tf_op jit(solution)/shard_map/all_to_all | solution.py:188
  65.1 24.4 %collective-permute-done.2.refs_1_.block = bf16[128,2048]{1,0:T(8,128)(2,1)S(1)} collective-permute-done((bf16[128,2048]{1,0:T(8,128)(2,1)S(1)}, bf16[128,2048]{1,0:T(8,128)(2,1)S(1)}, u32[]{:S(2)}, u32[]{:S(2)}) %collective-permute-start.2) | collective-permute-done | bytes 524320 | tf_op jit(solution)/shard_map/ppermute | solution.py:184
  91.0 3.8 %all-to-all-start.2 = ((bf16[8,32,2048]{2,1,0:T(8,128)(2,1)}), bf16[8,32,2048]{2,1,0:T(8,128)(2,1)S(1)}, u32[]{:S(2)}, u32[]{:S(2)}) async-start(bf16[8,32,2048]{2,1,0:T(8,128)(2,1)} %bitcast.12), calls=%async_computation.2 | async-start | bytes 2097152 | tf_op jit(solution)/shard_map/all_to_all | solution.py:188
  94.9 1.9 fusion.11
  99.2 3.0 %multiply_convert_fusion = (bf16[512,704]{1,0:T(8,128)(2,1)S(1)}, f32[512,704]{1,0:T(8,128)}) fusion(f32[512,704]{1,0:T(8,128)S(1)} %fusion.2.gate_ref, bf16[1,2048,704]{1,2,0:T(8,128)(2,1)S(1)} %copy-done.7, bf16[256,2048]{1,0:T(8,128)(2,1)S(1)} %bitcast.57, bf16[256,2048]{1,0:T(8,128)(2,1)S(1)} %bitcast.60), kind=kOutput, calls=%fused_computation.9 | convolution fusion | flops 1482752000 | bytes 8585216 | tf_op jit(solution)/shard_map/dot_general | solution.py:229
  102.2 2.0 convolution_convert_fusion.y_own
  104.2 1.9 convolution_convert_fusion.1
  106.3 5.0 %all-to-all-start.3 = ((bf16[8,32,2048]{2,1,0:T(8,128)(2,1)}), bf16[8,32,2048]{2,1,0:T(8,128)(2,1)S(1)}, u32[]{:S(2)}, u32[]{:S(2)}) async-start(bf16[8,32,2048]{2,1,0:T(8,128)(2,1)} %bitcast.67), calls=%async_computation.3 | async-start | bytes 2097152 | tf_op jit(solution)/shard_map/all_to_all | solution.py:188
  121.0 6.7 %shard_map.121 = (bf16[512,2048]{1,0:T(8,128)(2,1)S(1)}, bf16[256,2048]{1,0:T(8,128)(2,1)}, bf16[512,704]{1,0:T(8,128)(2,1)S(1)}, bf16[512,704]{1,0:T(8,128)(2,1)S(1)}) custom-call(bf16[256,2048]{1,0:T(8,128)(2,1)S(1)} %bitcast.51, bf16[256,2048]{1,0:T(8,128)(2,1)S(1)} %bitcast.49, f32[512,704]{1,0:T(8,128)S(1)} %copy-done.18, f32[512,704]{1,0:T(8,128)S(1)} %copy-done.19, ...), custom_call_target="tpu_custom_call" | custom-call | flops 1 | bytes 1 | tf_op jit(solution)/shard_map/pallas_call | solution.py:240
  128.9 4.7 %shard_map.122 = bf16[2112,2048]{1,0:T(8,128)(2,1)S(1)} custom-call(bf16[512,704]{1,0:T(8,128)(2,1)S(1)} %get-tuple-element.52.gg, bf16[512,704]{1,0:T(8,128)(2,1)S(1)} %get-tuple-element.53.gu, bf16[512,704]{1,0:T(8,128)(2,1)S(1)} %copy-done.22, bf16[256,2048]{1,0:T(8,128)(2,1)S(1)} %bitcast.61, bf16[256,2048]{1,0:T(8,128)(2,1)S(1)} %bitcast.58, ...), custom_call_target="tpu_custom_call" | custom-call | flops 1 | bytes 1 | tf_op jit(solution)/shard_map/pallas_call | solution.py:248
  133.6 3.4 %copy-done = bf16[2112,2048]{1,0:T(8,128)(2,1)} copy-done((bf16[2112,2048]{1,0:T(8,128)(2,1)}, bf16[2112,2048]{1,0:T(8,128)(2,1)S(1)}, u32[]{:S(2)}) %copy-start) | copy-done | bytes 8650776
  138.9 4.9 %all-to-all-start.4 = ((bf16[8,32,2048]{2,1,0:T(8,128)(2,1)}), bf16[8,32,2048]{2,1,0:T(8,128)(2,1)S(1)}, u32[]{:S(2)}, u32[]{:S(2)}) async-start(bf16[8,32,2048]{2,1,0:T(8,128)(2,1)} %bitcast.18), calls=%async_computation.4 | async-start | bytes 2097152 | tf_op jit(solution)/shard_map/all_to_all | solution.py:188
  144.4 2.3 %collective-permute-start.4 = (f32[128,128]{1,0:T(8,128)S(1)}, f32[128,128]{1,0:T(8,128)S(1)}, u32[]{:S(2)}, u32[]{:S(2)}) collective-permute-start(f32[128,128]{1,0:T(8,128)S(1)} %get-tuple-element.63), channel_id=1, source_target_pairs={{0,8},{1,9},{2,10},{3,11},{4,12},{5,13},{6,14},{7,15},{8,0},{9,1},... | collective-permute-start | bytes 196616 | tf_op jit(solution)/shard_map/ppermute | solution.py:184
  146.7 20.0 %all-to-all-done.4 = bf16[8,32,2048]{2,1,0:T(8,128)(2,1)S(1)} async-done(((bf16[8,32,2048]{2,1,0:T(8,128)(2,1)}), bf16[8,32,2048]{2,1,0:T(8,128)(2,1)S(1)}, u32[]{:S(2)}, u32[]{:S(2)}) %all-to-all-start.4) | async-done | bytes 1048608 | tf_op jit(solution)/shard_map/all_to_all | solution.py:188
  169.1 3.9 %all-to-all-start.5 = ((bf16[8,64,2048]{2,1,0:T(8,128)(2,1)}), bf16[8,64,2048]{2,1,0:T(8,128)(2,1)S(1)}, u32[]{:S(2)}, u32[]{:S(2)}) async-start(bf16[8,64,2048]{2,1,0:T(8,128)(2,1)} %bitcast.65), calls=%async_computation.5 | async-start | bytes 4194304 | tf_op jit(solution)/shard_map/all_to_all | solution.py:188
  173.0 2.9 %collective-permute-start.5 = (bf16[128,2048]{1,0:T(8,128)(2,1)}, bf16[128,2048]{1,0:T(8,128)(2,1)}, u32[]{:S(2)}, u32[]{:S(2)}) collective-permute-start(bf16[128,2048]{1,0:T(8,128)(2,1)} %copy-done.23), channel_id=1, source_target_pairs={{0,8},{1,9},{2,10},{3,11},{4,12},{5,13},{6,14},{7,15},{8,0},{9,1},... | collective-permute-start | bytes 1572872 | tf_op jit(solution)/shard_map/ppermute | solution.py:184
  175.9 6.1 %fusion.4 = (f32[1,704,1024]{2,1,0:T(8,128)}, f32[1,1024,704]{1,2,0:T(8,128)}, f32[1,1024,704]{1,2,0:T(8,128)}) fusion(bf16[2112,1024]{1,0:T(8,128)(2,1)} %reduce-scatter.2.cloned.1.call-done), kind=kLoop, calls=%fused_computation.11 | loop fusion | flops 2162688 | bytes 12976128 | tf_op jit(solution)/shard_map/broadcast_in_dim | solution.py:274
  182.0 25.0 %all-to-all-done.5 = bf16[8,64,2048]{2,1,0:T(8,128)(2,1)S(1)} async-done(((bf16[8,64,2048]{2,1,0:T(8,128)(2,1)}), bf16[8,64,2048]{2,1,0:T(8,128)(2,1)S(1)}, u32[]{:S(2)}, u32[]{:S(2)}) %all-to-all-start.5) | async-done | bytes 2097184 | tf_op jit(solution)/shard_map/all_to_all | solution.py:188
  207.0 3.3 %shard_map.125 = (bf16[128,2048]{1,0:T(8,128)(2,1)}, f32[128,128]{1,0:T(8,128)S(1)}, bf16[128,2048]{1,0:T(8,128)(2,1)}) custom-call(s32[1]{0:T(128)} %bitcast.me_ref, f32[4,128]{1,0:T(4,128)S(1)} %pad_maximum_fusion.3.refs_0_.refs_1_.meta, bf16[128,2048]{1,0:T(8,128)(2,1)S(1)} %copy-done.16, bf16[512,2048]{1,0:T(8,128)(2,1)S(1)} %bitcast.53, ...), custom_call_target="tpu_custom_call" | custom-call | flops 805306368 | bytes 4851712 | tf_op jit(solution)/shard_map/pallas_call | solution.py:20
  (72 shorter events, 26.1 us)
Async XLA Ops:
  12.8 6.3 %copy-start.25 = (bf16[128,2048]{1,0:T(8,128)(2,1)S(1)}, bf16[128,2048]{1,0:T(8,128)(2,1)}, u32[]{:S(2)}) copy-start(bf16[128,2048]{1,0:T(8,128)(2,1)} %refs_2_.1) | copy-start | bytes 1572868
  12.8 42.5 %all-to-all-start = ((bf16[8,64,2048]{2,1,0:T(8,128)(2,1)}), bf16[8,64,2048]{2,1,0:T(8,128)(2,1)}, u32[]{:S(2)}, u32[]{:S(2)}) async-start(bf16[8,64,2048]{2,1,0:T(8,128)(2,1)} %bitcast.3), calls=%async_computation | async-start | bytes 4194304 | tf_op jit(solution)/shard_map/all_to_all | solution.py:188
  19.1 45.8 %copy-start.15 = (bf16[128,2048]{1,0:T(8,128)(2,1)S(1)}, bf16[128,2048]{1,0:T(8,128)(2,1)}, u32[]{:S(2)}) copy-start(bf16[128,2048]{1,0:T(8,128)(2,1)} %block.1) | copy-start | bytes 1572868
  19.2 34.0 %collective-permute-start = (bf16[128,2048]{1,0:T(8,128)(2,1)S(1)}, bf16[128,2048]{1,0:T(8,128)(2,1)S(1)}, u32[]{:S(2)}, u32[]{:S(2)}) collective-permute-start(bf16[128,2048]{1,0:T(8,128)(2,1)S(1)} %copy-done.25), channel_id=1, source_target_pairs={{0,8},{1,9},{2,10},{3,11},{4,12},{5,13},{6,14},{7,15},{8,0},{9,1},... | collective-permute-start | bytes 1572872 | tf_op jit(solution)/shard_map/ppermute | solution.py:184
  21.8 31.4 %collective-permute-start.1 = (f32[4,128]{1,0:T(4,128)S(1)}, f32[4,128]{1,0:T(4,128)S(1)}, u32[]{:S(2)}, u32[]{:S(2)}) collective-permute-start(f32[4,128]{1,0:T(4,128)S(1)} %pad_maximum_fusion.3.refs_0_.refs_1_.meta), channel_id=1, source_target_pairs={{0,8},{1,9},{2,10},{3,11},{4,12},{5,13},{6,14},{7,15},{8,0},{9,1},... | collective-permute-start | bytes 6152 | tf_op jit(solution)/shard_map/ppermute | solution.py:184
  56.9 32.6 %all-to-all-start.1 = ((bf16[8,32,2048]{2,1,0:T(8,128)(2,1)}), bf16[8,32,2048]{2,1,0:T(8,128)(2,1)S(1)}, u32[]{:S(2)}, u32[]{:S(2)}) async-start(bf16[8,32,2048]{2,1,0:T(8,128)(2,1)} %bitcast.7), calls=%async_computation.1 | async-start | bytes 2097152 | tf_op jit(solution)/shard_map/all_to_all | solution.py:188
  65.0 24.5 %collective-permute-start.2 = (bf16[128,2048]{1,0:T(8,128)(2,1)S(1)}, bf16[128,2048]{1,0:T(8,128)(2,1)S(1)}, u32[]{:S(2)}, u32[]{:S(2)}) collective-permute-start(bf16[128,2048]{1,0:T(8,128)(2,1)S(1)} %copy-done.15), channel_id=1, source_target_pairs={{0,8},{1,9},{2,10},{3,11},{4,12},{5,13},{6,14},{7,15},{8,0},{9,1},... | collective-permute-start | bytes 1572872 | tf_op jit(solution)/shard_map/ppermute | solution.py:184
  89.5 9.7 %copy-start.1 = (bf16[8,32,2048]{2,1,0:T(8,128)(2,1)}, bf16[8,32,2048]{2,1,0:T(8,128)(2,1)S(1)}, u32[]{:S(2)}) copy-start(bf16[8,32,2048]{2,1,0:T(8,128)(2,1)S(1)} %all-to-all-done.1) | copy-start | bytes 3145732
  91.0 15.3 %all-to-all-start.2 = ((bf16[8,32,2048]{2,1,0:T(8,128)(2,1)}), bf16[8,32,2048]{2,1,0:T(8,128)(2,1)S(1)}, u32[]{:S(2)}, u32[]{:S(2)}) async-start(bf16[8,32,2048]{2,1,0:T(8,128)(2,1)} %bitcast.12), calls=%async_computation.2 | async-start | bytes 2097152 | tf_op jit(solution)/shard_map/all_to_all | solution.py:188
  94.9 2.4 %copy-start.5 = (bf16[1,2048,704]{1,2,0:T(8,128)(2,1)S(1)}, bf16[1,2048,704]{1,2,0:T(8,128)(2,1)}, u32[]{:S(2)}) copy-start(bf16[1,2048,704]{1,2,0:T(8,128)(2,1)} %param.10) | copy-start | bytes 8650756
  99.2 3.0 %copy-start.17 = (f32[512,704]{1,0:T(8,128)}, f32[512,704]{1,0:T(8,128)S(1)}, u32[]{:S(2)}) copy-start(f32[512,704]{1,0:T(8,128)S(1)} %fusion.2.gate_ref) | copy-start | bytes 4325380
  99.2 3.0 %copy-start.9 = (bf16[1,704,2048]{2,1,0:T(8,128)(2,1)S(1)}, bf16[1,704,2048]{2,1,0:T(8,128)(2,1)}, u32[]{:S(2)}) copy-start(bf16[1,704,2048]{2,1,0:T(8,128)(2,1)} %param.12) | copy-start | bytes 8650756
  106.3 30.7 %all-to-all-start.3 = ((bf16[8,32,2048]{2,1,0:T(8,128)(2,1)}), bf16[8,32,2048]{2,1,0:T(8,128)(2,1)S(1)}, u32[]{:S(2)}, u32[]{:S(2)}) async-start(bf16[8,32,2048]{2,1,0:T(8,128)(2,1)} %bitcast.67), calls=%async_computation.3 | async-start | bytes 2097152 | tf_op jit(solution)/shard_map/all_to_all | solution.py:188
  111.3 64.7 %reduce-scatter.2.cloned.1.call-start = ((), (), s32[]{:S(2)}) async-start(), calls=%async_computation.7 | async-start | bytes 12976128 | tf_op jit(solution)/shard_map/reduce_scatter | solution.py:266
  121.0 8.0 %copy-start.2 = (bf16[8,32,2048]{2,1,0:T(8,128)(2,1)S(1)}, bf16[8,32,2048]{2,1,0:T(8,128)(2,1)}, u32[]{:S(2)}) copy-start(bf16[8,32,2048]{2,1,0:T(8,128)(2,1)} %copy-done.1) | copy-start | bytes 3145732
  121.0 8.0 %copy-start.4 = (bf16[8,1,32,2048]{3,2,1,0:T(8,128)(2,1)S(1)}, bf16[8,1,32,2048]{3,2,1,0:T(8,128)(2,1)}, u32[]{:S(2)}) copy-start(bf16[8,1,32,2048]{3,2,1,0:T(8,128)(2,1)} %copy-done.3) | copy-start | bytes 3145732
  121.0 8.0 %copy-start.22 = (bf16[512,704]{1,0:T(8,128)(2,1)S(1)}, bf16[512,704]{1,0:T(8,128)(2,1)}, u32[]{:S(2)}) copy-start(bf16[512,704]{1,0:T(8,128)(2,1)} %copy-done.21) | copy-start | bytes 2162692
  133.6 3.4 %copy-start = (bf16[2112,2048]{1,0:T(8,128)(2,1)}, bf16[2112,2048]{1,0:T(8,128)(2,1)S(1)}, u32[]{:S(2)}) copy-start(bf16[2112,2048]{1,0:T(8,128)(2,1)S(1)} %shard_map.122) | copy-start | bytes 25952260
  138.9 27.8 %all-to-all-start.4 = ((bf16[8,32,2048]{2,1,0:T(8,128)(2,1)}), bf16[8,32,2048]{2,1,0:T(8,128)(2,1)S(1)}, u32[]{:S(2)}, u32[]{:S(2)}) async-start(bf16[8,32,2048]{2,1,0:T(8,128)(2,1)} %bitcast.18), calls=%async_computation.4 | async-start | bytes 2097152 | tf_op jit(solution)/shard_map/all_to_all | solution.py:188
  143.8 25.3 %collective-permute-start.3 = (bf16[128,2048]{1,0:T(8,128)(2,1)S(1)}, bf16[128,2048]{1,0:T(8,128)(2,1)S(1)}, u32[]{:S(2)}, u32[]{:S(2)}) collective-permute-start(bf16[128,2048]{1,0:T(8,128)(2,1)S(1)} %get-tuple-element.62), channel_id=1, source_target_pairs={{0,8},{1,9},{2,10},{3,11},{4,12},{5,13},{6,14},{7,15},{8,0},{9,1},... | collective-permute-start | bytes 1572872 | tf_op jit(solution)/shard_map/ppermute | solution.py:184
  144.4 24.7 %collective-permute-start.4 = (f32[128,128]{1,0:T(8,128)S(1)}, f32[128,128]{1,0:T(8,128)S(1)}, u32[]{:S(2)}, u32[]{:S(2)}) collective-permute-start(f32[128,128]{1,0:T(8,128)S(1)} %get-tuple-element.63), channel_id=1, source_target_pairs={{0,8},{1,9},{2,10},{3,11},{4,12},{5,13},{6,14},{7,15},{8,0},{9,1},... | collective-permute-start | bytes 196616 | tf_op jit(solution)/shard_map/ppermute | solution.py:184
  169.1 37.9 %all-to-all-start.5 = ((bf16[8,64,2048]{2,1,0:T(8,128)(2,1)}), bf16[8,64,2048]{2,1,0:T(8,128)(2,1)S(1)}, u32[]{:S(2)}, u32[]{:S(2)}) async-start(bf16[8,64,2048]{2,1,0:T(8,128)(2,1)} %bitcast.65), calls=%async_computation.5 | async-start | bytes 4194304 | tf_op jit(solution)/shard_map/all_to_all | solution.py:188
  173.0 34.0 %copy-start.16 = (bf16[128,2048]{1,0:T(8,128)(2,1)S(1)}, bf16[128,2048]{1,0:T(8,128)(2,1)}, u32[]{:S(2)}) copy-start(bf16[128,2048]{1,0:T(8,128)(2,1)} %block.1) | copy-start | bytes 1572868
  173.0 34.0 %collective-permute-start.5 = (bf16[128,2048]{1,0:T(8,128)(2,1)}, bf16[128,2048]{1,0:T(8,128)(2,1)}, u32[]{:S(2)}, u32[]{:S(2)}) collective-permute-start(bf16[128,2048]{1,0:T(8,128)(2,1)} %copy-done.23), channel_id=1, source_target_pairs={{0,8},{1,9},{2,10},{3,11},{4,12},{5,13},{6,14},{7,15},{8,0},{9,1},... | collective-permute-start | bytes 1572872 | tf_op jit(solution)/shard_map/ppermute | solution.py:184
  (15 other events, 22.5 us)
Sparse Core Ops, SparseCore 0:
  137.2 16.4 reduce-scatter.1

commit v9 on v8

--- a/solution.py
+++ b/solution.py
@@ -22,7 +22,7 @@
         out_shape=outs,
         in_specs=[SMEM] + [VMEM] * len(args),
         out_specs=[VMEM] * len(outs),
-        compiler_params=pltpu.CompilerParams(vmem_limit_bytes=16 * 1024 * 1024),
+        compiler_params=pltpu.CompilerParams(vmem_limit_bytes=6 * 1024 * 1024),
         cost_estimate=pl.CostEstimate(flops=flops, bytes_accessed=size, transcendentals=0),
     )(me, *args)
 
@@ -152,20 +152,34 @@
         both[:, c:e] = jnp.concatenate(pair, 1).reshape(2 * half, e - c).astype(BF16)
 
 
-def terms_kernel(gg, gu, hidden, x_own, x_far, d_own, d_far, out):
+def terms_kernel(gg, gu, hidden, x_own, x_far, d_own, d_far, out, tiles, sems):
     half, feature = x_own.shape
     units = gg.shape[1]
     pairs = ((gg, x_own, x_far), (gu, x_own, x_far), (hidden, d_own, d_far))
-    for n, (left, own, far) in enumerate(pairs):
-        for r, t in strips(units, 256):
-            for c, e in strips(feature, 1024):
-                got = lax.dot_general(
-                    left[:half, r:t], own[:, c:e], TRANSPOSED, preferred_element_type=F32
-                )
-                got += lax.dot_general(
-                    left[half:, r:t], far[:, c:e], TRANSPOSED, preferred_element_type=F32
-                )
-                out[n * units + r : n * units + t, c:e] = got.astype(BF16)
+    steps = [(n, r, t) for n in range(3) for r, t in strips(units, tiles.shape[1])]
+    copies = []
+    for step, (n, r, t) in enumerate(steps):
+        left, own, far = pairs[n]
+        slot = step % 2
+        if step > 1:
+            copies[step - 2].wait()
+        for c, e in strips(feature, 1024):
+            got = lax.dot_general(
+                left[:half, r:t], own[:, c:e], TRANSPOSED, preferred_element_type=F32
+            )
+            got += lax.dot_general(
+                left[half:, r:t], far[:, c:e], TRANSPOSED, preferred_element_type=F32
+            )
+            tiles[slot, : t - r, c:e] = got.astype(BF16)
+        copy = pltpu.make_async_copy(
+            tiles.at[slot, pl.ds(0, t - r)],
+            out.at[pl.ds(n * units + r, t - r)],
+            sems.at[slot],
+        )
+        copy.start()
+        copies.append(copy)
+    for copy in copies[-2:]:
+        copy.wait()
 
 
 def on_device(tokens, expert_ids, gate_prob, w_gate, w_up, w_down, d_mixed):
@@ -214,9 +228,7 @@
     own = exchange(pick([meta, meta], [tokens, d_mixed], (False, True)))
     own = own.reshape(side, 2, capacity, feature)
     x_far, meta_far = after(across(tokens), across(meta))
-    d_late, x_far = after(d_mixed, x_far)
-    d_far = across(d_late)
-    x_far, own = after(x_far, own)
+    x_far, d_far, own = after(x_far, across(d_mixed), own)
     x_own, d_own = (own[:, n].reshape(half, feature) for n in range(2))
     x_far_rows = exchange(pick([meta_far], [x_far], (False,)))
     x_rows = jnp.concatenate([x_own, x_far_rows], 0)
@@ -242,15 +254,16 @@
         out_shape=[shape((n_rows, feature), BF16), rows, units, units],
         in_specs=[VMEM] * 8,
         out_specs=[VMEM] * 4,
-        compiler_params=pltpu.CompilerParams(vmem_limit_bytes=32 * 1024 * 1024),
+        compiler_params=pltpu.CompilerParams(vmem_limit_bytes=10 * 1024 * 1024),
         cost_estimate=pl.CostEstimate(flops=1, bytes_accessed=1, transcendentals=0),
     )(d_own, d_far_rows, gate_pre, up_pre, y_own, gate_matrix.T, up_matrix.T, down_matrix)
     (terms,) = pl.pallas_call(
         terms_kernel,
         out_shape=[shape((3 * hidden_units, feature), BF16)],
         in_specs=[VMEM] * 7,
-        out_specs=[VMEM],
-        compiler_params=pltpu.CompilerParams(vmem_limit_bytes=32 * 1024 * 1024),
+        out_specs=[pl.BlockSpec(memory_space=pltpu.HBM)],
+        scratch_shapes=[pltpu.VMEM((2, 256, feature), BF16), pltpu.SemaphoreType.DMA((2,))],
+        compiler_params=pltpu.CompilerParams(vmem_limit_bytes=10 * 1024 * 1024),
         cost_estimate=pl.CostEstimate(flops=1, bytes_accessed=1, transcendentals=0),
     )(gg, gu, hidden, x_own, x_far_rows, d_own, d_far_rows)
     dx_far, both, terms, y_far_back = after(dx_far, both, terms, y_far_back)

time: 219 us -> 219 us (level)
  blocking collectives: 0 us -> 21.8 us
  waiting for transfers between devices: 104 us -> 88.8 us
  starting transfers between devices: 41.2 us -> 32.9 us
    all_to_all x0 -> x1, blocking collectives: none -> 21.8 us  [exchange(): lax.all_to_all(shaped, 'expert', 0, 0, axis_index_groups=sets, tiled=True)]
    ppermute x6, waiting for transfers between devices: 56.6 us -> 43.3 us  [across(): lax.ppermute(value, 'expert', [(e, (e + side) % experts) for e in range(e...]
    all_to_all x6 -> x5, starting transfers between devices: 32 us -> 23 us  [exchange(): lax.all_to_all(shaped, 'expert', 0, 0, axis_index_groups=sets, tiled=True)]
    all_to_all x6 -> x5, waiting for transfers between devices: 47.3 us -> 45.4 us  [exchange(): lax.all_to_all(shaped, 'expert', 0, 0, axis_index_groups=sets, tiled=True)]
  transfers between devices with their start and end apart: 13 -> 12, of which waited for: 7 -> 6; matrix products, arithmetic and copies ran while one was open for 8% -> 8% of each run, Pallas kernels for 6% -> 6%
where the time goes in v9:
time: 219 us; the launch traced here: 218 us
  waiting for transfers between devices  88.8 us (41%)
  starting transfers between devices  32.9 us (15%)
  Pallas kernels  22.2 us (10%)
  local copies, waits for them, and re-layouts  21.9 us (10%)
  blocking collectives  21.8 us (10%)
  between operations  14.2 us (6%)
  matrix products  8.77 us (4%)
  other arithmetic  7.44 us (3%)
    all_to_all x5, waiting for transfers between devices, exchange(): lax.all_to_all(shaped, 'expert', 0, 0, axis_index_groups=sets, tiled=True)  45.4 us
    ppermute x6, waiting for transfers between devices, across(): lax.ppermute(value, 'expert', [(e, (e + side) % experts) for e in range(e...  43.3 us
    all_to_all x5, starting transfers between devices, exchange(): lax.all_to_all(shaped, 'expert', 0, 0, axis_index_groups=sets, tiled=True)  23 us
    all_to_all x1, blocking collectives, exchange(): lax.all_to_all(shaped, 'expert', 0, 0, axis_index_groups=sets, tiled=True)  21.8 us
    unnamed x53, local copies, waits for them, and re-layouts  19.9 us
    pallas_call x6, Pallas kernels, local_call(): pl.pallas_call(kernel, out_shape=outs, in_specs=[SMEM] + [VMEM] * len(arg...  9.87 us
    ppermute x6, starting transfers between devices, across(): lax.ppermute(value, 'expert', [(e, (e + side) % experts) for e in range(e...  9.68 us
    pallas_call x1, Pallas kernels, on_device(): pl.pallas_call(terms_kernel, out_shape=[shape((3 * hidden_units, feature)...  6.87 us
  transfers between devices with their start and end apart: 12, of which 6 were waited for; matrix products, arithmetic and copies ran while one was open for 8% of the time, Pallas kernels for 6%

profile of v9, /device:TPU:0, one launch (start us, length us, event | category | flops | bytes accessed | tf_op | source)
XLA Modules:
  0.0 218.0 jit_solution(16439301349292223743)
XLA Ops:
  9.6 3.2 %shard_map.118 = bf16[512,2048]{1,0:T(8,128)(2,1)} custom-call(s32[1]{0:T(128)} %bitcast.me_ref, f32[4,128]{1,0:T(4,128)S(1)} %pad_maximum_fusion.3.refs_0_.refs_1_.meta, f32[4,128]{1,0:T(4,128)S(1)} %pad_maximum_fusion.3.refs_0_.refs_1_.meta, bf16[128,2048]{1,0:T(8,128)(2,1)} %refs_2_.1, bf16[128,2048]{1,0:T(8,128)(2,1)S(1)} %copy-done.14), custom_call_target="tpu_custom_call" | custom-call | flops 536870912 | bytes 3149824 | tf_op jit(solution)/shard_map/pallas_call | solution.py:20
  12.8 6.2 %all-to-all-start = ((bf16[8,64,2048]{2,1,0:T(8,128)(2,1)}), bf16[8,64,2048]{2,1,0:T(8,128)(2,1)}, u32[]{:S(2)}, u32[]{:S(2)}) async-start(bf16[8,64,2048]{2,1,0:T(8,128)(2,1)} %bitcast.3), calls=%async_computation | async-start | bytes 4194304 | tf_op jit(solution)/shard_map/all_to_all | solution.py:202
  19.0 2.6 %collective-permute-start = (bf16[128,2048]{1,0:T(8,128)(2,1)}, bf16[128,2048]{1,0:T(8,128)(2,1)S(1)}, u32[]{:S(2)}, u32[]{:S(2)}) collective-permute-start(bf16[128,2048]{1,0:T(8,128)(2,1)} %refs_2_.1), channel_id=1, source_target_pairs={{0,8},{1,9},{2,10},{3,11},{4,12},{5,13},{6,14},{7,15},{8,0},{9,1},... | collective-permute-start | bytes 1572872 | tf_op jit(solution)/shard_map/ppermute | solution.py:198
  21.9 2.6 %collective-permute-start.1 = (f32[4,128]{1,0:T(4,128)S(1)}, f32[4,128]{1,0:T(4,128)S(1)}, u32[]{:S(2)}, u32[]{:S(2)}) collective-permute-start(f32[4,128]{1,0:T(4,128)S(1)} %pad_maximum_fusion.3.refs_0_.refs_1_.meta), channel_id=1, source_target_pairs={{0,8},{1,9},{2,10},{3,11},{4,12},{5,13},{6,14},{7,15},{8,0},{9,1},... | collective-permute-start | bytes 6152 | tf_op jit(solution)/shard_map/ppermute | solution.py:198
  24.5 39.8 %collective-permute-done.1.refs_0_.meta = f32[4,128]{1,0:T(4,128)S(1)} collective-permute-done((f32[4,128]{1,0:T(4,128)S(1)}, f32[4,128]{1,0:T(4,128)S(1)}, u32[]{:S(2)}, u32[]{:S(2)}) %collective-permute-start.1) | collective-permute-done | bytes 2080 | tf_op jit(solution)/shard_map/ppermute | solution.py:198
  64.3 2.1 all-to-all-done
  67.0 21.8 %all_to_all.30 = bf16[8,32,2048]{2,1,0:T(8,128)(2,1)S(1)} all-to-all(bf16[8,32,2048]{2,1,0:T(8,128)(2,1)S(1)} %bitcast.56), channel_id=1, replica_groups={{0,1,2,3,4,5,6,7},{8,9,10,11,12,13,14,15},{16,17,18,19,20,21,22,23},{24..., dimensions={0} | all-to-all | bytes 2097152 | tf_op jit(solution)/shard_map/all_to_all | solution.py:202
  90.4 3.6 %all-to-all-start.2 = ((bf16[8,32,2048]{2,1,0:T(8,128)(2,1)}), bf16[8,32,2048]{2,1,0:T(8,128)(2,1)S(1)}, u32[]{:S(2)}, u32[]{:S(2)}) async-start(bf16[8,32,2048]{2,1,0:T(8,128)(2,1)} %bitcast.12), calls=%async_computation.2 | async-start | bytes 2097152 | tf_op jit(solution)/shard_map/all_to_all | solution.py:202
  93.9 1.9 fusion.11
  98.3 3.0 %multiply_convert_fusion = (bf16[512,704]{1,0:T(8,128)(2,1)S(1)}, f32[512,704]{1,0:T(8,128)}) fusion(f32[512,704]{1,0:T(8,128)S(1)} %fusion.2.gate_ref, bf16[1,2048,704]{1,2,0:T(8,128)(2,1)S(1)} %copy-done.7, bf16[256,2048]{1,0:T(8,128)(2,1)S(1)} %bitcast.58, bf16[256,2048]{1,0:T(8,128)(2,1)S(1)} %bitcast.61), kind=kOutput, calls=%fused_computation.9 | convolution fusion | flops 1482752000 | bytes 8585216 | tf_op jit(solution)/shard_map/dot_general | solution.py:241
  101.3 2.0 convolution_convert_fusion.y_own
  103.3 2.0 convolution_convert_fusion.1
  105.8 4.4 %all-to-all-start.3 = ((bf16[8,32,2048]{2,1,0:T(8,128)(2,1)}), bf16[8,32,2048]{2,1,0:T(8,128)(2,1)S(1)}, u32[]{:S(2)}, u32[]{:S(2)}) async-start(bf16[8,32,2048]{2,1,0:T(8,128)(2,1)} %bitcast.69), calls=%async_computation.3 | async-start | bytes 2097152 | tf_op jit(solution)/shard_map/all_to_all | solution.py:202
  120.0 5.5 %shard_map.121 = (bf16[512,2048]{1,0:T(8,128)(2,1)S(1)}, bf16[256,2048]{1,0:T(8,128)(2,1)S(1)}, bf16[512,704]{1,0:T(8,128)(2,1)S(1)}, bf16[512,704]{1,0:T(8,128)(2,1)S(1)}) custom-call(bf16[256,2048]{1,0:T(8,128)(2,1)S(1)} %bitcast.51, bf16[256,2048]{1,0:T(8,128)(2,1)S(1)} %bitcast.49, f32[512,704]{1,0:T(8,128)S(1)} %copy-done.17, ...), custom_call_target="tpu_custom_call" | custom-call | flops 1 | bytes 1 | tf_op jit(solution)/shard_map/pallas_call | solution.py:252
  127.8 6.9 %shard_map.122 = bf16[2112,2048]{1,0:T(8,128)(2,1)S(1)} custom-call(bf16[512,704]{1,0:T(8,128)(2,1)S(1)} %get-tuple-element.50.gg, bf16[512,704]{1,0:T(8,128)(2,1)S(1)} %get-tuple-element.51.gu, bf16[512,704]{1,0:T(8,128)(2,1)S(1)} %copy-done.22, bf16[256,2048]{1,0:T(8,128)(2,1)S(1)} %bitcast.62, bf16[256,2048]{1,0:T(8,128)(2,1)S(1)} %bitcast.59, ...), custom_call_target="tpu_custom_call" | custom-call | flops 1 | bytes 1 | tf_op jit(solution)/shard_map/pallas_call | solution.py:260
  134.7 3.4 %copy-done = bf16[2112,2048]{1,0:T(8,128)(2,1)} copy-done((bf16[2112,2048]{1,0:T(8,128)(2,1)}, bf16[2112,2048]{1,0:T(8,128)(2,1)S(1)}, u32[]{:S(2)}) %copy-start) | copy-done | bytes 8650776
  139.9 4.9 %all-to-all-start.4 = ((bf16[8,32,2048]{2,1,0:T(8,128)(2,1)}), bf16[8,32,2048]{2,1,0:T(8,128)(2,1)S(1)}, u32[]{:S(2)}, u32[]{:S(2)}) async-start(bf16[8,32,2048]{2,1,0:T(8,128)(2,1)} %bitcast.67), calls=%async_computation.4 | async-start | bytes 2097152 | tf_op jit(solution)/shard_map/all_to_all | solution.py:202
  144.8 2.9 %collective-permute-start.4 = (f32[128,128]{1,0:T(8,128)S(1)}, f32[128,128]{1,0:T(8,128)S(1)}, u32[]{:S(2)}, u32[]{:S(2)}) collective-permute-start(f32[128,128]{1,0:T(8,128)S(1)} %get-tuple-element.61), channel_id=1, source_target_pairs={{0,8},{1,9},{2,10},{3,11},{4,12},{5,13},{6,14},{7,15},{8,0},{9,1},... | collective-permute-start | bytes 196616 | tf_op jit(solution)/shard_map/ppermute | solution.py:198
  147.7 18.5 %all-to-all-done.4 = bf16[8,32,2048]{2,1,0:T(8,128)(2,1)S(1)} async-done(((bf16[8,32,2048]{2,1,0:T(8,128)(2,1)}), bf16[8,32,2048]{2,1,0:T(8,128)(2,1)S(1)}, u32[]{:S(2)}, u32[]{:S(2)}) %all-to-all-start.4) | async-done | bytes 1048608 | tf_op jit(solution)/shard_map/all_to_all | solution.py:202
  167.4 3.5 %collective-permute-done.4.far_grads = f32[128,128]{1,0:T(8,128)S(1)} collective-permute-done((f32[128,128]{1,0:T(8,128)S(1)}, f32[128,128]{1,0:T(8,128)S(1)}, u32[]{:S(2)}, u32[]{:S(2)}) %collective-permute-start.4) | collective-permute-done | bytes 65568 | tf_op jit(solution)/shard_map/ppermute | solution.py:198
  171.8 3.9 %all-to-all-start.5 = ((bf16[8,64,2048]{2,1,0:T(8,128)(2,1)}), bf16[8,64,2048]{2,1,0:T(8,128)(2,1)S(1)}, u32[]{:S(2)}, u32[]{:S(2)}) async-start(bf16[8,64,2048]{2,1,0:T(8,128)(2,1)} %bitcast.66), calls=%async_computation.5 | async-start | bytes 4194304 | tf_op jit(solution)/shard_map/all_to_all | solution.py:202
  177.0 6.1 %fusion.4 = (f32[1,704,1024]{2,1,0:T(8,128)}, f32[1,1024,704]{1,2,0:T(8,128)}, f32[1,1024,704]{1,2,0:T(8,128)}) fusion(bf16[2112,1024]{1,0:T(8,128)(2,1)} %reduce-scatter.2.cloned.1.call-done), kind=kLoop, calls=%fused_computation.11 | loop fusion | flops 2162688 | bytes 12976128 | tf_op jit(solution)/shard_map/broadcast_in_dim | solution.py:287
  183.0 24.3 %all-to-all-done.5 = bf16[8,64,2048]{2,1,0:T(8,128)(2,1)S(1)} async-done(((bf16[8,64,2048]{2,1,0:T(8,128)(2,1)}), bf16[8,64,2048]{2,1,0:T(8,128)(2,1)S(1)}, u32[]{:S(2)}, u32[]{:S(2)}) %all-to-all-start.5) | async-done | bytes 2097184 | tf_op jit(solution)/shard_map/all_to_all | solution.py:202
  207.3 3.3 %shard_map.125 = (bf16[128,2048]{1,0:T(8,128)(2,1)}, f32[128,128]{1,0:T(8,128)S(1)}, bf16[128,2048]{1,0:T(8,128)(2,1)}) custom-call(s32[1]{0:T(128)} %bitcast.me_ref, f32[4,128]{1,0:T(4,128)S(1)} %pad_maximum_fusion.3.refs_0_.refs_1_.meta, bf16[128,2048]{1,0:T(8,128)(2,1)S(1)} %copy-done.15, bf16[512,2048]{1,0:T(8,128)(2,1)S(1)} %bitcast.53, ...), custom_call_target="tpu_custom_call" | custom-call | flops 805306368 | bytes 4851712 | tf_op jit(solution)/shard_map/pallas_call | solution.py:20
  (71 shorter events, 25.6 us)
Async XLA Ops:
  12.8 53.6 %all-to-all-start = ((bf16[8,64,2048]{2,1,0:T(8,128)(2,1)}), bf16[8,64,2048]{2,1,0:T(8,128)(2,1)}, u32[]{:S(2)}, u32[]{:S(2)}) async-start(bf16[8,64,2048]{2,1,0:T(8,128)(2,1)} %bitcast.3), calls=%async_computation | async-start | bytes 4194304 | tf_op jit(solution)/shard_map/all_to_all | solution.py:202
  19.0 45.3 %collective-permute-start = (bf16[128,2048]{1,0:T(8,128)(2,1)}, bf16[128,2048]{1,0:T(8,128)(2,1)S(1)}, u32[]{:S(2)}, u32[]{:S(2)}) collective-permute-start(bf16[128,2048]{1,0:T(8,128)(2,1)} %refs_2_.1), channel_id=1, source_target_pairs={{0,8},{1,9},{2,10},{3,11},{4,12},{5,13},{6,14},{7,15},{8,0},{9,1},... | collective-permute-start | bytes 1572872 | tf_op jit(solution)/shard_map/ppermute | solution.py:198
  21.6 42.7 %collective-permute-start.2 = (bf16[128,2048]{1,0:T(8,128)(2,1)S(1)}, bf16[128,2048]{1,0:T(8,128)(2,1)S(1)}, u32[]{:S(2)}, u32[]{:S(2)}) collective-permute-start(bf16[128,2048]{1,0:T(8,128)(2,1)S(1)} %copy-done.14), channel_id=1, source_target_pairs={{0,8},{1,9},{2,10},{3,11},{4,12},{5,13},{6,14},{7,15},{8,0},{9,1},... | collective-permute-start | bytes 1572872 | tf_op jit(solution)/shard_map/ppermute | solution.py:198
  21.9 42.4 %collective-permute-start.1 = (f32[4,128]{1,0:T(4,128)S(1)}, f32[4,128]{1,0:T(4,128)S(1)}, u32[]{:S(2)}, u32[]{:S(2)}) collective-permute-start(f32[4,128]{1,0:T(4,128)S(1)} %pad_maximum_fusion.3.refs_0_.refs_1_.meta), channel_id=1, source_target_pairs={{0,8},{1,9},{2,10},{3,11},{4,12},{5,13},{6,14},{7,15},{8,0},{9,1},... | collective-permute-start | bytes 6152 | tf_op jit(solution)/shard_map/ppermute | solution.py:198
  64.3 26.0 %copy-start.11 = (bf16[128,2048]{1,0:T(8,128)(2,1)}, bf16[128,2048]{1,0:T(8,128)(2,1)S(1)}, u32[]{:S(2)}) copy-start(bf16[128,2048]{1,0:T(8,128)(2,1)S(1)} %collective-permute-done.2.refs_1_.block) | copy-start | bytes 1572868
  88.8 9.4 %copy-start.1 = (bf16[8,32,2048]{2,1,0:T(8,128)(2,1)}, bf16[8,32,2048]{2,1,0:T(8,128)(2,1)S(1)}, u32[]{:S(2)}) copy-start(bf16[8,32,2048]{2,1,0:T(8,128)(2,1)S(1)} %all_to_all.30) | copy-start | bytes 3145732
  90.4 15.5 %all-to-all-start.2 = ((bf16[8,32,2048]{2,1,0:T(8,128)(2,1)}), bf16[8,32,2048]{2,1,0:T(8,128)(2,1)S(1)}, u32[]{:S(2)}, u32[]{:S(2)}) async-start(bf16[8,32,2048]{2,1,0:T(8,128)(2,1)} %bitcast.12), calls=%async_computation.2 | async-start | bytes 2097152 | tf_op jit(solution)/shard_map/all_to_all | solution.py:202
  93.9 2.4 %copy-start.5 = (bf16[1,2048,704]{1,2,0:T(8,128)(2,1)S(1)}, bf16[1,2048,704]{1,2,0:T(8,128)(2,1)}, u32[]{:S(2)}) copy-start(bf16[1,2048,704]{1,2,0:T(8,128)(2,1)} %param.10) | copy-start | bytes 8650756
  95.9 2.4 %copy-start.3 = (bf16[8,1,32,2048]{3,2,1,0:T(8,128)(2,1)}, bf16[8,1,32,2048]{3,2,1,0:T(8,128)(2,1)S(1)}, u32[]{:S(2)}) copy-start(bf16[8,1,32,2048]{3,2,1,0:T(8,128)(2,1)S(1)} %get-tuple-element.95) | copy-start | bytes 3145732
  98.3 3.0 %copy-start.16 = (f32[512,704]{1,0:T(8,128)}, f32[512,704]{1,0:T(8,128)S(1)}, u32[]{:S(2)}) copy-start(f32[512,704]{1,0:T(8,128)S(1)} %fusion.2.gate_ref) | copy-start | bytes 4325380
  98.3 3.0 %copy-start.9 = (bf16[1,704,2048]{2,1,0:T(8,128)(2,1)S(1)}, bf16[1,704,2048]{2,1,0:T(8,128)(2,1)}, u32[]{:S(2)}) copy-start(bf16[1,704,2048]{2,1,0:T(8,128)(2,1)} %param.12) | copy-start | bytes 8650756
  105.8 32.2 %all-to-all-start.3 = ((bf16[8,32,2048]{2,1,0:T(8,128)(2,1)}), bf16[8,32,2048]{2,1,0:T(8,128)(2,1)S(1)}, u32[]{:S(2)}, u32[]{:S(2)}) async-start(bf16[8,32,2048]{2,1,0:T(8,128)(2,1)} %bitcast.69), calls=%async_computation.3 | async-start | bytes 2097152 | tf_op jit(solution)/shard_map/all_to_all | solution.py:202
  110.3 66.7 %reduce-scatter.2.cloned.1.call-start = ((), (), s32[]{:S(2)}) async-start(), calls=%async_computation.7 | async-start | bytes 12976128 | tf_op jit(solution)/shard_map/reduce_scatter | solution.py:279
  120.0 7.8 %copy-start.2 = (bf16[8,32,2048]{2,1,0:T(8,128)(2,1)S(1)}, bf16[8,32,2048]{2,1,0:T(8,128)(2,1)}, u32[]{:S(2)}) copy-start(bf16[8,32,2048]{2,1,0:T(8,128)(2,1)} %copy-done.1) | copy-start | bytes 3145732
  120.0 7.8 %copy-start.4 = (bf16[8,1,32,2048]{3,2,1,0:T(8,128)(2,1)S(1)}, bf16[8,1,32,2048]{3,2,1,0:T(8,128)(2,1)}, u32[]{:S(2)}) copy-start(bf16[8,1,32,2048]{3,2,1,0:T(8,128)(2,1)} %copy-done.3) | copy-start | bytes 3145732
  120.0 7.8 %copy-start.22 = (bf16[512,704]{1,0:T(8,128)(2,1)S(1)}, bf16[512,704]{1,0:T(8,128)(2,1)}, u32[]{:S(2)}) copy-start(bf16[512,704]{1,0:T(8,128)(2,1)} %copy-done.21) | copy-start | bytes 2162692
  134.6 3.4 %copy-start = (bf16[2112,2048]{1,0:T(8,128)(2,1)}, bf16[2112,2048]{1,0:T(8,128)(2,1)S(1)}, u32[]{:S(2)}) copy-start(bf16[2112,2048]{1,0:T(8,128)(2,1)S(1)} %shard_map.122) | copy-start | bytes 25952260
  139.9 26.3 %all-to-all-start.4 = ((bf16[8,32,2048]{2,1,0:T(8,128)(2,1)}), bf16[8,32,2048]{2,1,0:T(8,128)(2,1)S(1)}, u32[]{:S(2)}, u32[]{:S(2)}) async-start(bf16[8,32,2048]{2,1,0:T(8,128)(2,1)} %bitcast.67), calls=%async_computation.4 | async-start | bytes 2097152 | tf_op jit(solution)/shard_map/all_to_all | solution.py:202
  144.8 26.2 %collective-permute-start.3 = (bf16[128,2048]{1,0:T(8,128)(2,1)S(1)}, bf16[128,2048]{1,0:T(8,128)(2,1)S(1)}, u32[]{:S(2)}, u32[]{:S(2)}) collective-permute-start(bf16[128,2048]{1,0:T(8,128)(2,1)S(1)} %get-tuple-element.60), channel_id=1, source_target_pairs={{0,8},{1,9},{2,10},{3,11},{4,12},{5,13},{6,14},{7,15},{8,0},{9,1},... | collective-permute-start | bytes 1572872 | tf_op jit(solution)/shard_map/ppermute | solution.py:198
  144.8 26.2 %collective-permute-start.4 = (f32[128,128]{1,0:T(8,128)S(1)}, f32[128,128]{1,0:T(8,128)S(1)}, u32[]{:S(2)}, u32[]{:S(2)}) collective-permute-start(f32[128,128]{1,0:T(8,128)S(1)} %get-tuple-element.61), channel_id=1, source_target_pairs={{0,8},{1,9},{2,10},{3,11},{4,12},{5,13},{6,14},{7,15},{8,0},{9,1},... | collective-permute-start | bytes 196616 | tf_op jit(solution)/shard_map/ppermute | solution.py:198
  171.8 35.5 %all-to-all-start.5 = ((bf16[8,64,2048]{2,1,0:T(8,128)(2,1)}), bf16[8,64,2048]{2,1,0:T(8,128)(2,1)S(1)}, u32[]{:S(2)}, u32[]{:S(2)}) async-start(bf16[8,64,2048]{2,1,0:T(8,128)(2,1)} %bitcast.66), calls=%async_computation.5 | async-start | bytes 4194304 | tf_op jit(solution)/shard_map/all_to_all | solution.py:202
  175.7 31.6 %copy-start.15 = (bf16[128,2048]{1,0:T(8,128)(2,1)S(1)}, bf16[128,2048]{1,0:T(8,128)(2,1)}, u32[]{:S(2)}) copy-start(bf16[128,2048]{1,0:T(8,128)(2,1)} %block.1) | copy-start | bytes 1572868
  175.7 31.6 %copy-start.24 = (bf16[128,2048]{1,0:T(8,128)(2,1)S(1)}, bf16[128,2048]{1,0:T(8,128)(2,1)}, u32[]{:S(2)}) copy-start(bf16[128,2048]{1,0:T(8,128)(2,1)} %copy-done.23) | copy-start | bytes 1572868
  175.7 31.6 %collective-permute-start.5 = (bf16[128,2048]{1,0:T(8,128)(2,1)}, bf16[128,2048]{1,0:T(8,128)(2,1)}, u32[]{:S(2)}, u32[]{:S(2)}) collective-permute-start(bf16[128,2048]{1,0:T(8,128)(2,1)} %copy-done.25), channel_id=1, source_target_pairs={{0,8},{1,9},{2,10},{3,11},{4,12},{5,13},{6,14},{7,15},{8,0},{9,1},... | collective-permute-start | bytes 1572872 | tf_op jit(solution)/shard_map/ppermute | solution.py:198
  (14 other events, 19.3 us)
Sparse Core Ops, SparseCore 0:
  138.2 16.3 reduce-scatter.1

commit v10 on v8

--- a/solution.py
+++ b/solution.py
@@ -22,7 +22,7 @@
         out_shape=outs,
         in_specs=[SMEM] + [VMEM] * len(args),
         out_specs=[VMEM] * len(outs),
-        compiler_params=pltpu.CompilerParams(vmem_limit_bytes=16 * 1024 * 1024),
+        compiler_params=pltpu.CompilerParams(vmem_limit_bytes=6 * 1024 * 1024),
         cost_estimate=pl.CostEstimate(flops=flops, bytes_accessed=size, transcendentals=0),
     )(me, *args)
 
@@ -113,51 +113,80 @@
     mix(top, table, meta, block, back, out, grads)
 
 
-def last_kernel(
-    top, side, capacity, me_ref, meta, block, back, far, far_grads, far_dx, out, grads, dx
+def sum_last_kernel(top, side, capacity, me_ref, meta, back, far, out):
+    (table,) = slot_tables(me_ref[0], [meta], top, side, capacity)
+    held = functools.reduce(lambda p, q: p + q, table)
+    for c, e in strips(out.shape[1]):
+        out[:, c:e] = (picked_sum(held, back, c, e) + far[:, c:e].astype(F32)).astype(BF16)
+
+
+def mix_last_kernel(
+    top, side, capacity, me_ref, meta, block, back, far, far_grads, out, grads
 ):
-    tables = slot_tables(me_ref[0], [meta, meta], top, side, capacity)
-    mix(top, tables[0], meta, block, back, out, grads, far, far_grads)
-    held = functools.reduce(lambda p, q: p + q, tables[1])
-    for c, e in strips(dx.shape[1]):
-        dx[:, c:e] = (picked_sum(held, back, c, e) + far_dx[:, c:e].astype(F32)).astype(BF16)
-
-
-def dx_kernel(
-    side, d_own, d_far, gate_ref, up_ref, y_own, wg_ref, wu_ref, wd_ref, both, far, gg_ref, gu_ref
-):
-    half, feature = far.shape
-    units = gate_ref.shape[1]
+    (table,) = slot_tables(me_ref[0], [meta], top, side, capacity)
+    mix(top, table, meta, block, back, out, grads, far, far_grads)
+
+
+def fetch(sources, targets, sems):
+    copies = []
+    for n, (source, target) in enumerate(zip(sources, targets)):
+        copies.append(pltpu.make_async_copy(source, target, sems.at[n]))
+        copies[n].start()
+    return copies
+
+
+def dx_kernel(*refs):
+    sources, (own_out, far_out, gg_ref, gu_ref) = refs[:7], refs[7:11]
+    local, sems = refs[11:18], refs[18]
+    wd, d_own, gate, up, d_far, wg, wu = local
+    copies = fetch(sources, local, sems)
+    half, feature = d_own.shape
+    units = gate.shape[1]
     across_last = (((1,), (1,)), ((), ()))
-    for r, d_rows in ((0, d_own), (half, d_far)):
+    copies[0].wait()
+    for r, d_rows, needed in ((0, d_own, (1, 2, 3)), (half, d_far, (4,))):
         at = slice(r, r + half)
+        for n in needed:
+            copies[n].wait()
         for c, e in strips(units, 256):
             back = lax.dot_general(
-                d_rows[...], wd_ref[c:e, :], across_last, preferred_element_type=F32
+                d_rows[...], wd[c:e, :], across_last, preferred_element_type=F32
             )
-            gate = gate_ref[at, c:e]
-            sig = 1.0 / (1.0 + jnp.exp(-gate))
+            pre = gate[at, c:e]
+            sig = 1.0 / (1.0 + jnp.exp(-pre))
             gg_ref[at, c:e] = (
-                back * up_ref[at, c:e] * (sig * (1.0 + gate * (1.0 - sig)))
+                back * up[at, c:e] * (sig * (1.0 + pre * (1.0 - sig)))
             ).astype(BF16)
-            gu_ref[at, c:e] = (back * (gate * sig)).astype(BF16)
+            gu_ref[at, c:e] = (back * (pre * sig)).astype(BF16)
+    copies[5].wait()
+    copies[6].wait()
     for c, e in strips(feature):
-        got = jnp.dot(gg_ref[...], wg_ref[:, c:e], preferred_element_type=F32)
-        got += jnp.dot(gu_ref[...], wu_ref[:, c:e], preferred_element_type=F32)
-        far[:, c:e] = got[half:].astype(BF16)
-        pair = [
-            part.reshape(side, 1, half // side, e - c)
-            for part in (y_own[:, c:e].astype(F32), got[:half])
-        ]
-        both[:, c:e] = jnp.concatenate(pair, 1).reshape(2 * half, e - c).astype(BF16)
-
-
-def terms_kernel(gg, gu, hidden, x_own, x_far, d_own, d_far, out):
+        got = jnp.dot(gg_ref[...], wg[:, c:e], preferred_element_type=F32)
+        got += jnp.dot(gu_ref[...], wu[:, c:e], preferred_element_type=F32)
+        own_out[:, c:e] = got[:half].astype(BF16)
+        far_out[:, c:e] = got[half:].astype(BF16)
+
+
+def terms_kernel(*refs):
+    sources, out, local = refs[:7], refs[7], refs[8:15]
+    sems, tiles, tile_sems = refs[15:]
+    x_own, x_far, gg, gu, d_own, d_far, hidden = local
+    loads = fetch(sources, local, sems)
     half, feature = x_own.shape
     units = gg.shape[1]
-    pairs = ((gg, x_own, x_far), (gu, x_own, x_far), (hidden, d_own, d_far))
-    for n, (left, own, far) in enumerate(pairs):
-        for r, t in strips(units, 256):
+    pairs = (
+        (gg, x_own, x_far, (0, 1, 2)),
+        (gu, x_own, x_far, (3,)),
+        (hidden, d_own, d_far, (4, 5, 6)),
+    )
+    copies = []
+    for n, (left, own, far, needed) in enumerate(pairs):
+        for m in needed:
+            loads[m].wait()
+        for r, t in strips(units, tiles.shape[1]):
+            slot = len(copies) % 2
+            if len(copies) > 1:
+                copies[-2].wait()
             for c, e in strips(feature, 1024):
                 got = lax.dot_general(
                     left[:half, r:t], own[:, c:e], TRANSPOSED, preferred_element_type=F32
@@ -165,7 +194,32 @@
                 got += lax.dot_general(
                     left[half:, r:t], far[:, c:e], TRANSPOSED, preferred_element_type=F32
                 )
-                out[n * units + r : n * units + t, c:e] = got.astype(BF16)
+                tiles[slot, : t - r, c:e] = got.astype(BF16)
+            copy = pltpu.make_async_copy(
+                tiles.at[slot, pl.ds(0, t - r)],
+                out.at[pl.ds(n * units + r, t - r)],
+                tile_sems.at[slot],
+            )
+            copy.start()
+            copies.append(copy)
+    for copy in copies[-2:]:
+        copy.wait()
+
+
+def streamed_call(kernel, outs, args, out_space, scratch, limit):
+    return pl.pallas_call(
+        kernel,
+        out_shape=outs,
+        in_specs=[pl.BlockSpec(memory_space=pl.ANY)] * len(args),
+        out_specs=[pl.BlockSpec(memory_space=out_space)] * len(outs),
+        scratch_shapes=[
+            *[pltpu.VMEM(x.shape, x.dtype) for x in args],
+            pltpu.SemaphoreType.DMA((len(args),)),
+            *scratch,
+        ],
+        compiler_params=pltpu.CompilerParams(vmem_limit_bytes=limit * 1024 * 1024),
+        cost_estimate=pl.CostEstimate(flops=1, bytes_accessed=1, transcendentals=0),
+    )(*args)
 
 
 def on_device(tokens, expert_ids, gate_prob, w_gate, w_up, w_down, d_mixed):
@@ -214,14 +268,14 @@
     own = exchange(pick([meta, meta], [tokens, d_mixed], (False, True)))
     own = own.reshape(side, 2, capacity, feature)
     x_far, meta_far = after(across(tokens), across(meta))
-    d_late, x_far = after(d_mixed, x_far)
-    d_far = across(d_late)
-    x_far, own = after(x_far, own)
+    x_far, d_far, own = after(x_far, across(d_mixed), own)
     x_own, d_own = (own[:, n].reshape(half, feature) for n in range(2))
     x_far_rows = exchange(pick([meta_far], [x_far], (False,)))
     x_rows = jnp.concatenate([x_own, x_far_rows], 0)
-    x_far_rows, d_far = after(x_far_rows, d_far)
-    d_far_rows = exchange(pick([meta_far], [d_far], (True,)))
+    d_picked, x_own, d_own, _ = after(
+        pick([meta_far], [d_far], (True,)), x_own, d_own, x_far_rows
+    )
+    d_far_rows = exchange(d_picked)
 
     gate_matrix, up_matrix, down_matrix = w_gate[0], w_up[0], w_down[0]
     hidden_units = gate_matrix.shape[1]
@@ -235,50 +289,54 @@
     y_far, y_own, d_far_rows = after(y_far, y_own, d_far_rows)
     y_far_back = exchange(y_far)
 
-    n_rows = 2 * half
-    rows, units = shape((half, feature), BF16), shape((n_rows, hidden_units), BF16)
-    both, dx_far, gg, gu = pl.pallas_call(
-        functools.partial(dx_kernel, side),
-        out_shape=[shape((n_rows, feature), BF16), rows, units, units],
-        in_specs=[VMEM] * 8,
-        out_specs=[VMEM] * 4,
-        compiler_params=pltpu.CompilerParams(vmem_limit_bytes=32 * 1024 * 1024),
-        cost_estimate=pl.CostEstimate(flops=1, bytes_accessed=1, transcendentals=0),
-    )(d_own, d_far_rows, gate_pre, up_pre, y_own, gate_matrix.T, up_matrix.T, down_matrix)
-    (terms,) = pl.pallas_call(
-        terms_kernel,
-        out_shape=[shape((3 * hidden_units, feature), BF16)],
-        in_specs=[VMEM] * 7,
-        out_specs=[VMEM],
-        compiler_params=pltpu.CompilerParams(vmem_limit_bytes=32 * 1024 * 1024),
-        cost_estimate=pl.CostEstimate(flops=1, bytes_accessed=1, transcendentals=0),
-    )(gg, gu, hidden, x_own, x_far_rows, d_own, d_far_rows)
-    dx_far, both, terms, y_far_back = after(dx_far, both, terms, y_far_back)
+    rows, units = shape((half, feature), BF16), shape((2 * half, hidden_units), BF16)
+    dx_own, dx_far, gg, gu = streamed_call(
+        dx_kernel,
+        [rows, rows, units, units],
+        [down_matrix, d_own, gate_pre, up_pre, d_far_rows, gate_matrix.T, up_matrix.T],
+        pltpu.VMEM,
+        [],
+        24,
+    )
+    dx_own, dx_far, gg, gu, y_far_back = after(dx_own, dx_far, gg, gu, y_far_back)
 
     token_rows, grad_rows = ((tok, feature), BF16), ((tok, LANES), F32)
     work = 2 * half * tok * feature
     mixed_far, grads_far = call(
         mix_kernel, [token_rows, grad_rows], [meta_far, d_far, y_far_back], top * work
     )
-    dx_far, mixed_far, grads_far = after(dx_far, mixed_far, grads_far)
-    far_back = exchange(dx_far)
-    (tokens_far,) = call(sum_kernel, [token_rows], [meta_far, far_back], work)
+    y_own, gg, gu, mixed_far, grads_far = after(y_own, gg, gu, mixed_far, grads_far)
+    y_own_back = exchange(y_own)
+    (terms,) = streamed_call(
+        terms_kernel,
+        [shape((3 * hidden_units, feature), BF16)],
+        [x_own, x_far_rows, gg, gu, d_own, d_far_rows, hidden],
+        pltpu.HBM,
+        [pltpu.VMEM((2, 256, feature), BF16), pltpu.SemaphoreType.DMA((2,))],
+        16,
+    )
+    dx_far, dx_own, terms, y_own_back, mixed_far, grads_far = after(
+        dx_far, dx_own, terms, y_own_back, across(mixed_far), across(grads_far)
+    )
     summed = lax.psum_scatter(terms, "dp", scatter_dimension=1, tiled=True)
-    tokens_far, both, mixed_far, grads_far = after(
-        tokens_far, both, across(mixed_far), across(grads_far)
-    )
-    own_back = exchange(both)
+    dx_far_back = exchange(dx_far)
+    (tokens_far,) = call(sum_kernel, [token_rows], [meta_far, dx_far_back], work)
+    tokens_far, dx_own = after(tokens_far, dx_own)
+    dx_own_back = exchange(dx_own)
+    mixed, grads = call(
+        mix_last_kernel,
+        [token_rows, grad_rows],
+        [meta, d_mixed, y_own_back, mixed_far, grads_far],
+        top * work,
+    )
     weight_grads = (
         summed[:hidden_units].astype(F32).T[None],
         summed[hidden_units : 2 * hidden_units].astype(F32).T[None],
         summed[2 * hidden_units :].astype(F32)[None],
     )
-    own_back, *weight_grads = after(own_back, *weight_grads)
-    mixed, grads, d_tokens = call(
-        last_kernel,
-        [token_rows, grad_rows, token_rows],
-        [meta, d_mixed, own_back, mixed_far, grads_far, across(tokens_far)],
-        (top + 1) * 2 * work,
+    dx_own_back, mixed, grads, *weight_grads = after(dx_own_back, mixed, grads, *weight_grads)
+    (d_tokens,) = call(
+        sum_last_kernel, [token_rows], [meta, dx_own_back, across(tokens_far)], work
     )
     return (mixed, d_tokens, grads[:, :top], *weight_grads)
 

time: 219 us -> 219 us (level)
  waiting for transfers between devices: 104 us -> 74.1 us
  blocking collectives: 0 us -> 16.1 us
  local copies, waits for them, and re-layouts: 21.2 us -> 29.7 us
  Pallas kernels: 21.2 us -> 26.7 us
  starting transfers between devices: 41.2 us -> 38.9 us
  matrix products: 8.77 us -> 11 us
    all_to_all x6, waiting for transfers between devices: 47.3 us -> 24 us  [exchange(): lax.all_to_all(shaped, 'expert', 0, 0, axis_index_groups=sets, tiled=True)]
    all_to_all x0 -> x1, blocking collectives: none -> 16.1 us  [exchange(): lax.all_to_all(shaped, 'expert', 0, 0, axis_index_groups=sets, tiled=True)]
    unnamed x53 -> x61, local copies, waits for them, and re-layouts: 19.3 us -> 27 us
    ppermute x6, waiting for transfers between devices: 56.6 us -> 50 us  [across(): lax.ppermute(value, 'expert', [(e, (e + side) % experts) for e in range(e...]
    pallas_call x2, Pallas kernels: 11.3 us -> 14.4 us  [streamed_call(): pl.pallas_call(kernel, out_shape=outs, in_specs=[pl.BlockSpec(memory_spac...]
    pallas_call x6 -> x7, Pallas kernels: 9.89 us -> 12.3 us  [local_call(): pl.pallas_call(kernel, out_shape=outs, in_specs=[SMEM] + [VMEM] * len(arg...]
    dot_general x1, matrix products: 1.84 us -> 4.11 us  [on_device(): gate_pre = jnp.dot(x_rows, gate_matrix, preferred_element_type=F32)]
  transfers between devices with their start and end apart: 13 -> 13, of which waited for: 7 -> 7; matrix products, arithmetic and copies ran while one was open for 8% -> 9% of each run, Pallas kernels for 6% -> 9%
where the time goes in v10:
time: 219 us; the launch traced here: 218 us
  waiting for transfers between devices  74.1 us (34%)
  starting transfers between devices  38.9 us (18%)
  local copies, waits for them, and re-layouts  29.7 us (14%)
  Pallas kernels  26.7 us (12%)
  blocking collectives  16.1 us (7%)
  between operations  14.2 us (6%)
  matrix products  11 us (5%)
  other arithmetic  7.44 us (3%)
    ppermute x6, waiting for transfers between devices, across(): lax.ppermute(value, 'expert', [(e, (e + side) % experts) for e in range(e...  50 us
    all_to_all x6, starting transfers between devices, exchange(): lax.all_to_all(shaped, 'expert', 0, 0, axis_index_groups=sets, tiled=True)  30.2 us
    unnamed x61, local copies, waits for them, and re-layouts  27 us
    all_to_all x6, waiting for transfers between devices, exchange(): lax.all_to_all(shaped, 'expert', 0, 0, axis_index_groups=sets, tiled=True)  24 us
    all_to_all x1, blocking collectives, exchange(): lax.all_to_all(shaped, 'expert', 0, 0, axis_index_groups=sets, tiled=True)  16.1 us
    pallas_call x2, Pallas kernels, streamed_call(): pl.pallas_call(kernel, out_shape=outs, in_specs=[pl.BlockSpec(memory_spac...  14.4 us
    pallas_call x7, Pallas kernels, local_call(): pl.pallas_call(kernel, out_shape=outs, in_specs=[SMEM] + [VMEM] * len(arg...  12.3 us
    ppermute x6, starting transfers between devices, across(): lax.ppermute(value, 'expert', [(e, (e + side) % experts) for e in range(e...  8.63 us
  transfers between devices with their start and end apart: 13, of which 7 were waited for; matrix products, arithmetic and copies ran while one was open for 9% of the time, Pallas kernels for 9%

profile of v10, /device:TPU:0, one launch (start us, length us, event | category | flops | bytes accessed | tf_op | source)
XLA Modules:
  0.0 218.1 jit_solution(8249986948996448787)
XLA Ops:
  12.8 6.3 %all-to-all-start = ((bf16[8,64,2048]{2,1,0:T(8,128)(2,1)}), bf16[8,64,2048]{2,1,0:T(8,128)(2,1)}, u32[]{:S(2)}, u32[]{:S(2)}) async-start(bf16[8,64,2048]{2,1,0:T(8,128)(2,1)} %bitcast.4), calls=%async_computation | async-start | bytes 4194304 | tf_op jit(solution)/shard_map/all_to_all | solution.py:242
  19.1 2.7 %collective-permute-start = (bf16[128,2048]{1,0:T(8,128)(2,1)S(1)}, bf16[128,2048]{1,0:T(8,128)(2,1)S(1)}, u32[]{:S(2)}, u32[]{:S(2)}) collective-permute-start(bf16[128,2048]{1,0:T(8,128)(2,1)S(1)} %copy-done.28), channel_id=1, source_target_pairs={{0,8},{1,9},{2,10},{3,11},{4,12},{5,13},{6,14},{7,15},{8,0},{9,1},... | collective-permute-start | bytes 1572872 | tf_op jit(solution)/shard_map/ppermute | solution.py:238
  22.1 2.6 %collective-permute-start.1 = (f32[4,128]{1,0:T(4,128)S(1)}, f32[4,128]{1,0:T(4,128)S(1)}, u32[]{:S(2)}, u32[]{:S(2)}) collective-permute-start(f32[4,128]{1,0:T(4,128)S(1)} %pad_maximum_fusion.3.refs_0_.refs_1_.meta), channel_id=1, source_target_pairs={{0,8},{1,9},{2,10},{3,11},{4,12},{5,13},{6,14},{7,15},{8,0},{9,1},... | collective-permute-start | bytes 6152 | tf_op jit(solution)/shard_map/ppermute | solution.py:238
  24.7 39.7 %collective-permute-done.1.refs_0_.meta = f32[4,128]{1,0:T(4,128)S(1)} collective-permute-done((f32[4,128]{1,0:T(4,128)S(1)}, f32[4,128]{1,0:T(4,128)S(1)}, u32[]{:S(2)}, u32[]{:S(2)}) %collective-permute-start.1) | collective-permute-done | bytes 2080 | tf_op jit(solution)/shard_map/ppermute | solution.py:238
  68.1 8.2 %all-to-all-start.1 = ((bf16[8,32,2048]{2,1,0:T(8,128)(2,1)}), bf16[8,32,2048]{2,1,0:T(8,128)(2,1)S(1)}, u32[]{:S(2)}, u32[]{:S(2)}) async-start(bf16[8,32,2048]{2,1,0:T(8,128)(2,1)} %bitcast.8), calls=%async_computation.1 | async-start | bytes 2097152 | tf_op jit(solution)/shard_map/all_to_all | solution.py:242
  77.8 2.7 %fusion.11 = (bf16[8,1,32,2048]{3,2,1,0:T(8,128)(2,1)S(1)}, bf16[8,1,32,2048]{3,2,1,0:T(8,128)(2,1)}) fusion(bf16[8,2,32,2048]{3,2,1,0:T(8,128)(2,1)} %bitcast.5), kind=kLoop, calls=%fused_computation.20 | loop fusion | bytes 4194304 | tf_op jit(solution)/shard_map/slice | solution.py:272
  80.5 9.4 %all-to-all-done.1 = bf16[8,32,2048]{2,1,0:T(8,128)(2,1)S(1)} async-done(((bf16[8,32,2048]{2,1,0:T(8,128)(2,1)}), bf16[8,32,2048]{2,1,0:T(8,128)(2,1)S(1)}, u32[]{:S(2)}, u32[]{:S(2)}) %all-to-all-start.1) | async-done | bytes 1048608 | tf_op jit(solution)/shard_map/all_to_all | solution.py:242
  89.9 3.6 %all-to-all-start.2 = ((bf16[8,32,2048]{2,1,0:T(8,128)(2,1)}), bf16[8,32,2048]{2,1,0:T(8,128)(2,1)S(1)}, u32[]{:S(2)}, u32[]{:S(2)}) async-start(bf16[8,32,2048]{2,1,0:T(8,128)(2,1)} %bitcast.12), calls=%async_computation.2 | async-start | bytes 2097152 | tf_op jit(solution)/shard_map/all_to_all | solution.py:242
  93.4 4.1 %fusion.2.refs_2_ = f32[512,704]{1,0:T(8,128)S(1)} fusion(bf16[1,2048,704]{1,2,0:T(8,128)(2,1)} %param.10, bf16[256,2048]{1,0:T(8,128)(2,1)S(1)} %bitcast.59, bf16[256,2048]{1,0:T(8,128)(2,1)} %bitcast.62), kind=kOutput, calls=%fused_computation.2 | convolution fusion | flops 1480589312 | bytes 6422528 | tf_op jit(solution)/shard_map/dot_general | solution.py:282
  97.6 3.0 %multiply_convert_fusion = (bf16[512,704]{1,0:T(8,128)(2,1)S(1)}, f32[512,704]{1,0:T(8,128)}) fusion(f32[512,704]{1,0:T(8,128)S(1)} %fusion.2.refs_2_, bf16[1,2048,704]{1,2,0:T(8,128)(2,1)S(1)} %copy-done.6, bf16[256,2048]{1,0:T(8,128)(2,1)S(1)} %bitcast.60, bf16[256,2048]{1,0:T(8,128)(2,1)S(1)} %bitcast.63), kind=kOutput, calls=%fused_computation.9 | convolution fusion | flops 1482752000 | bytes 8585216 | tf_op jit(solution)/shard_map/dot_general | solution.py:283
  104.5 2.7 %all-to-all-done.2 = bf16[8,32,2048]{2,1,0:T(8,128)(2,1)S(1)} async-done(((bf16[8,32,2048]{2,1,0:T(8,128)(2,1)}), bf16[8,32,2048]{2,1,0:T(8,128)(2,1)S(1)}, u32[]{:S(2)}, u32[]{:S(2)}) %all-to-all-start.2) | async-done | bytes 1048608 | tf_op jit(solution)/shard_map/all_to_all | solution.py:242
  107.3 3.7 %all-to-all-start.3 = ((bf16[8,32,2048]{2,1,0:T(8,128)(2,1)}), bf16[8,32,2048]{2,1,0:T(8,128)(2,1)S(1)}, u32[]{:S(2)}, u32[]{:S(2)}) async-start(bf16[8,32,2048]{2,1,0:T(8,128)(2,1)} %bitcast.72), calls=%async_computation.3 | async-start | bytes 2097152 | tf_op jit(solution)/shard_map/all_to_all | solution.py:242
  119.3 7.0 %shard_map.121 = (bf16[256,2048]{1,0:T(8,128)(2,1)S(1)}, bf16[256,2048]{1,0:T(8,128)(2,1)S(1)}, bf16[512,704]{1,0:T(8,128)(2,1)S(1)}, bf16[512,704]{1,0:T(8,128)(2,1)S(1)}) custom-call(bf16[704,2048]{1,0:T(8,128)(2,1)S(1)} %bitcast.67, bf16[256,2048]{1,0:T(8,128)(2,1)S(1)} %bitcast.53, f32[512,704]{1,0:T(8,128)S(1)} %copy-done.16, ...), custom_call_target="tpu_custom_call" | custom-call | flops 1 | bytes 1 | tf_op jit(solution)/shard_map/pallas_call | solution.py:210
  132.7 4.9 %all-to-all-start.4 = ((bf16[8,32,2048]{2,1,0:T(8,128)(2,1)}), bf16[8,32,2048]{2,1,0:T(8,128)(2,1)S(1)}, u32[]{:S(2)}, u32[]{:S(2)}) async-start(bf16[8,32,2048]{2,1,0:T(8,128)(2,1)} %bitcast.71), calls=%async_computation.4 | async-start | bytes 2097152 | tf_op jit(solution)/shard_map/all_to_all | solution.py:242
  137.7 2.9 %collective-permute-start.4 = (f32[128,128]{1,0:T(8,128)S(1)}, f32[128,128]{1,0:T(8,128)S(1)}, u32[]{:S(2)}, u32[]{:S(2)}) collective-permute-start(f32[128,128]{1,0:T(8,128)S(1)} %get-tuple-element.75), channel_id=1, source_target_pairs={{0,8},{1,9},{2,10},{3,11},{4,12},{5,13},{6,14},{7,15},{8,0},{9,1},... | collective-permute-start | bytes 196616 | tf_op jit(solution)/shard_map/ppermute | solution.py:238
  146.4 7.4 %shard_map.123 = bf16[2112,2048]{1,0:T(8,128)(2,1)S(1)} custom-call(bf16[256,2048]{1,0:T(8,128)(2,1)S(1)} %bitcast.64, bf16[256,2048]{1,0:T(8,128)(2,1)S(1)} %bitcast.61, bf16[512,704]{1,0:T(8,128)(2,1)S(1)} %copy-done.24, bf16[512,704]{1,0:T(8,128)(2,1)S(1)} %copy-done.26, bf16[256,2048]{1,0:T(8,128)(2,1)S(1)} %bitcast.54, bf16[256,2048]{1,0:T(8,128)(2,1)S(1)} %bitcast.52, ...), custom_call_target="tpu_custom_call" | custom-call | flops 1 | bytes 1 | tf_op jit(solution)/shard_map/pallas_call | solution.py:210
  153.8 3.4 %copy-done = bf16[2112,2048]{1,0:T(8,128)(2,1)} copy-done((bf16[2112,2048]{1,0:T(8,128)(2,1)}, bf16[2112,2048]{1,0:T(8,128)(2,1)S(1)}, u32[]{:S(2)}) %copy-start) | copy-done | bytes 8650776
  157.2 7.7 %collective-permute-done.4.far_grads = f32[128,128]{1,0:T(8,128)S(1)} collective-permute-done((f32[128,128]{1,0:T(8,128)S(1)}, f32[128,128]{1,0:T(8,128)S(1)}, u32[]{:S(2)}, u32[]{:S(2)}) %collective-permute-start.4) | collective-permute-done | bytes 65568 | tf_op jit(solution)/shard_map/ppermute | solution.py:238
  166.1 16.1 %all_to_all.35 = bf16[8,32,2048]{2,1,0:T(8,128)(2,1)S(1)} all-to-all(bf16[8,32,2048]{2,1,0:T(8,128)(2,1)S(1)} %bitcast.69), channel_id=1, replica_groups={{0,1,2,3,4,5,6,7},{8,9,10,11,12,13,14,15},{16,17,18,19,20,21,22,23},{24..., dimensions={0} | all-to-all | bytes 2097152 | tf_op jit(solution)/shard_map/all_to_all | solution.py:242
  183.4 3.6 %all-to-all-start.6 = ((bf16[8,32,2048]{2,1,0:T(8,128)(2,1)}), bf16[8,32,2048]{2,1,0:T(8,128)(2,1)S(1)}, u32[]{:S(2)}, u32[]{:S(2)}) async-start(bf16[8,32,2048]{2,1,0:T(8,128)(2,1)} %bitcast.68), calls=%async_computation.6 | async-start | bytes 2097152 | tf_op jit(solution)/shard_map/all_to_all | solution.py:242
  187.1 2.6 %shard_map.125 = (bf16[128,2048]{1,0:T(8,128)(2,1)}, f32[128,128]{1,0:T(8,128)S(1)}) custom-call(s32[1]{0:T(128)} %bitcast.me_ref, f32[4,128]{1,0:T(4,128)S(1)} %pad_maximum_fusion.3.refs_0_.refs_1_.meta, bf16[128,2048]{1,0:T(8,128)(2,1)S(1)} %copy-done.14, bf16[256,2048]{1,0:T(8,128)(2,1)S(1)} %bitcast.55, bf16[128,2048]{1,0:T(8,128)(2,1)} %collective-permute-done.3.far, ...), custom_call_target="tpu_custom_call" | custom-call | flops 268435456 | bytes 2754560 | tf_op jit(solution)/shard_map/pallas_call | solution.py:20
  189.7 6.1 %fusion.4 = (f32[1,704,1024]{2,1,0:T(8,128)}, f32[1,1024,704]{1,2,0:T(8,128)}, f32[1,1024,704]{1,2,0:T(8,128)}) fusion(bf16[2112,1024]{1,0:T(8,128)(2,1)} %reduce-scatter.2.cloned.1.call-done), kind=kLoop, calls=%fused_computation.11 | loop fusion | flops 2162688 | bytes 12976128 | tf_op jit(solution)/shard_map/broadcast_in_dim | solution.py:335
  195.8 9.8 %all-to-all-done.6 = bf16[8,32,2048]{2,1,0:T(8,128)(2,1)S(1)} async-done(((bf16[8,32,2048]{2,1,0:T(8,128)(2,1)}), bf16[8,32,2048]{2,1,0:T(8,128)(2,1)S(1)}, u32[]{:S(2)}, u32[]{:S(2)}) %all-to-all-start.6) | async-done | bytes 1048608 | tf_op jit(solution)/shard_map/all_to_all | solution.py:242
  206.3 2.6 %collective-permute-done.5.far = bf16[128,2048]{1,0:T(8,128)(2,1)} collective-permute-done((bf16[128,2048]{1,0:T(8,128)(2,1)}, bf16[128,2048]{1,0:T(8,128)(2,1)}, u32[]{:S(2)}, u32[]{:S(2)}) %collective-permute-start.5) | collective-permute-done | bytes 524320 | tf_op jit(solution)/shard_map/ppermute | solution.py:238
  (82 shorter events, 41.2 us)
Async XLA Ops:
  12.8 6.3 %copy-start.28 = (bf16[128,2048]{1,0:T(8,128)(2,1)S(1)}, bf16[128,2048]{1,0:T(8,128)(2,1)}, u32[]{:S(2)}) copy-start(bf16[128,2048]{1,0:T(8,128)(2,1)} %refs_2_.1) | copy-start | bytes 1572868
  12.8 9.0 %copy-start.13 = (bf16[128,2048]{1,0:T(8,128)(2,1)S(1)}, bf16[128,2048]{1,0:T(8,128)(2,1)}, u32[]{:S(2)}) copy-start(bf16[128,2048]{1,0:T(8,128)(2,1)} %block.1) | copy-start | bytes 1572868
  12.8 53.8 %all-to-all-start = ((bf16[8,64,2048]{2,1,0:T(8,128)(2,1)}), bf16[8,64,2048]{2,1,0:T(8,128)(2,1)}, u32[]{:S(2)}, u32[]{:S(2)}) async-start(bf16[8,64,2048]{2,1,0:T(8,128)(2,1)} %bitcast.4), calls=%async_computation | async-start | bytes 4194304 | tf_op jit(solution)/shard_map/all_to_all | solution.py:242
  19.1 45.3 %collective-permute-start = (bf16[128,2048]{1,0:T(8,128)(2,1)S(1)}, bf16[128,2048]{1,0:T(8,128)(2,1)S(1)}, u32[]{:S(2)}, u32[]{:S(2)}) collective-permute-start(bf16[128,2048]{1,0:T(8,128)(2,1)S(1)} %copy-done.28), channel_id=1, source_target_pairs={{0,8},{1,9},{2,10},{3,11},{4,12},{5,13},{6,14},{7,15},{8,0},{9,1},... | collective-permute-start | bytes 1572872 | tf_op jit(solution)/shard_map/ppermute | solution.py:238
  21.8 42.7 %collective-permute-start.2 = (bf16[128,2048]{1,0:T(8,128)(2,1)S(1)}, bf16[128,2048]{1,0:T(8,128)(2,1)S(1)}, u32[]{:S(2)}, u32[]{:S(2)}) collective-permute-start(bf16[128,2048]{1,0:T(8,128)(2,1)S(1)} %copy-done.13), channel_id=1, source_target_pairs={{0,8},{1,9},{2,10},{3,11},{4,12},{5,13},{6,14},{7,15},{8,0},{9,1},... | collective-permute-start | bytes 1572872 | tf_op jit(solution)/shard_map/ppermute | solution.py:238
  22.1 42.3 %collective-permute-start.1 = (f32[4,128]{1,0:T(4,128)S(1)}, f32[4,128]{1,0:T(4,128)S(1)}, u32[]{:S(2)}, u32[]{:S(2)}) collective-permute-start(f32[4,128]{1,0:T(4,128)S(1)} %pad_maximum_fusion.3.refs_0_.refs_1_.meta), channel_id=1, source_target_pairs={{0,8},{1,9},{2,10},{3,11},{4,12},{5,13},{6,14},{7,15},{8,0},{9,1},... | collective-permute-start | bytes 6152 | tf_op jit(solution)/shard_map/ppermute | solution.py:238
  64.5 11.8 %copy-start.10 = (bf16[128,2048]{1,0:T(8,128)(2,1)}, bf16[128,2048]{1,0:T(8,128)(2,1)S(1)}, u32[]{:S(2)}) copy-start(bf16[128,2048]{1,0:T(8,128)(2,1)S(1)} %collective-permute-done.2.refs_1_.block) | copy-start | bytes 1572868
  68.1 21.8 %all-to-all-start.1 = ((bf16[8,32,2048]{2,1,0:T(8,128)(2,1)}), bf16[8,32,2048]{2,1,0:T(8,128)(2,1)S(1)}, u32[]{:S(2)}, u32[]{:S(2)}) async-start(bf16[8,32,2048]{2,1,0:T(8,128)(2,1)} %bitcast.8), calls=%async_computation.1 | async-start | bytes 2097152 | tf_op jit(solution)/shard_map/all_to_all | solution.py:242
  89.9 7.7 %copy-start.1 = (bf16[8,32,2048]{2,1,0:T(8,128)(2,1)}, bf16[8,32,2048]{2,1,0:T(8,128)(2,1)S(1)}, u32[]{:S(2)}) copy-start(bf16[8,32,2048]{2,1,0:T(8,128)(2,1)S(1)} %all-to-all-done.1) | copy-start | bytes 3145732
  89.9 17.4 %all-to-all-start.2 = ((bf16[8,32,2048]{2,1,0:T(8,128)(2,1)}), bf16[8,32,2048]{2,1,0:T(8,128)(2,1)S(1)}, u32[]{:S(2)}, u32[]{:S(2)}) async-start(bf16[8,32,2048]{2,1,0:T(8,128)(2,1)} %bitcast.12), calls=%async_computation.2 | async-start | bytes 2097152 | tf_op jit(solution)/shard_map/all_to_all | solution.py:242
  93.4 4.2 %copy-start.3 = (bf16[8,1,32,2048]{3,2,1,0:T(8,128)(2,1)S(1)}, bf16[8,1,32,2048]{3,2,1,0:T(8,128)(2,1)}, u32[]{:S(2)}) copy-start(bf16[8,1,32,2048]{3,2,1,0:T(8,128)(2,1)} %get-tuple-element.114) | copy-start | bytes 3145732
  93.4 4.2 %copy-start.6 = (bf16[1,2048,704]{1,2,0:T(8,128)(2,1)S(1)}, bf16[1,2048,704]{1,2,0:T(8,128)(2,1)}, u32[]{:S(2)}) copy-start(bf16[1,2048,704]{1,2,0:T(8,128)(2,1)} %param.11) | copy-start | bytes 8650756
  97.6 3.0 %copy-start.15 = (f32[512,704]{1,0:T(8,128)}, f32[512,704]{1,0:T(8,128)S(1)}, u32[]{:S(2)}) copy-start(f32[512,704]{1,0:T(8,128)S(1)} %fusion.2.refs_2_) | copy-start | bytes 4325380
  97.6 3.0 %copy-start.8 = (bf16[1,704,2048]{2,1,0:T(8,128)(2,1)S(1)}, bf16[1,704,2048]{2,1,0:T(8,128)(2,1)}, u32[]{:S(2)}) copy-start(bf16[1,704,2048]{2,1,0:T(8,128)(2,1)} %param.12) | copy-start | bytes 8650756
  100.6 2.0 copy-start.21
  107.3 22.8 %all-to-all-start.3 = ((bf16[8,32,2048]{2,1,0:T(8,128)(2,1)}), bf16[8,32,2048]{2,1,0:T(8,128)(2,1)S(1)}, u32[]{:S(2)}, u32[]{:S(2)}) async-start(bf16[8,32,2048]{2,1,0:T(8,128)(2,1)} %bitcast.72), calls=%async_computation.3 | async-start | bytes 2097152 | tf_op jit(solution)/shard_map/all_to_all | solution.py:242
  132.7 32.2 %all-to-all-start.4 = ((bf16[8,32,2048]{2,1,0:T(8,128)(2,1)}), bf16[8,32,2048]{2,1,0:T(8,128)(2,1)S(1)}, u32[]{:S(2)}, u32[]{:S(2)}) async-start(bf16[8,32,2048]{2,1,0:T(8,128)(2,1)} %bitcast.71), calls=%async_computation.4 | async-start | bytes 2097152 | tf_op jit(solution)/shard_map/all_to_all | solution.py:242
  137.5 52.2 %reduce-scatter.2.cloned.1.call-start = ((), (), s32[]{:S(2)}) async-start(), calls=%async_computation.8 | async-start | bytes 12976128 | tf_op jit(solution)/shard_map/reduce_scatter | solution.py:321
  137.6 27.3 %collective-permute-start.3 = (bf16[128,2048]{1,0:T(8,128)(2,1)}, bf16[128,2048]{1,0:T(8,128)(2,1)}, u32[]{:S(2)}, u32[]{:S(2)}) collective-permute-start(bf16[128,2048]{1,0:T(8,128)(2,1)} %copy-done.29), channel_id=1, source_target_pairs={{0,8},{1,9},{2,10},{3,11},{4,12},{5,13},{6,14},{7,15},{8,0},{9,1},... | collective-permute-start | bytes 1572872 | tf_op jit(solution)/shard_map/ppermute | solution.py:238
  137.7 27.2 %collective-permute-start.4 = (f32[128,128]{1,0:T(8,128)S(1)}, f32[128,128]{1,0:T(8,128)S(1)}, u32[]{:S(2)}, u32[]{:S(2)}) collective-permute-start(f32[128,128]{1,0:T(8,128)S(1)} %get-tuple-element.75), channel_id=1, source_target_pairs={{0,8},{1,9},{2,10},{3,11},{4,12},{5,13},{6,14},{7,15},{8,0},{9,1},... | collective-permute-start | bytes 196616 | tf_op jit(solution)/shard_map/ppermute | solution.py:238
  153.8 3.4 %copy-start = (bf16[2112,2048]{1,0:T(8,128)(2,1)}, bf16[2112,2048]{1,0:T(8,128)(2,1)S(1)}, u32[]{:S(2)}) copy-start(bf16[2112,2048]{1,0:T(8,128)(2,1)S(1)} %shard_map.123) | copy-start | bytes 25952260
  166.1 21.0 %copy-start.14 = (bf16[128,2048]{1,0:T(8,128)(2,1)S(1)}, bf16[128,2048]{1,0:T(8,128)(2,1)}, u32[]{:S(2)}) copy-start(bf16[128,2048]{1,0:T(8,128)(2,1)} %block.1) | copy-start | bytes 1572868
  183.4 22.2 %all-to-all-start.6 = ((bf16[8,32,2048]{2,1,0:T(8,128)(2,1)}), bf16[8,32,2048]{2,1,0:T(8,128)(2,1)S(1)}, u32[]{:S(2)}, u32[]{:S(2)}) async-start(bf16[8,32,2048]{2,1,0:T(8,128)(2,1)} %bitcast.68), calls=%async_computation.6 | async-start | bytes 2097152 | tf_op jit(solution)/shard_map/all_to_all | solution.py:242
  187.0 21.9 %collective-permute-start.5 = (bf16[128,2048]{1,0:T(8,128)(2,1)}, bf16[128,2048]{1,0:T(8,128)(2,1)}, u32[]{:S(2)}, u32[]{:S(2)}) collective-permute-start(bf16[128,2048]{1,0:T(8,128)(2,1)} %shard_map.124), channel_id=1, source_target_pairs={{0,8},{1,9},{2,10},{3,11},{4,12},{5,13},{6,14},{7,15},{8,0},{9,1},... | collective-permute-start | bytes 1572872 | tf_op jit(solution)/shard_map/ppermute | solution.py:238
  (19 other events, 23.0 us)
Sparse Core Ops, SparseCore 0:
  165.0 15.9 reduce-scatter.1

commit v11 on v10

--- a/solution.py
+++ b/solution.py
@@ -135,50 +135,40 @@
     return copies
 
 
-def dx_kernel(*refs):
-    sources, (own_out, far_out, gg_ref, gu_ref) = refs[:7], refs[7:11]
-    local, sems = refs[11:18], refs[18]
-    wd, d_own, gate, up, d_far, wg, wu = local
-    copies = fetch(sources, local, sems)
+def backward_kernel(*refs):
+    sources, (own_out, far_out, terms_out), local = refs[:10], refs[10:13], refs[13:23]
+    sems, gg, gu, dx, tiles, out_sems = refs[23:]
+    wd, d_own, gate, up, d_far, wg, wu, x_own, x_far, hidden = local
+    loads = fetch(sources, local, sems)
     half, feature = d_own.shape
     units = gate.shape[1]
     across_last = (((1,), (1,)), ((), ()))
-    copies[0].wait()
+    loads[0].wait()
     for r, d_rows, needed in ((0, d_own, (1, 2, 3)), (half, d_far, (4,))):
         at = slice(r, r + half)
         for n in needed:
-            copies[n].wait()
+            loads[n].wait()
         for c, e in strips(units, 256):
             back = lax.dot_general(
                 d_rows[...], wd[c:e, :], across_last, preferred_element_type=F32
             )
             pre = gate[at, c:e]
             sig = 1.0 / (1.0 + jnp.exp(-pre))
-            gg_ref[at, c:e] = (
-                back * up[at, c:e] * (sig * (1.0 + pre * (1.0 - sig)))
-            ).astype(BF16)
-            gu_ref[at, c:e] = (back * (pre * sig)).astype(BF16)
-    copies[5].wait()
-    copies[6].wait()
+            gg[at, c:e] = (back * up[at, c:e] * (sig * (1.0 + pre * (1.0 - sig)))).astype(BF16)
+            gu[at, c:e] = (back * (pre * sig)).astype(BF16)
+    loads[5].wait()
+    loads[6].wait()
     for c, e in strips(feature):
-        got = jnp.dot(gg_ref[...], wg[:, c:e], preferred_element_type=F32)
-        got += jnp.dot(gu_ref[...], wu[:, c:e], preferred_element_type=F32)
-        own_out[:, c:e] = got[:half].astype(BF16)
-        far_out[:, c:e] = got[half:].astype(BF16)
-
-
-def terms_kernel(*refs):
-    sources, out, local = refs[:7], refs[7], refs[8:15]
-    sems, tiles, tile_sems = refs[15:]
-    x_own, x_far, gg, gu, d_own, d_far, hidden = local
-    loads = fetch(sources, local, sems)
-    half, feature = x_own.shape
-    units = gg.shape[1]
-    pairs = (
-        (gg, x_own, x_far, (0, 1, 2)),
-        (gu, x_own, x_far, (3,)),
-        (hidden, d_own, d_far, (4, 5, 6)),
-    )
+        got = jnp.dot(gg[...], wg[:, c:e], preferred_element_type=F32)
+        got += jnp.dot(gu[...], wu[:, c:e], preferred_element_type=F32)
+        dx[:, c:e] = got.astype(BF16)
+    dx_copies = [
+        pltpu.make_async_copy(dx.at[pl.ds(half, half)], far_out, out_sems.at[2]),
+        pltpu.make_async_copy(dx.at[pl.ds(0, half)], own_out, out_sems.at[3]),
+    ]
+    for copy in dx_copies:
+        copy.start()
+    pairs = ((gg, x_own, x_far, (7, 8)), (gu, x_own, x_far, ()), (hidden, d_own, d_far, (9,)))
     copies = []
     for n, (left, own, far, needed) in enumerate(pairs):
         for m in needed:
@@ -197,27 +187,34 @@
                 tiles[slot, : t - r, c:e] = got.astype(BF16)
             copy = pltpu.make_async_copy(
                 tiles.at[slot, pl.ds(0, t - r)],
-                out.at[pl.ds(n * units + r, t - r)],
-                tile_sems.at[slot],
+                terms_out.at[pl.ds(n * units + r, t - r)],
+                out_sems.at[slot],
             )
             copy.start()
             copies.append(copy)
-    for copy in copies[-2:]:
+    for copy in (*copies[-2:], *dx_copies):
         copy.wait()
 
 
-def streamed_call(kernel, outs, args, out_space, scratch, limit):
+def backward(side_rows, args):
+    half, feature = side_rows.shape
+    units = args[0].shape[0]
+    anywhere = pl.BlockSpec(memory_space=pltpu.HBM)
     return pl.pallas_call(
-        kernel,
-        out_shape=outs,
-        in_specs=[pl.BlockSpec(memory_space=pl.ANY)] * len(args),
-        out_specs=[pl.BlockSpec(memory_space=out_space)] * len(outs),
+        backward_kernel,
+        out_shape=[side_rows, side_rows, jax.ShapeDtypeStruct((3 * units, feature), BF16)],
+        in_specs=[anywhere] * len(args),
+        out_specs=[anywhere] * 3,
         scratch_shapes=[
             *[pltpu.VMEM(x.shape, x.dtype) for x in args],
             pltpu.SemaphoreType.DMA((len(args),)),
-            *scratch,
+            pltpu.VMEM((2 * half, units), BF16),
+            pltpu.VMEM((2 * half, units), BF16),
+            pltpu.VMEM((2 * half, feature), BF16),
+            pltpu.VMEM((2, 256, feature), BF16),
+            pltpu.SemaphoreType.DMA((4,)),
         ],
-        compiler_params=pltpu.CompilerParams(vmem_limit_bytes=limit * 1024 * 1024),
+        compiler_params=pltpu.CompilerParams(vmem_limit_bytes=60 * 1024 * 1024),
         cost_estimate=pl.CostEstimate(flops=1, bytes_accessed=1, transcendentals=0),
     )(*args)
 
@@ -289,39 +286,37 @@
     y_far, y_own, d_far_rows = after(y_far, y_own, d_far_rows)
     y_far_back = exchange(y_far)
 
-    rows, units = shape((half, feature), BF16), shape((2 * half, hidden_units), BF16)
-    dx_own, dx_far, gg, gu = streamed_call(
-        dx_kernel,
-        [rows, rows, units, units],
-        [down_matrix, d_own, gate_pre, up_pre, d_far_rows, gate_matrix.T, up_matrix.T],
-        pltpu.VMEM,
-        [],
-        24,
-    )
-    dx_own, dx_far, gg, gu, y_far_back = after(dx_own, dx_far, gg, gu, y_far_back)
+    dx_own, dx_far, terms = backward(
+        shape((half, feature), BF16),
+        [
+            down_matrix,
+            d_own,
+            gate_pre,
+            up_pre,
+            d_far_rows,
+            gate_matrix.T,
+            up_matrix.T,
+            x_own,
+            x_far_rows,
+            hidden,
+        ],
+    )
+    dx_own, dx_far, terms, y_far_back = after(dx_own, dx_far, terms, y_far_back)
+    summed = lax.psum_scatter(terms, "dp", scatter_dimension=1, tiled=True)
 
     token_rows, grad_rows = ((tok, feature), BF16), ((tok, LANES), F32)
     work = 2 * half * tok * feature
     mixed_far, grads_far = call(
         mix_kernel, [token_rows, grad_rows], [meta_far, d_far, y_far_back], top * work
     )
-    y_own, gg, gu, mixed_far, grads_far = after(y_own, gg, gu, mixed_far, grads_far)
-    y_own_back = exchange(y_own)
-    (terms,) = streamed_call(
-        terms_kernel,
-        [shape((3 * hidden_units, feature), BF16)],
-        [x_own, x_far_rows, gg, gu, d_own, d_far_rows, hidden],
-        pltpu.HBM,
-        [pltpu.VMEM((2, 256, feature), BF16), pltpu.SemaphoreType.DMA((2,))],
-        16,
-    )
-    dx_far, dx_own, terms, y_own_back, mixed_far, grads_far = after(
-        dx_far, dx_own, terms, y_own_back, across(mixed_far), across(grads_far)
-    )
-    summed = lax.psum_scatter(terms, "dp", scatter_dimension=1, tiled=True)
+    dx_far, mixed_far, grads_far = after(dx_far, mixed_far, grads_far)
     dx_far_back = exchange(dx_far)
     (tokens_far,) = call(sum_kernel, [token_rows], [meta_far, dx_far_back], work)
-    tokens_far, dx_own = after(tokens_far, dx_own)
+    tokens_far, y_own, mixed_far, grads_far = after(
+        tokens_far, y_own, across(mixed_far), across(grads_far)
+    )
+    y_own_back = exchange(y_own)
+    y_own_back, dx_own = after(y_own_back, dx_own)
     dx_own_back = exchange(dx_own)
     mixed, grads = call(
         mix_last_kernel,

time: 219 us -> 214 us (0.977)
  local copies, waits for them, and re-layouts: 29.7 us -> 7.68 us
  waiting for transfers between devices: 74.1 us -> 88.7 us
    unnamed x61 -> x25, local copies, waits for them, and re-layouts: 27 us -> 4.59 us
    all_to_all x6, waiting for transfers between devices: 24 us -> 42.1 us  [exchange(): lax.all_to_all(shaped, 'expert', 0, 0, axis_index_groups=sets, tiled=True)]
    ppermute x6, waiting for transfers between devices: 50 us -> 46.5 us  [across(): lax.ppermute(value, 'expert', [(e, (e + side) % experts) for e in range(e...]
    pallas_call x2 -> x1, Pallas kernels: 14.4 us -> 17.5 us  [backward(): pl.pallas_call(backward_kernel, out_shape=[side_rows, side_rows, jax.Shap...]
  transfers between devices with their start and end apart: 13 -> 13, of which waited for: 7 -> 8; matrix products, arithmetic and copies ran while one was open for 9% -> 10% of each run, Pallas kernels for 9% -> 10%
where the time goes in v11:
time: 214 us; the launch traced here: 213 us
  waiting for transfers between devices  88.7 us (41%)
  starting transfers between devices  39.4 us (18%)
  Pallas kernels  28 us (13%)
  blocking collectives  16.4 us (8%)
  between operations  14.2 us (7%)
  matrix products  11 us (5%)
  local copies, waits for them, and re-layouts  7.68 us (4%)
  other arithmetic  7.44 us (3%)
    ppermute x6, waiting for transfers between devices, across(): lax.ppermute(value, 'expert', [(e, (e + side) % experts) for e in range(e...  46.5 us
    all_to_all x6, waiting for transfers between devices, exchange(): lax.all_to_all(shaped, 'expert', 0, 0, axis_index_groups=sets, tiled=True)  42.1 us
    all_to_all x6, starting transfers between devices, exchange(): lax.all_to_all(shaped, 'expert', 0, 0, axis_index_groups=sets, tiled=True)  30.6 us
    pallas_call x1, Pallas kernels, backward(): pl.pallas_call(backward_kernel, out_shape=[side_rows, side_rows, jax.Shap...  17.5 us
    all_to_all x1, blocking collectives, exchange(): lax.all_to_all(shaped, 'expert', 0, 0, axis_index_groups=sets, tiled=True)  16.4 us
    pallas_call x7, Pallas kernels, local_call(): pl.pallas_call(kernel, out_shape=outs, in_specs=[SMEM] + [VMEM] * len(arg...  10.5 us
    ppermute x6, starting transfers between devices, across(): lax.ppermute(value, 'expert', [(e, (e + side) % experts) for e in range(e...  8.57 us
    broadcast_in_dim x1, other arithmetic, on_device(): summed[2 * hidden_units:].astype(F32)[None]  6.07 us
  transfers between devices with their start and end apart: 13, of which 8 were waited for; matrix products, arithmetic and copies ran while one was open for 10% of the time, Pallas kernels for 10%

profile of v11, /device:TPU:0, one launch (start us, length us, event | category | flops | bytes accessed | tf_op | source)
XLA Modules:
  0.0 212.7 jit_solution(714732862615890194)
XLA Ops:
  10.6 2.2 %shard_map.118 = bf16[512,2048]{1,0:T(8,128)(2,1)} custom-call(s32[1]{0:T(128)} %bitcast.me_ref, f32[4,128]{1,0:T(4,128)S(1)} %pad_maximum_fusion.3.refs_0_.refs_1_.meta, f32[4,128]{1,0:T(4,128)S(1)} %pad_maximum_fusion.3.refs_0_.refs_1_.meta, bf16[128,2048]{1,0:T(8,128)(2,1)S(1)} %copy-done.2, bf16[128,2048]{1,0:T(8,128)(2,1)S(1)} %copy-done), custom_call_target="tpu_custom_call" | custom-call | flops 536870912 | bytes 3149824 | tf_op jit(solution)/shard_map/pallas_call | solution.py:20
  12.9 6.3 %all-to-all-start = ((bf16[8,64,2048]{2,1,0:T(8,128)(2,1)}), bf16[8,64,2048]{2,1,0:T(8,128)(2,1)}, u32[]{:S(2)}, u32[]{:S(2)}) async-start(bf16[8,64,2048]{2,1,0:T(8,128)(2,1)} %bitcast.4), calls=%async_computation | async-start | bytes 4194304 | tf_op jit(solution)/shard_map/all_to_all | solution.py:239
  19.2 2.7 %collective-permute-start = (bf16[128,2048]{1,0:T(8,128)(2,1)S(1)}, bf16[128,2048]{1,0:T(8,128)(2,1)S(1)}, u32[]{:S(2)}, u32[]{:S(2)}) collective-permute-start(bf16[128,2048]{1,0:T(8,128)(2,1)S(1)} %copy-done.3), channel_id=1, source_target_pairs={{0,8},{1,9},{2,10},{3,11},{4,12},{5,13},{6,14},{7,15},{8,0},{9,1},... | collective-permute-start | bytes 1572872 | tf_op jit(solution)/shard_map/ppermute | solution.py:235
  22.2 2.6 %collective-permute-start.1 = (f32[4,128]{1,0:T(4,128)S(1)}, f32[4,128]{1,0:T(4,128)S(1)}, u32[]{:S(2)}, u32[]{:S(2)}) collective-permute-start(f32[4,128]{1,0:T(4,128)S(1)} %pad_maximum_fusion.3.refs_0_.refs_1_.meta), channel_id=1, source_target_pairs={{0,8},{1,9},{2,10},{3,11},{4,12},{5,13},{6,14},{7,15},{8,0},{9,1},... | collective-permute-start | bytes 6152 | tf_op jit(solution)/shard_map/ppermute | solution.py:235
  24.7 39.7 %collective-permute-done.1.refs_0_.meta = f32[4,128]{1,0:T(4,128)S(1)} collective-permute-done((f32[4,128]{1,0:T(4,128)S(1)}, f32[4,128]{1,0:T(4,128)S(1)}, u32[]{:S(2)}, u32[]{:S(2)}) %collective-permute-start.1) | collective-permute-done | bytes 2080 | tf_op jit(solution)/shard_map/ppermute | solution.py:235
  64.5 2.1 all-to-all-done
  68.1 8.2 %all-to-all-start.1 = ((bf16[8,32,2048]{2,1,0:T(8,128)(2,1)}), bf16[8,32,2048]{2,1,0:T(8,128)(2,1)S(1)}, u32[]{:S(2)}, u32[]{:S(2)}) async-start(bf16[8,32,2048]{2,1,0:T(8,128)(2,1)} %bitcast.8), calls=%async_computation.1 | async-start | bytes 2097152 | tf_op jit(solution)/shard_map/all_to_all | solution.py:239
  77.8 3.1 %fusion.11 = (bf16[8,1,32,2048]{3,2,1,0:T(8,128)(2,1)}, bf16[8,1,32,2048]{3,2,1,0:T(8,128)(2,1)}) fusion(bf16[8,2,32,2048]{3,2,1,0:T(8,128)(2,1)} %bitcast.5), kind=kLoop, calls=%fused_computation.20 | loop fusion | bytes 4194304 | tf_op jit(solution)/shard_map/slice | solution.py:269
  80.9 9.0 %all-to-all-done.1 = bf16[8,32,2048]{2,1,0:T(8,128)(2,1)S(1)} async-done(((bf16[8,32,2048]{2,1,0:T(8,128)(2,1)}), bf16[8,32,2048]{2,1,0:T(8,128)(2,1)S(1)}, u32[]{:S(2)}, u32[]{:S(2)}) %all-to-all-start.1) | async-done | bytes 1048608 | tf_op jit(solution)/shard_map/all_to_all | solution.py:239
  89.8 4.3 %all-to-all-start.2 = ((bf16[8,32,2048]{2,1,0:T(8,128)(2,1)}), bf16[8,32,2048]{2,1,0:T(8,128)(2,1)}, u32[]{:S(2)}, u32[]{:S(2)}) async-start(bf16[8,32,2048]{2,1,0:T(8,128)(2,1)} %bitcast.12), calls=%async_computation.2 | async-start | bytes 2097152 | tf_op jit(solution)/shard_map/all_to_all | solution.py:239
  94.1 4.1 %fusion.2.refs_2_ = f32[512,704]{1,0:T(8,128)S(1)} fusion(bf16[1,2048,704]{1,2,0:T(8,128)(2,1)} %param.10, bf16[256,2048]{1,0:T(8,128)(2,1)S(1)} %bitcast.56, bf16[256,2048]{1,0:T(8,128)(2,1)} %bitcast.60), kind=kOutput, calls=%fused_computation.2 | convolution fusion | flops 1480589312 | bytes 6422528 | tf_op jit(solution)/shard_map/dot_general | solution.py:279
  98.3 3.0 %multiply_convert_fusion = (bf16[512,704]{1,0:T(8,128)(2,1)S(1)}, f32[512,704]{1,0:T(8,128)}) fusion(f32[512,704]{1,0:T(8,128)S(1)} %fusion.2.refs_2_, bf16[1,2048,704]{1,2,0:T(8,128)(2,1)S(1)} %copy-done.8, bf16[256,2048]{1,0:T(8,128)(2,1)S(1)} %bitcast.57, bf16[256,2048]{1,0:T(8,128)(2,1)S(1)} %bitcast.62), kind=kOutput, calls=%fused_computation.9 | convolution fusion | flops 1482752000 | bytes 8585216 | tf_op jit(solution)/shard_map/dot_general | solution.py:280
  107.2 3.6 %all-to-all-start.3 = ((bf16[8,32,2048]{2,1,0:T(8,128)(2,1)}), bf16[8,32,2048]{2,1,0:T(8,128)(2,1)S(1)}, u32[]{:S(2)}, u32[]{:S(2)}) async-start(bf16[8,32,2048]{2,1,0:T(8,128)(2,1)} %bitcast.69), calls=%async_computation.3 | async-start | bytes 2097152 | tf_op jit(solution)/shard_map/all_to_all | solution.py:239
  111.0 17.5 %shard_map.121 = (bf16[256,2048]{1,0:T(8,128)(2,1)}, bf16[256,2048]{1,0:T(8,128)(2,1)}, bf16[2112,2048]{1,0:T(8,128)(2,1)}) custom-call(bf16[704,2048]{1,0:T(8,128)(2,1)} %bitcast.65, bf16[256,2048]{1,0:T(8,128)(2,1)} %bitcast.59, f32[512,704]{1,0:T(8,128)} %copy-done.10, f32[512,704]{1,0:T(8,128)} %get-tuple-element.104.refs_3_, ...), custom_call_target="tpu_custom_call" | custom-call | flops 1 | bytes 1 | tf_op jit(solution)/shard_map/pallas_call | solution.py:203
  129.3 4.8 %all-to-all-start.4 = ((bf16[8,32,2048]{2,1,0:T(8,128)(2,1)}), bf16[8,32,2048]{2,1,0:T(8,128)(2,1)S(1)}, u32[]{:S(2)}, u32[]{:S(2)}) async-start(bf16[8,32,2048]{2,1,0:T(8,128)(2,1)} %bitcast.68), calls=%async_computation.4 | async-start | bytes 2097152 | tf_op jit(solution)/shard_map/all_to_all | solution.py:239
  134.2 2.9 %collective-permute-start.4 = (f32[128,128]{1,0:T(8,128)S(1)}, f32[128,128]{1,0:T(8,128)S(1)}, u32[]{:S(2)}, u32[]{:S(2)}) collective-permute-start(f32[128,128]{1,0:T(8,128)S(1)} %get-tuple-element.63), channel_id=1, source_target_pairs={{0,8},{1,9},{2,10},{3,11},{4,12},{5,13},{6,14},{7,15},{8,0},{9,1},... | collective-permute-start | bytes 196616 | tf_op jit(solution)/shard_map/ppermute | solution.py:235
  137.1 19.1 %all-to-all-done.4 = bf16[8,32,2048]{2,1,0:T(8,128)(2,1)S(1)} async-done(((bf16[8,32,2048]{2,1,0:T(8,128)(2,1)}), bf16[8,32,2048]{2,1,0:T(8,128)(2,1)S(1)}, u32[]{:S(2)}, u32[]{:S(2)}) %all-to-all-start.4) | async-done | bytes 1048608 | tf_op jit(solution)/shard_map/all_to_all | solution.py:239
  156.7 4.6 %collective-permute-done.4.far_grads = f32[128,128]{1,0:T(8,128)S(1)} collective-permute-done((f32[128,128]{1,0:T(8,128)S(1)}, f32[128,128]{1,0:T(8,128)S(1)}, u32[]{:S(2)}, u32[]{:S(2)}) %collective-permute-start.4) | collective-permute-done | bytes 65568 | tf_op jit(solution)/shard_map/ppermute | solution.py:235
  162.1 16.4 %all_to_all.35 = bf16[8,32,2048]{2,1,0:T(8,128)(2,1)S(1)} all-to-all(bf16[8,32,2048]{2,1,0:T(8,128)(2,1)} %bitcast.67), channel_id=1, replica_groups={{0,1,2,3,4,5,6,7},{8,9,10,11,12,13,14,15},{16,17,18,19,20,21,22,23},{24..., dimensions={0} | all-to-all | bytes 2097152 | tf_op jit(solution)/shard_map/all_to_all | solution.py:239
  178.4 3.6 %all-to-all-start.6 = ((bf16[8,32,2048]{2,1,0:T(8,128)(2,1)}), bf16[8,32,2048]{2,1,0:T(8,128)(2,1)S(1)}, u32[]{:S(2)}, u32[]{:S(2)}) async-start(bf16[8,32,2048]{2,1,0:T(8,128)(2,1)} %bitcast.66), calls=%async_computation.6 | async-start | bytes 2097152 | tf_op jit(solution)/shard_map/all_to_all | solution.py:239
  184.7 6.1 %fusion.4 = (f32[1,704,1024]{2,1,0:T(8,128)}, f32[1,1024,704]{1,2,0:T(8,128)}, f32[1,1024,704]{1,2,0:T(8,128)}) fusion(bf16[2112,1024]{1,0:T(8,128)(2,1)} %reduce-scatter.2.cloned.1.call-done), kind=kLoop, calls=%fused_computation.11 | loop fusion | flops 2162688 | bytes 12976128 | tf_op jit(solution)/shard_map/broadcast_in_dim | solution.py:330
  190.8 9.9 %all-to-all-done.6 = bf16[8,32,2048]{2,1,0:T(8,128)(2,1)S(1)} async-done(((bf16[8,32,2048]{2,1,0:T(8,128)(2,1)}), bf16[8,32,2048]{2,1,0:T(8,128)(2,1)S(1)}, u32[]{:S(2)}, u32[]{:S(2)}) %all-to-all-start.6) | async-done | bytes 1048608 | tf_op jit(solution)/shard_map/all_to_all | solution.py:239
  201.3 2.2 %collective-permute-done.5.far = bf16[128,2048]{1,0:T(8,128)(2,1)} collective-permute-done((bf16[128,2048]{1,0:T(8,128)(2,1)S(1)}, bf16[128,2048]{1,0:T(8,128)(2,1)}, u32[]{:S(2)}, u32[]{:S(2)}) %collective-permute-start.5) | collective-permute-done | bytes 524320 | tf_op jit(solution)/shard_map/ppermute | solution.py:235
  203.6 2.3 %shard_map.125 = bf16[128,2048]{1,0:T(8,128)(2,1)} custom-call(s32[1]{0:T(128)} %bitcast.me_ref, f32[4,128]{1,0:T(4,128)S(1)} %pad_maximum_fusion.3.refs_0_.refs_1_.meta, bf16[256,2048]{1,0:T(8,128)(2,1)S(1)} %bitcast.51, bf16[128,2048]{1,0:T(8,128)(2,1)} %collective-permute-done.5.far), custom_call_target="tpu_custom_call" | custom-call | flops 134217728 | bytes 2099200 | tf_op jit(solution)/shard_map/pallas_call | solution.py:20
  (45 shorter events, 18.5 us)
Async XLA Ops:
  8.5 1.0 copy-start
  9.6 1.0 copy-start.2
  12.8 6.3 %copy-start.3 = (bf16[128,2048]{1,0:T(8,128)(2,1)S(1)}, bf16[128,2048]{1,0:T(8,128)(2,1)}, u32[]{:S(2)}) copy-start(bf16[128,2048]{1,0:T(8,128)(2,1)} %refs_2_.1) | copy-start | bytes 1572868
  12.9 9.0 %copy-start.1 = (bf16[128,2048]{1,0:T(8,128)(2,1)S(1)}, bf16[128,2048]{1,0:T(8,128)(2,1)}, u32[]{:S(2)}) copy-start(bf16[128,2048]{1,0:T(8,128)(2,1)} %block.1) | copy-start | bytes 1572868
  12.9 53.7 %all-to-all-start = ((bf16[8,64,2048]{2,1,0:T(8,128)(2,1)}), bf16[8,64,2048]{2,1,0:T(8,128)(2,1)}, u32[]{:S(2)}, u32[]{:S(2)}) async-start(bf16[8,64,2048]{2,1,0:T(8,128)(2,1)} %bitcast.4), calls=%async_computation | async-start | bytes 4194304 | tf_op jit(solution)/shard_map/all_to_all | solution.py:239
  19.2 45.3 %collective-permute-start = (bf16[128,2048]{1,0:T(8,128)(2,1)S(1)}, bf16[128,2048]{1,0:T(8,128)(2,1)S(1)}, u32[]{:S(2)}, u32[]{:S(2)}) collective-permute-start(bf16[128,2048]{1,0:T(8,128)(2,1)S(1)} %copy-done.3), channel_id=1, source_target_pairs={{0,8},{1,9},{2,10},{3,11},{4,12},{5,13},{6,14},{7,15},{8,0},{9,1},... | collective-permute-start | bytes 1572872 | tf_op jit(solution)/shard_map/ppermute | solution.py:235
  21.8 42.7 %collective-permute-start.2 = (bf16[128,2048]{1,0:T(8,128)(2,1)S(1)}, bf16[128,2048]{1,0:T(8,128)(2,1)S(1)}, u32[]{:S(2)}, u32[]{:S(2)}) collective-permute-start(bf16[128,2048]{1,0:T(8,128)(2,1)S(1)} %copy-done.1), channel_id=1, source_target_pairs={{0,8},{1,9},{2,10},{3,11},{4,12},{5,13},{6,14},{7,15},{8,0},{9,1},... | collective-permute-start | bytes 1572872 | tf_op jit(solution)/shard_map/ppermute | solution.py:235
  22.2 42.3 %collective-permute-start.1 = (f32[4,128]{1,0:T(4,128)S(1)}, f32[4,128]{1,0:T(4,128)S(1)}, u32[]{:S(2)}, u32[]{:S(2)}) collective-permute-start(f32[4,128]{1,0:T(4,128)S(1)} %pad_maximum_fusion.3.refs_0_.refs_1_.meta), channel_id=1, source_target_pairs={{0,8},{1,9},{2,10},{3,11},{4,12},{5,13},{6,14},{7,15},{8,0},{9,1},... | collective-permute-start | bytes 6152 | tf_op jit(solution)/shard_map/ppermute | solution.py:235
  68.1 21.7 %all-to-all-start.1 = ((bf16[8,32,2048]{2,1,0:T(8,128)(2,1)}), bf16[8,32,2048]{2,1,0:T(8,128)(2,1)S(1)}, u32[]{:S(2)}, u32[]{:S(2)}) async-start(bf16[8,32,2048]{2,1,0:T(8,128)(2,1)} %bitcast.8), calls=%async_computation.1 | async-start | bytes 2097152 | tf_op jit(solution)/shard_map/all_to_all | solution.py:239
  89.8 8.4 %copy-start.6 = (bf16[8,32,2048]{2,1,0:T(8,128)(2,1)}, bf16[8,32,2048]{2,1,0:T(8,128)(2,1)S(1)}, u32[]{:S(2)}) copy-start(bf16[8,32,2048]{2,1,0:T(8,128)(2,1)S(1)} %all-to-all-done.1) | copy-start | bytes 3145732
  89.8 17.4 %all-to-all-start.2 = ((bf16[8,32,2048]{2,1,0:T(8,128)(2,1)}), bf16[8,32,2048]{2,1,0:T(8,128)(2,1)}, u32[]{:S(2)}, u32[]{:S(2)}) async-start(bf16[8,32,2048]{2,1,0:T(8,128)(2,1)} %bitcast.12), calls=%async_computation.2 | async-start | bytes 2097152 | tf_op jit(solution)/shard_map/all_to_all | solution.py:239
  94.1 4.2 %copy-start.7 = (bf16[8,1,32,2048]{3,2,1,0:T(8,128)(2,1)S(1)}, bf16[8,1,32,2048]{3,2,1,0:T(8,128)(2,1)}, u32[]{:S(2)}) copy-start(bf16[8,1,32,2048]{3,2,1,0:T(8,128)(2,1)} %get-tuple-element.102) | copy-start | bytes 3145732
  94.1 4.2 %copy-start.8 = (bf16[1,2048,704]{1,2,0:T(8,128)(2,1)S(1)}, bf16[1,2048,704]{1,2,0:T(8,128)(2,1)}, u32[]{:S(2)}) copy-start(bf16[1,2048,704]{1,2,0:T(8,128)(2,1)} %param.11) | copy-start | bytes 8650756
  98.3 3.0 %copy-start.10 = (f32[512,704]{1,0:T(8,128)}, f32[512,704]{1,0:T(8,128)S(1)}, u32[]{:S(2)}) copy-start(f32[512,704]{1,0:T(8,128)S(1)} %fusion.2.refs_2_) | copy-start | bytes 4325380
  98.3 3.0 %copy-start.9 = (bf16[1,704,2048]{2,1,0:T(8,128)(2,1)S(1)}, bf16[1,704,2048]{2,1,0:T(8,128)(2,1)}, u32[]{:S(2)}) copy-start(bf16[1,704,2048]{2,1,0:T(8,128)(2,1)} %param.12) | copy-start | bytes 8650756
  101.3 2.0 copy-start.11
  107.2 21.3 %all-to-all-start.3 = ((bf16[8,32,2048]{2,1,0:T(8,128)(2,1)}), bf16[8,32,2048]{2,1,0:T(8,128)(2,1)S(1)}, u32[]{:S(2)}, u32[]{:S(2)}) async-start(bf16[8,32,2048]{2,1,0:T(8,128)(2,1)} %bitcast.69), calls=%async_computation.3 | async-start | bytes 2097152 | tf_op jit(solution)/shard_map/all_to_all | solution.py:239
  110.8 73.9 %reduce-scatter.2.cloned.1.call-start = ((), (), s32[]{:S(2)}) async-start(), calls=%async_computation.8 | async-start | bytes 12976128 | tf_op jit(solution)/shard_map/reduce_scatter | solution.py:305
  129.3 26.9 %all-to-all-start.4 = ((bf16[8,32,2048]{2,1,0:T(8,128)(2,1)}), bf16[8,32,2048]{2,1,0:T(8,128)(2,1)S(1)}, u32[]{:S(2)}, u32[]{:S(2)}) async-start(bf16[8,32,2048]{2,1,0:T(8,128)(2,1)} %bitcast.68), calls=%async_computation.4 | async-start | bytes 2097152 | tf_op jit(solution)/shard_map/all_to_all | solution.py:239
  134.1 27.1 %collective-permute-start.3 = (bf16[128,2048]{1,0:T(8,128)(2,1)S(1)}, bf16[128,2048]{1,0:T(8,128)(2,1)S(1)}, u32[]{:S(2)}, u32[]{:S(2)}) collective-permute-start(bf16[128,2048]{1,0:T(8,128)(2,1)S(1)} %get-tuple-element.62), channel_id=1, source_target_pairs={{0,8},{1,9},{2,10},{3,11},{4,12},{5,13},{6,14},{7,15},{8,0},{9,1},... | collective-permute-start | bytes 1572872 | tf_op jit(solution)/shard_map/ppermute | solution.py:235
  134.2 27.1 %collective-permute-start.4 = (f32[128,128]{1,0:T(8,128)S(1)}, f32[128,128]{1,0:T(8,128)S(1)}, u32[]{:S(2)}, u32[]{:S(2)}) collective-permute-start(f32[128,128]{1,0:T(8,128)S(1)} %get-tuple-element.63), channel_id=1, source_target_pairs={{0,8},{1,9},{2,10},{3,11},{4,12},{5,13},{6,14},{7,15},{8,0},{9,1},... | collective-permute-start | bytes 196616 | tf_op jit(solution)/shard_map/ppermute | solution.py:235
  178.4 22.3 %all-to-all-start.6 = ((bf16[8,32,2048]{2,1,0:T(8,128)(2,1)}), bf16[8,32,2048]{2,1,0:T(8,128)(2,1)S(1)}, u32[]{:S(2)}, u32[]{:S(2)}) async-start(bf16[8,32,2048]{2,1,0:T(8,128)(2,1)} %bitcast.66), calls=%async_computation.6 | async-start | bytes 2097152 | tf_op jit(solution)/shard_map/all_to_all | solution.py:239
  182.0 21.6 %collective-permute-start.5 = (bf16[128,2048]{1,0:T(8,128)(2,1)S(1)}, bf16[128,2048]{1,0:T(8,128)(2,1)}, u32[]{:S(2)}, u32[]{:S(2)}) collective-permute-start(bf16[128,2048]{1,0:T(8,128)(2,1)S(1)} %shard_map.123), channel_id=1, source_target_pairs={{0,8},{1,9},{2,10},{3,11},{4,12},{5,13},{6,14},{7,15},{8,0},{9,1},... | collective-permute-start | bytes 1572872 | tf_op jit(solution)/shard_map/ppermute | solution.py:235
  182.1 1.0 copy-start.5
  (1 other events, 0.8 us)
Sparse Core Ops, SparseCore 0:
  128.6 16.3 reduce-scatter.1

commit v12 on v10

--- a/solution.py
+++ b/solution.py
@@ -56,7 +56,7 @@
 
 def pick_kernel(top, side, capacity, scaled, me_ref, *refs):
     count = len(scaled)
-    metas, blocks, out = refs[:count], refs[count : 2 * count], refs[2 * count]
+    metas, blocks, out = refs[:count], refs[count:-1], refs[-1]
     tables = slot_tables(me_ref[0], metas, top, side, capacity)
     held = jnp.concatenate([functools.reduce(lambda p, q: p + q, ks) for ks in tables], 1)
     held = held.astype(BF16)
@@ -88,19 +88,23 @@
         out[:, c:e] = picked_sum(held, back, c, e).astype(BF16)
 
 
-def mix(top, table, meta, block, back, out, grads, far=None, far_grads=None):
+def mix(top, table, meta, blocks, back, outs, grads, fars=(), far_grads=None):
     tok = meta.shape[1]
     gates = [meta[top + k : top + k + 1, :] for k in range(top)]
     gates = [jnp.transpose(jnp.broadcast_to(g, (8, tok)))[:, :1] for g in gates]
     sums = [jnp.zeros((tok, 1), F32) for _ in range(top)]
-    for c, e in strips(out.shape[1]):
-        cotangent = block[:, c:e].astype(F32)
-        mixed = 0.0 if far is None else far[:, c:e].astype(F32)
+    for c, e in strips(back.shape[1]):
+        cotangent = jnp.concatenate([ref[:, c:e] for ref in blocks], 0).astype(F32)
+        mixed = 0.0
+        if fars:
+            mixed = jnp.concatenate([ref[:, c:e] for ref in fars], 0).astype(F32)
         for k in range(top):
             got = picked_sum(table[k], back, c, e)
             mixed += gates[k] * got
             sums[k] += jnp.sum(cotangent * got, 1, keepdims=True)
-        out[:, c:e] = mixed.astype(BF16)
+        for n, out in enumerate(outs):
+            rows = out.shape[0]
+            out[:, c:e] = mixed[n * rows : (n + 1) * rows].astype(BF16)
     lane = lax.broadcasted_iota(jnp.int32, (tok, LANES), 1)
     grad = jnp.zeros((tok, LANES), F32) if far_grads is None else far_grads[...]
     for k in range(top):
@@ -108,9 +112,16 @@
     grads[...] = grad
 
 
-def mix_kernel(top, side, capacity, me_ref, meta, block, back, out, grads):
+def mix_kernel(top, side, capacity, me_ref, meta, one, two, back, out_one, out_two, grads):
     (table,) = slot_tables(me_ref[0], [meta], top, side, capacity)
-    mix(top, table, meta, block, back, out, grads)
+    mix(top, table, meta, (one, two), back, (out_one, out_two), grads)
+
+
+def mix_last_kernel(
+    top, side, capacity, me_ref, meta, block, back, one, two, far_grads, out, grads
+):
+    (table,) = slot_tables(me_ref[0], [meta], top, side, capacity)
+    mix(top, table, meta, (block,), back, (out,), grads, (one, two), far_grads)
 
 
 def sum_last_kernel(top, side, capacity, me_ref, meta, back, far, out):
@@ -118,13 +129,6 @@
     held = functools.reduce(lambda p, q: p + q, table)
     for c, e in strips(out.shape[1]):
         out[:, c:e] = (picked_sum(held, back, c, e) + far[:, c:e].astype(F32)).astype(BF16)
-
-
-def mix_last_kernel(
-    top, side, capacity, me_ref, meta, block, back, far, far_grads, out, grads
-):
-    (table,) = slot_tables(me_ref[0], [meta], top, side, capacity)
-    mix(top, table, meta, block, back, out, grads, far, far_grads)
 
 
 def fetch(sources, targets, sems):
@@ -136,35 +140,44 @@
 
 
 def dx_kernel(*refs):
-    sources, (own_out, far_out, gg_ref, gu_ref) = refs[:7], refs[7:11]
-    local, sems = refs[11:18], refs[18]
+    sources, outs, local = refs[:7], refs[7:11], refs[11:18]
+    sems, gg, gu, dx, out_sems = refs[18:]
     wd, d_own, gate, up, d_far, wg, wu = local
-    copies = fetch(sources, local, sems)
+    loads = fetch(sources, local, sems)
     half, feature = d_own.shape
     units = gate.shape[1]
     across_last = (((1,), (1,)), ((), ()))
-    copies[0].wait()
+    loads[0].wait()
     for r, d_rows, needed in ((0, d_own, (1, 2, 3)), (half, d_far, (4,))):
         at = slice(r, r + half)
         for n in needed:
-            copies[n].wait()
+            loads[n].wait()
         for c, e in strips(units, 256):
             back = lax.dot_general(
                 d_rows[...], wd[c:e, :], across_last, preferred_element_type=F32
             )
             pre = gate[at, c:e]
             sig = 1.0 / (1.0 + jnp.exp(-pre))
-            gg_ref[at, c:e] = (
-                back * up[at, c:e] * (sig * (1.0 + pre * (1.0 - sig)))
-            ).astype(BF16)
-            gu_ref[at, c:e] = (back * (pre * sig)).astype(BF16)
-    copies[5].wait()
-    copies[6].wait()
+            gg[at, c:e] = (back * up[at, c:e] * (sig * (1.0 + pre * (1.0 - sig)))).astype(BF16)
+            gu[at, c:e] = (back * (pre * sig)).astype(BF16)
+    copies = [
+        pltpu.make_async_copy(gg, outs[2], out_sems.at[0]),
+        pltpu.make_async_copy(gu, outs[3], out_sems.at[1]),
+        pltpu.make_async_copy(dx.at[pl.ds(half, half)], outs[1], out_sems.at[2]),
+        pltpu.make_async_copy(dx.at[pl.ds(0, half)], outs[0], out_sems.at[3]),
+    ]
+    copies[0].start()
+    copies[1].start()
+    loads[5].wait()
+    loads[6].wait()
     for c, e in strips(feature):
-        got = jnp.dot(gg_ref[...], wg[:, c:e], preferred_element_type=F32)
-        got += jnp.dot(gu_ref[...], wu[:, c:e], preferred_element_type=F32)
-        own_out[:, c:e] = got[:half].astype(BF16)
-        far_out[:, c:e] = got[half:].astype(BF16)
+        got = jnp.dot(gg[...], wg[:, c:e], preferred_element_type=F32)
+        got += jnp.dot(gu[...], wu[:, c:e], preferred_element_type=F32)
+        dx[:, c:e] = got.astype(BF16)
+    copies[2].start()
+    copies[3].start()
+    for copy in copies:
+        copy.wait()
 
 
 def terms_kernel(*refs):
@@ -206,18 +219,19 @@
         copy.wait()
 
 
-def streamed_call(kernel, outs, args, out_space, scratch, limit):
+def streamed_call(kernel, outs, args, scratch):
+    anywhere = pl.BlockSpec(memory_space=pltpu.HBM)
     return pl.pallas_call(
         kernel,
         out_shape=outs,
-        in_specs=[pl.BlockSpec(memory_space=pl.ANY)] * len(args),
-        out_specs=[pl.BlockSpec(memory_space=out_space)] * len(outs),
+        in_specs=[anywhere] * len(args),
+        out_specs=[anywhere] * len(outs),
         scratch_shapes=[
             *[pltpu.VMEM(x.shape, x.dtype) for x in args],
             pltpu.SemaphoreType.DMA((len(args),)),
             *scratch,
         ],
-        compiler_params=pltpu.CompilerParams(vmem_limit_bytes=limit * 1024 * 1024),
+        compiler_params=pltpu.CompilerParams(vmem_limit_bytes=60 * 1024 * 1024),
         cost_estimate=pl.CostEstimate(flops=1, bytes_accessed=1, transcendentals=0),
     )(*args)
 
@@ -268,12 +282,13 @@
     own = exchange(pick([meta, meta], [tokens, d_mixed], (False, True)))
     own = own.reshape(side, 2, capacity, feature)
     x_far, meta_far = after(across(tokens), across(meta))
-    x_far, d_far, own = after(x_far, across(d_mixed), own)
+    d_far = [across(d_mixed[n * (tok // 2) : (n + 1) * (tok // 2)]) for n in range(2)]
+    x_far, d_far[0], own = after(x_far, d_far[0], own)
     x_own, d_own = (own[:, n].reshape(half, feature) for n in range(2))
     x_far_rows = exchange(pick([meta_far], [x_far], (False,)))
     x_rows = jnp.concatenate([x_own, x_far_rows], 0)
     d_picked, x_own, d_own, _ = after(
-        pick([meta_far], [d_far], (True,)), x_own, d_own, x_far_rows
+        pick([meta_far], d_far, (True,)), x_own, d_own, x_far_rows
     )
     d_far_rows = exchange(d_picked)
 
@@ -294,39 +309,48 @@
         dx_kernel,
         [rows, rows, units, units],
         [down_matrix, d_own, gate_pre, up_pre, d_far_rows, gate_matrix.T, up_matrix.T],
-        pltpu.VMEM,
-        [],
-        24,
+        [
+            pltpu.VMEM(units.shape, BF16),
+            pltpu.VMEM(units.shape, BF16),
+            pltpu.VMEM((2 * half, feature), BF16),
+            pltpu.SemaphoreType.DMA((4,)),
+        ],
     )
     dx_own, dx_far, gg, gu, y_far_back = after(dx_own, dx_far, gg, gu, y_far_back)
 
     token_rows, grad_rows = ((tok, feature), BF16), ((tok, LANES), F32)
+    some_rows = ((tok // 2, feature), BF16)
     work = 2 * half * tok * feature
-    mixed_far, grads_far = call(
-        mix_kernel, [token_rows, grad_rows], [meta_far, d_far, y_far_back], top * work
-    )
-    y_own, gg, gu, mixed_far, grads_far = after(y_own, gg, gu, mixed_far, grads_far)
+    mixed_one, mixed_two, grads_far = call(
+        mix_kernel,
+        [some_rows, some_rows, grad_rows],
+        [meta_far, *d_far, y_far_back],
+        top * work,
+    )
+    y_own, gg, gu, mixed_one, mixed_two, grads_far = after(
+        y_own, gg, gu, mixed_one, mixed_two, grads_far
+    )
     y_own_back = exchange(y_own)
     (terms,) = streamed_call(
         terms_kernel,
         [shape((3 * hidden_units, feature), BF16)],
         [x_own, x_far_rows, gg, gu, d_own, d_far_rows, hidden],
-        pltpu.HBM,
         [pltpu.VMEM((2, 256, feature), BF16), pltpu.SemaphoreType.DMA((2,))],
-        16,
-    )
-    dx_far, dx_own, terms, y_own_back, mixed_far, grads_far = after(
-        dx_far, dx_own, terms, y_own_back, across(mixed_far), across(grads_far)
+    )
+    dx_far, dx_own, terms, y_own_back, mixed_one = after(
+        dx_far, dx_own, terms, y_own_back, across(mixed_one)
     )
     summed = lax.psum_scatter(terms, "dp", scatter_dimension=1, tiled=True)
     dx_far_back = exchange(dx_far)
     (tokens_far,) = call(sum_kernel, [token_rows], [meta_far, dx_far_back], work)
-    tokens_far, dx_own = after(tokens_far, dx_own)
+    tokens_far, dx_own, mixed_two, grads_far = after(
+        tokens_far, dx_own, across(mixed_two), across(grads_far)
+    )
     dx_own_back = exchange(dx_own)
     mixed, grads = call(
         mix_last_kernel,
         [token_rows, grad_rows],
-        [meta, d_mixed, y_own_back, mixed_far, grads_far],
+        [meta, d_mixed, y_own_back, mixed_one, mixed_two, grads_far],
         top * work,
     )
     weight_grads = (

time: 219 us -> 213 us (0.973)
  local copies, waits for them, and re-layouts: 29.7 us -> 5.92 us
  waiting for transfers between devices: 74.1 us -> 92.7 us
  blocking collectives: 16.1 us -> 0 us
  starting transfers between devices: 38.9 us -> 48.2 us
  Pallas kernels: 26.7 us -> 32.8 us
    unnamed x61 -> x23, local copies, waits for them, and re-layouts: 27 us -> 2.76 us
    all_to_all x1 -> x0, blocking collectives: 16.1 us -> none  [exchange(): lax.all_to_all(shaped, 'expert', 0, 0, axis_index_groups=sets, tiled=True)]
    all_to_all x6 -> x7, waiting for transfers between devices: 24 us -> 37.5 us  [exchange(): lax.all_to_all(shaped, 'expert', 0, 0, axis_index_groups=sets, tiled=True)]
    pallas_call x2, Pallas kernels: 14.4 us -> 20.7 us  [streamed_call(): pl.pallas_call(kernel, out_shape=outs, in_specs=[anywhere] * len(args), o...]
    all_to_all x6 -> x7, starting transfers between devices: 30.2 us -> 35.8 us  [exchange(): lax.all_to_all(shaped, 'expert', 0, 0, axis_index_groups=sets, tiled=True)]
    ppermute x6 -> x8, waiting for transfers between devices: 50 us -> 55.2 us  [across(): lax.ppermute(value, 'expert', [(e, (e + side) % experts) for e in range(e...]
    ppermute x6 -> x8, starting transfers between devices: 8.63 us -> 12.3 us  [across(): lax.ppermute(value, 'expert', [(e, (e + side) % experts) for e in range(e...]
  transfers between devices with their start and end apart: 13 -> 16, of which waited for: 7 -> 10; matrix products, arithmetic and copies ran while one was open for 9% -> 10% of each run, Pallas kernels for 9% -> 12%
where the time goes in v12:
time: 213 us; the launch traced here: 212 us
  waiting for transfers between devices  92.7 us (44%)
  starting transfers between devices  48.2 us (23%)
  Pallas kernels  32.8 us (15%)
  between operations  14.2 us (7%)
  matrix products  11.1 us (5%)
  other arithmetic  7.44 us (3%)
  local copies, waits for them, and re-layouts  5.92 us (3%)
    ppermute x8, waiting for transfers between devices, across(): lax.ppermute(value, 'expert', [(e, (e + side) % experts) for e in range(e...  55.2 us
    all_to_all x7, waiting for transfers between devices, exchange(): lax.all_to_all(shaped, 'expert', 0, 0, axis_index_groups=sets, tiled=True)  37.5 us
    all_to_all x7, starting transfers between devices, exchange(): lax.all_to_all(shaped, 'expert', 0, 0, axis_index_groups=sets, tiled=True)  35.8 us
    pallas_call x2, Pallas kernels, streamed_call(): pl.pallas_call(kernel, out_shape=outs, in_specs=[anywhere] * len(args), o...  20.7 us
    ppermute x8, starting transfers between devices, across(): lax.ppermute(value, 'expert', [(e, (e + side) % experts) for e in range(e...  12.3 us
    pallas_call x7, Pallas kernels, local_call(): pl.pallas_call(kernel, out_shape=outs, in_specs=[SMEM] + [VMEM] * len(arg...  12.1 us
    broadcast_in_dim x1, other arithmetic, on_device(): summed[2 * hidden_units:].astype(F32)[None]  6.07 us
  transfers between devices with their start and end apart: 16, of which 10 were waited for; matrix products, arithmetic and copies ran while one was open for 10% of the time, Pallas kernels for 12%

profile of v12, /device:TPU:0, one launch (start us, length us, event | category | flops | bytes accessed | tf_op | source)
XLA Modules:
  0.0 212.3 jit_solution(17850130649482138735)
XLA Ops:
  12.8 6.3 %all-to-all-start = ((bf16[8,64,2048]{2,1,0:T(8,128)(2,1)}), bf16[8,64,2048]{2,1,0:T(8,128)(2,1)}, u32[]{:S(2)}, u32[]{:S(2)}) async-start(bf16[8,64,2048]{2,1,0:T(8,128)(2,1)} %bitcast.4), calls=%async_computation | async-start | bytes 4194304 | tf_op jit(solution)/shard_map/all_to_all | solution.py:256
  19.1 2.7 %collective-permute-start = (bf16[128,2048]{1,0:T(8,128)(2,1)S(1)}, bf16[128,2048]{1,0:T(8,128)(2,1)S(1)}, u32[]{:S(2)}, u32[]{:S(2)}) collective-permute-start(bf16[128,2048]{1,0:T(8,128)(2,1)S(1)} %copy-done.3), channel_id=1, source_target_pairs={{0,8},{1,9},{2,10},{3,11},{4,12},{5,13},{6,14},{7,15},{8,0},{9,1},... | collective-permute-start | bytes 1572872 | tf_op jit(solution)/shard_map/ppermute | solution.py:252
  22.2 2.6 %collective-permute-start.1 = (f32[4,128]{1,0:T(4,128)S(1)}, f32[4,128]{1,0:T(4,128)S(1)}, u32[]{:S(2)}, u32[]{:S(2)}) collective-permute-start(f32[4,128]{1,0:T(4,128)S(1)} %pad_maximum_fusion.3.refs_0_.refs_1_.meta), channel_id=1, source_target_pairs={{0,8},{1,9},{2,10},{3,11},{4,12},{5,13},{6,14},{7,15},{8,0},{9,1},... | collective-permute-start | bytes 6152 | tf_op jit(solution)/shard_map/ppermute | solution.py:252
  24.8 34.0 %collective-permute-done.1.refs_0_.meta = f32[4,128]{1,0:T(4,128)S(1)} collective-permute-done((f32[4,128]{1,0:T(4,128)S(1)}, f32[4,128]{1,0:T(4,128)S(1)}, u32[]{:S(2)}, u32[]{:S(2)}) %collective-permute-start.1) | collective-permute-done | bytes 2080 | tf_op jit(solution)/shard_map/ppermute | solution.py:252
  62.5 8.1 %all-to-all-start.1 = ((bf16[8,32,2048]{2,1,0:T(8,128)(2,1)}), bf16[8,32,2048]{2,1,0:T(8,128)(2,1)S(1)}, u32[]{:S(2)}, u32[]{:S(2)}) async-start(bf16[8,32,2048]{2,1,0:T(8,128)(2,1)} %bitcast.8), calls=%async_computation.1 | async-start | bytes 2097152 | tf_op jit(solution)/shard_map/all_to_all | solution.py:256
  70.6 16.1 %collective-permute-done.3.refs_2_.two = bf16[64,2048]{1,0:T(8,128)(2,1)S(1)} collective-permute-done((bf16[64,2048]{1,0:T(8,128)(2,1)S(1)}, bf16[64,2048]{1,0:T(8,128)(2,1)S(1)}, u32[]{:S(2)}, u32[]{:S(2)}) %collective-permute-start.3) | collective-permute-done | bytes 262176 | tf_op jit(solution)/shard_map/ppermute | solution.py:252
  88.2 3.1 %fusion.11 = (bf16[8,1,32,2048]{3,2,1,0:T(8,128)(2,1)}, bf16[8,1,32,2048]{3,2,1,0:T(8,128)(2,1)}) fusion(bf16[8,2,32,2048]{3,2,1,0:T(8,128)(2,1)} %bitcast.5), kind=kLoop, calls=%fused_computation.20 | loop fusion | bytes 4194304 | tf_op jit(solution)/shard_map/slice | solution.py:287
  91.4 4.8 %all-to-all-start.2 = ((bf16[8,32,2048]{2,1,0:T(8,128)(2,1)}), bf16[8,32,2048]{2,1,0:T(8,128)(2,1)S(1)}, u32[]{:S(2)}, u32[]{:S(2)}) async-start(bf16[8,32,2048]{2,1,0:T(8,128)(2,1)} %bitcast.12), calls=%async_computation.2 | async-start | bytes 2097152 | tf_op jit(solution)/shard_map/all_to_all | solution.py:256
  96.2 4.1 %fusion.2.refs_2_ = f32[512,704]{1,0:T(8,128)S(1)} fusion(bf16[1,2048,704]{1,2,0:T(8,128)(2,1)} %param.10, bf16[256,2048]{1,0:T(8,128)(2,1)S(1)} %bitcast.60, bf16[256,2048]{1,0:T(8,128)(2,1)} %bitcast.63), kind=kOutput, calls=%fused_computation.2 | convolution fusion | flops 1480589312 | bytes 6422528 | tf_op jit(solution)/shard_map/dot_general | solution.py:297
  100.4 3.0 %multiply_convert_fusion = (bf16[512,704]{1,0:T(8,128)(2,1)S(1)}, f32[512,704]{1,0:T(8,128)}) fusion(f32[512,704]{1,0:T(8,128)S(1)} %fusion.2.refs_2_, bf16[1,2048,704]{1,2,0:T(8,128)(2,1)S(1)} %copy-done.7, bf16[256,2048]{1,0:T(8,128)(2,1)S(1)} %bitcast.61, bf16[256,2048]{1,0:T(8,128)(2,1)S(1)} %bitcast.65), kind=kOutput, calls=%fused_computation.9 | convolution fusion | flops 1482752000 | bytes 8585216 | tf_op jit(solution)/shard_map/dot_general | solution.py:298
  108.5 3.9 %all-to-all-start.3 = ((bf16[8,32,2048]{2,1,0:T(8,128)(2,1)}), bf16[8,32,2048]{2,1,0:T(8,128)(2,1)S(1)}, u32[]{:S(2)}, u32[]{:S(2)}) async-start(bf16[8,32,2048]{2,1,0:T(8,128)(2,1)} %bitcast.72), calls=%async_computation.3 | async-start | bytes 2097152 | tf_op jit(solution)/shard_map/all_to_all | solution.py:256
  112.5 10.6 %shard_map.121 = (bf16[256,2048]{1,0:T(8,128)(2,1)}, bf16[256,2048]{1,0:T(8,128)(2,1)}, bf16[512,704]{1,0:T(8,128)(2,1)}, bf16[512,704]{1,0:T(8,128)(2,1)}) custom-call(bf16[704,2048]{1,0:T(8,128)(2,1)} %bitcast.68, bf16[256,2048]{1,0:T(8,128)(2,1)} %bitcast.58, f32[512,704]{1,0:T(8,128)} %copy-done.9, f32[512,704]{1,0:T(8,128)} %get-tuple-element.124.refs_3_, ...), custom_call_target="tpu_custom_call" | custom-call | flops 1 | bytes 1 | tf_op jit(solution)/shard_map/pallas_call | solution.py:224
  123.1 3.0 %all-to-all-done.3 = bf16[8,32,2048]{2,1,0:T(8,128)(2,1)S(1)} async-done(((bf16[8,32,2048]{2,1,0:T(8,128)(2,1)}), bf16[8,32,2048]{2,1,0:T(8,128)(2,1)S(1)}, u32[]{:S(2)}, u32[]{:S(2)}) %all-to-all-start.3) | async-done | bytes 1048608 | tf_op jit(solution)/shard_map/all_to_all | solution.py:256
  127.6 3.6 %all-to-all-start.4 = ((bf16[8,32,2048]{2,1,0:T(8,128)(2,1)}), bf16[8,32,2048]{2,1,0:T(8,128)(2,1)S(1)}, u32[]{:S(2)}, u32[]{:S(2)}) async-start(bf16[8,32,2048]{2,1,0:T(8,128)(2,1)} %bitcast.71), calls=%async_computation.4 | async-start | bytes 2097152 | tf_op jit(solution)/shard_map/all_to_all | solution.py:256
  131.2 2.5 %collective-permute-start.4 = (bf16[64,2048]{1,0:T(8,128)(2,1)S(1)}, bf16[64,2048]{1,0:T(8,128)(2,1)S(1)}, u32[]{:S(2)}, u32[]{:S(2)}) collective-permute-start(bf16[64,2048]{1,0:T(8,128)(2,1)S(1)} %get-tuple-element.78), channel_id=1, source_target_pairs={{0,8},{1,9},{2,10},{3,11},{4,12},{5,13},{6,14},{7,15},{8,0},{9,1},... | collective-permute-start | bytes 786440 | tf_op jit(solution)/shard_map/ppermute | solution.py:252
  133.7 10.0 %shard_map.123 = bf16[2112,2048]{1,0:T(8,128)(2,1)} custom-call(bf16[256,2048]{1,0:T(8,128)(2,1)} %bitcast.64, bf16[256,2048]{1,0:T(8,128)(2,1)} %bitcast.62, bf16[512,704]{1,0:T(8,128)(2,1)} %get-tuple-element.75.refs_2_, bf16[512,704]{1,0:T(8,128)(2,1)} %get-tuple-element.76.refs_3_, bf16[256,2048]{1,0:T(8,128)(2,1)} %bitcast.59, ...), custom_call_target="tpu_custom_call" | custom-call | flops 1 | bytes 1 | tf_op jit(solution)/shard_map/pallas_call | solution.py:224
  143.8 3.5 %collective-permute-done.4.one = bf16[64,2048]{1,0:T(8,128)(2,1)S(1)} collective-permute-done((bf16[64,2048]{1,0:T(8,128)(2,1)S(1)}, bf16[64,2048]{1,0:T(8,128)(2,1)S(1)}, u32[]{:S(2)}, u32[]{:S(2)}) %collective-permute-start.4) | collective-permute-done | bytes 262176 | tf_op jit(solution)/shard_map/ppermute | solution.py:252
  149.6 5.5 %all-to-all-start.5 = ((bf16[8,32,2048]{2,1,0:T(8,128)(2,1)}), bf16[8,32,2048]{2,1,0:T(8,128)(2,1)S(1)}, u32[]{:S(2)}, u32[]{:S(2)}) async-start(bf16[8,32,2048]{2,1,0:T(8,128)(2,1)} %bitcast.70), calls=%async_computation.5 | async-start | bytes 2097152 | tf_op jit(solution)/shard_map/all_to_all | solution.py:256
  155.6 2.5 %collective-permute-start.6 = (f32[128,128]{1,0:T(8,128)}, f32[128,128]{1,0:T(8,128)S(1)}, u32[]{:S(2)}, u32[]{:S(2)}) collective-permute-start(f32[128,128]{1,0:T(8,128)} %get-tuple-element.82), channel_id=1, source_target_pairs={{0,8},{1,9},{2,10},{3,11},{4,12},{5,13},{6,14},{7,15},{8,0},{9,1},... | collective-permute-start | bytes 196616 | tf_op jit(solution)/shard_map/ppermute | solution.py:252
  158.1 16.0 %all-to-all-done.5 = bf16[8,32,2048]{2,1,0:T(8,128)(2,1)S(1)} async-done(((bf16[8,32,2048]{2,1,0:T(8,128)(2,1)}), bf16[8,32,2048]{2,1,0:T(8,128)(2,1)S(1)}, u32[]{:S(2)}, u32[]{:S(2)}) %all-to-all-start.5) | async-done | bytes 1048608 | tf_op jit(solution)/shard_map/all_to_all | solution.py:256
  174.6 3.6 %all-to-all-start.6 = ((bf16[8,32,2048]{2,1,0:T(8,128)(2,1)}), bf16[8,32,2048]{2,1,0:T(8,128)(2,1)S(1)}, u32[]{:S(2)}, u32[]{:S(2)}) async-start(bf16[8,32,2048]{2,1,0:T(8,128)(2,1)} %bitcast.69), calls=%async_computation.6 | async-start | bytes 2097152 | tf_op jit(solution)/shard_map/all_to_all | solution.py:256
  179.4 2.6 %shard_map.125 = (bf16[128,2048]{1,0:T(8,128)(2,1)}, f32[128,128]{1,0:T(8,128)S(1)}) custom-call(s32[1]{0:T(128)} %bitcast.me_ref, f32[4,128]{1,0:T(4,128)S(1)} %pad_maximum_fusion.3.refs_0_.refs_1_.meta, bf16[128,2048]{1,0:T(8,128)(2,1)S(1)} %copy-done.1, bf16[256,2048]{1,0:T(8,128)(2,1)S(1)} %bitcast.51, bf16[64,2048]{1,0:T(8,128)(2,1)S(1)} %collective-permute-done.4.one, ...), custom_call_target="tpu_custom_call" | custom-call | flops 268435456 | bytes 2754560 | tf_op jit(solution)/shard_map/pallas_call | solution.py:20
  182.0 6.1 %fusion.4 = (f32[1,704,1024]{2,1,0:T(8,128)}, f32[1,1024,704]{1,2,0:T(8,128)}, f32[1,1024,704]{1,2,0:T(8,128)}) fusion(bf16[2112,1024]{1,0:T(8,128)(2,1)} %reduce-scatter.2.cloned.1.call-done), kind=kLoop, calls=%fused_computation.11 | loop fusion | flops 2162688 | bytes 12976128 | tf_op jit(solution)/shard_map/broadcast_in_dim | solution.py:359
  188.0 12.7 %all-to-all-done.6 = bf16[8,32,2048]{2,1,0:T(8,128)(2,1)S(1)} async-done(((bf16[8,32,2048]{2,1,0:T(8,128)(2,1)}), bf16[8,32,2048]{2,1,0:T(8,128)(2,1)S(1)}, u32[]{:S(2)}, u32[]{:S(2)}) %all-to-all-start.6) | async-done | bytes 1048608 | tf_op jit(solution)/shard_map/all_to_all | solution.py:256
  (50 shorter events, 27.1 us)
Async XLA Ops:
  12.8 6.3 %copy-start.3 = (bf16[128,2048]{1,0:T(8,128)(2,1)S(1)}, bf16[128,2048]{1,0:T(8,128)(2,1)}, u32[]{:S(2)}) copy-start(bf16[128,2048]{1,0:T(8,128)(2,1)} %refs_2_.1) | copy-start | bytes 1572868
  12.8 9.0 %copy-start.1 = (bf16[128,2048]{1,0:T(8,128)(2,1)S(1)}, bf16[128,2048]{1,0:T(8,128)(2,1)}, u32[]{:S(2)}) copy-start(bf16[128,2048]{1,0:T(8,128)(2,1)} %block.1) | copy-start | bytes 1572868
  12.8 48.1 %all-to-all-start = ((bf16[8,64,2048]{2,1,0:T(8,128)(2,1)}), bf16[8,64,2048]{2,1,0:T(8,128)(2,1)}, u32[]{:S(2)}, u32[]{:S(2)}) async-start(bf16[8,64,2048]{2,1,0:T(8,128)(2,1)} %bitcast.4), calls=%async_computation | async-start | bytes 4194304 | tf_op jit(solution)/shard_map/all_to_all | solution.py:256
  19.1 39.7 %collective-permute-start = (bf16[128,2048]{1,0:T(8,128)(2,1)S(1)}, bf16[128,2048]{1,0:T(8,128)(2,1)S(1)}, u32[]{:S(2)}, u32[]{:S(2)}) collective-permute-start(bf16[128,2048]{1,0:T(8,128)(2,1)S(1)} %copy-done.3), channel_id=1, source_target_pairs={{0,8},{1,9},{2,10},{3,11},{4,12},{5,13},{6,14},{7,15},{8,0},{9,1},... | collective-permute-start | bytes 1572872 | tf_op jit(solution)/shard_map/ppermute | solution.py:252
  21.9 37.0 %collective-permute-start.2 = (bf16[64,2048]{1,0:T(8,128)(2,1)S(1)}, bf16[64,2048]{1,0:T(8,128)(2,1)S(1)}, u32[]{:S(2)}, u32[]{:S(2)}) collective-permute-start(bf16[64,2048]{1,0:T(8,128)(2,1)S(1)} %get-tuple-element.122), channel_id=1, source_target_pairs={{0,8},{1,9},{2,10},{3,11},{4,12},{5,13},{6,14},{7,15},{8,0},{9,1},... | collective-permute-start | bytes 786440 | tf_op jit(solution)/shard_map/ppermute | solution.py:252
  22.2 36.5 %collective-permute-start.1 = (f32[4,128]{1,0:T(4,128)S(1)}, f32[4,128]{1,0:T(4,128)S(1)}, u32[]{:S(2)}, u32[]{:S(2)}) collective-permute-start(f32[4,128]{1,0:T(4,128)S(1)} %pad_maximum_fusion.3.refs_0_.refs_1_.meta), channel_id=1, source_target_pairs={{0,8},{1,9},{2,10},{3,11},{4,12},{5,13},{6,14},{7,15},{8,0},{9,1},... | collective-permute-start | bytes 6152 | tf_op jit(solution)/shard_map/ppermute | solution.py:252
  62.5 28.9 %all-to-all-start.1 = ((bf16[8,32,2048]{2,1,0:T(8,128)(2,1)}), bf16[8,32,2048]{2,1,0:T(8,128)(2,1)S(1)}, u32[]{:S(2)}, u32[]{:S(2)}) async-start(bf16[8,32,2048]{2,1,0:T(8,128)(2,1)} %bitcast.8), calls=%async_computation.1 | async-start | bytes 2097152 | tf_op jit(solution)/shard_map/all_to_all | solution.py:256
  70.6 16.1 %collective-permute-start.3 = (bf16[64,2048]{1,0:T(8,128)(2,1)S(1)}, bf16[64,2048]{1,0:T(8,128)(2,1)S(1)}, u32[]{:S(2)}, u32[]{:S(2)}) collective-permute-start(bf16[64,2048]{1,0:T(8,128)(2,1)S(1)} %get-tuple-element.121), channel_id=1, source_target_pairs={{0,8},{1,9},{2,10},{3,11},{4,12},{5,13},{6,14},{7,15},{8,0},{9,1},... | collective-permute-start | bytes 786440 | tf_op jit(solution)/shard_map/ppermute | solution.py:252
  91.3 9.0 %copy-start.5 = (bf16[8,32,2048]{2,1,0:T(8,128)(2,1)}, bf16[8,32,2048]{2,1,0:T(8,128)(2,1)S(1)}, u32[]{:S(2)}) copy-start(bf16[8,32,2048]{2,1,0:T(8,128)(2,1)S(1)} %all-to-all-done.1) | copy-start | bytes 3145732
  91.4 17.2 %all-to-all-start.2 = ((bf16[8,32,2048]{2,1,0:T(8,128)(2,1)}), bf16[8,32,2048]{2,1,0:T(8,128)(2,1)S(1)}, u32[]{:S(2)}, u32[]{:S(2)}) async-start(bf16[8,32,2048]{2,1,0:T(8,128)(2,1)} %bitcast.12), calls=%async_computation.2 | async-start | bytes 2097152 | tf_op jit(solution)/shard_map/all_to_all | solution.py:256
  96.2 4.2 %copy-start.6 = (bf16[8,1,32,2048]{3,2,1,0:T(8,128)(2,1)S(1)}, bf16[8,1,32,2048]{3,2,1,0:T(8,128)(2,1)}, u32[]{:S(2)}) copy-start(bf16[8,1,32,2048]{3,2,1,0:T(8,128)(2,1)} %get-tuple-element.120) | copy-start | bytes 3145732
  96.2 4.2 %copy-start.7 = (bf16[1,2048,704]{1,2,0:T(8,128)(2,1)S(1)}, bf16[1,2048,704]{1,2,0:T(8,128)(2,1)}, u32[]{:S(2)}) copy-start(bf16[1,2048,704]{1,2,0:T(8,128)(2,1)} %param.11) | copy-start | bytes 8650756
  100.4 3.1 %copy-start.9 = (f32[512,704]{1,0:T(8,128)}, f32[512,704]{1,0:T(8,128)S(1)}, u32[]{:S(2)}) copy-start(f32[512,704]{1,0:T(8,128)S(1)} %fusion.2.refs_2_) | copy-start | bytes 4325380
  100.4 3.0 %copy-start.8 = (bf16[1,704,2048]{2,1,0:T(8,128)(2,1)S(1)}, bf16[1,704,2048]{2,1,0:T(8,128)(2,1)}, u32[]{:S(2)}) copy-start(bf16[1,704,2048]{2,1,0:T(8,128)(2,1)} %param.12) | copy-start | bytes 8650756
  108.5 3.9 %copy-start.4 = (bf16[8,32,2048]{2,1,0:T(8,128)(2,1)}, bf16[8,32,2048]{2,1,0:T(8,128)(2,1)S(1)}, u32[]{:S(2)}) copy-start(bf16[8,32,2048]{2,1,0:T(8,128)(2,1)S(1)} %all-to-all-done.2) | copy-start | bytes 3145732
  108.5 17.6 %all-to-all-start.3 = ((bf16[8,32,2048]{2,1,0:T(8,128)(2,1)}), bf16[8,32,2048]{2,1,0:T(8,128)(2,1)S(1)}, u32[]{:S(2)}, u32[]{:S(2)}) async-start(bf16[8,32,2048]{2,1,0:T(8,128)(2,1)} %bitcast.72), calls=%async_computation.3 | async-start | bytes 2097152 | tf_op jit(solution)/shard_map/all_to_all | solution.py:256
  127.6 22.0 %all-to-all-start.4 = ((bf16[8,32,2048]{2,1,0:T(8,128)(2,1)}), bf16[8,32,2048]{2,1,0:T(8,128)(2,1)S(1)}, u32[]{:S(2)}, u32[]{:S(2)}) async-start(bf16[8,32,2048]{2,1,0:T(8,128)(2,1)} %bitcast.71), calls=%async_computation.4 | async-start | bytes 2097152 | tf_op jit(solution)/shard_map/all_to_all | solution.py:256
  131.1 50.8 %reduce-scatter.2.cloned.1.call-start = ((), (), s32[]{:S(2)}) async-start(), calls=%async_computation.8 | async-start | bytes 12976128 | tf_op jit(solution)/shard_map/reduce_scatter | solution.py:343
  131.2 16.1 %collective-permute-start.4 = (bf16[64,2048]{1,0:T(8,128)(2,1)S(1)}, bf16[64,2048]{1,0:T(8,128)(2,1)S(1)}, u32[]{:S(2)}, u32[]{:S(2)}) collective-permute-start(bf16[64,2048]{1,0:T(8,128)(2,1)S(1)} %get-tuple-element.78), channel_id=1, source_target_pairs={{0,8},{1,9},{2,10},{3,11},{4,12},{5,13},{6,14},{7,15},{8,0},{9,1},... | collective-permute-start | bytes 786440 | tf_op jit(solution)/shard_map/ppermute | solution.py:252
  149.6 24.5 %all-to-all-start.5 = ((bf16[8,32,2048]{2,1,0:T(8,128)(2,1)}), bf16[8,32,2048]{2,1,0:T(8,128)(2,1)S(1)}, u32[]{:S(2)}, u32[]{:S(2)}) async-start(bf16[8,32,2048]{2,1,0:T(8,128)(2,1)} %bitcast.70), calls=%async_computation.5 | async-start | bytes 2097152 | tf_op jit(solution)/shard_map/all_to_all | solution.py:256
  155.1 19.5 %collective-permute-start.5 = (bf16[64,2048]{1,0:T(8,128)(2,1)}, bf16[64,2048]{1,0:T(8,128)(2,1)}, u32[]{:S(2)}, u32[]{:S(2)}) collective-permute-start(bf16[64,2048]{1,0:T(8,128)(2,1)} %get-tuple-element.81), channel_id=1, source_target_pairs={{0,8},{1,9},{2,10},{3,11},{4,12},{5,13},{6,14},{7,15},{8,0},{9,1},... | collective-permute-start | bytes 786440 | tf_op jit(solution)/shard_map/ppermute | solution.py:252
  155.6 19.0 %collective-permute-start.6 = (f32[128,128]{1,0:T(8,128)}, f32[128,128]{1,0:T(8,128)S(1)}, u32[]{:S(2)}, u32[]{:S(2)}) collective-permute-start(f32[128,128]{1,0:T(8,128)} %get-tuple-element.82), channel_id=1, source_target_pairs={{0,8},{1,9},{2,10},{3,11},{4,12},{5,13},{6,14},{7,15},{8,0},{9,1},... | collective-permute-start | bytes 196616 | tf_op jit(solution)/shard_map/ppermute | solution.py:252
  174.6 26.1 %all-to-all-start.6 = ((bf16[8,32,2048]{2,1,0:T(8,128)(2,1)}), bf16[8,32,2048]{2,1,0:T(8,128)(2,1)S(1)}, u32[]{:S(2)}, u32[]{:S(2)}) async-start(bf16[8,32,2048]{2,1,0:T(8,128)(2,1)} %bitcast.69), calls=%async_computation.6 | async-start | bytes 2097152 | tf_op jit(solution)/shard_map/all_to_all | solution.py:256
  178.2 24.9 %collective-permute-start.7 = (bf16[128,2048]{1,0:T(8,128)(2,1)S(1)}, bf16[128,2048]{1,0:T(8,128)(2,1)}, u32[]{:S(2)}, u32[]{:S(2)}) collective-permute-start(bf16[128,2048]{1,0:T(8,128)(2,1)S(1)} %shard_map.124), channel_id=1, source_target_pairs={{0,8},{1,9},{2,10},{3,11},{4,12},{5,13},{6,14},{7,15},{8,0},{9,1},... | collective-permute-start | bytes 1572872 | tf_op jit(solution)/shard_map/ppermute | solution.py:252
  (3 other events, 4.0 us)
Sparse Core Ops, SparseCore 0:
  149.7 17.0 reduce-scatter.1

commit v13 on v11

--- a/solution.py
+++ b/solution.py
@@ -56,7 +56,7 @@
 
 def pick_kernel(top, side, capacity, scaled, me_ref, *refs):
     count = len(scaled)
-    metas, blocks, out = refs[:count], refs[count : 2 * count], refs[2 * count]
+    metas, blocks, out = refs[:count], refs[count:-1], refs[-1]
     tables = slot_tables(me_ref[0], metas, top, side, capacity)
     held = jnp.concatenate([functools.reduce(lambda p, q: p + q, ks) for ks in tables], 1)
     held = held.astype(BF16)
@@ -88,19 +88,23 @@
         out[:, c:e] = picked_sum(held, back, c, e).astype(BF16)
 
 
-def mix(top, table, meta, block, back, out, grads, far=None, far_grads=None):
+def mix(top, table, meta, blocks, back, outs, grads, fars=(), far_grads=None):
     tok = meta.shape[1]
     gates = [meta[top + k : top + k + 1, :] for k in range(top)]
     gates = [jnp.transpose(jnp.broadcast_to(g, (8, tok)))[:, :1] for g in gates]
     sums = [jnp.zeros((tok, 1), F32) for _ in range(top)]
-    for c, e in strips(out.shape[1]):
-        cotangent = block[:, c:e].astype(F32)
-        mixed = 0.0 if far is None else far[:, c:e].astype(F32)
+    for c, e in strips(back.shape[1]):
+        cotangent = jnp.concatenate([ref[:, c:e] for ref in blocks], 0).astype(F32)
+        mixed = 0.0
+        if fars:
+            mixed = jnp.concatenate([ref[:, c:e] for ref in fars], 0).astype(F32)
         for k in range(top):
             got = picked_sum(table[k], back, c, e)
             mixed += gates[k] * got
             sums[k] += jnp.sum(cotangent * got, 1, keepdims=True)
-        out[:, c:e] = mixed.astype(BF16)
+        for n, out in enumerate(outs):
+            rows = out.shape[0]
+            out[:, c:e] = mixed[n * rows : (n + 1) * rows].astype(BF16)
     lane = lax.broadcasted_iota(jnp.int32, (tok, LANES), 1)
     grad = jnp.zeros((tok, LANES), F32) if far_grads is None else far_grads[...]
     for k in range(top):
@@ -108,9 +112,18 @@
     grads[...] = grad
 
 
-def mix_kernel(top, side, capacity, me_ref, meta, block, back, out, grads):
-    (table,) = slot_tables(me_ref[0], [meta], top, side, capacity)
-    mix(top, table, meta, block, back, out, grads)
+def mix_kernel(
+    top, side, capacity, me_ref, meta, meta_far, one, two, back, out, grads
+):
+    tables = slot_tables(me_ref[0], [meta, meta_far], top, side, capacity)
+    mix(top, tables[1], meta_far, (one, two), back, (out,), grads)
+
+
+def mix_last_kernel(
+    top, side, capacity, me_ref, meta, meta_far, block, back, far, far_grads, out, grads
+):
+    tables = slot_tables(me_ref[0], [meta, meta_far], top, side, capacity)
+    mix(top, tables[0], meta, (block,), back, (out,), grads, (far,), far_grads)
 
 
 def sum_last_kernel(top, side, capacity, me_ref, meta, back, far, out):
@@ -118,13 +131,6 @@
     held = functools.reduce(lambda p, q: p + q, table)
     for c, e in strips(out.shape[1]):
         out[:, c:e] = (picked_sum(held, back, c, e) + far[:, c:e].astype(F32)).astype(BF16)
-
-
-def mix_last_kernel(
-    top, side, capacity, me_ref, meta, block, back, far, far_grads, out, grads
-):
-    (table,) = slot_tables(me_ref[0], [meta], top, side, capacity)
-    mix(top, table, meta, block, back, out, grads, far, far_grads)
 
 
 def fetch(sources, targets, sems):
@@ -135,27 +141,62 @@
     return copies
 
 
+ACROSS_LAST = (((1,), (1,)), ((), ()))
+
+
+def forward_kernel(side, *refs):
+    sources, outs = refs[:5], refs[5:9]
+    wg, wu, wd, x, gate, up, hidden, y, sems, out_sems = refs[9:]
+    rows, feature = x.shape
+    units, half = gate.shape[1], rows // 2
+    targets = [wg, x.at[pl.ds(0, half)], x.at[pl.ds(half, half)], wu, wd]
+    loads = fetch(sources, targets, sems)
+    for load in loads[:3]:
+        load.wait()
+    for c, e in strips(units, 256):
+        gate[:, c:e] = lax.dot_general(
+            x[...], wg[c:e, :], ACROSS_LAST, preferred_element_type=F32
+        )
+    loads[3].wait()
+    for c, e in strips(units, 256):
+        got = lax.dot_general(x[...], wu[c:e, :], ACROSS_LAST, preferred_element_type=F32)
+        up[:, c:e] = got
+        pre = gate[:, c:e]
+        hidden[:, c:e] = (pre * (1.0 / (1.0 + jnp.exp(-pre))) * got).astype(BF16)
+    copies = [
+        pltpu.make_async_copy(source, out, out_sems.at[n])
+        for n, (source, out) in enumerate(zip((gate, up, hidden, y), outs))
+    ]
+    for copy in copies[:3]:
+        copy.start()
+    loads[4].wait()
+    for c, e in strips(feature):
+        got = jnp.dot(hidden[...], wd[:, c:e], preferred_element_type=F32)
+        pair = [
+            part.reshape(side, 1, half // side, e - c) for part in (got[:half], got[half:])
+        ]
+        y[:, c:e] = jnp.concatenate(pair, 1).reshape(rows, e - c).astype(BF16)
+    copies[3].start()
+    for copy in copies:
+        copy.wait()
+
+
 def backward_kernel(*refs):
-    sources, (own_out, far_out, terms_out), local = refs[:10], refs[10:13], refs[13:23]
-    sems, gg, gu, dx, tiles, out_sems = refs[23:]
-    wd, d_own, gate, up, d_far, wg, wu, x_own, x_far, hidden = local
-    loads = fetch(sources, local, sems)
-    half, feature = d_own.shape
-    units = gate.shape[1]
-    across_last = (((1,), (1,)), ((), ()))
-    loads[0].wait()
-    for r, d_rows, needed in ((0, d_own, (1, 2, 3)), (half, d_far, (4,))):
-        at = slice(r, r + half)
-        for n in needed:
-            loads[n].wait()
-        for c, e in strips(units, 256):
-            back = lax.dot_general(
-                d_rows[...], wd[c:e, :], across_last, preferred_element_type=F32
-            )
-            pre = gate[at, c:e]
-            sig = 1.0 / (1.0 + jnp.exp(-pre))
-            gg[at, c:e] = (back * up[at, c:e] * (sig * (1.0 + pre * (1.0 - sig)))).astype(BF16)
-            gu[at, c:e] = (back * (pre * sig)).astype(BF16)
+    sources, (own_out, far_out, terms_out) = refs[:10], refs[10:13]
+    wd, gate, up, wg, wu, hidden, d, x, gg, gu, dx, tiles, sems, out_sems = refs[13:]
+    rows, feature = d.shape
+    units, half = gate.shape[1], rows // 2
+    first, second = pl.ds(0, half), pl.ds(half, half)
+    targets = [wd, d.at[first], d.at[second], gate, up, wg, wu, x.at[first], x.at[second], hidden]
+    loads = fetch(sources, targets, sems)
+    for load in loads[:5]:
+        load.wait()
+    for c, e in strips(units, 256):
+        back = lax.dot_general(d[...], wd[c:e, :], ACROSS_LAST, preferred_element_type=F32)
+        pre = gate[:, c:e]
+        sig = 1.0 / (1.0 + jnp.exp(-pre))
+        gg[:, c:e] = (back * up[:, c:e] * (sig * (1.0 + pre * (1.0 - sig)))).astype(BF16)
+        gu[:, c:e] = (back * (pre * sig)).astype(BF16)
     loads[5].wait()
     loads[6].wait()
     for c, e in strips(feature):
@@ -163,28 +204,23 @@
         got += jnp.dot(gu[...], wu[:, c:e], preferred_element_type=F32)
         dx[:, c:e] = got.astype(BF16)
     dx_copies = [
-        pltpu.make_async_copy(dx.at[pl.ds(half, half)], far_out, out_sems.at[2]),
-        pltpu.make_async_copy(dx.at[pl.ds(0, half)], own_out, out_sems.at[3]),
+        pltpu.make_async_copy(dx.at[second], far_out, out_sems.at[2]),
+        pltpu.make_async_copy(dx.at[first], own_out, out_sems.at[3]),
     ]
     for copy in dx_copies:
         copy.start()
-    pairs = ((gg, x_own, x_far, (7, 8)), (gu, x_own, x_far, ()), (hidden, d_own, d_far, (9,)))
+    for load in loads[7:]:
+        load.wait()
     copies = []
-    for n, (left, own, far, needed) in enumerate(pairs):
-        for m in needed:
-            loads[m].wait()
+    for n, (left, right) in enumerate(((gg, x), (gu, x), (hidden, d))):
         for r, t in strips(units, tiles.shape[1]):
             slot = len(copies) % 2
             if len(copies) > 1:
                 copies[-2].wait()
             for c, e in strips(feature, 1024):
-                got = lax.dot_general(
-                    left[:half, r:t], own[:, c:e], TRANSPOSED, preferred_element_type=F32
-                )
-                got += lax.dot_general(
-                    left[half:, r:t], far[:, c:e], TRANSPOSED, preferred_element_type=F32
-                )
-                tiles[slot, : t - r, c:e] = got.astype(BF16)
+                tiles[slot, : t - r, c:e] = lax.dot_general(
+                    left[:, r:t], right[:, c:e], TRANSPOSED, preferred_element_type=F32
+                ).astype(BF16)
             copy = pltpu.make_async_copy(
                 tiles.at[slot, pl.ds(0, t - r)],
                 terms_out.at[pl.ds(n * units + r, t - r)],
@@ -196,24 +232,14 @@
         copy.wait()
 
 
-def backward(side_rows, args):
-    half, feature = side_rows.shape
-    units = args[0].shape[0]
+def streamed_call(kernel, outs, args, scratch):
     anywhere = pl.BlockSpec(memory_space=pltpu.HBM)
     return pl.pallas_call(
-        backward_kernel,
-        out_shape=[side_rows, side_rows, jax.ShapeDtypeStruct((3 * units, feature), BF16)],
+        kernel,
+        out_shape=outs,
         in_specs=[anywhere] * len(args),
-        out_specs=[anywhere] * 3,
-        scratch_shapes=[
-            *[pltpu.VMEM(x.shape, x.dtype) for x in args],
-            pltpu.SemaphoreType.DMA((len(args),)),
-            pltpu.VMEM((2 * half, units), BF16),
-            pltpu.VMEM((2 * half, units), BF16),
-            pltpu.VMEM((2 * half, feature), BF16),
-            pltpu.VMEM((2, 256, feature), BF16),
-            pltpu.SemaphoreType.DMA((4,)),
-        ],
+        out_specs=[anywhere] * len(outs),
+        scratch_shapes=scratch,
         compiler_params=pltpu.CompilerParams(vmem_limit_bytes=60 * 1024 * 1024),
         cost_estimate=pl.CostEstimate(flops=1, bytes_accessed=1, transcendentals=0),
     )(*args)
@@ -265,69 +291,92 @@
     own = exchange(pick([meta, meta], [tokens, d_mixed], (False, True)))
     own = own.reshape(side, 2, capacity, feature)
     x_far, meta_far = after(across(tokens), across(meta))
-    x_far, d_far, own = after(x_far, across(d_mixed), own)
+    d_far = [across(d_mixed[n * (tok // 2) : (n + 1) * (tok // 2)]) for n in range(2)]
+    x_far, d_far[0], own = after(x_far, d_far[0], own)
+    x_far_rows = exchange(pick([meta_far], [x_far], (False,)))
+    d_picked, _ = after(pick([meta_far], d_far, (True,)), x_far_rows)
+    d_far_rows = exchange(d_picked)
     x_own, d_own = (own[:, n].reshape(half, feature) for n in range(2))
-    x_far_rows = exchange(pick([meta_far], [x_far], (False,)))
-    x_rows = jnp.concatenate([x_own, x_far_rows], 0)
-    d_picked, x_own, d_own, _ = after(
-        pick([meta_far], [d_far], (True,)), x_own, d_own, x_far_rows
-    )
-    d_far_rows = exchange(d_picked)
-
-    gate_matrix, up_matrix, down_matrix = w_gate[0], w_up[0], w_down[0]
-    hidden_units = gate_matrix.shape[1]
-    gate_pre = jnp.dot(x_rows, gate_matrix, preferred_element_type=F32)
-    up_pre = jnp.dot(x_rows, up_matrix, preferred_element_type=F32)
-    hidden = (gate_pre * jax.nn.sigmoid(gate_pre) * up_pre).astype(BF16)
-    y_far, y_own = (
-        jnp.dot(part, down_matrix, preferred_element_type=F32).astype(BF16)
-        for part in (hidden[half:], hidden[:half])
-    )
-    y_far, y_own, d_far_rows = after(y_far, y_own, d_far_rows)
-    y_far_back = exchange(y_far)
-
-    dx_own, dx_far, terms = backward(
-        shape((half, feature), BF16),
+
+    gate_matrix, up_matrix, down_matrix = w_gate[0].T, w_up[0].T, w_down[0]
+    units, n_rows = gate_matrix.shape[0], 2 * half
+    weight = pltpu.VMEM((units, feature), BF16)
+    inner, wide = (n_rows, units), pltpu.VMEM((n_rows, feature), BF16)
+    gate_pre, up_pre, hidden, y = streamed_call(
+        functools.partial(forward_kernel, side),
+        [shape(inner, F32), shape(inner, F32), shape(inner, BF16), shape((n_rows, feature), BF16)],
+        [gate_matrix, x_own, x_far_rows, up_matrix, down_matrix],
+        [
+            *[weight] * 3,
+            wide,
+            pltpu.VMEM(inner, F32),
+            pltpu.VMEM(inner, F32),
+            pltpu.VMEM(inner, BF16),
+            wide,
+            pltpu.SemaphoreType.DMA((5,)),
+            pltpu.SemaphoreType.DMA((4,)),
+        ],
+    )
+    y, d_far_rows = after(y, d_far_rows)
+    y_back = exchange(y)
+
+    dx_own, dx_far, terms = streamed_call(
+        backward_kernel,
+        [shape((half, feature), BF16)] * 2 + [shape((3 * units, feature), BF16)],
         [
             down_matrix,
             d_own,
+            d_far_rows,
             gate_pre,
             up_pre,
-            d_far_rows,
-            gate_matrix.T,
-            up_matrix.T,
+            gate_matrix,
+            up_matrix,
             x_own,
             x_far_rows,
             hidden,
         ],
-    )
-    dx_own, dx_far, terms, y_far_back = after(dx_own, dx_far, terms, y_far_back)
+        [
+            weight,
+            pltpu.VMEM(inner, F32),
+            pltpu.VMEM(inner, F32),
+            weight,
+            weight,
+            pltpu.VMEM(inner, BF16),
+            wide,
+            wide,
+            pltpu.VMEM(inner, BF16),
+            pltpu.VMEM(inner, BF16),
+            wide,
+            pltpu.VMEM((2, 256, feature), BF16),
+            pltpu.SemaphoreType.DMA((10,)),
+            pltpu.SemaphoreType.DMA((4,)),
+        ],
+    )
+    dx_own, dx_far, terms, y_back = after(dx_own, dx_far, terms, y_back)
     summed = lax.psum_scatter(terms, "dp", scatter_dimension=1, tiled=True)
 
     token_rows, grad_rows = ((tok, feature), BF16), ((tok, LANES), F32)
     work = 2 * half * tok * feature
     mixed_far, grads_far = call(
-        mix_kernel, [token_rows, grad_rows], [meta_far, d_far, y_far_back], top * work
+        mix_kernel, [token_rows, grad_rows], [meta, meta_far, *d_far, y_back], 2 * top * work
     )
     dx_far, mixed_far, grads_far = after(dx_far, mixed_far, grads_far)
     dx_far_back = exchange(dx_far)
     (tokens_far,) = call(sum_kernel, [token_rows], [meta_far, dx_far_back], work)
-    tokens_far, y_own, mixed_far, grads_far = after(
-        tokens_far, y_own, across(mixed_far), across(grads_far)
-    )
-    y_own_back = exchange(y_own)
-    y_own_back, dx_own = after(y_own_back, dx_own)
+    tokens_far, dx_own, mixed_far, grads_far = after(
+        tokens_far, dx_own, across(mixed_far), across(grads_far)
+    )
     dx_own_back = exchange(dx_own)
     mixed, grads = call(
         mix_last_kernel,
         [token_rows, grad_rows],
-        [meta, d_mixed, y_own_back, mixed_far, grads_far],
-        top * work,
+        [meta, meta_far, d_mixed, y_back, mixed_far, grads_far],
+        2 * top * work,
     )
     weight_grads = (
-        summed[:hidden_units].astype(F32).T[None],
-        summed[hidden_units : 2 * hidden_units].astype(F32).T[None],
-        summed[2 * hidden_units :].astype(F32)[None],
+        summed[:units].astype(F32).T[None],
+        summed[units : 2 * units].astype(F32).T[None],
+        summed[2 * units :].astype(F32)[None],
     )
     dx_own_back, mixed, grads, *weight_grads = after(dx_own_back, mixed, grads, *weight_grads)
     (d_tokens,) = call(

time: 214 us -> 211 us (0.986)
  blocking collectives: 16.4 us -> 0 us
  Pallas kernels: 28 us -> 42.2 us
  matrix products: 11 us -> 0 us
  waiting for transfers between devices: 88.7 us -> 96.8 us
  starting transfers between devices: 39.4 us -> 42.4 us
    all_to_all x1 -> x0, blocking collectives: 16.4 us -> none  [exchange(): lax.all_to_all(shaped, 'expert', 0, 0, axis_index_groups=sets, tiled=True)]
    pallas_call x1 -> x2, Pallas kernels: 17.5 us -> 28.5 us  [streamed_call(): pl.pallas_call(kernel, out_shape=outs, in_specs=[anywhere] * len(args), o...]
    dot_general x4 -> x0, matrix products: 11 us -> none  [the longest x1 4.11 us: on_device(): gate_pre = jnp.dot(x_rows, gate_matrix, preferred_element_type=F32)]
    ppermute x6 -> x7, waiting for transfers between devices: 46.5 us -> 54.3 us  [across(): lax.ppermute(value, 'expert', [(e, (e + side) % experts) for e in range(e...]
    pallas_call x7, Pallas kernels: 10.5 us -> 13.7 us  [local_call(): pl.pallas_call(kernel, out_shape=outs, in_specs=[SMEM] + [VMEM] * len(arg...]
    ppermute x6 -> x7, starting transfers between devices: 8.57 us -> 9.85 us  [across(): lax.ppermute(value, 'expert', [(e, (e + side) % experts) for e in range(e...]
    unnamed x25 -> x15, local copies, waits for them, and re-layouts: 4.59 us -> 4.55 us
  transfers between devices with their start and end apart: 13 -> 14, of which waited for: 8 -> 9; matrix products, arithmetic and copies ran while one was open for 10% -> 5% of each run, Pallas kernels for 10% -> 17%
where the time goes in v13:
time: 211 us
  waiting for transfers between devices  96.8 us (46%)
  starting transfers between devices  42.4 us (20%)
  Pallas kernels  42.2 us (20%)
  between operations  14.1 us (7%)
  local copies, waits for them, and re-layouts  7.7 us (4%)
  other arithmetic  7.44 us (4%)
    ppermute x7, waiting for transfers between devices, across(): lax.ppermute(value, 'expert', [(e, (e + side) % experts) for e in range(e...  54.3 us
    all_to_all x6, waiting for transfers between devices, exchange(): lax.all_to_all(shaped, 'expert', 0, 0, axis_index_groups=sets, tiled=True)  42.5 us
    all_to_all x6, starting transfers between devices, exchange(): lax.all_to_all(shaped, 'expert', 0, 0, axis_index_groups=sets, tiled=True)  32.3 us
    pallas_call x2, Pallas kernels, streamed_call(): pl.pallas_call(kernel, out_shape=outs, in_specs=[anywhere] * len(args), o...  28.5 us
    pallas_call x7, Pallas kernels, local_call(): pl.pallas_call(kernel, out_shape=outs, in_specs=[SMEM] + [VMEM] * len(arg...  13.7 us
    ppermute x7, starting transfers between devices, across(): lax.ppermute(value, 'expert', [(e, (e + side) % experts) for e in range(e...  9.85 us
    broadcast_in_dim x1, other arithmetic, on_device(): summed[2 * units:].astype(F32)[None]  6.07 us
    unnamed x15, local copies, waits for them, and re-layouts  4.55 us
  transfers between devices with their start and end apart: 14, of which 9 were waited for; matrix products, arithmetic and copies ran while one was open for 5% of the time, Pallas kernels for 17%

profile of v13, /device:TPU:0, one launch (start us, length us, event | category | flops | bytes accessed | tf_op | source)
XLA Modules:
  0.0 210.6 jit_solution(10477111647555110094)
XLA Ops:
  10.6 2.2 %shard_map.118 = bf16[512,2048]{1,0:T(8,128)(2,1)} custom-call(s32[1]{0:T(128)} %bitcast.me_ref, f32[4,128]{1,0:T(4,128)S(1)} %pad_maximum_fusion.refs_0_.refs_1_.meta, f32[4,128]{1,0:T(4,128)S(1)} %pad_maximum_fusion.refs_0_.refs_1_.meta, bf16[128,2048]{1,0:T(8,128)(2,1)S(1)} %copy-done.2, bf16[128,2048]{1,0:T(8,128)(2,1)S(1)} %copy-done), custom_call_target="tpu_custom_call" | custom-call | flops 536870912 | bytes 3149824 | tf_op jit(solution)/shard_map/pallas_call | solution.py:20
  12.9 6.3 %all-to-all-start = ((bf16[8,64,2048]{2,1,0:T(8,128)(2,1)}), bf16[8,64,2048]{2,1,0:T(8,128)(2,1)}, u32[]{:S(2)}, u32[]{:S(2)}) async-start(bf16[8,64,2048]{2,1,0:T(8,128)(2,1)} %bitcast.4), calls=%async_computation | async-start | bytes 4194304 | tf_op jit(solution)/shard_map/all_to_all | solution.py:265
  19.2 2.7 %collective-permute-start = (bf16[128,2048]{1,0:T(8,128)(2,1)S(1)}, bf16[128,2048]{1,0:T(8,128)(2,1)S(1)}, u32[]{:S(2)}, u32[]{:S(2)}) collective-permute-start(bf16[128,2048]{1,0:T(8,128)(2,1)S(1)} %copy-done.3), channel_id=1, source_target_pairs={{0,8},{1,9},{2,10},{3,11},{4,12},{5,13},{6,14},{7,15},{8,0},{9,1},... | collective-permute-start | bytes 1572872 | tf_op jit(solution)/shard_map/ppermute | solution.py:261
  22.3 2.6 %collective-permute-start.1 = (f32[4,128]{1,0:T(4,128)S(1)}, f32[4,128]{1,0:T(4,128)S(1)}, u32[]{:S(2)}, u32[]{:S(2)}) collective-permute-start(f32[4,128]{1,0:T(4,128)S(1)} %pad_maximum_fusion.refs_0_.refs_1_.meta), channel_id=1, source_target_pairs={{0,8},{1,9},{2,10},{3,11},{4,12},{5,13},{6,14},{7,15},{8,0},{9,1},... | collective-permute-start | bytes 6152 | tf_op jit(solution)/shard_map/ppermute | solution.py:261
  24.9 34.0 %collective-permute-done.1.refs_0_.meta_far.meta = f32[4,128]{1,0:T(4,128)S(1)} collective-permute-done((f32[4,128]{1,0:T(4,128)S(1)}, f32[4,128]{1,0:T(4,128)S(1)}, u32[]{:S(2)}, u32[]{:S(2)}) %collective-permute-start.1) | collective-permute-done | bytes 2080 | tf_op jit(solution)/shard_map/ppermute | solution.py:261
  58.8 2.2 %all-to-all-done = bf16[8,64,2048]{2,1,0:T(8,128)(2,1)} async-done(((bf16[8,64,2048]{2,1,0:T(8,128)(2,1)}), bf16[8,64,2048]{2,1,0:T(8,128)(2,1)}, u32[]{:S(2)}, u32[]{:S(2)}) %all-to-all-start) | async-done | bytes 2097184 | tf_op jit(solution)/shard_map/all_to_all | solution.py:265
  62.5 8.2 %all-to-all-start.1 = ((bf16[8,32,2048]{2,1,0:T(8,128)(2,1)}), bf16[8,32,2048]{2,1,0:T(8,128)(2,1)S(1)}, u32[]{:S(2)}, u32[]{:S(2)}) async-start(bf16[8,32,2048]{2,1,0:T(8,128)(2,1)} %bitcast.10), calls=%async_computation.1 | async-start | bytes 2097152 | tf_op jit(solution)/shard_map/all_to_all | solution.py:265
  70.7 16.1 %collective-permute-done.3.refs_2_.two = bf16[64,2048]{1,0:T(8,128)(2,1)S(1)} collective-permute-done((bf16[64,2048]{1,0:T(8,128)(2,1)S(1)}, bf16[64,2048]{1,0:T(8,128)(2,1)S(1)}, u32[]{:S(2)}, u32[]{:S(2)}) %collective-permute-start.3) | collective-permute-done | bytes 262176 | tf_op jit(solution)/shard_map/ppermute | solution.py:261
  88.8 4.3 %all-to-all-start.2 = ((bf16[8,32,2048]{2,1,0:T(8,128)(2,1)}), bf16[8,32,2048]{2,1,0:T(8,128)(2,1)S(1)}, u32[]{:S(2)}, u32[]{:S(2)}) async-start(bf16[8,32,2048]{2,1,0:T(8,128)(2,1)} %bitcast.14), calls=%async_computation.2 | async-start | bytes 2097152 | tf_op jit(solution)/shard_map/all_to_all | solution.py:265
  93.1 3.1 %fusion.1 = (bf16[8,1,32,2048]{3,2,1,0:T(8,128)(2,1)}, bf16[8,1,32,2048]{3,2,1,0:T(8,128)(2,1)}) fusion(bf16[8,2,32,2048]{3,2,1,0:T(8,128)(2,1)} %bitcast.5), kind=kLoop, calls=%fused_computation.6 | loop fusion | bytes 4194304 | tf_op jit(solution)/shard_map/slice | solution.py:299
  96.2 10.3 %shard_map.120 = (f32[512,704]{1,0:T(8,128)}, f32[512,704]{1,0:T(8,128)}, bf16[512,704]{1,0:T(8,128)(2,1)}, bf16[512,2048]{1,0:T(8,128)(2,1)}) custom-call(bf16[704,2048]{1,0:T(8,128)(2,1)} %bitcast.42, bf16[256,2048]{1,0:T(8,128)(2,1)} %bitcast.50, bf16[256,2048]{1,0:T(8,128)(2,1)} %bitcast.48, bf16[704,2048]{1,0:T(8,128)(2,1)} %bitcast.44, ...), custom_call_target="tpu_custom_call" | custom-call | flops 1 | bytes 1 | tf_op jit(solution)/shard_map/pallas_call | solution.py:237
  107.6 5.1 %all-to-all-start.3 = ((bf16[8,64,2048]{2,1,0:T(8,128)(2,1)}), bf16[8,64,2048]{2,1,0:T(8,128)(2,1)S(1)}, u32[]{:S(2)}, u32[]{:S(2)}) async-start(bf16[8,64,2048]{2,1,0:T(8,128)(2,1)} %bitcast.54), calls=%async_computation.3 | async-start | bytes 4194304 | tf_op jit(solution)/shard_map/all_to_all | solution.py:265
  112.9 18.2 %shard_map.122 = (bf16[256,2048]{1,0:T(8,128)(2,1)}, bf16[256,2048]{1,0:T(8,128)(2,1)}, bf16[2112,2048]{1,0:T(8,128)(2,1)}) custom-call(bf16[704,2048]{1,0:T(8,128)(2,1)} %bitcast.47, bf16[256,2048]{1,0:T(8,128)(2,1)} %bitcast.53, bf16[256,2048]{1,0:T(8,128)(2,1)} %bitcast.52, f32[512,704]{1,0:T(8,128)} %get-tuple-element.50.refs_3_, ...), custom_call_target="tpu_custom_call" | custom-call | flops 1 | bytes 1 | tf_op jit(solution)/shard_map/pallas_call | solution.py:237
  131.1 6.1 %all-to-all-done.3 = bf16[8,64,2048]{2,1,0:T(8,128)(2,1)S(1)} async-done(((bf16[8,64,2048]{2,1,0:T(8,128)(2,1)}), bf16[8,64,2048]{2,1,0:T(8,128)(2,1)S(1)}, u32[]{:S(2)}, u32[]{:S(2)}) %all-to-all-start.3) | async-done | bytes 2097184 | tf_op jit(solution)/shard_map/all_to_all | solution.py:265
  139.1 4.3 %all-to-all-start.4 = ((bf16[8,32,2048]{2,1,0:T(8,128)(2,1)}), bf16[8,32,2048]{2,1,0:T(8,128)(2,1)}, u32[]{:S(2)}, u32[]{:S(2)}) async-start(bf16[8,32,2048]{2,1,0:T(8,128)(2,1)} %bitcast.56), calls=%async_computation.4 | async-start | bytes 2097152 | tf_op jit(solution)/shard_map/all_to_all | solution.py:265
  143.4 1.7 collective-permute-start.4
  146.4 21.4 %all-to-all-done.4 = bf16[8,32,2048]{2,1,0:T(8,128)(2,1)} async-done(((bf16[8,32,2048]{2,1,0:T(8,128)(2,1)}), bf16[8,32,2048]{2,1,0:T(8,128)(2,1)}, u32[]{:S(2)}, u32[]{:S(2)}) %all-to-all-start.4) | async-done | bytes 1048608 | tf_op jit(solution)/shard_map/all_to_all | solution.py:265
  169.5 2.4 %collective-permute-done.5.far_grads = f32[128,128]{1,0:T(8,128)S(1)} collective-permute-done((f32[128,128]{1,0:T(8,128)S(1)}, f32[128,128]{1,0:T(8,128)S(1)}, u32[]{:S(2)}, u32[]{:S(2)}) %collective-permute-start.5) | collective-permute-done | bytes 65568 | tf_op jit(solution)/shard_map/ppermute | solution.py:261
  172.0 4.2 %all-to-all-start.5 = ((bf16[8,32,2048]{2,1,0:T(8,128)(2,1)}), bf16[8,32,2048]{2,1,0:T(8,128)(2,1)}, u32[]{:S(2)}, u32[]{:S(2)}) async-start(bf16[8,32,2048]{2,1,0:T(8,128)(2,1)} %bitcast.55), calls=%async_computation.5 | async-start | bytes 2097152 | tf_op jit(solution)/shard_map/all_to_all | solution.py:265
  177.5 2.9 %shard_map.125 = (bf16[128,2048]{1,0:T(8,128)(2,1)}, f32[128,128]{1,0:T(8,128)S(1)}) custom-call(s32[1]{0:T(128)} %bitcast.me_ref, f32[4,128]{1,0:T(4,128)S(1)} %pad_maximum_fusion.refs_0_.refs_1_.meta, f32[4,128]{1,0:T(4,128)S(1)} %collective-permute-done.1.refs_0_.meta_far.meta, bf16[128,2048]{1,0:T(8,128)(2,1)S(1)} %copy-done.1, ...), custom_call_target="tpu_custom_call" | custom-call | flops 536870912 | bytes 3805184 | tf_op jit(solution)/shard_map/pallas_call | solution.py:20
  180.4 6.1 %fusion = (f32[1,704,1024]{2,1,0:T(8,128)}, f32[1,1024,704]{1,2,0:T(8,128)}, f32[1,1024,704]{1,2,0:T(8,128)}) fusion(bf16[2112,1024]{1,0:T(8,128)(2,1)} %reduce-scatter.2.cloned.1.call-done), kind=kLoop, calls=%fused_computation.3 | loop fusion | flops 2162688 | bytes 12976128 | tf_op jit(solution)/shard_map/broadcast_in_dim | solution.py:379
  186.4 12.2 %all-to-all-done.5 = bf16[8,32,2048]{2,1,0:T(8,128)(2,1)} async-done(((bf16[8,32,2048]{2,1,0:T(8,128)(2,1)}), bf16[8,32,2048]{2,1,0:T(8,128)(2,1)}, u32[]{:S(2)}, u32[]{:S(2)}) %all-to-all-start.5) | async-done | bytes 1048608 | tf_op jit(solution)/shard_map/all_to_all | solution.py:265
  199.3 1.8 collective-permute-done.6.far
  201.1 2.7 %shard_map.126 = bf16[128,2048]{1,0:T(8,128)(2,1)} custom-call(s32[1]{0:T(128)} %bitcast.me_ref, f32[4,128]{1,0:T(4,128)S(1)} %pad_maximum_fusion.refs_0_.refs_1_.meta, bf16[256,2048]{1,0:T(8,128)(2,1)} %bitcast.21.back, bf16[128,2048]{1,0:T(8,128)(2,1)} %collective-permute-done.6.far), custom_call_target="tpu_custom_call" | custom-call | flops 134217728 | bytes 2099200 | tf_op jit(solution)/shard_map/pallas_call | solution.py:20
  (34 shorter events, 15.6 us)
Async XLA Ops:
  8.5 1.0 copy-start
  9.6 1.0 copy-start.2
  12.8 6.3 %copy-start.3 = (bf16[128,2048]{1,0:T(8,128)(2,1)S(1)}, bf16[128,2048]{1,0:T(8,128)(2,1)}, u32[]{:S(2)}) copy-start(bf16[128,2048]{1,0:T(8,128)(2,1)} %refs_2_.1) | copy-start | bytes 1572868
  12.9 9.0 %copy-start.1 = (bf16[128,2048]{1,0:T(8,128)(2,1)S(1)}, bf16[128,2048]{1,0:T(8,128)(2,1)}, u32[]{:S(2)}) copy-start(bf16[128,2048]{1,0:T(8,128)(2,1)} %block.1) | copy-start | bytes 1572868
  12.9 48.1 %all-to-all-start = ((bf16[8,64,2048]{2,1,0:T(8,128)(2,1)}), bf16[8,64,2048]{2,1,0:T(8,128)(2,1)}, u32[]{:S(2)}, u32[]{:S(2)}) async-start(bf16[8,64,2048]{2,1,0:T(8,128)(2,1)} %bitcast.4), calls=%async_computation | async-start | bytes 4194304 | tf_op jit(solution)/shard_map/all_to_all | solution.py:265
  19.2 39.6 %collective-permute-start = (bf16[128,2048]{1,0:T(8,128)(2,1)S(1)}, bf16[128,2048]{1,0:T(8,128)(2,1)S(1)}, u32[]{:S(2)}, u32[]{:S(2)}) collective-permute-start(bf16[128,2048]{1,0:T(8,128)(2,1)S(1)} %copy-done.3), channel_id=1, source_target_pairs={{0,8},{1,9},{2,10},{3,11},{4,12},{5,13},{6,14},{7,15},{8,0},{9,1},... | collective-permute-start | bytes 1572872 | tf_op jit(solution)/shard_map/ppermute | solution.py:261
  21.9 36.9 %collective-permute-start.2 = (bf16[64,2048]{1,0:T(8,128)(2,1)S(1)}, bf16[64,2048]{1,0:T(8,128)(2,1)S(1)}, u32[]{:S(2)}, u32[]{:S(2)}) collective-permute-start(bf16[64,2048]{1,0:T(8,128)(2,1)S(1)} %get-tuple-element.96), channel_id=1, source_target_pairs={{0,8},{1,9},{2,10},{3,11},{4,12},{5,13},{6,14},{7,15},{8,0},{9,1},... | collective-permute-start | bytes 786440 | tf_op jit(solution)/shard_map/ppermute | solution.py:261
  22.3 36.5 %collective-permute-start.1 = (f32[4,128]{1,0:T(4,128)S(1)}, f32[4,128]{1,0:T(4,128)S(1)}, u32[]{:S(2)}, u32[]{:S(2)}) collective-permute-start(f32[4,128]{1,0:T(4,128)S(1)} %pad_maximum_fusion.refs_0_.refs_1_.meta), channel_id=1, source_target_pairs={{0,8},{1,9},{2,10},{3,11},{4,12},{5,13},{6,14},{7,15},{8,0},{9,1},... | collective-permute-start | bytes 6152 | tf_op jit(solution)/shard_map/ppermute | solution.py:261
  62.5 26.3 %all-to-all-start.1 = ((bf16[8,32,2048]{2,1,0:T(8,128)(2,1)}), bf16[8,32,2048]{2,1,0:T(8,128)(2,1)S(1)}, u32[]{:S(2)}, u32[]{:S(2)}) async-start(bf16[8,32,2048]{2,1,0:T(8,128)(2,1)} %bitcast.10), calls=%async_computation.1 | async-start | bytes 2097152 | tf_op jit(solution)/shard_map/all_to_all | solution.py:265
  70.6 16.1 %collective-permute-start.3 = (bf16[64,2048]{1,0:T(8,128)(2,1)S(1)}, bf16[64,2048]{1,0:T(8,128)(2,1)S(1)}, u32[]{:S(2)}, u32[]{:S(2)}) collective-permute-start(bf16[64,2048]{1,0:T(8,128)(2,1)S(1)} %get-tuple-element.95), channel_id=1, source_target_pairs={{0,8},{1,9},{2,10},{3,11},{4,12},{5,13},{6,14},{7,15},{8,0},{9,1},... | collective-permute-start | bytes 786440 | tf_op jit(solution)/shard_map/ppermute | solution.py:261
  88.8 7.4 %copy-start.5 = (bf16[8,32,2048]{2,1,0:T(8,128)(2,1)}, bf16[8,32,2048]{2,1,0:T(8,128)(2,1)S(1)}, u32[]{:S(2)}) copy-start(bf16[8,32,2048]{2,1,0:T(8,128)(2,1)S(1)} %all-to-all-done.1) | copy-start | bytes 3145732
  88.8 17.7 %all-to-all-start.2 = ((bf16[8,32,2048]{2,1,0:T(8,128)(2,1)}), bf16[8,32,2048]{2,1,0:T(8,128)(2,1)S(1)}, u32[]{:S(2)}, u32[]{:S(2)}) async-start(bf16[8,32,2048]{2,1,0:T(8,128)(2,1)} %bitcast.14), calls=%async_computation.2 | async-start | bytes 2097152 | tf_op jit(solution)/shard_map/all_to_all | solution.py:265
  106.5 1.0 copy-start.6
  107.6 29.6 %all-to-all-start.3 = ((bf16[8,64,2048]{2,1,0:T(8,128)(2,1)}), bf16[8,64,2048]{2,1,0:T(8,128)(2,1)S(1)}, u32[]{:S(2)}, u32[]{:S(2)}) async-start(bf16[8,64,2048]{2,1,0:T(8,128)(2,1)} %bitcast.54), calls=%async_computation.3 | async-start | bytes 4194304 | tf_op jit(solution)/shard_map/all_to_all | solution.py:265
  112.6 67.7 %reduce-scatter.2.cloned.1.call-start = ((), (), s32[]{:S(2)}) async-start(), calls=%async_computation.7 | async-start | bytes 12976128 | tf_op jit(solution)/shard_map/reduce_scatter | solution.py:356
  138.3 0.8 copy-start.4
  139.1 28.7 %all-to-all-start.4 = ((bf16[8,32,2048]{2,1,0:T(8,128)(2,1)}), bf16[8,32,2048]{2,1,0:T(8,128)(2,1)}, u32[]{:S(2)}, u32[]{:S(2)}) async-start(bf16[8,32,2048]{2,1,0:T(8,128)(2,1)} %bitcast.56), calls=%async_computation.4 | async-start | bytes 2097152 | tf_op jit(solution)/shard_map/all_to_all | solution.py:265
  143.4 28.5 %collective-permute-start.4 = (bf16[128,2048]{1,0:T(8,128)(2,1)}, bf16[128,2048]{1,0:T(8,128)(2,1)}, u32[]{:S(2)}, u32[]{:S(2)}) collective-permute-start(bf16[128,2048]{1,0:T(8,128)(2,1)} %copy-done.4), channel_id=1, source_target_pairs={{0,8},{1,9},{2,10},{3,11},{4,12},{5,13},{6,14},{7,15},{8,0},{9,1},... | collective-permute-start | bytes 1572872 | tf_op jit(solution)/shard_map/ppermute | solution.py:261
  145.2 26.8 %collective-permute-start.5 = (f32[128,128]{1,0:T(8,128)S(1)}, f32[128,128]{1,0:T(8,128)S(1)}, u32[]{:S(2)}, u32[]{:S(2)}) collective-permute-start(f32[128,128]{1,0:T(8,128)S(1)} %get-tuple-element.64), channel_id=1, source_target_pairs={{0,8},{1,9},{2,10},{3,11},{4,12},{5,13},{6,14},{7,15},{8,0},{9,1},... | collective-permute-start | bytes 196616 | tf_op jit(solution)/shard_map/ppermute | solution.py:261
  172.0 26.7 %all-to-all-start.5 = ((bf16[8,32,2048]{2,1,0:T(8,128)(2,1)}), bf16[8,32,2048]{2,1,0:T(8,128)(2,1)}, u32[]{:S(2)}, u32[]{:S(2)}) async-start(bf16[8,32,2048]{2,1,0:T(8,128)(2,1)} %bitcast.55), calls=%async_computation.5 | async-start | bytes 2097152 | tf_op jit(solution)/shard_map/all_to_all | solution.py:265
  176.2 24.9 %collective-permute-start.6 = (bf16[128,2048]{1,0:T(8,128)(2,1)S(1)}, bf16[128,2048]{1,0:T(8,128)(2,1)}, u32[]{:S(2)}, u32[]{:S(2)}) collective-permute-start(bf16[128,2048]{1,0:T(8,128)(2,1)S(1)} %shard_map.124), channel_id=1, source_target_pairs={{0,8},{1,9},{2,10},{3,11},{4,12},{5,13},{6,14},{7,15},{8,0},{9,1},... | collective-permute-start | bytes 1572872 | tf_op jit(solution)/shard_map/ppermute | solution.py:261
Sparse Core Ops, SparseCore 0:
  137.3 16.7 reduce-scatter.1

commit v14 on v13

--- a/solution.py
+++ b/solution.py
@@ -70,6 +70,12 @@
         block = jnp.concatenate([ref[:, c:e] for ref in blocks], 0)
         got = jnp.dot(held, block, preferred_element_type=F32)
         out[:, c:e] = ((gate * got) if any(scaled) else got).astype(BF16)
+
+
+def own_pick_kernel(top, side, capacity, me_ref, meta, x_hbm, d_hbm, out, x, d, sems):
+    for load in fetch((x_hbm, d_hbm), (x, d), sems):
+        load.wait()
+    pick_kernel(top, side, capacity, (False, True), me_ref, meta, meta, x, d, out)
 
 
 TRANSPOSED = (((0,), (0,)), ((), ()))
@@ -277,23 +283,40 @@
             flops,
         )
 
-    def pick(metas, blocks, scaled):
+    def pick(metas, blocks, scaled, work=None):
         count = len(metas)
         return local_call(
             functools.partial(pick_kernel, top, side, capacity, scaled),
             [shape((count * half, feature), BF16)],
             me_arr,
             [*metas, *blocks],
-            2 * count * count * half * tok * feature,
+            work or 2 * count * count * half * tok * feature,
         )[0]
 
     meta = jnp.concatenate([expert_ids.T.astype(F32), gate_prob.T], 0)
-    own = exchange(pick([meta, meta], [tokens, d_mixed], (False, True)))
+    anywhere = pl.BlockSpec(memory_space=pltpu.HBM)
+    picked = pl.pallas_call(
+        functools.partial(own_pick_kernel, top, side, capacity),
+        out_shape=shape((2 * half, feature), BF16),
+        in_specs=[SMEM, VMEM, anywhere, anywhere],
+        out_specs=VMEM,
+        scratch_shapes=[
+            pltpu.VMEM((tok, feature), BF16),
+            pltpu.VMEM((tok, feature), BF16),
+            pltpu.SemaphoreType.DMA((2,)),
+        ],
+        compiler_params=pltpu.CompilerParams(vmem_limit_bytes=60 * 1024 * 1024),
+        cost_estimate=pl.CostEstimate(
+            flops=8 * half * tok * feature, bytes_accessed=1, transcendentals=0
+        ),
+    )(me_arr, meta, tokens, d_mixed)
+    own = exchange(picked)
     own = own.reshape(side, 2, capacity, feature)
     x_far, meta_far = after(across(tokens), across(meta))
     d_far = [across(d_mixed[n * (tok // 2) : (n + 1) * (tok // 2)]) for n in range(2)]
-    x_far, d_far[0], own = after(x_far, d_far[0], own)
-    x_far_rows = exchange(pick([meta_far], [x_far], (False,)))
+    x_far, d_far[0] = after(x_far, d_far[0])
+    x_picked, own = after(pick([meta_far], [x_far], (False,), 10**11), own)
+    x_far_rows = exchange(x_picked)
     d_picked, _ = after(pick([meta_far], d_far, (True,)), x_far_rows)
     d_far_rows = exchange(d_picked)
     x_own, d_own = (own[:, n].reshape(half, feature) for n in range(2))
@@ -362,17 +385,17 @@
     )
     dx_far, mixed_far, grads_far = after(dx_far, mixed_far, grads_far)
     dx_far_back = exchange(dx_far)
-    (tokens_far,) = call(sum_kernel, [token_rows], [meta_far, dx_far_back], work)
-    tokens_far, dx_own, mixed_far, grads_far = after(
-        tokens_far, dx_own, across(mixed_far), across(grads_far)
-    )
-    dx_own_back = exchange(dx_own)
+    mixed_far, grads_far = after(across(mixed_far), across(grads_far))
     mixed, grads = call(
         mix_last_kernel,
         [token_rows, grad_rows],
         [meta, meta_far, d_mixed, y_back, mixed_far, grads_far],
-        2 * top * work,
-    )
+        10**11,
+    )
+    dx_far_back, mixed, grads = after(dx_far_back, mixed, grads)
+    (tokens_far,) = call(sum_kernel, [token_rows], [meta_far, dx_far_back], work)
+    tokens_far, dx_own = after(tokens_far, dx_own)
+    dx_own_back = exchange(dx_own)
     weight_grads = (
         summed[:units].astype(F32).T[None],
         summed[units : 2 * units].astype(F32).T[None],

time: 211 us -> 209 us (level)
    all_to_all x6, starting transfers between devices: 32.3 us -> 28 us  [exchange(): lax.all_to_all(shaped, 'expert', 0, 0, axis_index_groups=sets, tiled=True)]
    pallas_call x7 -> x6, Pallas kernels: 13.7 us -> 9.57 us  [local_call(): pl.pallas_call(kernel, out_shape=outs, in_specs=[SMEM] + [VMEM] * len(arg...]
    pallas_call x0 -> x1, Pallas kernels: none -> 4.07 us  [on_device(): pl.pallas_call(functools.partial(own_pick_kernel, top, side, capacity), o...]
    ppermute x7, starting transfers between devices: 9.85 us -> 12.6 us  [across(): lax.ppermute(value, 'expert', [(e, (e + side) % experts) for e in range(e...]
    unnamed x15 -> x11, local copies, waits for them, and re-layouts: 4.55 us -> 3.35 us
  transfers between devices with their start and end apart: 14 -> 14, of which waited for: 9 -> 8; matrix products, arithmetic and copies ran while one was open for 5% -> 6% of each run, Pallas kernels for 17% -> 20%
where the time goes in v14:
time: 209 us
  waiting for transfers between devices  96.5 us (46%)
  Pallas kernels  42.1 us (20%)
  starting transfers between devices  40.8 us (20%)
  between operations  14.1 us (7%)
  local copies, waits for them, and re-layouts  7.62 us (4%)
  other arithmetic  7.43 us (4%)
    ppermute x7, waiting for transfers between devices, across(): lax.ppermute(value, 'expert', [(e, (e + side) % experts) for e in range(e...  55.7 us
    all_to_all x6, waiting for transfers between devices, exchange(): lax.all_to_all(shaped, 'expert', 0, 0, axis_index_groups=sets, tiled=True)  40.7 us
    pallas_call x2, Pallas kernels, streamed_call(): pl.pallas_call(kernel, out_shape=outs, in_specs=[anywhere] * len(args), o...  28.5 us
    all_to_all x6, starting transfers between devices, exchange(): lax.all_to_all(shaped, 'expert', 0, 0, axis_index_groups=sets, tiled=True)  28 us
    ppermute x7, starting transfers between devices, across(): lax.ppermute(value, 'expert', [(e, (e + side) % experts) for e in range(e...  12.6 us
    pallas_call x6, Pallas kernels, local_call(): pl.pallas_call(kernel, out_shape=outs, in_specs=[SMEM] + [VMEM] * len(arg...  9.57 us
    broadcast_in_dim x1, other arithmetic, on_device(): summed[2 * units:].astype(F32)[None]  6.07 us
  transfers between devices with their start and end apart: 14, of which 8 were waited for; matrix products, arithmetic and copies ran while one was open for 6% of the time, Pallas kernels for 20%

profile of v14, /device:TPU:0, one launch (start us, length us, event | category | flops | bytes accessed | tf_op | source)
XLA Modules:
  0.0 208.6 jit_solution(1488521009829537275)
XLA Ops:
  7.2 4.1 %collective-permute-start = (bf16[128,2048]{1,0:T(8,128)(2,1)}, bf16[128,2048]{1,0:T(8,128)(2,1)S(1)}, u32[]{:S(2)}, u32[]{:S(2)}) collective-permute-start(bf16[128,2048]{1,0:T(8,128)(2,1)} %x_hbm.1), channel_id=1, source_target_pairs={{0,8},{1,9},{2,10},{3,11},{4,12},{5,13},{6,14},{7,15},{8,0},{9,1},... | collective-permute-start | bytes 1572872 | tf_op jit(solution)/shard_map/ppermute | solution.py:267
  13.8 2.9 %collective-permute-start.1 = (f32[4,128]{1,0:T(4,128)S(1)}, f32[4,128]{1,0:T(4,128)S(1)}, u32[]{:S(2)}, u32[]{:S(2)}) collective-permute-start(f32[4,128]{1,0:T(4,128)S(1)} %pad_maximum_fusion.meta), channel_id=1, source_target_pairs={{0,8},{1,9},{2,10},{3,11},{4,12},{5,13},{6,14},{7,15},{8,0},{9,1},... | collective-permute-start | bytes 6152 | tf_op jit(solution)/shard_map/ppermute | solution.py:267
  16.7 4.1 %shard_map.119 = bf16[512,2048]{1,0:T(8,128)(2,1)} custom-call(s32[1]{0:T(128)} %bitcast.me_ref, f32[4,128]{1,0:T(4,128)} %copy-done.1, bf16[128,2048]{1,0:T(8,128)(2,1)} %x_hbm.1, bf16[128,2048]{1,0:T(8,128)(2,1)} %block.1), custom_call_target="tpu_custom_call" | custom-call | flops 536870912 | bytes 1 | tf_op jit(solution)/shard_map/pallas_call | solution.py:298
  20.8 4.8 %all-to-all-start = ((bf16[8,64,2048]{2,1,0:T(8,128)(2,1)}), bf16[8,64,2048]{2,1,0:T(8,128)(2,1)}, u32[]{:S(2)}, u32[]{:S(2)}) async-start(bf16[8,64,2048]{2,1,0:T(8,128)(2,1)} %bitcast.54), calls=%async_computation | async-start | bytes 4194304 | tf_op jit(solution)/shard_map/all_to_all | solution.py:271
  25.5 20.5 %collective-permute-done.1.refs_0_.meta_far.meta = f32[4,128]{1,0:T(4,128)S(1)} collective-permute-done((f32[4,128]{1,0:T(4,128)S(1)}, f32[4,128]{1,0:T(4,128)S(1)}, u32[]{:S(2)}, u32[]{:S(2)}) %collective-permute-start.1) | collective-permute-done | bytes 2080 | tf_op jit(solution)/shard_map/ppermute | solution.py:267
  47.6 17.9 %all-to-all-done = bf16[8,64,2048]{2,1,0:T(8,128)(2,1)} async-done(((bf16[8,64,2048]{2,1,0:T(8,128)(2,1)}), bf16[8,64,2048]{2,1,0:T(8,128)(2,1)}, u32[]{:S(2)}, u32[]{:S(2)}) %all-to-all-start) | async-done | bytes 2097184 | tf_op jit(solution)/shard_map/all_to_all | solution.py:271
  65.4 3.6 %all-to-all-start.1 = ((bf16[8,32,2048]{2,1,0:T(8,128)(2,1)}), bf16[8,32,2048]{2,1,0:T(8,128)(2,1)S(1)}, u32[]{:S(2)}, u32[]{:S(2)}) async-start(bf16[8,32,2048]{2,1,0:T(8,128)(2,1)} %bitcast.10), calls=%async_computation.1 | async-start | bytes 2097152 | tf_op jit(solution)/shard_map/all_to_all | solution.py:271
  69.1 1.9 collective-permute-start.3
  70.9 13.5 %collective-permute-done.3.refs_2_.two = bf16[64,2048]{1,0:T(8,128)(2,1)S(1)} collective-permute-done((bf16[64,2048]{1,0:T(8,128)(2,1)S(1)}, bf16[64,2048]{1,0:T(8,128)(2,1)S(1)}, u32[]{:S(2)}, u32[]{:S(2)}) %collective-permute-start.3) | collective-permute-done | bytes 262176 | tf_op jit(solution)/shard_map/ppermute | solution.py:267
  84.5 1.5 shard_map.121
  86.6 6.9 %all-to-all-start.2 = ((bf16[8,32,2048]{2,1,0:T(8,128)(2,1)}), bf16[8,32,2048]{2,1,0:T(8,128)(2,1)S(1)}, u32[]{:S(2)}, u32[]{:S(2)}) async-start(bf16[8,32,2048]{2,1,0:T(8,128)(2,1)} %bitcast.14), calls=%async_computation.2 | async-start | bytes 2097152 | tf_op jit(solution)/shard_map/all_to_all | solution.py:271
  93.6 3.2 %fusion.1 = (bf16[8,1,32,2048]{3,2,1,0:T(8,128)(2,1)}, bf16[8,1,32,2048]{3,2,1,0:T(8,128)(2,1)}) fusion(bf16[8,2,32,2048]{3,2,1,0:T(8,128)(2,1)} %bitcast.5), kind=kLoop, calls=%fused_computation.6 | loop fusion | bytes 4194304 | tf_op jit(solution)/shard_map/slice | solution.py:322
  96.8 10.3 %shard_map.120 = (f32[512,704]{1,0:T(8,128)}, f32[512,704]{1,0:T(8,128)}, bf16[512,704]{1,0:T(8,128)(2,1)}, bf16[512,2048]{1,0:T(8,128)(2,1)}) custom-call(bf16[704,2048]{1,0:T(8,128)(2,1)} %bitcast.44, bf16[256,2048]{1,0:T(8,128)(2,1)} %bitcast.52, bf16[256,2048]{1,0:T(8,128)(2,1)} %bitcast.50, bf16[704,2048]{1,0:T(8,128)(2,1)} %bitcast.46, ...), custom_call_target="tpu_custom_call" | custom-call | flops 1 | bytes 1 | tf_op jit(solution)/shard_map/pallas_call | solution.py:243
  108.1 5.1 %all-to-all-start.3 = ((bf16[8,64,2048]{2,1,0:T(8,128)(2,1)}), bf16[8,64,2048]{2,1,0:T(8,128)(2,1)S(1)}, u32[]{:S(2)}, u32[]{:S(2)}) async-start(bf16[8,64,2048]{2,1,0:T(8,128)(2,1)} %bitcast.57), calls=%async_computation.3 | async-start | bytes 4194304 | tf_op jit(solution)/shard_map/all_to_all | solution.py:271
  113.4 18.2 %shard_map.122 = (bf16[256,2048]{1,0:T(8,128)(2,1)}, bf16[256,2048]{1,0:T(8,128)(2,1)}, bf16[2112,2048]{1,0:T(8,128)(2,1)}) custom-call(bf16[704,2048]{1,0:T(8,128)(2,1)} %bitcast.49, bf16[256,2048]{1,0:T(8,128)(2,1)} %bitcast.56, bf16[256,2048]{1,0:T(8,128)(2,1)} %bitcast.55, f32[512,704]{1,0:T(8,128)} %get-tuple-element.55.refs_3_, ...), custom_call_target="tpu_custom_call" | custom-call | flops 1 | bytes 1 | tf_op jit(solution)/shard_map/pallas_call | solution.py:243
  131.6 5.0 %all-to-all-done.3 = bf16[8,64,2048]{2,1,0:T(8,128)(2,1)S(1)} async-done(((bf16[8,64,2048]{2,1,0:T(8,128)(2,1)}), bf16[8,64,2048]{2,1,0:T(8,128)(2,1)S(1)}, u32[]{:S(2)}, u32[]{:S(2)}) %all-to-all-start.3) | async-done | bytes 2097184 | tf_op jit(solution)/shard_map/all_to_all | solution.py:271
  137.3 1.8 shard_map.123
  139.2 2.9 %collective-permute-start.5 = (f32[128,128]{1,0:T(8,128)S(1)}, f32[128,128]{1,0:T(8,128)S(1)}, u32[]{:S(2)}, u32[]{:S(2)}) collective-permute-start(f32[128,128]{1,0:T(8,128)S(1)} %get-tuple-element.68), channel_id=1, source_target_pairs={{0,8},{1,9},{2,10},{3,11},{4,12},{5,13},{6,14},{7,15},{8,0},{9,1},... | collective-permute-start | bytes 196616 | tf_op jit(solution)/shard_map/ppermute | solution.py:267
  142.1 4.0 %all-to-all-start.4 = ((bf16[8,32,2048]{2,1,0:T(8,128)(2,1)}), bf16[8,32,2048]{2,1,0:T(8,128)(2,1)S(1)}, u32[]{:S(2)}, u32[]{:S(2)}) async-start(bf16[8,32,2048]{2,1,0:T(8,128)(2,1)} %bitcast.59), calls=%async_computation.4 | async-start | bytes 2097152 | tf_op jit(solution)/shard_map/all_to_all | solution.py:271
  146.0 20.5 %collective-permute-done.5.far_grads = f32[128,128]{1,0:T(8,128)S(1)} collective-permute-done((f32[128,128]{1,0:T(8,128)S(1)}, f32[128,128]{1,0:T(8,128)S(1)}, u32[]{:S(2)}, u32[]{:S(2)}) %collective-permute-start.5) | collective-permute-done | bytes 65568 | tf_op jit(solution)/shard_map/ppermute | solution.py:267
  167.6 2.9 %shard_map.124 = (bf16[128,2048]{1,0:T(8,128)(2,1)}, f32[128,128]{1,0:T(8,128)S(1)}) custom-call(s32[1]{0:T(128)} %bitcast.me_ref, f32[4,128]{1,0:T(4,128)S(1)} %copy-done.2, f32[4,128]{1,0:T(4,128)S(1)} %collective-permute-done.1.refs_0_.meta_far.meta, bf16[128,2048]{1,0:T(8,128)(2,1)S(1)} %copy-done, bf16[512,2048]{1,0:T(8,128)(2,1)S(1)} %bitcast.40, ...), custom_call_target="tpu_custom_call" | custom-call | flops 99999997952 | bytes 3805184 | tf_op jit(solution)/shard_map/pallas_call | solution.py:20
  171.0 3.6 %all-to-all-start.5 = ((bf16[8,32,2048]{2,1,0:T(8,128)(2,1)}), bf16[8,32,2048]{2,1,0:T(8,128)(2,1)S(1)}, u32[]{:S(2)}, u32[]{:S(2)}) async-start(bf16[8,32,2048]{2,1,0:T(8,128)(2,1)} %bitcast.58), calls=%async_computation.5 | async-start | bytes 2097152 | tf_op jit(solution)/shard_map/all_to_all | solution.py:271
  175.3 6.1 %fusion = (f32[1,704,1024]{2,1,0:T(8,128)}, f32[1,1024,704]{1,2,0:T(8,128)}, f32[1,1024,704]{1,2,0:T(8,128)}) fusion(bf16[2112,1024]{1,0:T(8,128)(2,1)} %reduce-scatter.2.cloned.1.call-done), kind=kLoop, calls=%fused_computation.3 | loop fusion | flops 2162688 | bytes 12976128 | tf_op jit(solution)/shard_map/broadcast_in_dim | solution.py:402
  181.4 17.2 %all-to-all-done.5 = bf16[8,32,2048]{2,1,0:T(8,128)(2,1)S(1)} async-done(((bf16[8,32,2048]{2,1,0:T(8,128)(2,1)}), bf16[8,32,2048]{2,1,0:T(8,128)(2,1)S(1)}, u32[]{:S(2)}, u32[]{:S(2)}) %all-to-all-start.5) | async-done | bytes 1048608 | tf_op jit(solution)/shard_map/all_to_all | solution.py:271
  (30 shorter events, 11.9 us)
Async XLA Ops:
  7.2 38.9 %collective-permute-start = (bf16[128,2048]{1,0:T(8,128)(2,1)}, bf16[128,2048]{1,0:T(8,128)(2,1)S(1)}, u32[]{:S(2)}, u32[]{:S(2)}) collective-permute-start(bf16[128,2048]{1,0:T(8,128)(2,1)} %x_hbm.1), channel_id=1, source_target_pairs={{0,8},{1,9},{2,10},{3,11},{4,12},{5,13},{6,14},{7,15},{8,0},{9,1},... | collective-permute-start | bytes 1572872 | tf_op jit(solution)/shard_map/ppermute | solution.py:267
  12.3 33.7 %collective-permute-start.2 = (bf16[64,2048]{1,0:T(8,128)(2,1)S(1)}, bf16[64,2048]{1,0:T(8,128)(2,1)S(1)}, u32[]{:S(2)}, u32[]{:S(2)}) collective-permute-start(bf16[64,2048]{1,0:T(8,128)(2,1)S(1)} %get-tuple-element.104), channel_id=1, source_target_pairs={{0,8},{1,9},{2,10},{3,11},{4,12},{5,13},{6,14},{7,15},{8,0},{9,1},... | collective-permute-start | bytes 786440 | tf_op jit(solution)/shard_map/ppermute | solution.py:267
  13.8 2.9 %copy-start.1 = (f32[4,128]{1,0:T(4,128)}, f32[4,128]{1,0:T(4,128)S(1)}, u32[]{:S(2)}) copy-start(f32[4,128]{1,0:T(4,128)S(1)} %pad_maximum_fusion.meta) | copy-start | bytes 6148
  13.8 32.3 %collective-permute-start.1 = (f32[4,128]{1,0:T(4,128)S(1)}, f32[4,128]{1,0:T(4,128)S(1)}, u32[]{:S(2)}, u32[]{:S(2)}) collective-permute-start(f32[4,128]{1,0:T(4,128)S(1)} %pad_maximum_fusion.meta), channel_id=1, source_target_pairs={{0,8},{1,9},{2,10},{3,11},{4,12},{5,13},{6,14},{7,15},{8,0},{9,1},... | collective-permute-start | bytes 6152 | tf_op jit(solution)/shard_map/ppermute | solution.py:267
  20.8 44.7 %all-to-all-start = ((bf16[8,64,2048]{2,1,0:T(8,128)(2,1)}), bf16[8,64,2048]{2,1,0:T(8,128)(2,1)}, u32[]{:S(2)}, u32[]{:S(2)}) async-start(bf16[8,64,2048]{2,1,0:T(8,128)(2,1)} %bitcast.54), calls=%async_computation | async-start | bytes 4194304 | tf_op jit(solution)/shard_map/all_to_all | solution.py:271
  65.4 21.2 %all-to-all-start.1 = ((bf16[8,32,2048]{2,1,0:T(8,128)(2,1)}), bf16[8,32,2048]{2,1,0:T(8,128)(2,1)S(1)}, u32[]{:S(2)}, u32[]{:S(2)}) async-start(bf16[8,32,2048]{2,1,0:T(8,128)(2,1)} %bitcast.10), calls=%async_computation.1 | async-start | bytes 2097152 | tf_op jit(solution)/shard_map/all_to_all | solution.py:271
  69.1 15.4 %collective-permute-start.3 = (bf16[64,2048]{1,0:T(8,128)(2,1)S(1)}, bf16[64,2048]{1,0:T(8,128)(2,1)S(1)}, u32[]{:S(2)}, u32[]{:S(2)}) collective-permute-start(bf16[64,2048]{1,0:T(8,128)(2,1)S(1)} %get-tuple-element.103), channel_id=1, source_target_pairs={{0,8},{1,9},{2,10},{3,11},{4,12},{5,13},{6,14},{7,15},{8,0},{9,1},... | collective-permute-start | bytes 786440 | tf_op jit(solution)/shard_map/ppermute | solution.py:267
  86.6 10.1 %copy-start.3 = (bf16[8,32,2048]{2,1,0:T(8,128)(2,1)}, bf16[8,32,2048]{2,1,0:T(8,128)(2,1)S(1)}, u32[]{:S(2)}) copy-start(bf16[8,32,2048]{2,1,0:T(8,128)(2,1)S(1)} %all-to-all-done.1) | copy-start | bytes 3145732
  86.6 20.5 %all-to-all-start.2 = ((bf16[8,32,2048]{2,1,0:T(8,128)(2,1)}), bf16[8,32,2048]{2,1,0:T(8,128)(2,1)S(1)}, u32[]{:S(2)}, u32[]{:S(2)}) async-start(bf16[8,32,2048]{2,1,0:T(8,128)(2,1)} %bitcast.14), calls=%async_computation.2 | async-start | bytes 2097152 | tf_op jit(solution)/shard_map/all_to_all | solution.py:271
  107.1 1.0 copy-start.4
  108.1 28.5 %all-to-all-start.3 = ((bf16[8,64,2048]{2,1,0:T(8,128)(2,1)}), bf16[8,64,2048]{2,1,0:T(8,128)(2,1)S(1)}, u32[]{:S(2)}, u32[]{:S(2)}) async-start(bf16[8,64,2048]{2,1,0:T(8,128)(2,1)} %bitcast.57), calls=%async_computation.3 | async-start | bytes 4194304 | tf_op jit(solution)/shard_map/all_to_all | solution.py:271
  113.2 62.1 %reduce-scatter.2.cloned.1.call-start = ((), (), s32[]{:S(2)}) async-start(), calls=%async_computation.7 | async-start | bytes 12976128 | tf_op jit(solution)/shard_map/reduce_scatter | solution.py:379
  136.6 0.7 copy-start.2
  139.2 27.4 %collective-permute-start.4 = (bf16[128,2048]{1,0:T(8,128)(2,1)}, bf16[128,2048]{1,0:T(8,128)(2,1)}, u32[]{:S(2)}, u32[]{:S(2)}) collective-permute-start(bf16[128,2048]{1,0:T(8,128)(2,1)} %get-tuple-element.67), channel_id=1, source_target_pairs={{0,8},{1,9},{2,10},{3,11},{4,12},{5,13},{6,14},{7,15},{8,0},{9,1},... | collective-permute-start | bytes 1572872 | tf_op jit(solution)/shard_map/ppermute | solution.py:267
  139.2 27.4 %collective-permute-start.5 = (f32[128,128]{1,0:T(8,128)S(1)}, f32[128,128]{1,0:T(8,128)S(1)}, u32[]{:S(2)}, u32[]{:S(2)}) collective-permute-start(f32[128,128]{1,0:T(8,128)S(1)} %get-tuple-element.68), channel_id=1, source_target_pairs={{0,8},{1,9},{2,10},{3,11},{4,12},{5,13},{6,14},{7,15},{8,0},{9,1},... | collective-permute-start | bytes 196616 | tf_op jit(solution)/shard_map/ppermute | solution.py:267
  142.1 28.4 %all-to-all-start.4 = ((bf16[8,32,2048]{2,1,0:T(8,128)(2,1)}), bf16[8,32,2048]{2,1,0:T(8,128)(2,1)S(1)}, u32[]{:S(2)}, u32[]{:S(2)}) async-start(bf16[8,32,2048]{2,1,0:T(8,128)(2,1)} %bitcast.59), calls=%async_computation.4 | async-start | bytes 2097152 | tf_op jit(solution)/shard_map/all_to_all | solution.py:271
  166.6 1.0 copy-start
  171.0 27.6 %all-to-all-start.5 = ((bf16[8,32,2048]{2,1,0:T(8,128)(2,1)}), bf16[8,32,2048]{2,1,0:T(8,128)(2,1)S(1)}, u32[]{:S(2)}, u32[]{:S(2)}) async-start(bf16[8,32,2048]{2,1,0:T(8,128)(2,1)} %bitcast.58), calls=%async_computation.5 | async-start | bytes 2097152 | tf_op jit(solution)/shard_map/all_to_all | solution.py:271
  174.6 25.8 %collective-permute-start.6 = (bf16[128,2048]{1,0:T(8,128)(2,1)S(1)}, bf16[128,2048]{1,0:T(8,128)(2,1)S(1)}, u32[]{:S(2)}, u32[]{:S(2)}) collective-permute-start(bf16[128,2048]{1,0:T(8,128)(2,1)S(1)} %shard_map.125), channel_id=1, source_target_pairs={{0,8},{1,9},{2,10},{3,11},{4,12},{5,13},{6,14},{7,15},{8,0},{9,1},... | collective-permute-start | bytes 1572872 | tf_op jit(solution)/shard_map/ppermute | solution.py:267
Sparse Core Ops, SparseCore 0:
  136.8 15.4 reduce-scatter.1

commit v15 on v14

--- a/solution.py
+++ b/solution.py
@@ -11,6 +11,7 @@
 F32 = jnp.float32
 LANES = 128
 STRIP = 512
+LONG = 10**11
 VMEM = pl.BlockSpec(memory_space=pltpu.VMEM)
 SMEM = pl.BlockSpec(memory_space=pltpu.SMEM)
 
@@ -25,6 +26,10 @@
         compiler_params=pltpu.CompilerParams(vmem_limit_bytes=6 * 1024 * 1024),
         cost_estimate=pl.CostEstimate(flops=flops, bytes_accessed=size, transcendentals=0),
     )(me, *args)
+
+
+def local_call_plain(kernel, outs, args, flops):
+    return local_call(lambda me_ref, *refs: kernel(*refs), outs, jnp.zeros((1,), jnp.int32), args, flops)
 
 
 def strips(width, step=STRIP):
@@ -87,11 +92,18 @@
     )
 
 
-def sum_kernel(top, side, capacity, me_ref, meta, back, out):
+def table_kernel(top, side, capacity, me_ref, meta, came, out):
     (table,) = slot_tables(me_ref[0], [meta], top, side, capacity)
-    held = functools.reduce(lambda p, q: p + q, table)
+    out[...] = functools.reduce(lambda p, q: p + q, table).astype(BF16)
+
+
+def sum_kernel(table, back, *refs):
+    out = refs[-1]
     for c, e in strips(out.shape[1]):
-        out[:, c:e] = picked_sum(held, back, c, e).astype(BF16)
+        got = picked_sum(table[...], back, c, e)
+        for far in refs[:-1]:
+            got += far[:, c:e].astype(F32)
+        out[:, c:e] = got.astype(BF16)
 
 
 def mix(top, table, meta, blocks, back, outs, grads, fars=(), far_grads=None):
@@ -119,10 +131,10 @@
 
 
 def mix_kernel(
-    top, side, capacity, me_ref, meta, meta_far, one, two, back, out, grads
+    top, side, capacity, me_ref, meta, meta_far, block, back, out, grads
 ):
     tables = slot_tables(me_ref[0], [meta, meta_far], top, side, capacity)
-    mix(top, tables[1], meta_far, (one, two), back, (out,), grads)
+    mix(top, tables[1], meta_far, (block,), back, (out,), grads)
 
 
 def mix_last_kernel(
@@ -130,13 +142,6 @@
 ):
     tables = slot_tables(me_ref[0], [meta, meta_far], top, side, capacity)
     mix(top, tables[0], meta, (block,), back, (out,), grads, (far,), far_grads)
-
-
-def sum_last_kernel(top, side, capacity, me_ref, meta, back, far, out):
-    (table,) = slot_tables(me_ref[0], [meta], top, side, capacity)
-    held = functools.reduce(lambda p, q: p + q, table)
-    for c, e in strips(out.shape[1]):
-        out[:, c:e] = (picked_sum(held, back, c, e) + far[:, c:e].astype(F32)).astype(BF16)
 
 
 def fetch(sources, targets, sems):
@@ -283,14 +288,14 @@
             flops,
         )
 
-    def pick(metas, blocks, scaled, work=None):
+    def pick(metas, blocks, scaled):
         count = len(metas)
         return local_call(
             functools.partial(pick_kernel, top, side, capacity, scaled),
             [shape((count * half, feature), BF16)],
             me_arr,
             [*metas, *blocks],
-            work or 2 * count * count * half * tok * feature,
+            LONG,
         )[0]
 
     meta = jnp.concatenate([expert_ids.T.astype(F32), gate_prob.T], 0)
@@ -313,11 +318,11 @@
     own = exchange(picked)
     own = own.reshape(side, 2, capacity, feature)
     x_far, meta_far = after(across(tokens), across(meta))
-    d_far = [across(d_mixed[n * (tok // 2) : (n + 1) * (tok // 2)]) for n in range(2)]
-    x_far, d_far[0] = after(x_far, d_far[0])
-    x_picked, own = after(pick([meta_far], [x_far], (False,), 10**11), own)
+    d_late, x_far = after(d_mixed, x_far)
+    d_far = across(d_late)
+    x_picked, own = after(pick([meta_far], [x_far], (False,)), own)
     x_far_rows = exchange(x_picked)
-    d_picked, _ = after(pick([meta_far], d_far, (True,)), x_far_rows)
+    d_picked, x_far_rows = after(pick([meta_far], [d_far], (True,)), x_far_rows)
     d_far_rows = exchange(d_picked)
     x_own, d_own = (own[:, n].reshape(half, feature) for n in range(2))
 
@@ -381,30 +386,47 @@
     token_rows, grad_rows = ((tok, feature), BF16), ((tok, LANES), F32)
     work = 2 * half * tok * feature
     mixed_far, grads_far = call(
-        mix_kernel, [token_rows, grad_rows], [meta, meta_far, *d_far, y_back], 2 * top * work
+        mix_kernel, [token_rows, grad_rows], [meta, meta_far, d_far, y_back], 2 * top * work
     )
     dx_far, mixed_far, grads_far = after(dx_far, mixed_far, grads_far)
     dx_far_back = exchange(dx_far)
     mixed_far, grads_far = after(across(mixed_far), across(grads_far))
+
+    def table(meta, came):
+        return pl.pallas_call(
+            functools.partial(table_kernel, top, side, capacity),
+            out_shape=shape((half, tok), BF16),
+            in_specs=[SMEM, VMEM, anywhere],
+            out_specs=VMEM,
+            compiler_params=pltpu.CompilerParams(vmem_limit_bytes=60 * 1024 * 1024),
+            cost_estimate=pl.CostEstimate(flops=LONG, bytes_accessed=1, transcendentals=0),
+        )(me_arr, meta, came)
+
+    def total(table, back, *far):
+        return local_call_plain(
+            sum_kernel, [shape((tok, feature), BF16)], [table, back, *far], work
+        )[0]
+
+    far_table, mixed_far, grads_far, dx_far_back = after(
+        table(meta_far, mixed_far), mixed_far, grads_far, dx_far_back
+    )
+    tokens_far, dx_own = after(total(far_table, dx_far_back), dx_own)
+    dx_own_back = exchange(dx_own)
     mixed, grads = call(
         mix_last_kernel,
         [token_rows, grad_rows],
         [meta, meta_far, d_mixed, y_back, mixed_far, grads_far],
-        10**11,
-    )
-    dx_far_back, mixed, grads = after(dx_far_back, mixed, grads)
-    (tokens_far,) = call(sum_kernel, [token_rows], [meta_far, dx_far_back], work)
-    tokens_far, dx_own = after(tokens_far, dx_own)
-    dx_own_back = exchange(dx_own)
+        2 * top * work,
+    )
+    tokens_far = across(tokens_far)
     weight_grads = (
         summed[:units].astype(F32).T[None],
         summed[units : 2 * units].astype(F32).T[None],
         summed[2 * units :].astype(F32)[None],
     )
-    dx_own_back, mixed, grads, *weight_grads = after(dx_own_back, mixed, grads, *weight_grads)
-    (d_tokens,) = call(
-        sum_last_kernel, [token_rows], [meta, dx_own_back, across(tokens_far)], work
-    )
+    tokens_far, mixed, grads, *weight_grads = after(tokens_far, mixed, grads, *weight_grads)
+    own_table, tokens_far, dx_own_back = after(table(meta, tokens_far), tokens_far, dx_own_back)
+    d_tokens = total(own_table, dx_own_back, tokens_far)
     return (mixed, d_tokens, grads[:, :top], *weight_grads)
 
 

time: 209 us -> 211 us (level)
  starting transfers between devices: 40.8 us -> 34.4 us
  Pallas kernels: 42.1 us -> 45.8 us
    all_to_all x6, waiting for transfers between devices: 40.7 us -> 55.1 us  [exchange(): lax.all_to_all(shaped, 'expert', 0, 0, axis_index_groups=sets, tiled=True)]
    ppermute x7 -> x6, waiting for transfers between devices: 55.7 us -> 42.3 us  [across(): lax.ppermute(value, 'expert', [(e, (e + side) % experts) for e in range(e...]
    all_to_all x6, starting transfers between devices: 28 us -> 24.5 us  [exchange(): lax.all_to_all(shaped, 'expert', 0, 0, axis_index_groups=sets, tiled=True)]
    pallas_call x0 -> x2, Pallas kernels: none -> 2.98 us  [table(): pl.pallas_call(functools.partial(table_kernel, top, side, capacity), out_...]
    unnamed x11 -> x21, local copies, waits for them, and re-layouts: 3.35 us -> 6.31 us
    ppermute x7 -> x6, starting transfers between devices: 12.6 us -> 9.7 us  [across(): lax.ppermute(value, 'expert', [(e, (e + side) % experts) for e in range(e...]
  transfers between devices with their start and end apart: 14 -> 13, of which waited for: 8 -> 9; matrix products, arithmetic and copies ran while one was open for 6% -> 5% of each run, Pallas kernels for 20% -> 21%
where the time goes in v15:
time: 211 us; the launch traced here: 209 us
  waiting for transfers between devices  97.5 us (46%)
  Pallas kernels  45.8 us (22%)
  starting transfers between devices  34.4 us (16%)
  between operations  14.2 us (7%)
  local copies, waits for them, and re-layouts  9.41 us (4%)
  other arithmetic  7.43 us (4%)
    all_to_all x6, waiting for transfers between devices, exchange(): lax.all_to_all(shaped, 'expert', 0, 0, axis_index_groups=sets, tiled=True)  55.1 us
    ppermute x6, waiting for transfers between devices, across(): lax.ppermute(value, 'expert', [(e, (e + side) % experts) for e in range(e...  42.3 us
    pallas_call x2, Pallas kernels, streamed_call(): pl.pallas_call(kernel, out_shape=outs, in_specs=[anywhere] * len(args), o...  28.5 us
    all_to_all x6, starting transfers between devices, exchange(): lax.all_to_all(shaped, 'expert', 0, 0, axis_index_groups=sets, tiled=True)  24.5 us
    pallas_call x6, Pallas kernels, local_call(): pl.pallas_call(kernel, out_shape=outs, in_specs=[SMEM] + [VMEM] * len(arg...  10.3 us
    ppermute x6, starting transfers between devices, across(): lax.ppermute(value, 'expert', [(e, (e + side) % experts) for e in range(e...  9.7 us
    unnamed x21, local copies, waits for them, and re-layouts  6.31 us
    broadcast_in_dim x1, other arithmetic, on_device(): summed[2 * units:].astype(F32)[None]  6.07 us
  transfers between devices with their start and end apart: 13, of which 9 were waited for; matrix products, arithmetic and copies ran while one was open for 5% of the time, Pallas kernels for 21%

profile of v15, /device:TPU:0, one launch (start us, length us, event | category | flops | bytes accessed | tf_op | source)
XLA Modules:
  0.0 208.6 jit_solution(9995274275766761360)
XLA Ops:
  7.2 4.1 %collective-permute-start = (bf16[128,2048]{1,0:T(8,128)(2,1)}, bf16[128,2048]{1,0:T(8,128)(2,1)S(1)}, u32[]{:S(2)}, u32[]{:S(2)}) collective-permute-start(bf16[128,2048]{1,0:T(8,128)(2,1)} %x_hbm.1), channel_id=1, source_target_pairs={{0,8},{1,9},{2,10},{3,11},{4,12},{5,13},{6,14},{7,15},{8,0},{9,1},... | collective-permute-start | bytes 1572872 | tf_op jit(solution)/shard_map/ppermute | solution.py:272
  13.2 4.0 %shard_map.119 = bf16[512,2048]{1,0:T(8,128)(2,1)} custom-call(s32[1]{0:T(128)} %bitcast.me_ref, f32[4,128]{1,0:T(4,128)} %copy-done.5, bf16[128,2048]{1,0:T(8,128)(2,1)} %x_hbm.1, bf16[128,2048]{1,0:T(8,128)(2,1)} %block.1), custom_call_target="tpu_custom_call" | custom-call | flops 536870912 | bytes 1 | tf_op jit(solution)/shard_map/pallas_call | solution.py:303
  17.2 4.9 %all-to-all-start = ((bf16[8,64,2048]{2,1,0:T(8,128)(2,1)}), bf16[8,64,2048]{2,1,0:T(8,128)(2,1)}, u32[]{:S(2)}, u32[]{:S(2)}) async-start(bf16[8,64,2048]{2,1,0:T(8,128)(2,1)} %bitcast.52), calls=%async_computation | async-start | bytes 4194304 | tf_op jit(solution)/shard_map/all_to_all | solution.py:276
  22.1 12.7 %collective-permute-done.1.refs_0_.meta_far.meta = f32[4,128]{1,0:T(4,128)S(1)} collective-permute-done((f32[4,128]{1,0:T(4,128)S(1)}, f32[4,128]{1,0:T(4,128)S(1)}, u32[]{:S(2)}, u32[]{:S(2)}) %collective-permute-start.1) | collective-permute-done | bytes 2080 | tf_op jit(solution)/shard_map/ppermute | solution.py:272
  36.4 31.7 %all-to-all-done = bf16[8,64,2048]{2,1,0:T(8,128)(2,1)} async-done(((bf16[8,64,2048]{2,1,0:T(8,128)(2,1)}), bf16[8,64,2048]{2,1,0:T(8,128)(2,1)}, u32[]{:S(2)}, u32[]{:S(2)}) %all-to-all-start) | async-done | bytes 2097184 | tf_op jit(solution)/shard_map/all_to_all | solution.py:276
  68.1 4.2 %all-to-all-start.1 = ((bf16[8,32,2048]{2,1,0:T(8,128)(2,1)}), bf16[8,32,2048]{2,1,0:T(8,128)(2,1)}, u32[]{:S(2)}, u32[]{:S(2)}) async-start(bf16[8,32,2048]{2,1,0:T(8,128)(2,1)} %bitcast.10), calls=%async_computation.1 | async-start | bytes 2097152 | tf_op jit(solution)/shard_map/all_to_all | solution.py:276
  73.9 13.0 %all-to-all-done.1 = bf16[8,32,2048]{2,1,0:T(8,128)(2,1)} async-done(((bf16[8,32,2048]{2,1,0:T(8,128)(2,1)}), bf16[8,32,2048]{2,1,0:T(8,128)(2,1)}, u32[]{:S(2)}, u32[]{:S(2)}) %all-to-all-start.1) | async-done | bytes 1048608 | tf_op jit(solution)/shard_map/all_to_all | solution.py:276
  87.0 3.6 %all-to-all-start.2 = ((bf16[8,32,2048]{2,1,0:T(8,128)(2,1)}), bf16[8,32,2048]{2,1,0:T(8,128)(2,1)S(1)}, u32[]{:S(2)}, u32[]{:S(2)}) async-start(bf16[8,32,2048]{2,1,0:T(8,128)(2,1)} %bitcast.14), calls=%async_computation.2 | async-start | bytes 2097152 | tf_op jit(solution)/shard_map/all_to_all | solution.py:276
  90.5 3.1 %fusion.1 = (bf16[8,1,32,2048]{3,2,1,0:T(8,128)(2,1)}, bf16[8,1,32,2048]{3,2,1,0:T(8,128)(2,1)}) fusion(bf16[8,2,32,2048]{3,2,1,0:T(8,128)(2,1)} %bitcast.5), kind=kLoop, calls=%fused_computation.6 | loop fusion | bytes 4194304 | tf_op jit(solution)/shard_map/slice | solution.py:327
  93.6 10.3 %shard_map.121 = (f32[512,704]{1,0:T(8,128)}, f32[512,704]{1,0:T(8,128)}, bf16[512,704]{1,0:T(8,128)(2,1)}, bf16[512,2048]{1,0:T(8,128)(2,1)}) custom-call(bf16[704,2048]{1,0:T(8,128)(2,1)} %bitcast.44, bf16[256,2048]{1,0:T(8,128)(2,1)} %bitcast.50, bf16[256,2048]{1,0:T(8,128)(2,1)} %bitcast.11.refs_2_.refs_8_, bf16[704,2048]{1,0:T(8,128)(2,1)} %bitcast.46, ...), custom_call_target="tpu_custom_call" | custom-call | flops 1 | bytes 1 | tf_op jit(solution)/shard_map/pallas_call | solution.py:248
  106.1 3.9 %all-to-all-start.3 = ((bf16[8,64,2048]{2,1,0:T(8,128)(2,1)}), bf16[8,64,2048]{2,1,0:T(8,128)(2,1)S(1)}, u32[]{:S(2)}, u32[]{:S(2)}) async-start(bf16[8,64,2048]{2,1,0:T(8,128)(2,1)} %bitcast.55), calls=%async_computation.3 | async-start | bytes 4194304 | tf_op jit(solution)/shard_map/all_to_all | solution.py:276
  110.2 18.2 %shard_map.122 = (bf16[256,2048]{1,0:T(8,128)(2,1)}, bf16[256,2048]{1,0:T(8,128)(2,1)}, bf16[2112,2048]{1,0:T(8,128)(2,1)}) custom-call(bf16[704,2048]{1,0:T(8,128)(2,1)} %bitcast.49, bf16[256,2048]{1,0:T(8,128)(2,1)} %bitcast.54, bf16[256,2048]{1,0:T(8,128)(2,1)} %bitcast.53, f32[512,704]{1,0:T(8,128)} %get-tuple-element.61.refs_3_, ...), custom_call_target="tpu_custom_call" | custom-call | flops 1 | bytes 1 | tf_op jit(solution)/shard_map/pallas_call | solution.py:248
  128.4 7.2 %all-to-all-done.3 = bf16[8,64,2048]{2,1,0:T(8,128)(2,1)S(1)} async-done(((bf16[8,64,2048]{2,1,0:T(8,128)(2,1)}), bf16[8,64,2048]{2,1,0:T(8,128)(2,1)S(1)}, u32[]{:S(2)}, u32[]{:S(2)}) %all-to-all-start.3) | async-done | bytes 2097184 | tf_op jit(solution)/shard_map/all_to_all | solution.py:276
  136.3 1.8 shard_map.123
  139.5 1.6 collective-permute-start.4
  141.1 4.3 %all-to-all-start.4 = ((bf16[8,32,2048]{2,1,0:T(8,128)(2,1)}), bf16[8,32,2048]{2,1,0:T(8,128)(2,1)S(1)}, u32[]{:S(2)}, u32[]{:S(2)}) async-start(bf16[8,32,2048]{2,1,0:T(8,128)(2,1)} %bitcast.57), calls=%async_computation.4 | async-start | bytes 2097152 | tf_op jit(solution)/shard_map/all_to_all | solution.py:276
  145.4 20.8 %collective-permute-done.4.far_grads = f32[128,128]{1,0:T(8,128)S(1)} collective-permute-done((f32[128,128]{1,0:T(8,128)S(1)}, f32[128,128]{1,0:T(8,128)S(1)}, u32[]{:S(2)}, u32[]{:S(2)}) %collective-permute-start.4) | collective-permute-done | bytes 65568 | tf_op jit(solution)/shard_map/ppermute | solution.py:272
  167.8 1.9 all-to-all-done.4
  171.7 3.6 %all-to-all-start.5 = ((bf16[8,32,2048]{2,1,0:T(8,128)(2,1)}), bf16[8,32,2048]{2,1,0:T(8,128)(2,1)S(1)}, u32[]{:S(2)}, u32[]{:S(2)}) async-start(bf16[8,32,2048]{2,1,0:T(8,128)(2,1)} %bitcast.56), calls=%async_computation.6 | async-start | bytes 2097152 | tf_op jit(solution)/shard_map/all_to_all | solution.py:276
  175.3 2.6 %collective-permute-start.5 = (bf16[128,2048]{1,0:T(8,128)(2,1)}, bf16[128,2048]{1,0:T(8,128)(2,1)}, u32[]{:S(2)}, u32[]{:S(2)}) collective-permute-start(bf16[128,2048]{1,0:T(8,128)(2,1)} %copy-done.2), channel_id=1, source_target_pairs={{0,8},{1,9},{2,10},{3,11},{4,12},{5,13},{6,14},{7,15},{8,0},{9,1},... | collective-permute-start | bytes 1572872 | tf_op jit(solution)/shard_map/ppermute | solution.py:272
  178.9 2.9 %shard_map.126 = (bf16[128,2048]{1,0:T(8,128)(2,1)}, f32[128,128]{1,0:T(8,128)S(1)}) custom-call(s32[1]{0:T(128)} %bitcast.me_ref, f32[4,128]{1,0:T(4,128)S(1)} %copy-done.6, f32[4,128]{1,0:T(4,128)S(1)} %copy-done.8, bf16[128,2048]{1,0:T(8,128)(2,1)S(1)} %copy-done.1, bf16[512,2048]{1,0:T(8,128)(2,1)S(1)} %bitcast.40, ...), custom_call_target="tpu_custom_call" | custom-call | flops 536870912 | bytes 3805184 | tf_op jit(solution)/shard_map/pallas_call | solution.py:21
  181.8 6.1 %fusion = (f32[1,704,1024]{2,1,0:T(8,128)}, f32[1,1024,704]{1,2,0:T(8,128)}, f32[1,1024,704]{1,2,0:T(8,128)}) fusion(bf16[2112,1024]{1,0:T(8,128)(2,1)} %reduce-scatter.2.cloned.1.call-done), kind=kLoop, calls=%fused_computation.3 | loop fusion | flops 2162688 | bytes 12976128 | tf_op jit(solution)/shard_map/broadcast_in_dim | solution.py:425
  187.9 8.7 %collective-permute-done.5.came.refs_2_ = bf16[128,2048]{1,0:T(8,128)(2,1)} collective-permute-done((bf16[128,2048]{1,0:T(8,128)(2,1)}, bf16[128,2048]{1,0:T(8,128)(2,1)}, u32[]{:S(2)}, u32[]{:S(2)}) %collective-permute-start.5) | collective-permute-done | bytes 524320 | tf_op jit(solution)/shard_map/ppermute | solution.py:272
  199.6 2.2 %shard_map.128 = bf16[128,2048]{1,0:T(8,128)(2,1)} custom-call(s32[1]{0:T(128)} %constant.2.clone.1.me_ref, bf16[256,128]{1,0:T(8,128)(2,1)S(1)} %copy-done.3, bf16[256,2048]{1,0:T(8,128)(2,1)S(1)} %bitcast.41, bf16[128,2048]{1,0:T(8,128)(2,1)} %collective-permute-done.5.came.refs_2_), custom_call_target="tpu_custom_call" | custom-call | flops 134217728 | bytes 2162688 | tf_op jit(solution)/shard_map/pallas_call | solution.py:21
  (39 shorter events, 16.9 us)
Async XLA Ops:
  7.2 27.7 %collective-permute-start = (bf16[128,2048]{1,0:T(8,128)(2,1)}, bf16[128,2048]{1,0:T(8,128)(2,1)S(1)}, u32[]{:S(2)}, u32[]{:S(2)}) collective-permute-start(bf16[128,2048]{1,0:T(8,128)(2,1)} %x_hbm.1), channel_id=1, source_target_pairs={{0,8},{1,9},{2,10},{3,11},{4,12},{5,13},{6,14},{7,15},{8,0},{9,1},... | collective-permute-start | bytes 1572872 | tf_op jit(solution)/shard_map/ppermute | solution.py:272
  12.6 0.5 copy-start.5
  12.6 22.2 %collective-permute-start.1 = (f32[4,128]{1,0:T(4,128)S(1)}, f32[4,128]{1,0:T(4,128)S(1)}, u32[]{:S(2)}, u32[]{:S(2)}) collective-permute-start(f32[4,128]{1,0:T(4,128)S(1)} %pad_maximum_fusion.meta), channel_id=1, source_target_pairs={{0,8},{1,9},{2,10},{3,11},{4,12},{5,13},{6,14},{7,15},{8,0},{9,1},... | collective-permute-start | bytes 6152 | tf_op jit(solution)/shard_map/ppermute | solution.py:272
  17.2 17.6 %copy-start = (bf16[128,2048]{1,0:T(8,128)(2,1)S(1)}, bf16[128,2048]{1,0:T(8,128)(2,1)}, u32[]{:S(2)}) copy-start(bf16[128,2048]{1,0:T(8,128)(2,1)} %block.1) | copy-start | bytes 1572868
  17.2 50.9 %all-to-all-start = ((bf16[8,64,2048]{2,1,0:T(8,128)(2,1)}), bf16[8,64,2048]{2,1,0:T(8,128)(2,1)}, u32[]{:S(2)}, u32[]{:S(2)}) async-start(bf16[8,64,2048]{2,1,0:T(8,128)(2,1)} %bitcast.52), calls=%async_computation | async-start | bytes 4194304 | tf_op jit(solution)/shard_map/all_to_all | solution.py:276
  34.8 100.9 %copy-start.7 = (f32[4,128]{1,0:T(4,128)}, f32[4,128]{1,0:T(4,128)S(1)}, u32[]{:S(2)}) copy-start(f32[4,128]{1,0:T(4,128)S(1)} %collective-permute-done.1.refs_0_.meta_far.meta) | copy-start | bytes 6148
  34.8 37.5 %collective-permute-start.2 = (bf16[128,2048]{1,0:T(8,128)(2,1)S(1)}, bf16[128,2048]{1,0:T(8,128)(2,1)S(1)}, u32[]{:S(2)}, u32[]{:S(2)}) collective-permute-start(bf16[128,2048]{1,0:T(8,128)(2,1)S(1)} %copy-done), channel_id=1, source_target_pairs={{0,8},{1,9},{2,10},{3,11},{4,12},{5,13},{6,14},{7,15},{8,0},{9,1},... | collective-permute-start | bytes 1572872 | tf_op jit(solution)/shard_map/ppermute | solution.py:272
  68.1 18.9 %all-to-all-start.1 = ((bf16[8,32,2048]{2,1,0:T(8,128)(2,1)}), bf16[8,32,2048]{2,1,0:T(8,128)(2,1)}, u32[]{:S(2)}, u32[]{:S(2)}) async-start(bf16[8,32,2048]{2,1,0:T(8,128)(2,1)} %bitcast.10), calls=%async_computation.1 | async-start | bytes 2097152 | tf_op jit(solution)/shard_map/all_to_all | solution.py:276
  87.0 18.1 %all-to-all-start.2 = ((bf16[8,32,2048]{2,1,0:T(8,128)(2,1)}), bf16[8,32,2048]{2,1,0:T(8,128)(2,1)S(1)}, u32[]{:S(2)}, u32[]{:S(2)}) async-start(bf16[8,32,2048]{2,1,0:T(8,128)(2,1)} %bitcast.14), calls=%async_computation.2 | async-start | bytes 2097152 | tf_op jit(solution)/shard_map/all_to_all | solution.py:276
  105.0 1.0 copy-start.9
  106.1 29.6 %all-to-all-start.3 = ((bf16[8,64,2048]{2,1,0:T(8,128)(2,1)}), bf16[8,64,2048]{2,1,0:T(8,128)(2,1)S(1)}, u32[]{:S(2)}, u32[]{:S(2)}) async-start(bf16[8,64,2048]{2,1,0:T(8,128)(2,1)} %bitcast.55), calls=%async_computation.3 | async-start | bytes 4194304 | tf_op jit(solution)/shard_map/all_to_all | solution.py:276
  110.0 71.8 %reduce-scatter.2.cloned.1.call-start = ((), (), s32[]{:S(2)}) async-start(), calls=%async_computation.7 | async-start | bytes 12976128 | tf_op jit(solution)/shard_map/reduce_scatter | solution.py:384
  135.7 0.6 copy-start.6
  138.1 28.1 %collective-permute-start.3 = (bf16[128,2048]{1,0:T(8,128)(2,1)}, bf16[128,2048]{1,0:T(8,128)(2,1)}, u32[]{:S(2)}, u32[]{:S(2)}) collective-permute-start(bf16[128,2048]{1,0:T(8,128)(2,1)} %get-tuple-element.72), channel_id=1, source_target_pairs={{0,8},{1,9},{2,10},{3,11},{4,12},{5,13},{6,14},{7,15},{8,0},{9,1},... | collective-permute-start | bytes 1572872 | tf_op jit(solution)/shard_map/ppermute | solution.py:272
  139.5 26.8 %collective-permute-start.4 = (f32[128,128]{1,0:T(8,128)S(1)}, f32[128,128]{1,0:T(8,128)S(1)}, u32[]{:S(2)}, u32[]{:S(2)}) collective-permute-start(f32[128,128]{1,0:T(8,128)S(1)} %get-tuple-element.73), channel_id=1, source_target_pairs={{0,8},{1,9},{2,10},{3,11},{4,12},{5,13},{6,14},{7,15},{8,0},{9,1},... | collective-permute-start | bytes 196616 | tf_op jit(solution)/shard_map/ppermute | solution.py:272
  141.1 28.7 %all-to-all-start.4 = ((bf16[8,32,2048]{2,1,0:T(8,128)(2,1)}), bf16[8,32,2048]{2,1,0:T(8,128)(2,1)S(1)}, u32[]{:S(2)}, u32[]{:S(2)}) async-start(bf16[8,32,2048]{2,1,0:T(8,128)(2,1)} %bitcast.57), calls=%async_computation.4 | async-start | bytes 2097152 | tf_op jit(solution)/shard_map/all_to_all | solution.py:276
  166.2 11.6 %copy-start.8 = (f32[4,128]{1,0:T(4,128)S(1)}, f32[4,128]{1,0:T(4,128)}, u32[]{:S(2)}) copy-start(f32[4,128]{1,0:T(4,128)} %copy-done.7) | copy-start | bytes 6148
  169.7 0.8 copy-start.4
  170.9 0.8 copy-start.2
  171.7 27.1 %all-to-all-start.5 = ((bf16[8,32,2048]{2,1,0:T(8,128)(2,1)}), bf16[8,32,2048]{2,1,0:T(8,128)(2,1)S(1)}, u32[]{:S(2)}, u32[]{:S(2)}) async-start(bf16[8,32,2048]{2,1,0:T(8,128)(2,1)} %bitcast.56), calls=%async_computation.6 | async-start | bytes 2097152 | tf_op jit(solution)/shard_map/all_to_all | solution.py:276
  175.3 21.3 %collective-permute-start.5 = (bf16[128,2048]{1,0:T(8,128)(2,1)}, bf16[128,2048]{1,0:T(8,128)(2,1)}, u32[]{:S(2)}, u32[]{:S(2)}) collective-permute-start(bf16[128,2048]{1,0:T(8,128)(2,1)} %copy-done.2), channel_id=1, source_target_pairs={{0,8},{1,9},{2,10},{3,11},{4,12},{5,13},{6,14},{7,15},{8,0},{9,1},... | collective-permute-start | bytes 1572872 | tf_op jit(solution)/shard_map/ppermute | solution.py:272
  177.8 1.0 copy-start.1
  198.8 0.8 copy-start.3
Sparse Core Ops, SparseCore 0:
  135.8 16.3 reduce-scatter.1

commit v16 on v15

--- a/solution.py
+++ b/solution.py
@@ -124,10 +124,11 @@
             rows = out.shape[0]
             out[:, c:e] = mixed[n * rows : (n + 1) * rows].astype(BF16)
     lane = lax.broadcasted_iota(jnp.int32, (tok, LANES), 1)
-    grad = jnp.zeros((tok, LANES), F32) if far_grads is None else far_grads[...]
+    grad = jnp.zeros((tok, LANES), F32)
     for k in range(top):
         grad += jnp.where(lane == k, sums[k], 0.0)
-    grads[...] = grad
+    grad = jnp.transpose(grad)[: grads.shape[0]]
+    grads[...] = grad if far_grads is None else grad + far_grads[...]
 
 
 def mix_kernel(
@@ -248,7 +249,7 @@
     return pl.pallas_call(
         kernel,
         out_shape=outs,
-        in_specs=[anywhere] * len(args),
+        in_specs=[pl.BlockSpec(memory_space=pl.ANY)] * len(args),
         out_specs=[anywhere] * len(outs),
         scratch_shapes=scratch,
         compiler_params=pltpu.CompilerParams(vmem_limit_bytes=60 * 1024 * 1024),
@@ -383,7 +384,7 @@
     dx_own, dx_far, terms, y_back = after(dx_own, dx_far, terms, y_back)
     summed = lax.psum_scatter(terms, "dp", scatter_dimension=1, tiled=True)
 
-    token_rows, grad_rows = ((tok, feature), BF16), ((tok, LANES), F32)
+    token_rows, grad_rows = ((tok, feature), BF16), ((8, tok), F32)
     work = 2 * half * tok * feature
     mixed_far, grads_far = call(
         mix_kernel, [token_rows, grad_rows], [meta, meta_far, d_far, y_back], 2 * top * work
@@ -427,7 +428,7 @@
     tokens_far, mixed, grads, *weight_grads = after(tokens_far, mixed, grads, *weight_grads)
     own_table, tokens_far, dx_own_back = after(table(meta, tokens_far), tokens_far, dx_own_back)
     d_tokens = total(own_table, dx_own_back, tokens_far)
-    return (mixed, d_tokens, grads[:, :top], *weight_grads)
+    return (mixed, d_tokens, grads[:top].T, *weight_grads)
 
 
 def solution(mesh):

time: 211 us -> 208 us (0.986)
  waiting for transfers between devices: 97.5 us -> 94.4 us
    ppermute x6, waiting for transfers between devices: 42.3 us -> 39.8 us  [across(): lax.ppermute(value, 'expert', [(e, (e + side) % experts) for e in range(e...]
    unnamed x21 -> x20, local copies, waits for them, and re-layouts: 6.31 us -> 4.63 us
where the time goes in v16:
time: 208 us; the launch traced here: 206 us
  waiting for transfers between devices  94.4 us (45%)
  Pallas kernels  45.8 us (22%)
  starting transfers between devices  35.7 us (17%)
  between operations  14.1 us (7%)
  local copies, waits for them, and re-layouts  8.3 us (4%)
  other arithmetic  7.43 us (4%)
    all_to_all x6, waiting for transfers between devices, exchange(): lax.all_to_all(shaped, 'expert', 0, 0, axis_index_groups=sets, tiled=True)  54.6 us
    ppermute x6, waiting for transfers between devices, across(): lax.ppermute(value, 'expert', [(e, (e + side) % experts) for e in range(e...  39.8 us
    pallas_call x2, Pallas kernels, streamed_call(): pl.pallas_call(kernel, out_shape=outs, in_specs=[pl.BlockSpec(memory_spac...  28.5 us
    all_to_all x6, starting transfers between devices, exchange(): lax.all_to_all(shaped, 'expert', 0, 0, axis_index_groups=sets, tiled=True)  25.2 us
    pallas_call x6, Pallas kernels, local_call(): pl.pallas_call(kernel, out_shape=outs, in_specs=[SMEM] + [VMEM] * len(arg...  10.3 us
    ppermute x6, starting transfers between devices, across(): lax.ppermute(value, 'expert', [(e, (e + side) % experts) for e in range(e...  10.3 us
    broadcast_in_dim x1, other arithmetic, on_device(): summed[2 * units:].astype(F32)[None]  6.07 us
    unnamed x20, local copies, waits for them, and re-layouts  4.63 us
  transfers between devices with their start and end apart: 13, of which 9 were waited for; matrix products, arithmetic and copies ran while one was open for 5% of the time, Pallas kernels for 21%

profile of v16, /device:TPU:0, one launch (start us, length us, event | category | flops | bytes accessed | tf_op | source)
XLA Modules:
  0.0 205.7 jit_solution(3961127657567866654)
XLA Ops:
  7.2 4.1 %collective-permute-start = (bf16[128,2048]{1,0:T(8,128)(2,1)}, bf16[128,2048]{1,0:T(8,128)(2,1)S(1)}, u32[]{:S(2)}, u32[]{:S(2)}) collective-permute-start(bf16[128,2048]{1,0:T(8,128)(2,1)} %x_hbm.1), channel_id=1, source_target_pairs={{0,8},{1,9},{2,10},{3,11},{4,12},{5,13},{6,14},{7,15},{8,0},{9,1},... | collective-permute-start | bytes 1572872 | tf_op jit(solution)/shard_map/ppermute | solution.py:273
  13.2 4.0 %shard_map.119 = bf16[512,2048]{1,0:T(8,128)(2,1)} custom-call(s32[1]{0:T(128)} %bitcast.me_ref, f32[4,128]{1,0:T(4,128)} %copy-done.5, bf16[128,2048]{1,0:T(8,128)(2,1)} %x_hbm.1, bf16[128,2048]{1,0:T(8,128)(2,1)} %block.1), custom_call_target="tpu_custom_call" | custom-call | flops 536870912 | bytes 1 | tf_op jit(solution)/shard_map/pallas_call | solution.py:304
  17.2 4.9 %all-to-all-start = ((bf16[8,64,2048]{2,1,0:T(8,128)(2,1)}), bf16[8,64,2048]{2,1,0:T(8,128)(2,1)}, u32[]{:S(2)}, u32[]{:S(2)}) async-start(bf16[8,64,2048]{2,1,0:T(8,128)(2,1)} %bitcast.54), calls=%async_computation | async-start | bytes 4194304 | tf_op jit(solution)/shard_map/all_to_all | solution.py:277
  22.1 12.7 %collective-permute-done.1.refs_0_.meta_far.meta = f32[4,128]{1,0:T(4,128)S(1)} collective-permute-done((f32[4,128]{1,0:T(4,128)S(1)}, f32[4,128]{1,0:T(4,128)S(1)}, u32[]{:S(2)}, u32[]{:S(2)}) %collective-permute-start.1) | collective-permute-done | bytes 2080 | tf_op jit(solution)/shard_map/ppermute | solution.py:273
  36.4 31.7 %all-to-all-done = bf16[8,64,2048]{2,1,0:T(8,128)(2,1)} async-done(((bf16[8,64,2048]{2,1,0:T(8,128)(2,1)}), bf16[8,64,2048]{2,1,0:T(8,128)(2,1)}, u32[]{:S(2)}, u32[]{:S(2)}) %all-to-all-start) | async-done | bytes 2097184 | tf_op jit(solution)/shard_map/all_to_all | solution.py:277
  68.1 3.7 %all-to-all-start.1 = ((bf16[8,32,2048]{2,1,0:T(8,128)(2,1)}), bf16[8,32,2048]{2,1,0:T(8,128)(2,1)S(1)}, u32[]{:S(2)}, u32[]{:S(2)}) async-start(bf16[8,32,2048]{2,1,0:T(8,128)(2,1)} %bitcast.10), calls=%async_computation.1 | async-start | bytes 2097152 | tf_op jit(solution)/shard_map/all_to_all | solution.py:277
  73.4 12.8 %all-to-all-done.1 = bf16[8,32,2048]{2,1,0:T(8,128)(2,1)S(1)} async-done(((bf16[8,32,2048]{2,1,0:T(8,128)(2,1)}), bf16[8,32,2048]{2,1,0:T(8,128)(2,1)S(1)}, u32[]{:S(2)}, u32[]{:S(2)}) %all-to-all-start.1) | async-done | bytes 1048608 | tf_op jit(solution)/shard_map/all_to_all | solution.py:277
  86.2 4.2 %all-to-all-start.2 = ((bf16[8,32,2048]{2,1,0:T(8,128)(2,1)}), bf16[8,32,2048]{2,1,0:T(8,128)(2,1)}, u32[]{:S(2)}, u32[]{:S(2)}) async-start(bf16[8,32,2048]{2,1,0:T(8,128)(2,1)} %bitcast.14), calls=%async_computation.2 | async-start | bytes 2097152 | tf_op jit(solution)/shard_map/all_to_all | solution.py:277
  90.4 3.1 %fusion.1 = (bf16[8,1,32,2048]{3,2,1,0:T(8,128)(2,1)}, bf16[8,1,32,2048]{3,2,1,0:T(8,128)(2,1)}) fusion(bf16[8,2,32,2048]{3,2,1,0:T(8,128)(2,1)} %bitcast.5), kind=kLoop, calls=%fused_computation.7 | loop fusion | bytes 4194304 | tf_op jit(solution)/shard_map/slice | solution.py:328
  93.5 10.3 %shard_map.121 = (f32[512,704]{1,0:T(8,128)}, f32[512,704]{1,0:T(8,128)}, bf16[512,704]{1,0:T(8,128)(2,1)}, bf16[512,2048]{1,0:T(8,128)(2,1)}) custom-call(bf16[704,2048]{1,0:T(8,128)(2,1)} %bitcast.44, bf16[256,2048]{1,0:T(8,128)(2,1)} %bitcast.52, bf16[256,2048]{1,0:T(8,128)(2,1)} %bitcast.50, bf16[704,2048]{1,0:T(8,128)(2,1)} %bitcast.46, ...), custom_call_target="tpu_custom_call" | custom-call | flops 1 | bytes 1 | tf_op jit(solution)/shard_map/pallas_call | solution.py:249
  104.3 4.6 %all-to-all-start.3 = ((bf16[8,64,2048]{2,1,0:T(8,128)(2,1)}), bf16[8,64,2048]{2,1,0:T(8,128)(2,1)S(1)}, u32[]{:S(2)}, u32[]{:S(2)}) async-start(bf16[8,64,2048]{2,1,0:T(8,128)(2,1)} %bitcast.56), calls=%async_computation.3 | async-start | bytes 4194304 | tf_op jit(solution)/shard_map/all_to_all | solution.py:277
  109.1 18.2 %shard_map.122 = (bf16[256,2048]{1,0:T(8,128)(2,1)}, bf16[256,2048]{1,0:T(8,128)(2,1)}, bf16[2112,2048]{1,0:T(8,128)(2,1)}) custom-call(bf16[704,2048]{1,0:T(8,128)(2,1)} %bitcast.49, bf16[256,2048]{1,0:T(8,128)(2,1)} %bitcast.55, bf16[256,2048]{1,0:T(8,128)(2,1)} %bitcast.15.refs_2_, f32[512,704]{1,0:T(8,128)} %get-tuple-element.61.refs_3_, ...), custom_call_target="tpu_custom_call" | custom-call | flops 1 | bytes 1 | tf_op jit(solution)/shard_map/pallas_call | solution.py:249
  127.3 6.4 %all-to-all-done.3 = bf16[8,64,2048]{2,1,0:T(8,128)(2,1)S(1)} async-done(((bf16[8,64,2048]{2,1,0:T(8,128)(2,1)}), bf16[8,64,2048]{2,1,0:T(8,128)(2,1)S(1)}, u32[]{:S(2)}, u32[]{:S(2)}) %all-to-all-start.3) | async-done | bytes 2097184 | tf_op jit(solution)/shard_map/all_to_all | solution.py:277
  134.4 1.8 shard_map.123
  136.2 2.0 collective-permute-start.3
  139.1 4.2 %all-to-all-start.4 = ((bf16[8,32,2048]{2,1,0:T(8,128)(2,1)}), bf16[8,32,2048]{2,1,0:T(8,128)(2,1)S(1)}, u32[]{:S(2)}, u32[]{:S(2)}) async-start(bf16[8,32,2048]{2,1,0:T(8,128)(2,1)} %bitcast.58), calls=%async_computation.4 | async-start | bytes 2097152 | tf_op jit(solution)/shard_map/all_to_all | solution.py:277
  143.3 18.5 %collective-permute-done.4.far_grads = f32[8,128]{1,0:T(8,128)S(1)} collective-permute-done((f32[8,128]{1,0:T(8,128)S(1)}, f32[8,128]{1,0:T(8,128)S(1)}, u32[]{:S(2)}, u32[]{:S(2)}) %collective-permute-start.4) | collective-permute-done | bytes 4128 | tf_op jit(solution)/shard_map/ppermute | solution.py:273
  163.3 3.2 %all-to-all-done.4 = bf16[8,32,2048]{2,1,0:T(8,128)(2,1)S(1)} async-done(((bf16[8,32,2048]{2,1,0:T(8,128)(2,1)}), bf16[8,32,2048]{2,1,0:T(8,128)(2,1)S(1)}, u32[]{:S(2)}, u32[]{:S(2)}) %all-to-all-start.4) | async-done | bytes 1048608 | tf_op jit(solution)/shard_map/all_to_all | solution.py:277
  168.5 3.6 %all-to-all-start.5 = ((bf16[8,32,2048]{2,1,0:T(8,128)(2,1)}), bf16[8,32,2048]{2,1,0:T(8,128)(2,1)S(1)}, u32[]{:S(2)}, u32[]{:S(2)}) async-start(bf16[8,32,2048]{2,1,0:T(8,128)(2,1)} %bitcast.57), calls=%async_computation.6 | async-start | bytes 2097152 | tf_op jit(solution)/shard_map/all_to_all | solution.py:277
  172.0 3.2 %collective-permute-start.5 = (bf16[128,2048]{1,0:T(8,128)(2,1)}, bf16[128,2048]{1,0:T(8,128)(2,1)}, u32[]{:S(2)}, u32[]{:S(2)}) collective-permute-start(bf16[128,2048]{1,0:T(8,128)(2,1)} %copy-done.2), channel_id=1, source_target_pairs={{0,8},{1,9},{2,10},{3,11},{4,12},{5,13},{6,14},{7,15},{8,0},{9,1},... | collective-permute-start | bytes 1572872 | tf_op jit(solution)/shard_map/ppermute | solution.py:273
  176.2 2.9 %shard_map.126 = (bf16[128,2048]{1,0:T(8,128)(2,1)}, f32[8,128]{1,0:T(8,128)S(1)}) custom-call(s32[1]{0:T(128)} %bitcast.me_ref, f32[4,128]{1,0:T(4,128)S(1)} %copy-done.6, f32[4,128]{1,0:T(4,128)S(1)} %copy-done.8, bf16[128,2048]{1,0:T(8,128)(2,1)S(1)} %copy-done.1, bf16[512,2048]{1,0:T(8,128)(2,1)S(1)} %bitcast.41, ...), custom_call_target="tpu_custom_call" | custom-call | flops 536870912 | bytes 3682304 | tf_op jit(solution)/shard_map/pallas_call | solution.py:21
  179.1 6.1 %fusion = (f32[1,704,1024]{2,1,0:T(8,128)}, f32[1,1024,704]{1,2,0:T(8,128)}, f32[1,1024,704]{1,2,0:T(8,128)}) fusion(bf16[2112,1024]{1,0:T(8,128)(2,1)} %reduce-scatter.2.cloned.1.call-done), kind=kLoop, calls=%fused_computation.3 | loop fusion | flops 2162688 | bytes 12976128 | tf_op jit(solution)/shard_map/broadcast_in_dim | solution.py:426
  185.2 8.5 %collective-permute-done.5.came.refs_2_ = bf16[128,2048]{1,0:T(8,128)(2,1)} collective-permute-done((bf16[128,2048]{1,0:T(8,128)(2,1)}, bf16[128,2048]{1,0:T(8,128)(2,1)}, u32[]{:S(2)}, u32[]{:S(2)}) %collective-permute-start.5) | collective-permute-done | bytes 524320 | tf_op jit(solution)/shard_map/ppermute | solution.py:273
  196.7 2.2 %shard_map.128 = bf16[128,2048]{1,0:T(8,128)(2,1)} custom-call(s32[1]{0:T(128)} %constant.2.clone.1.me_ref, bf16[256,128]{1,0:T(8,128)(2,1)S(1)} %copy-done.3, bf16[256,2048]{1,0:T(8,128)(2,1)S(1)} %bitcast.42, bf16[128,2048]{1,0:T(8,128)(2,1)} %collective-permute-done.5.came.refs_2_), custom_call_target="tpu_custom_call" | custom-call | flops 134217728 | bytes 2162688 | tf_op jit(solution)/shard_map/pallas_call | solution.py:21
  (39 shorter events, 14.7 us)
Async XLA Ops:
  7.2 27.7 %collective-permute-start = (bf16[128,2048]{1,0:T(8,128)(2,1)}, bf16[128,2048]{1,0:T(8,128)(2,1)S(1)}, u32[]{:S(2)}, u32[]{:S(2)}) collective-permute-start(bf16[128,2048]{1,0:T(8,128)(2,1)} %x_hbm.1), channel_id=1, source_target_pairs={{0,8},{1,9},{2,10},{3,11},{4,12},{5,13},{6,14},{7,15},{8,0},{9,1},... | collective-permute-start | bytes 1572872 | tf_op jit(solution)/shard_map/ppermute | solution.py:273
  12.6 0.5 copy-start.5
  12.6 22.2 %collective-permute-start.1 = (f32[4,128]{1,0:T(4,128)S(1)}, f32[4,128]{1,0:T(4,128)S(1)}, u32[]{:S(2)}, u32[]{:S(2)}) collective-permute-start(f32[4,128]{1,0:T(4,128)S(1)} %pad_maximum_fusion.meta), channel_id=1, source_target_pairs={{0,8},{1,9},{2,10},{3,11},{4,12},{5,13},{6,14},{7,15},{8,0},{9,1},... | collective-permute-start | bytes 6152 | tf_op jit(solution)/shard_map/ppermute | solution.py:273
  17.2 17.6 %copy-start = (bf16[128,2048]{1,0:T(8,128)(2,1)S(1)}, bf16[128,2048]{1,0:T(8,128)(2,1)}, u32[]{:S(2)}) copy-start(bf16[128,2048]{1,0:T(8,128)(2,1)} %block.1) | copy-start | bytes 1572868
  17.2 50.9 %all-to-all-start = ((bf16[8,64,2048]{2,1,0:T(8,128)(2,1)}), bf16[8,64,2048]{2,1,0:T(8,128)(2,1)}, u32[]{:S(2)}, u32[]{:S(2)}) async-start(bf16[8,64,2048]{2,1,0:T(8,128)(2,1)} %bitcast.54), calls=%async_computation | async-start | bytes 4194304 | tf_op jit(solution)/shard_map/all_to_all | solution.py:277
  34.8 99.0 %copy-start.7 = (f32[4,128]{1,0:T(4,128)}, f32[4,128]{1,0:T(4,128)S(1)}, u32[]{:S(2)}) copy-start(f32[4,128]{1,0:T(4,128)S(1)} %collective-permute-done.1.refs_0_.meta_far.meta) | copy-start | bytes 6148
  34.8 37.0 %collective-permute-start.2 = (bf16[128,2048]{1,0:T(8,128)(2,1)S(1)}, bf16[128,2048]{1,0:T(8,128)(2,1)S(1)}, u32[]{:S(2)}, u32[]{:S(2)}) collective-permute-start(bf16[128,2048]{1,0:T(8,128)(2,1)S(1)} %copy-done), channel_id=1, source_target_pairs={{0,8},{1,9},{2,10},{3,11},{4,12},{5,13},{6,14},{7,15},{8,0},{9,1},... | collective-permute-start | bytes 1572872 | tf_op jit(solution)/shard_map/ppermute | solution.py:273
  68.1 18.1 %all-to-all-start.1 = ((bf16[8,32,2048]{2,1,0:T(8,128)(2,1)}), bf16[8,32,2048]{2,1,0:T(8,128)(2,1)S(1)}, u32[]{:S(2)}, u32[]{:S(2)}) async-start(bf16[8,32,2048]{2,1,0:T(8,128)(2,1)} %bitcast.10), calls=%async_computation.1 | async-start | bytes 2097152 | tf_op jit(solution)/shard_map/all_to_all | solution.py:277
  86.2 7.4 %copy-start.9 = (bf16[8,32,2048]{2,1,0:T(8,128)(2,1)}, bf16[8,32,2048]{2,1,0:T(8,128)(2,1)S(1)}, u32[]{:S(2)}) copy-start(bf16[8,32,2048]{2,1,0:T(8,128)(2,1)S(1)} %all-to-all-done.1) | copy-start | bytes 3145732
  86.2 18.1 %all-to-all-start.2 = ((bf16[8,32,2048]{2,1,0:T(8,128)(2,1)}), bf16[8,32,2048]{2,1,0:T(8,128)(2,1)}, u32[]{:S(2)}, u32[]{:S(2)}) async-start(bf16[8,32,2048]{2,1,0:T(8,128)(2,1)} %bitcast.14), calls=%async_computation.2 | async-start | bytes 2097152 | tf_op jit(solution)/shard_map/all_to_all | solution.py:277
  104.3 29.5 %all-to-all-start.3 = ((bf16[8,64,2048]{2,1,0:T(8,128)(2,1)}), bf16[8,64,2048]{2,1,0:T(8,128)(2,1)S(1)}, u32[]{:S(2)}, u32[]{:S(2)}) async-start(bf16[8,64,2048]{2,1,0:T(8,128)(2,1)} %bitcast.56), calls=%async_computation.3 | async-start | bytes 4194304 | tf_op jit(solution)/shard_map/all_to_all | solution.py:277
  108.9 70.3 %reduce-scatter.2.cloned.1.call-start = ((), (), s32[]{:S(2)}) async-start(), calls=%async_computation.7 | async-start | bytes 12976128 | tf_op jit(solution)/shard_map/reduce_scatter | solution.py:385
  133.8 0.6 copy-start.6
  136.2 25.6 %collective-permute-start.3 = (bf16[128,2048]{1,0:T(8,128)(2,1)}, bf16[128,2048]{1,0:T(8,128)(2,1)}, u32[]{:S(2)}, u32[]{:S(2)}) collective-permute-start(bf16[128,2048]{1,0:T(8,128)(2,1)} %get-tuple-element.72), channel_id=1, source_target_pairs={{0,8},{1,9},{2,10},{3,11},{4,12},{5,13},{6,14},{7,15},{8,0},{9,1},... | collective-permute-start | bytes 1572872 | tf_op jit(solution)/shard_map/ppermute | solution.py:273
  138.2 23.5 %collective-permute-start.4 = (f32[8,128]{1,0:T(8,128)S(1)}, f32[8,128]{1,0:T(8,128)S(1)}, u32[]{:S(2)}, u32[]{:S(2)}) collective-permute-start(f32[8,128]{1,0:T(8,128)S(1)} %get-tuple-element.73), channel_id=1, source_target_pairs={{0,8},{1,9},{2,10},{3,11},{4,12},{5,13},{6,14},{7,15},{8,0},{9,1},... | collective-permute-start | bytes 12296 | tf_op jit(solution)/shard_map/ppermute | solution.py:273
  139.1 27.4 %all-to-all-start.4 = ((bf16[8,32,2048]{2,1,0:T(8,128)(2,1)}), bf16[8,32,2048]{2,1,0:T(8,128)(2,1)S(1)}, u32[]{:S(2)}, u32[]{:S(2)}) async-start(bf16[8,32,2048]{2,1,0:T(8,128)(2,1)} %bitcast.58), calls=%async_computation.4 | async-start | bytes 2097152 | tf_op jit(solution)/shard_map/all_to_all | solution.py:277
  161.8 13.4 %copy-start.8 = (f32[4,128]{1,0:T(4,128)S(1)}, f32[4,128]{1,0:T(4,128)}, u32[]{:S(2)}) copy-start(f32[4,128]{1,0:T(4,128)} %copy-done.7) | copy-start | bytes 6148
  166.5 0.8 copy-start.4
  167.7 0.8 copy-start.2
  168.5 27.4 %all-to-all-start.5 = ((bf16[8,32,2048]{2,1,0:T(8,128)(2,1)}), bf16[8,32,2048]{2,1,0:T(8,128)(2,1)S(1)}, u32[]{:S(2)}, u32[]{:S(2)}) async-start(bf16[8,32,2048]{2,1,0:T(8,128)(2,1)} %bitcast.57), calls=%async_computation.6 | async-start | bytes 2097152 | tf_op jit(solution)/shard_map/all_to_all | solution.py:277
  172.0 21.7 %collective-permute-start.5 = (bf16[128,2048]{1,0:T(8,128)(2,1)}, bf16[128,2048]{1,0:T(8,128)(2,1)}, u32[]{:S(2)}, u32[]{:S(2)}) collective-permute-start(bf16[128,2048]{1,0:T(8,128)(2,1)} %copy-done.2), channel_id=1, source_target_pairs={{0,8},{1,9},{2,10},{3,11},{4,12},{5,13},{6,14},{7,15},{8,0},{9,1},... | collective-permute-start | bytes 1572872 | tf_op jit(solution)/shard_map/ppermute | solution.py:273
  175.2 1.0 copy-start.1
  195.8 0.8 copy-start.3
Sparse Core Ops, SparseCore 0:
  133.9 17.3 reduce-scatter.1

commit v17 on v16

--- a/solution.py
+++ b/solution.py
@@ -59,7 +59,7 @@
     return tables
 
 
-def pick_kernel(top, side, capacity, scaled, me_ref, *refs):
+def pick_kernel(top, side, capacity, scaled, me_ref, *refs, loads=()):
     count = len(scaled)
     metas, blocks, out = refs[:count], refs[count:-1], refs[-1]
     tables = slot_tables(me_ref[0], metas, top, side, capacity)
@@ -71,6 +71,8 @@
             if has:
                 part = part * meta[top + k : top + k + 1, :]
             gate += jnp.sum(part, 1, keepdims=True)
+    for load in loads:
+        load.wait()
     for c, e in strips(out.shape[1]):
         block = jnp.concatenate([ref[:, c:e] for ref in blocks], 0)
         got = jnp.dot(held, block, preferred_element_type=F32)
@@ -78,9 +80,10 @@
 
 
 def own_pick_kernel(top, side, capacity, me_ref, meta, x_hbm, d_hbm, out, x, d, sems):
-    for load in fetch((x_hbm, d_hbm), (x, d), sems):
-        load.wait()
-    pick_kernel(top, side, capacity, (False, True), me_ref, meta, meta, x, d, out)
+    loads = fetch((x_hbm, d_hbm), (x, d), sems)
+    pick_kernel(
+        top, side, capacity, (False, True), me_ref, meta, meta, x, d, out, loads=loads
+    )
 
 
 TRANSPOSED = (((0,), (0,)), ((), ()))
@@ -319,13 +322,15 @@
     own = exchange(picked)
     own = own.reshape(side, 2, capacity, feature)
     x_far, meta_far = after(across(tokens), across(meta))
-    d_late, x_far = after(d_mixed, x_far)
+    x_picked, own = after(pick([meta_far], [x_far], (False,)), own)
+    d_late, own = after(d_mixed, own)
     d_far = across(d_late)
-    x_picked, own = after(pick([meta_far], [x_far], (False,)), own)
     x_far_rows = exchange(x_picked)
-    d_picked, x_far_rows = after(pick([meta_far], [d_far], (True,)), x_far_rows)
+    x_own, d_own = (own[:, n].reshape(half, feature) for n in range(2))
+    d_picked, x_own, d_own, x_far_rows = after(
+        pick([meta_far], [d_far], (True,)), x_own, d_own, x_far_rows
+    )
     d_far_rows = exchange(d_picked)
-    x_own, d_own = (own[:, n].reshape(half, feature) for n in range(2))
 
     gate_matrix, up_matrix, down_matrix = w_gate[0].T, w_up[0].T, w_down[0]
     units, n_rows = gate_matrix.shape[0], 2 * half

time: 208 us -> 207 us (level)
  waiting for transfers between devices: 94.4 us -> 90.5 us
  starting transfers between devices: 35.7 us -> 39.4 us
    all_to_all x6, waiting for transfers between devices: 54.6 us -> 33.5 us  [exchange(): lax.all_to_all(shaped, 'expert', 0, 0, axis_index_groups=sets, tiled=True)]
    ppermute x6, waiting for transfers between devices: 39.8 us -> 57 us  [across(): lax.ppermute(value, 'expert', [(e, (e + side) % experts) for e in range(e...]
  transfers between devices with their start and end apart: 13 -> 13, of which waited for: 9 -> 10; matrix products, arithmetic and copies ran while one was open for 5% -> 5% of each run, Pallas kernels for 21% -> 21%
where the time goes in v17:
time: 207 us; the launch traced here: 205 us
  waiting for transfers between devices  90.5 us (44%)
  Pallas kernels  45.6 us (22%)
  starting transfers between devices  39.4 us (19%)
  between operations  14.1 us (7%)
  local copies, waits for them, and re-layouts  8.3 us (4%)
  other arithmetic  7.43 us (4%)
    ppermute x6, waiting for transfers between devices, across(): lax.ppermute(value, 'expert', [(e, (e + side) % experts) for e in range(e...  57 us
    all_to_all x6, waiting for transfers between devices, exchange(): lax.all_to_all(shaped, 'expert', 0, 0, axis_index_groups=sets, tiled=True)  33.5 us
    pallas_call x2, Pallas kernels, streamed_call(): pl.pallas_call(kernel, out_shape=outs, in_specs=[pl.BlockSpec(memory_spac...  28.5 us
    all_to_all x6, starting transfers between devices, exchange(): lax.all_to_all(shaped, 'expert', 0, 0, axis_index_groups=sets, tiled=True)  27.2 us
    ppermute x6, starting transfers between devices, across(): lax.ppermute(value, 'expert', [(e, (e + side) % experts) for e in range(e...  12 us
    pallas_call x6, Pallas kernels, local_call(): pl.pallas_call(kernel, out_shape=outs, in_specs=[SMEM] + [VMEM] * len(arg...  10.3 us
    broadcast_in_dim x1, other arithmetic, on_device(): summed[2 * units:].astype(F32)[None]  6.07 us
    unnamed x20, local copies, waits for them, and re-layouts  4.63 us
  transfers between devices with their start and end apart: 13, of which 10 were waited for; matrix products, arithmetic and copies ran while one was open for 5% of the time, Pallas kernels for 21%

profile of v17, /device:TPU:0, one launch (start us, length us, event | category | flops | bytes accessed | tf_op | source)
XLA Modules:
  0.0 205.5 jit_solution(9102498538706741469)
XLA Ops:
  7.2 4.1 %collective-permute-start = (bf16[128,2048]{1,0:T(8,128)(2,1)}, bf16[128,2048]{1,0:T(8,128)(2,1)S(1)}, u32[]{:S(2)}, u32[]{:S(2)}) collective-permute-start(bf16[128,2048]{1,0:T(8,128)(2,1)} %x_hbm.1), channel_id=1, source_target_pairs={{0,8},{1,9},{2,10},{3,11},{4,12},{5,13},{6,14},{7,15},{8,0},{9,1},... | collective-permute-start | bytes 1572872 | tf_op jit(solution)/shard_map/ppermute | solution.py:276
  13.2 3.9 %shard_map.119 = bf16[512,2048]{1,0:T(8,128)(2,1)} custom-call(s32[1]{0:T(128)} %bitcast.me_ref, f32[4,128]{1,0:T(4,128)} %copy-done.5, bf16[128,2048]{1,0:T(8,128)(2,1)} %x_hbm.1, bf16[128,2048]{1,0:T(8,128)(2,1)} %block.1), custom_call_target="tpu_custom_call" | custom-call | flops 536870912 | bytes 1 | tf_op jit(solution)/shard_map/pallas_call | solution.py:307
  17.1 4.7 %all-to-all-start = ((bf16[8,64,2048]{2,1,0:T(8,128)(2,1)}), bf16[8,64,2048]{2,1,0:T(8,128)(2,1)}, u32[]{:S(2)}, u32[]{:S(2)}) async-start(bf16[8,64,2048]{2,1,0:T(8,128)(2,1)} %bitcast.54), calls=%async_computation | async-start | bytes 4194304 | tf_op jit(solution)/shard_map/all_to_all | solution.py:280
  21.8 13.0 %collective-permute-done.1.refs_0_.meta_far.meta = f32[4,128]{1,0:T(4,128)S(1)} collective-permute-done((f32[4,128]{1,0:T(4,128)S(1)}, f32[4,128]{1,0:T(4,128)S(1)}, u32[]{:S(2)}, u32[]{:S(2)}) %collective-permute-start.1) | collective-permute-done | bytes 2080 | tf_op jit(solution)/shard_map/ppermute | solution.py:276
  36.3 20.2 %all-to-all-done = bf16[8,64,2048]{2,1,0:T(8,128)(2,1)} async-done(((bf16[8,64,2048]{2,1,0:T(8,128)(2,1)}), bf16[8,64,2048]{2,1,0:T(8,128)(2,1)}, u32[]{:S(2)}, u32[]{:S(2)}) %all-to-all-start) | async-done | bytes 2097184 | tf_op jit(solution)/shard_map/all_to_all | solution.py:280
  56.6 3.8 %all-to-all-start.1 = ((bf16[8,32,2048]{2,1,0:T(8,128)(2,1)}), bf16[8,32,2048]{2,1,0:T(8,128)(2,1)S(1)}, u32[]{:S(2)}, u32[]{:S(2)}) async-start(bf16[8,32,2048]{2,1,0:T(8,128)(2,1)} %bitcast.8), calls=%async_computation.1 | async-start | bytes 2097152 | tf_op jit(solution)/shard_map/all_to_all | solution.py:280
  60.4 3.1 %collective-permute-start.2 = (bf16[128,2048]{1,0:T(8,128)(2,1)S(1)}, bf16[128,2048]{1,0:T(8,128)(2,1)S(1)}, u32[]{:S(2)}, u32[]{:S(2)}) collective-permute-start(bf16[128,2048]{1,0:T(8,128)(2,1)S(1)} %copy-done), channel_id=1, source_target_pairs={{0,8},{1,9},{2,10},{3,11},{4,12},{5,13},{6,14},{7,15},{8,0},{9,1},... | collective-permute-start | bytes 1572872 | tf_op jit(solution)/shard_map/ppermute | solution.py:276
  63.5 3.1 %fusion.1 = (bf16[8,1,32,2048]{3,2,1,0:T(8,128)(2,1)}, bf16[8,1,32,2048]{3,2,1,0:T(8,128)(2,1)}) fusion(bf16[8,2,32,2048]{3,2,1,0:T(8,128)(2,1)} %bitcast.5), kind=kLoop, calls=%fused_computation.7 | loop fusion | bytes 4194304 | tf_op jit(solution)/shard_map/slice | solution.py:329
  66.6 15.8 %collective-permute-done.2.refs_1_.block = bf16[128,2048]{1,0:T(8,128)(2,1)S(1)} collective-permute-done((bf16[128,2048]{1,0:T(8,128)(2,1)S(1)}, bf16[128,2048]{1,0:T(8,128)(2,1)S(1)}, u32[]{:S(2)}, u32[]{:S(2)}) %collective-permute-start.2) | collective-permute-done | bytes 524320 | tf_op jit(solution)/shard_map/ppermute | solution.py:276
  84.7 7.3 %all-to-all-start.2 = ((bf16[8,32,2048]{2,1,0:T(8,128)(2,1)}), bf16[8,32,2048]{2,1,0:T(8,128)(2,1)}, u32[]{:S(2)}, u32[]{:S(2)}) async-start(bf16[8,32,2048]{2,1,0:T(8,128)(2,1)} %bitcast.14), calls=%async_computation.2 | async-start | bytes 2097152 | tf_op jit(solution)/shard_map/all_to_all | solution.py:280
  92.1 10.3 %shard_map.121 = (f32[512,704]{1,0:T(8,128)}, f32[512,704]{1,0:T(8,128)}, bf16[512,704]{1,0:T(8,128)(2,1)}, bf16[512,2048]{1,0:T(8,128)(2,1)}) custom-call(bf16[704,2048]{1,0:T(8,128)(2,1)} %bitcast.44, bf16[256,2048]{1,0:T(8,128)(2,1)} %bitcast.52, bf16[256,2048]{1,0:T(8,128)(2,1)} %bitcast.50, bf16[704,2048]{1,0:T(8,128)(2,1)} %bitcast.46, ...), custom_call_target="tpu_custom_call" | custom-call | flops 1 | bytes 1 | tf_op jit(solution)/shard_map/pallas_call | solution.py:252
  102.4 2.2 %all-to-all-done.2 = bf16[8,32,2048]{2,1,0:T(8,128)(2,1)} async-done(((bf16[8,32,2048]{2,1,0:T(8,128)(2,1)}), bf16[8,32,2048]{2,1,0:T(8,128)(2,1)}, u32[]{:S(2)}, u32[]{:S(2)}) %all-to-all-start.2) | async-done | bytes 1048608 | tf_op jit(solution)/shard_map/all_to_all | solution.py:280
  104.6 3.6 %all-to-all-start.3 = ((bf16[8,64,2048]{2,1,0:T(8,128)(2,1)}), bf16[8,64,2048]{2,1,0:T(8,128)(2,1)S(1)}, u32[]{:S(2)}, u32[]{:S(2)}) async-start(bf16[8,64,2048]{2,1,0:T(8,128)(2,1)} %bitcast.56), calls=%async_computation.3 | async-start | bytes 4194304 | tf_op jit(solution)/shard_map/all_to_all | solution.py:280
  108.4 18.2 %shard_map.122 = (bf16[256,2048]{1,0:T(8,128)(2,1)}, bf16[256,2048]{1,0:T(8,128)(2,1)}, bf16[2112,2048]{1,0:T(8,128)(2,1)}) custom-call(bf16[704,2048]{1,0:T(8,128)(2,1)} %bitcast.49, bf16[256,2048]{1,0:T(8,128)(2,1)} %bitcast.55, bf16[256,2048]{1,0:T(8,128)(2,1)} %bitcast.15.refs_2_, f32[512,704]{1,0:T(8,128)} %get-tuple-element.65.refs_3_, ...), custom_call_target="tpu_custom_call" | custom-call | flops 1 | bytes 1 | tf_op jit(solution)/shard_map/pallas_call | solution.py:252
  126.6 7.1 %all-to-all-done.3 = bf16[8,64,2048]{2,1,0:T(8,128)(2,1)S(1)} async-done(((bf16[8,64,2048]{2,1,0:T(8,128)(2,1)}), bf16[8,64,2048]{2,1,0:T(8,128)(2,1)S(1)}, u32[]{:S(2)}, u32[]{:S(2)}) %all-to-all-start.3) | async-done | bytes 2097184 | tf_op jit(solution)/shard_map/all_to_all | solution.py:280
  136.2 2.9 %collective-permute-start.4 = (f32[8,128]{1,0:T(8,128)S(1)}, f32[8,128]{1,0:T(8,128)S(1)}, u32[]{:S(2)}, u32[]{:S(2)}) collective-permute-start(f32[8,128]{1,0:T(8,128)S(1)} %get-tuple-element.77), channel_id=1, source_target_pairs={{0,8},{1,9},{2,10},{3,11},{4,12},{5,13},{6,14},{7,15},{8,0},{9,1},... | collective-permute-start | bytes 12296 | tf_op jit(solution)/shard_map/ppermute | solution.py:276
  139.1 4.2 %all-to-all-start.4 = ((bf16[8,32,2048]{2,1,0:T(8,128)(2,1)}), bf16[8,32,2048]{2,1,0:T(8,128)(2,1)S(1)}, u32[]{:S(2)}, u32[]{:S(2)}) async-start(bf16[8,32,2048]{2,1,0:T(8,128)(2,1)} %bitcast.58), calls=%async_computation.4 | async-start | bytes 2097152 | tf_op jit(solution)/shard_map/all_to_all | solution.py:280
  143.3 18.4 %collective-permute-done.4.far_grads = f32[8,128]{1,0:T(8,128)S(1)} collective-permute-done((f32[8,128]{1,0:T(8,128)S(1)}, f32[8,128]{1,0:T(8,128)S(1)}, u32[]{:S(2)}, u32[]{:S(2)}) %collective-permute-start.4) | collective-permute-done | bytes 4128 | tf_op jit(solution)/shard_map/ppermute | solution.py:276
  163.2 3.1 %all-to-all-done.4 = bf16[8,32,2048]{2,1,0:T(8,128)(2,1)S(1)} async-done(((bf16[8,32,2048]{2,1,0:T(8,128)(2,1)}), bf16[8,32,2048]{2,1,0:T(8,128)(2,1)S(1)}, u32[]{:S(2)}, u32[]{:S(2)}) %all-to-all-start.4) | async-done | bytes 1048608 | tf_op jit(solution)/shard_map/all_to_all | solution.py:280
  168.3 3.6 %all-to-all-start.5 = ((bf16[8,32,2048]{2,1,0:T(8,128)(2,1)}), bf16[8,32,2048]{2,1,0:T(8,128)(2,1)S(1)}, u32[]{:S(2)}, u32[]{:S(2)}) async-start(bf16[8,32,2048]{2,1,0:T(8,128)(2,1)} %bitcast.57), calls=%async_computation.6 | async-start | bytes 2097152 | tf_op jit(solution)/shard_map/all_to_all | solution.py:280
  174.7 2.9 %shard_map.126 = (bf16[128,2048]{1,0:T(8,128)(2,1)}, f32[8,128]{1,0:T(8,128)S(1)}) custom-call(s32[1]{0:T(128)} %bitcast.me_ref, f32[4,128]{1,0:T(4,128)S(1)} %copy-done.6, f32[4,128]{1,0:T(4,128)S(1)} %copy-done.8, bf16[128,2048]{1,0:T(8,128)(2,1)S(1)} %copy-done.1, bf16[512,2048]{1,0:T(8,128)(2,1)S(1)} %bitcast.41, ...), custom_call_target="tpu_custom_call" | custom-call | flops 536870912 | bytes 3682304 | tf_op jit(solution)/shard_map/pallas_call | solution.py:21
  177.6 6.1 %fusion = (f32[1,704,1024]{2,1,0:T(8,128)}, f32[1,1024,704]{1,2,0:T(8,128)}, f32[1,1024,704]{1,2,0:T(8,128)}) fusion(bf16[2112,1024]{1,0:T(8,128)(2,1)} %reduce-scatter.2.cloned.1.call-done), kind=kLoop, calls=%fused_computation.3 | loop fusion | flops 2162688 | bytes 12976128 | tf_op jit(solution)/shard_map/broadcast_in_dim | solution.py:431
  183.7 9.8 %collective-permute-done.5.came.refs_2_ = bf16[128,2048]{1,0:T(8,128)(2,1)} collective-permute-done((bf16[128,2048]{1,0:T(8,128)(2,1)}, bf16[128,2048]{1,0:T(8,128)(2,1)}, u32[]{:S(2)}, u32[]{:S(2)}) %collective-permute-start.5) | collective-permute-done | bytes 524320 | tf_op jit(solution)/shard_map/ppermute | solution.py:276
  196.4 2.2 %shard_map.128 = bf16[128,2048]{1,0:T(8,128)(2,1)} custom-call(s32[1]{0:T(128)} %constant.2.clone.1.me_ref, bf16[256,128]{1,0:T(8,128)(2,1)S(1)} %copy-done.3, bf16[256,2048]{1,0:T(8,128)(2,1)S(1)} %bitcast.42, bf16[128,2048]{1,0:T(8,128)(2,1)} %collective-permute-done.5.came.refs_2_), custom_call_target="tpu_custom_call" | custom-call | flops 134217728 | bytes 2162688 | tf_op jit(solution)/shard_map/pallas_call | solution.py:21
  (39 shorter events, 17.7 us)
Async XLA Ops:
  7.2 27.7 %collective-permute-start = (bf16[128,2048]{1,0:T(8,128)(2,1)}, bf16[128,2048]{1,0:T(8,128)(2,1)S(1)}, u32[]{:S(2)}, u32[]{:S(2)}) collective-permute-start(bf16[128,2048]{1,0:T(8,128)(2,1)} %x_hbm.1), channel_id=1, source_target_pairs={{0,8},{1,9},{2,10},{3,11},{4,12},{5,13},{6,14},{7,15},{8,0},{9,1},... | collective-permute-start | bytes 1572872 | tf_op jit(solution)/shard_map/ppermute | solution.py:276
  12.6 0.5 copy-start.5
  12.6 22.2 %collective-permute-start.1 = (f32[4,128]{1,0:T(4,128)S(1)}, f32[4,128]{1,0:T(4,128)S(1)}, u32[]{:S(2)}, u32[]{:S(2)}) collective-permute-start(f32[4,128]{1,0:T(4,128)S(1)} %pad_maximum_fusion.meta), channel_id=1, source_target_pairs={{0,8},{1,9},{2,10},{3,11},{4,12},{5,13},{6,14},{7,15},{8,0},{9,1},... | collective-permute-start | bytes 6152 | tf_op jit(solution)/shard_map/ppermute | solution.py:276
  17.1 39.5 %all-to-all-start = ((bf16[8,64,2048]{2,1,0:T(8,128)(2,1)}), bf16[8,64,2048]{2,1,0:T(8,128)(2,1)}, u32[]{:S(2)}, u32[]{:S(2)}) async-start(bf16[8,64,2048]{2,1,0:T(8,128)(2,1)} %bitcast.54), calls=%async_computation | async-start | bytes 4194304 | tf_op jit(solution)/shard_map/all_to_all | solution.py:280
  21.8 38.6 %copy-start = (bf16[128,2048]{1,0:T(8,128)(2,1)S(1)}, bf16[128,2048]{1,0:T(8,128)(2,1)}, u32[]{:S(2)}) copy-start(bf16[128,2048]{1,0:T(8,128)(2,1)} %block.1) | copy-start | bytes 1572868
  34.8 98.9 %copy-start.7 = (f32[4,128]{1,0:T(4,128)}, f32[4,128]{1,0:T(4,128)S(1)}, u32[]{:S(2)}) copy-start(f32[4,128]{1,0:T(4,128)S(1)} %collective-permute-done.1.refs_0_.meta_far.meta) | copy-start | bytes 6148
  56.6 28.2 %all-to-all-start.1 = ((bf16[8,32,2048]{2,1,0:T(8,128)(2,1)}), bf16[8,32,2048]{2,1,0:T(8,128)(2,1)S(1)}, u32[]{:S(2)}, u32[]{:S(2)}) async-start(bf16[8,32,2048]{2,1,0:T(8,128)(2,1)} %bitcast.8), calls=%async_computation.1 | async-start | bytes 2097152 | tf_op jit(solution)/shard_map/all_to_all | solution.py:280
  60.4 22.1 %collective-permute-start.2 = (bf16[128,2048]{1,0:T(8,128)(2,1)S(1)}, bf16[128,2048]{1,0:T(8,128)(2,1)S(1)}, u32[]{:S(2)}, u32[]{:S(2)}) collective-permute-start(bf16[128,2048]{1,0:T(8,128)(2,1)S(1)} %copy-done), channel_id=1, source_target_pairs={{0,8},{1,9},{2,10},{3,11},{4,12},{5,13},{6,14},{7,15},{8,0},{9,1},... | collective-permute-start | bytes 1572872 | tf_op jit(solution)/shard_map/ppermute | solution.py:276
  84.7 7.3 %copy-start.9 = (bf16[8,32,2048]{2,1,0:T(8,128)(2,1)}, bf16[8,32,2048]{2,1,0:T(8,128)(2,1)S(1)}, u32[]{:S(2)}) copy-start(bf16[8,32,2048]{2,1,0:T(8,128)(2,1)S(1)} %all-to-all-done.1) | copy-start | bytes 3145732
  84.7 19.9 %all-to-all-start.2 = ((bf16[8,32,2048]{2,1,0:T(8,128)(2,1)}), bf16[8,32,2048]{2,1,0:T(8,128)(2,1)}, u32[]{:S(2)}, u32[]{:S(2)}) async-start(bf16[8,32,2048]{2,1,0:T(8,128)(2,1)} %bitcast.14), calls=%async_computation.2 | async-start | bytes 2097152 | tf_op jit(solution)/shard_map/all_to_all | solution.py:280
  104.6 29.1 %all-to-all-start.3 = ((bf16[8,64,2048]{2,1,0:T(8,128)(2,1)}), bf16[8,64,2048]{2,1,0:T(8,128)(2,1)S(1)}, u32[]{:S(2)}, u32[]{:S(2)}) async-start(bf16[8,64,2048]{2,1,0:T(8,128)(2,1)} %bitcast.56), calls=%async_computation.3 | async-start | bytes 4194304 | tf_op jit(solution)/shard_map/all_to_all | solution.py:280
  108.2 69.4 %reduce-scatter.2.cloned.1.call-start = ((), (), s32[]{:S(2)}) async-start(), calls=%async_computation.7 | async-start | bytes 12976128 | tf_op jit(solution)/shard_map/reduce_scatter | solution.py:390
  133.7 0.6 copy-start.6
  136.2 25.5 %collective-permute-start.3 = (bf16[128,2048]{1,0:T(8,128)(2,1)}, bf16[128,2048]{1,0:T(8,128)(2,1)}, u32[]{:S(2)}, u32[]{:S(2)}) collective-permute-start(bf16[128,2048]{1,0:T(8,128)(2,1)} %get-tuple-element.76), channel_id=1, source_target_pairs={{0,8},{1,9},{2,10},{3,11},{4,12},{5,13},{6,14},{7,15},{8,0},{9,1},... | collective-permute-start | bytes 1572872 | tf_op jit(solution)/shard_map/ppermute | solution.py:276
  136.2 25.5 %collective-permute-start.4 = (f32[8,128]{1,0:T(8,128)S(1)}, f32[8,128]{1,0:T(8,128)S(1)}, u32[]{:S(2)}, u32[]{:S(2)}) collective-permute-start(f32[8,128]{1,0:T(8,128)S(1)} %get-tuple-element.77), channel_id=1, source_target_pairs={{0,8},{1,9},{2,10},{3,11},{4,12},{5,13},{6,14},{7,15},{8,0},{9,1},... | collective-permute-start | bytes 12296 | tf_op jit(solution)/shard_map/ppermute | solution.py:276
  139.1 27.2 %all-to-all-start.4 = ((bf16[8,32,2048]{2,1,0:T(8,128)(2,1)}), bf16[8,32,2048]{2,1,0:T(8,128)(2,1)S(1)}, u32[]{:S(2)}, u32[]{:S(2)}) async-start(bf16[8,32,2048]{2,1,0:T(8,128)(2,1)} %bitcast.58), calls=%async_computation.4 | async-start | bytes 2097152 | tf_op jit(solution)/shard_map/all_to_all | solution.py:280
  161.7 12.0 %copy-start.8 = (f32[4,128]{1,0:T(4,128)S(1)}, f32[4,128]{1,0:T(4,128)}, u32[]{:S(2)}) copy-start(f32[4,128]{1,0:T(4,128)} %copy-done.7) | copy-start | bytes 6148
  166.3 0.8 copy-start.4
  167.5 0.8 copy-start.2
  168.3 27.3 %all-to-all-start.5 = ((bf16[8,32,2048]{2,1,0:T(8,128)(2,1)}), bf16[8,32,2048]{2,1,0:T(8,128)(2,1)S(1)}, u32[]{:S(2)}, u32[]{:S(2)}) async-start(bf16[8,32,2048]{2,1,0:T(8,128)(2,1)} %bitcast.57), calls=%async_computation.6 | async-start | bytes 2097152 | tf_op jit(solution)/shard_map/all_to_all | solution.py:280
  171.9 21.6 %collective-permute-start.5 = (bf16[128,2048]{1,0:T(8,128)(2,1)}, bf16[128,2048]{1,0:T(8,128)(2,1)}, u32[]{:S(2)}, u32[]{:S(2)}) collective-permute-start(bf16[128,2048]{1,0:T(8,128)(2,1)} %copy-done.2), channel_id=1, source_target_pairs={{0,8},{1,9},{2,10},{3,11},{4,12},{5,13},{6,14},{7,15},{8,0},{9,1},... | collective-permute-start | bytes 1572872 | tf_op jit(solution)/shard_map/ppermute | solution.py:276
  173.7 1.0 copy-start.1
  195.6 0.8 copy-start.3
Sparse Core Ops, SparseCore 0:
  133.9 15.7 reduce-scatter.1

commit v18 on v17

--- a/solution.py
+++ b/solution.py
@@ -159,20 +159,30 @@
 ACROSS_LAST = (((1,), (1,)), ((), ()))
 
 
+def own_rows(own, stream, target):
+    side, _, capacity, _ = own.shape
+    return (
+        [own.at[q, stream] for q in range(side)],
+        [target.at[pl.ds(q * capacity, capacity)] for q in range(side)],
+    )
+
+
 def forward_kernel(side, *refs):
-    sources, outs = refs[:5], refs[5:9]
+    (wg_in, own, far, wu_in, wd_in), outs = refs[:5], refs[5:9]
     wg, wu, wd, x, gate, up, hidden, y, sems, out_sems = refs[9:]
     rows, feature = x.shape
     units, half = gate.shape[1], rows // 2
-    targets = [wg, x.at[pl.ds(0, half)], x.at[pl.ds(half, half)], wu, wd]
-    loads = fetch(sources, targets, sems)
-    for load in loads[:3]:
+    x_from, x_to = own_rows(own, 0, x)
+    loads = fetch(
+        [wg_in, far, *x_from, wu_in, wd_in], [wg, x.at[pl.ds(half, half)], *x_to, wu, wd], sems
+    )
+    for load in loads[:-2]:
         load.wait()
     for c, e in strips(units, 256):
         gate[:, c:e] = lax.dot_general(
             x[...], wg[c:e, :], ACROSS_LAST, preferred_element_type=F32
         )
-    loads[3].wait()
+    loads[-2].wait()
     for c, e in strips(units, 256):
         got = lax.dot_general(x[...], wu[c:e, :], ACROSS_LAST, preferred_element_type=F32)
         up[:, c:e] = got
@@ -184,7 +194,7 @@
     ]
     for copy in copies[:3]:
         copy.start()
-    loads[4].wait()
+    loads[-1].wait()
     for c, e in strips(feature):
         got = jnp.dot(hidden[...], wd[:, c:e], preferred_element_type=F32)
         pair = [
@@ -197,14 +207,21 @@
 
 
 def backward_kernel(*refs):
-    sources, (own_out, far_out, terms_out) = refs[:10], refs[10:13]
-    wd, gate, up, wg, wu, hidden, d, x, gg, gu, dx, tiles, sems, out_sems = refs[13:]
+    (wd_in, own, d_far, gate_in, up_in, wg_in, wu_in, x_far, hidden_in) = refs[:9]
+    own_out, far_out, terms_out = refs[9:12]
+    wd, gate, up, wg, wu, hidden, d, x, gg, gu, dx, tiles, sems, out_sems = refs[12:]
     rows, feature = d.shape
     units, half = gate.shape[1], rows // 2
     first, second = pl.ds(0, half), pl.ds(half, half)
-    targets = [wd, d.at[first], d.at[second], gate, up, wg, wu, x.at[first], x.at[second], hidden]
-    loads = fetch(sources, targets, sems)
-    for load in loads[:5]:
+    d_from, d_to = own_rows(own, 1, d)
+    x_from, x_to = own_rows(own, 0, x)
+    loads = fetch(
+        [wd_in, *d_from, d_far, gate_in, up_in, wg_in, wu_in, *x_from, x_far, hidden_in],
+        [wd, *d_to, d.at[second], gate, up, wg, wu, *x_to, x.at[second], hidden],
+        sems,
+    )
+    side = len(d_to)
+    for load in loads[: side + 4]:
         load.wait()
     for c, e in strips(units, 256):
         back = lax.dot_general(d[...], wd[c:e, :], ACROSS_LAST, preferred_element_type=F32)
@@ -212,8 +229,8 @@
         sig = 1.0 / (1.0 + jnp.exp(-pre))
         gg[:, c:e] = (back * up[:, c:e] * (sig * (1.0 + pre * (1.0 - sig)))).astype(BF16)
         gu[:, c:e] = (back * (pre * sig)).astype(BF16)
-    loads[5].wait()
-    loads[6].wait()
+    for load in loads[side + 4 : side + 6]:
+        load.wait()
     for c, e in strips(feature):
         got = jnp.dot(gg[...], wg[:, c:e], preferred_element_type=F32)
         got += jnp.dot(gu[...], wu[:, c:e], preferred_element_type=F32)
@@ -224,7 +241,7 @@
     ]
     for copy in dx_copies:
         copy.start()
-    for load in loads[7:]:
+    for load in loads[side + 6 :]:
         load.wait()
     copies = []
     for n, (left, right) in enumerate(((gg, x), (gu, x), (hidden, d))):
@@ -326,10 +343,7 @@
     d_late, own = after(d_mixed, own)
     d_far = across(d_late)
     x_far_rows = exchange(x_picked)
-    x_own, d_own = (own[:, n].reshape(half, feature) for n in range(2))
-    d_picked, x_own, d_own, x_far_rows = after(
-        pick([meta_far], [d_far], (True,)), x_own, d_own, x_far_rows
-    )
+    d_picked, x_far_rows = after(pick([meta_far], [d_far], (True,)), x_far_rows)
     d_far_rows = exchange(d_picked)
 
     gate_matrix, up_matrix, down_matrix = w_gate[0].T, w_up[0].T, w_down[0]
@@ -339,7 +353,7 @@
     gate_pre, up_pre, hidden, y = streamed_call(
         functools.partial(forward_kernel, side),
         [shape(inner, F32), shape(inner, F32), shape(inner, BF16), shape((n_rows, feature), BF16)],
-        [gate_matrix, x_own, x_far_rows, up_matrix, down_matrix],
+        [gate_matrix, own, x_far_rows, up_matrix, down_matrix],
         [
             *[weight] * 3,
             wide,
@@ -347,7 +361,7 @@
             pltpu.VMEM(inner, F32),
             pltpu.VMEM(inner, BF16),
             wide,
-            pltpu.SemaphoreType.DMA((5,)),
+            pltpu.SemaphoreType.DMA((side + 4,)),
             pltpu.SemaphoreType.DMA((4,)),
         ],
     )
@@ -359,13 +373,12 @@
         [shape((half, feature), BF16)] * 2 + [shape((3 * units, feature), BF16)],
         [
             down_matrix,
-            d_own,
+            own,
             d_far_rows,
             gate_pre,
             up_pre,
             gate_matrix,
             up_matrix,
-            x_own,
             x_far_rows,
             hidden,
         ],
@@ -382,7 +395,7 @@
             pltpu.VMEM(inner, BF16),
             wide,
             pltpu.VMEM((2, 256, feature), BF16),
-            pltpu.SemaphoreType.DMA((10,)),
+            pltpu.SemaphoreType.DMA((2 * side + 8,)),
             pltpu.SemaphoreType.DMA((4,)),
         ],
     )

time: 207 us -> 208 us (level)
  waiting for transfers between devices: 90.5 us -> 95.6 us
  starting transfers between devices: 39.4 us -> 36.2 us
    slice x1 -> x0, local copies, waits for them, and re-layouts: 3.11 us -> none  [on_device(): x_own, d_own = (own[:, n].reshape(half, feature) for n in range(2))]
    ppermute x6, waiting for transfers between devices: 57 us -> 59.7 us  [across(): lax.ppermute(value, 'expert', [(e, (e + side) % experts) for e in range(e...]
    all_to_all x6, waiting for transfers between devices: 33.5 us -> 35.9 us  [exchange(): lax.all_to_all(shaped, 'expert', 0, 0, axis_index_groups=sets, tiled=True)]
    unnamed x20 -> x22, local copies, waits for them, and re-layouts: 4.63 us -> 6.02 us
  transfers between devices with their start and end apart: 13 -> 13, of which waited for: 10 -> 10; matrix products, arithmetic and copies ran while one was open for 5% -> 4% of each run, Pallas kernels for 21% -> 21%
where the time goes in v18:
time: 208 us; the launch traced here: 206 us
  waiting for transfers between devices  95.6 us (46%)
  Pallas kernels  45.8 us (22%)
  starting transfers between devices  36.2 us (17%)
  between operations  14.1 us (7%)
  other arithmetic  7.43 us (4%)
  local copies, waits for them, and re-layouts  6.59 us (3%)
    ppermute x6, waiting for transfers between devices, across(): lax.ppermute(value, 'expert', [(e, (e + side) % experts) for e in range(e...  59.7 us
    all_to_all x6, waiting for transfers between devices, exchange(): lax.all_to_all(shaped, 'expert', 0, 0, axis_index_groups=sets, tiled=True)  35.9 us
    pallas_call x2, Pallas kernels, streamed_call(): pl.pallas_call(kernel, out_shape=outs, in_specs=[pl.BlockSpec(memory_spac...  28.6 us
    all_to_all x6, starting transfers between devices, exchange(): lax.all_to_all(shaped, 'expert', 0, 0, axis_index_groups=sets, tiled=True)  26.1 us
    pallas_call x6, Pallas kernels, local_call(): pl.pallas_call(kernel, out_shape=outs, in_specs=[SMEM] + [VMEM] * len(arg...  10.3 us
    ppermute x6, starting transfers between devices, across(): lax.ppermute(value, 'expert', [(e, (e + side) % experts) for e in range(e...  9.93 us
    broadcast_in_dim x1, other arithmetic, on_device(): summed[2 * units:].astype(F32)[None]  6.07 us
    unnamed x22, local copies, waits for them, and re-layouts  6.02 us
  transfers between devices with their start and end apart: 13, of which 10 were waited for; matrix products, arithmetic and copies ran while one was open for 4% of the time, Pallas kernels for 21%

profile of v18, /device:TPU:0, one launch (start us, length us, event | category | flops | bytes accessed | tf_op | source)
XLA Modules:
  0.0 205.8 jit_solution(13380035994940789950)
XLA Ops:
  7.2 4.1 %collective-permute-start = (bf16[128,2048]{1,0:T(8,128)(2,1)}, bf16[128,2048]{1,0:T(8,128)(2,1)S(1)}, u32[]{:S(2)}, u32[]{:S(2)}) collective-permute-start(bf16[128,2048]{1,0:T(8,128)(2,1)} %x_hbm.1), channel_id=1, source_target_pairs={{0,8},{1,9},{2,10},{3,11},{4,12},{5,13},{6,14},{7,15},{8,0},{9,1},... | collective-permute-start | bytes 1572872 | tf_op jit(solution)/shard_map/ppermute | solution.py:293
  13.2 3.9 %shard_map.119 = bf16[512,2048]{1,0:T(8,128)(2,1)} custom-call(s32[1]{0:T(128)} %bitcast.me_ref, f32[4,128]{1,0:T(4,128)} %copy-done.5, bf16[128,2048]{1,0:T(8,128)(2,1)} %x_hbm.1, bf16[128,2048]{1,0:T(8,128)(2,1)} %block.1), custom_call_target="tpu_custom_call" | custom-call | flops 536870912 | bytes 1 | tf_op jit(solution)/shard_map/pallas_call | solution.py:324
  17.1 4.7 %all-to-all-start = ((bf16[8,64,2048]{2,1,0:T(8,128)(2,1)}), bf16[8,64,2048]{2,1,0:T(8,128)(2,1)S(1)}, u32[]{:S(2)}, u32[]{:S(2)}) async-start(bf16[8,64,2048]{2,1,0:T(8,128)(2,1)} %bitcast.52), calls=%async_computation | async-start | bytes 4194304 | tf_op jit(solution)/shard_map/all_to_all | solution.py:297
  21.9 12.9 %collective-permute-done.1.refs_0_.meta_far.meta = f32[4,128]{1,0:T(4,128)S(1)} collective-permute-done((f32[4,128]{1,0:T(4,128)S(1)}, f32[4,128]{1,0:T(4,128)S(1)}, u32[]{:S(2)}, u32[]{:S(2)}) %collective-permute-start.1) | collective-permute-done | bytes 2080 | tf_op jit(solution)/shard_map/ppermute | solution.py:293
  36.3 20.2 %all-to-all-done = bf16[8,64,2048]{2,1,0:T(8,128)(2,1)S(1)} async-done(((bf16[8,64,2048]{2,1,0:T(8,128)(2,1)}), bf16[8,64,2048]{2,1,0:T(8,128)(2,1)S(1)}, u32[]{:S(2)}, u32[]{:S(2)}) %all-to-all-start) | async-done | bytes 2097184 | tf_op jit(solution)/shard_map/all_to_all | solution.py:297
  59.0 5.7 %all-to-all-start.1 = ((bf16[8,32,2048]{2,1,0:T(8,128)(2,1)}), bf16[8,32,2048]{2,1,0:T(8,128)(2,1)S(1)}, u32[]{:S(2)}, u32[]{:S(2)}) async-start(bf16[8,32,2048]{2,1,0:T(8,128)(2,1)} %bitcast.8), calls=%async_computation.1 | async-start | bytes 2097152 | tf_op jit(solution)/shard_map/all_to_all | solution.py:297
  64.7 18.5 %collective-permute-done.2.refs_1_.block = bf16[128,2048]{1,0:T(8,128)(2,1)S(1)} collective-permute-done((bf16[128,2048]{1,0:T(8,128)(2,1)S(1)}, bf16[128,2048]{1,0:T(8,128)(2,1)S(1)}, u32[]{:S(2)}, u32[]{:S(2)}) %collective-permute-start.2) | collective-permute-done | bytes 524320 | tf_op jit(solution)/shard_map/ppermute | solution.py:293
  84.7 4.1 %all-to-all-done.1 = bf16[8,32,2048]{2,1,0:T(8,128)(2,1)S(1)} async-done(((bf16[8,32,2048]{2,1,0:T(8,128)(2,1)}), bf16[8,32,2048]{2,1,0:T(8,128)(2,1)S(1)}, u32[]{:S(2)}, u32[]{:S(2)}) %all-to-all-start.1) | async-done | bytes 1048608 | tf_op jit(solution)/shard_map/all_to_all | solution.py:297
  88.8 4.2 %all-to-all-start.2 = ((bf16[8,32,2048]{2,1,0:T(8,128)(2,1)}), bf16[8,32,2048]{2,1,0:T(8,128)(2,1)}, u32[]{:S(2)}, u32[]{:S(2)}) async-start(bf16[8,32,2048]{2,1,0:T(8,128)(2,1)} %bitcast.12), calls=%async_computation.2 | async-start | bytes 2097152 | tf_op jit(solution)/shard_map/all_to_all | solution.py:297
  93.1 10.3 %shard_map.121 = (f32[512,704]{1,0:T(8,128)}, f32[512,704]{1,0:T(8,128)}, bf16[512,704]{1,0:T(8,128)(2,1)}, bf16[512,2048]{1,0:T(8,128)(2,1)}) custom-call(bf16[704,2048]{1,0:T(8,128)(2,1)} %bitcast.44, bf16[8,2,32,2048]{3,2,1,0:T(8,128)(2,1)} %bitcast.42, bf16[256,2048]{1,0:T(8,128)(2,1)} %bitcast.50, bf16[704,2048]{1,0:T(8,128)(2,1)} %bitcast.46, ...), custom_call_target="tpu_custom_call" | custom-call | flops 1 | bytes 1 | tf_op jit(solution)/shard_map/pallas_call | solution.py:269
  104.9 3.6 %all-to-all-start.3 = ((bf16[8,64,2048]{2,1,0:T(8,128)(2,1)}), bf16[8,64,2048]{2,1,0:T(8,128)(2,1)S(1)}, u32[]{:S(2)}, u32[]{:S(2)}) async-start(bf16[8,64,2048]{2,1,0:T(8,128)(2,1)} %bitcast.53), calls=%async_computation.3 | async-start | bytes 4194304 | tf_op jit(solution)/shard_map/all_to_all | solution.py:297
  108.8 18.3 %shard_map.122 = (bf16[256,2048]{1,0:T(8,128)(2,1)}, bf16[256,2048]{1,0:T(8,128)(2,1)}, bf16[2112,2048]{1,0:T(8,128)(2,1)}) custom-call(bf16[704,2048]{1,0:T(8,128)(2,1)} %bitcast.49, bf16[8,2,32,2048]{3,2,1,0:T(8,128)(2,1)} %bitcast.43, bf16[256,2048]{1,0:T(8,128)(2,1)} %bitcast.13.refs_2_, f32[512,704]{1,0:T(8,128)} %get-tuple-element.61.refs_3_, ...), custom_call_target="tpu_custom_call" | custom-call | flops 1 | bytes 1 | tf_op jit(solution)/shard_map/pallas_call | solution.py:269
  127.1 7.0 %all-to-all-done.3 = bf16[8,64,2048]{2,1,0:T(8,128)(2,1)S(1)} async-done(((bf16[8,64,2048]{2,1,0:T(8,128)(2,1)}), bf16[8,64,2048]{2,1,0:T(8,128)(2,1)S(1)}, u32[]{:S(2)}, u32[]{:S(2)}) %all-to-all-start.3) | async-done | bytes 2097184 | tf_op jit(solution)/shard_map/all_to_all | solution.py:297
  134.7 1.8 shard_map.123
  136.6 2.9 %collective-permute-start.4 = (f32[8,128]{1,0:T(8,128)S(1)}, f32[8,128]{1,0:T(8,128)S(1)}, u32[]{:S(2)}, u32[]{:S(2)}) collective-permute-start(f32[8,128]{1,0:T(8,128)S(1)} %get-tuple-element.73), channel_id=1, source_target_pairs={{0,8},{1,9},{2,10},{3,11},{4,12},{5,13},{6,14},{7,15},{8,0},{9,1},... | collective-permute-start | bytes 12296 | tf_op jit(solution)/shard_map/ppermute | solution.py:293
  139.5 4.2 %all-to-all-start.4 = ((bf16[8,32,2048]{2,1,0:T(8,128)(2,1)}), bf16[8,32,2048]{2,1,0:T(8,128)(2,1)S(1)}, u32[]{:S(2)}, u32[]{:S(2)}) async-start(bf16[8,32,2048]{2,1,0:T(8,128)(2,1)} %bitcast.55), calls=%async_computation.4 | async-start | bytes 2097152 | tf_op jit(solution)/shard_map/all_to_all | solution.py:297
  143.6 18.4 %collective-permute-done.4.far_grads = f32[8,128]{1,0:T(8,128)S(1)} collective-permute-done((f32[8,128]{1,0:T(8,128)S(1)}, f32[8,128]{1,0:T(8,128)S(1)}, u32[]{:S(2)}, u32[]{:S(2)}) %collective-permute-start.4) | collective-permute-done | bytes 4128 | tf_op jit(solution)/shard_map/ppermute | solution.py:293
  163.6 3.1 %all-to-all-done.4 = bf16[8,32,2048]{2,1,0:T(8,128)(2,1)S(1)} async-done(((bf16[8,32,2048]{2,1,0:T(8,128)(2,1)}), bf16[8,32,2048]{2,1,0:T(8,128)(2,1)S(1)}, u32[]{:S(2)}, u32[]{:S(2)}) %all-to-all-start.4) | async-done | bytes 1048608 | tf_op jit(solution)/shard_map/all_to_all | solution.py:297
  168.6 3.6 %all-to-all-start.5 = ((bf16[8,32,2048]{2,1,0:T(8,128)(2,1)}), bf16[8,32,2048]{2,1,0:T(8,128)(2,1)S(1)}, u32[]{:S(2)}, u32[]{:S(2)}) async-start(bf16[8,32,2048]{2,1,0:T(8,128)(2,1)} %bitcast.54), calls=%async_computation.6 | async-start | bytes 2097152 | tf_op jit(solution)/shard_map/all_to_all | solution.py:297
  172.2 1.8 collective-permute-start.5
  175.0 2.9 %shard_map.126 = (bf16[128,2048]{1,0:T(8,128)(2,1)}, f32[8,128]{1,0:T(8,128)S(1)}) custom-call(s32[1]{0:T(128)} %bitcast.me_ref, f32[4,128]{1,0:T(4,128)S(1)} %copy-done.6, f32[4,128]{1,0:T(4,128)S(1)} %copy-done.8, bf16[128,2048]{1,0:T(8,128)(2,1)S(1)} %copy-done.1, bf16[512,2048]{1,0:T(8,128)(2,1)S(1)} %bitcast.39, ...), custom_call_target="tpu_custom_call" | custom-call | flops 536870912 | bytes 3682304 | tf_op jit(solution)/shard_map/pallas_call | solution.py:21
  177.9 6.1 %fusion = (f32[1,704,1024]{2,1,0:T(8,128)}, f32[1,1024,704]{1,2,0:T(8,128)}, f32[1,1024,704]{1,2,0:T(8,128)}) fusion(bf16[2112,1024]{1,0:T(8,128)(2,1)} %reduce-scatter.2.cloned.1.call-done), kind=kLoop, calls=%fused_computation.3 | loop fusion | flops 2162688 | bytes 12976128 | tf_op jit(solution)/shard_map/broadcast_in_dim | solution.py:444
  184.0 9.9 %collective-permute-done.5.came.refs_2_ = bf16[128,2048]{1,0:T(8,128)(2,1)} collective-permute-done((bf16[128,2048]{1,0:T(8,128)(2,1)}, bf16[128,2048]{1,0:T(8,128)(2,1)}, u32[]{:S(2)}, u32[]{:S(2)}) %collective-permute-start.5) | collective-permute-done | bytes 524320 | tf_op jit(solution)/shard_map/ppermute | solution.py:293
  196.8 2.2 %shard_map.128 = bf16[128,2048]{1,0:T(8,128)(2,1)} custom-call(s32[1]{0:T(128)} %constant.2.clone.1.me_ref, bf16[256,128]{1,0:T(8,128)(2,1)S(1)} %copy-done.3, bf16[256,2048]{1,0:T(8,128)(2,1)S(1)} %bitcast.40, bf16[128,2048]{1,0:T(8,128)(2,1)} %collective-permute-done.5.came.refs_2_), custom_call_target="tpu_custom_call" | custom-call | flops 134217728 | bytes 2162688 | tf_op jit(solution)/shard_map/pallas_call | solution.py:21
  (40 shorter events, 17.4 us)
Async XLA Ops:
  7.2 27.7 %collective-permute-start = (bf16[128,2048]{1,0:T(8,128)(2,1)}, bf16[128,2048]{1,0:T(8,128)(2,1)S(1)}, u32[]{:S(2)}, u32[]{:S(2)}) collective-permute-start(bf16[128,2048]{1,0:T(8,128)(2,1)} %x_hbm.1), channel_id=1, source_target_pairs={{0,8},{1,9},{2,10},{3,11},{4,12},{5,13},{6,14},{7,15},{8,0},{9,1},... | collective-permute-start | bytes 1572872 | tf_op jit(solution)/shard_map/ppermute | solution.py:293
  12.6 0.6 copy-start.5
  12.6 22.2 %collective-permute-start.1 = (f32[4,128]{1,0:T(4,128)S(1)}, f32[4,128]{1,0:T(4,128)S(1)}, u32[]{:S(2)}, u32[]{:S(2)}) collective-permute-start(f32[4,128]{1,0:T(4,128)S(1)} %pad_maximum_fusion.meta), channel_id=1, source_target_pairs={{0,8},{1,9},{2,10},{3,11},{4,12},{5,13},{6,14},{7,15},{8,0},{9,1},... | collective-permute-start | bytes 6152 | tf_op jit(solution)/shard_map/ppermute | solution.py:293
  17.1 39.4 %all-to-all-start = ((bf16[8,64,2048]{2,1,0:T(8,128)(2,1)}), bf16[8,64,2048]{2,1,0:T(8,128)(2,1)S(1)}, u32[]{:S(2)}, u32[]{:S(2)}) async-start(bf16[8,64,2048]{2,1,0:T(8,128)(2,1)} %bitcast.52), calls=%async_computation | async-start | bytes 4194304 | tf_op jit(solution)/shard_map/all_to_all | solution.py:297
  21.9 36.0 %copy-start = (bf16[128,2048]{1,0:T(8,128)(2,1)S(1)}, bf16[128,2048]{1,0:T(8,128)(2,1)}, u32[]{:S(2)}) copy-start(bf16[128,2048]{1,0:T(8,128)(2,1)} %block.1) | copy-start | bytes 1572868
  34.8 99.2 %copy-start.7 = (f32[4,128]{1,0:T(4,128)}, f32[4,128]{1,0:T(4,128)S(1)}, u32[]{:S(2)}) copy-start(f32[4,128]{1,0:T(4,128)S(1)} %collective-permute-done.1.refs_0_.meta_far.meta) | copy-start | bytes 6148
  56.5 1.3 copy-start.9
  57.9 25.3 %collective-permute-start.2 = (bf16[128,2048]{1,0:T(8,128)(2,1)S(1)}, bf16[128,2048]{1,0:T(8,128)(2,1)S(1)}, u32[]{:S(2)}, u32[]{:S(2)}) collective-permute-start(bf16[128,2048]{1,0:T(8,128)(2,1)S(1)} %copy-done), channel_id=1, source_target_pairs={{0,8},{1,9},{2,10},{3,11},{4,12},{5,13},{6,14},{7,15},{8,0},{9,1},... | collective-permute-start | bytes 1572872 | tf_op jit(solution)/shard_map/ppermute | solution.py:293
  59.0 29.9 %all-to-all-start.1 = ((bf16[8,32,2048]{2,1,0:T(8,128)(2,1)}), bf16[8,32,2048]{2,1,0:T(8,128)(2,1)S(1)}, u32[]{:S(2)}, u32[]{:S(2)}) async-start(bf16[8,32,2048]{2,1,0:T(8,128)(2,1)} %bitcast.8), calls=%async_computation.1 | async-start | bytes 2097152 | tf_op jit(solution)/shard_map/all_to_all | solution.py:297
  88.8 4.3 %copy-start.10 = (bf16[8,32,2048]{2,1,0:T(8,128)(2,1)}, bf16[8,32,2048]{2,1,0:T(8,128)(2,1)S(1)}, u32[]{:S(2)}) copy-start(bf16[8,32,2048]{2,1,0:T(8,128)(2,1)S(1)} %all-to-all-done.1) | copy-start | bytes 3145732
  88.8 16.1 %all-to-all-start.2 = ((bf16[8,32,2048]{2,1,0:T(8,128)(2,1)}), bf16[8,32,2048]{2,1,0:T(8,128)(2,1)}, u32[]{:S(2)}, u32[]{:S(2)}) async-start(bf16[8,32,2048]{2,1,0:T(8,128)(2,1)} %bitcast.12), calls=%async_computation.2 | async-start | bytes 2097152 | tf_op jit(solution)/shard_map/all_to_all | solution.py:297
  104.9 29.1 %all-to-all-start.3 = ((bf16[8,64,2048]{2,1,0:T(8,128)(2,1)}), bf16[8,64,2048]{2,1,0:T(8,128)(2,1)S(1)}, u32[]{:S(2)}, u32[]{:S(2)}) async-start(bf16[8,64,2048]{2,1,0:T(8,128)(2,1)} %bitcast.53), calls=%async_computation.3 | async-start | bytes 4194304 | tf_op jit(solution)/shard_map/all_to_all | solution.py:297
  108.5 69.4 %reduce-scatter.2.cloned.1.call-start = ((), (), s32[]{:S(2)}) async-start(), calls=%async_computation.7 | async-start | bytes 12976128 | tf_op jit(solution)/shard_map/reduce_scatter | solution.py:403
  134.0 0.7 copy-start.6
  136.5 25.5 %collective-permute-start.3 = (bf16[128,2048]{1,0:T(8,128)(2,1)}, bf16[128,2048]{1,0:T(8,128)(2,1)}, u32[]{:S(2)}, u32[]{:S(2)}) collective-permute-start(bf16[128,2048]{1,0:T(8,128)(2,1)} %get-tuple-element.72), channel_id=1, source_target_pairs={{0,8},{1,9},{2,10},{3,11},{4,12},{5,13},{6,14},{7,15},{8,0},{9,1},... | collective-permute-start | bytes 1572872 | tf_op jit(solution)/shard_map/ppermute | solution.py:293
  136.6 25.4 %collective-permute-start.4 = (f32[8,128]{1,0:T(8,128)S(1)}, f32[8,128]{1,0:T(8,128)S(1)}, u32[]{:S(2)}, u32[]{:S(2)}) collective-permute-start(f32[8,128]{1,0:T(8,128)S(1)} %get-tuple-element.73), channel_id=1, source_target_pairs={{0,8},{1,9},{2,10},{3,11},{4,12},{5,13},{6,14},{7,15},{8,0},{9,1},... | collective-permute-start | bytes 12296 | tf_op jit(solution)/shard_map/ppermute | solution.py:293
  139.5 27.2 %all-to-all-start.4 = ((bf16[8,32,2048]{2,1,0:T(8,128)(2,1)}), bf16[8,32,2048]{2,1,0:T(8,128)(2,1)S(1)}, u32[]{:S(2)}, u32[]{:S(2)}) async-start(bf16[8,32,2048]{2,1,0:T(8,128)(2,1)} %bitcast.55), calls=%async_computation.4 | async-start | bytes 2097152 | tf_op jit(solution)/shard_map/all_to_all | solution.py:297
  162.0 12.0 %copy-start.8 = (f32[4,128]{1,0:T(4,128)S(1)}, f32[4,128]{1,0:T(4,128)}, u32[]{:S(2)}) copy-start(f32[4,128]{1,0:T(4,128)} %copy-done.7) | copy-start | bytes 6148
  166.7 0.8 copy-start.4
  167.8 0.8 copy-start.2
  168.6 27.3 %all-to-all-start.5 = ((bf16[8,32,2048]{2,1,0:T(8,128)(2,1)}), bf16[8,32,2048]{2,1,0:T(8,128)(2,1)S(1)}, u32[]{:S(2)}, u32[]{:S(2)}) async-start(bf16[8,32,2048]{2,1,0:T(8,128)(2,1)} %bitcast.54), calls=%async_computation.6 | async-start | bytes 2097152 | tf_op jit(solution)/shard_map/all_to_all | solution.py:297
  172.2 21.6 %collective-permute-start.5 = (bf16[128,2048]{1,0:T(8,128)(2,1)}, bf16[128,2048]{1,0:T(8,128)(2,1)}, u32[]{:S(2)}, u32[]{:S(2)}) collective-permute-start(bf16[128,2048]{1,0:T(8,128)(2,1)} %copy-done.2), channel_id=1, source_target_pairs={{0,8},{1,9},{2,10},{3,11},{4,12},{5,13},{6,14},{7,15},{8,0},{9,1},... | collective-permute-start | bytes 1572872 | tf_op jit(solution)/shard_map/ppermute | solution.py:293
  174.0 1.0 copy-start.1
  196.0 0.8 copy-start.3
Sparse Core Ops, SparseCore 0:
  134.2 15.6 reduce-scatter.1

commit v19 on v18

--- a/solution.py
+++ b/solution.py
@@ -36,7 +36,7 @@
     return [(c, min(c + step, width)) for c in range(0, width, step)]
 
 
-def slot_tables(me, metas, top, side, capacity):
+def slot_tables(me, metas, top, side, capacity, wanted=None):
     count = len(metas)
     span = count * capacity
     tok = metas[0].shape[1]
@@ -48,7 +48,7 @@
     column = lax.broadcasted_iota(jnp.int32, (tok, tok), 1)
     earlier = jnp.where(row < column, 1.0, 0.0).astype(BF16)
     tables = []
-    for b in range(count):
+    for b in range(count) if wanted is None else (wanted,):
         named = [jnp.where(metas[b][k : k + 1, :] == expert, 1.0, 0.0) for k in range(top)]
         member = functools.reduce(lambda p, q: p + q, named)
         rank = jnp.dot(member.astype(BF16), earlier, preferred_element_type=F32)
@@ -103,13 +103,13 @@
 def sum_kernel(table, back, *refs):
     out = refs[-1]
     for c, e in strips(out.shape[1]):
-        got = picked_sum(table[...], back, c, e)
+        got = picked_sum(table, back, c, e)
         for far in refs[:-1]:
             got += far[:, c:e].astype(F32)
         out[:, c:e] = got.astype(BF16)
 
 
-def mix(top, table, meta, blocks, back, outs, grads, fars=(), far_grads=None):
+def mix(top, table, meta, blocks, back, outs, grads, fars=()):
     tok = meta.shape[1]
     gates = [meta[top + k : top + k + 1, :] for k in range(top)]
     gates = [jnp.transpose(jnp.broadcast_to(g, (8, tok)))[:, :1] for g in gates]
@@ -130,22 +130,19 @@
     grad = jnp.zeros((tok, LANES), F32)
     for k in range(top):
         grad += jnp.where(lane == k, sums[k], 0.0)
-    grad = jnp.transpose(grad)[: grads.shape[0]]
-    grads[...] = grad if far_grads is None else grad + far_grads[...]
+    grads[...] = jnp.transpose(grad)[: grads.shape[0]]
 
 
 def mix_kernel(
     top, side, capacity, me_ref, meta, meta_far, block, back, out, grads
 ):
-    tables = slot_tables(me_ref[0], [meta, meta_far], top, side, capacity)
-    mix(top, tables[1], meta_far, (block,), back, (out,), grads)
-
-
-def mix_last_kernel(
-    top, side, capacity, me_ref, meta, meta_far, block, back, far, far_grads, out, grads
-):
-    tables = slot_tables(me_ref[0], [meta, meta_far], top, side, capacity)
-    mix(top, tables[0], meta, (block,), back, (out,), grads, (far,), far_grads)
+    (table,) = slot_tables(me_ref[0], [meta, meta_far], top, side, capacity, 1)
+    mix(top, table, meta_far, (block,), back, (out,), grads)
+
+
+def mix_last_kernel(top, side, capacity, me_ref, meta, meta_far, block, back, far, out, grads):
+    (table,) = slot_tables(me_ref[0], [meta, meta_far], top, side, capacity, 0)
+    mix(top, table, meta, (block,), back, (out,), grads, (far,))
 
 
 def fetch(sources, targets, sems):
@@ -409,7 +406,7 @@
     )
     dx_far, mixed_far, grads_far = after(dx_far, mixed_far, grads_far)
     dx_far_back = exchange(dx_far)
-    mixed_far, grads_far = after(across(mixed_far), across(grads_far))
+    mixed_far = across(mixed_far)
 
     def table(meta, came):
         return pl.pallas_call(
@@ -423,18 +420,21 @@
 
     def total(table, back, *far):
         return local_call_plain(
-            sum_kernel, [shape((tok, feature), BF16)], [table, back, *far], work
+            lambda table, *refs: sum_kernel(table[...], *refs),
+            [shape((tok, feature), BF16)],
+            [table, back, *far],
+            work,
         )[0]
 
-    far_table, mixed_far, grads_far, dx_far_back = after(
-        table(meta_far, mixed_far), mixed_far, grads_far, dx_far_back
-    )
-    tokens_far, dx_own = after(total(far_table, dx_far_back), dx_own)
+    far_table, mixed_far, dx_far_back = after(
+        table(meta_far, mixed_far), mixed_far, dx_far_back
+    )
+    tokens_far, dx_own, grads_far = after(total(far_table, dx_far_back), dx_own, grads_far)
     dx_own_back = exchange(dx_own)
     mixed, grads = call(
         mix_last_kernel,
         [token_rows, grad_rows],
-        [meta, meta_far, d_mixed, y_back, mixed_far, grads_far],
+        [meta, meta_far, d_mixed, y_back, mixed_far],
         2 * top * work,
     )
     tokens_far = across(tokens_far)
@@ -443,7 +443,9 @@
         summed[units : 2 * units].astype(F32).T[None],
         summed[2 * units :].astype(F32)[None],
     )
-    tokens_far, mixed, grads, *weight_grads = after(tokens_far, mixed, grads, *weight_grads)
+    mixed, grads, grads_far, *weight_grads = after(mixed, grads, grads_far, *weight_grads)
+    grads = grads + across(grads_far)
+    tokens_far, mixed, *weight_grads = after(tokens_far, mixed, *weight_grads)
     own_table, tokens_far, dx_own_back = after(table(meta, tokens_far), tokens_far, dx_own_back)
     d_tokens = total(own_table, dx_own_back, tokens_far)
     return (mixed, d_tokens, grads[:top].T, *weight_grads)

time: 208 us -> 210 us (level)
  starting transfers between devices: 36.2 us -> 39.2 us
    ppermute x6, starting transfers between devices: 9.93 us -> 12.9 us  [across(): lax.ppermute(value, 'expert', [(e, (e + side) % experts) for e in range(e...]
    all_to_all x6, waiting for transfers between devices: 35.9 us -> 33.5 us  [exchange(): lax.all_to_all(shaped, 'expert', 0, 0, axis_index_groups=sets, tiled=True)]
  transfers between devices with their start and end apart: 13 -> 13, of which waited for: 10 -> 9; matrix products, arithmetic and copies ran while one was open for 4% -> 4% of each run, Pallas kernels for 21% -> 22%
where the time goes in v19:
time: 210 us; the launch traced here: 207 us
  waiting for transfers between devices  93.8 us (45%)
  Pallas kernels  45.8 us (22%)
  starting transfers between devices  39.2 us (19%)
  between operations  14.1 us (7%)
  other arithmetic  7.44 us (4%)
  local copies, waits for them, and re-layouts  6.59 us (3%)
    ppermute x6, waiting for transfers between devices, across(): lax.ppermute(value, 'expert', [(e, (e + side) % experts) for e in range(e...  60.3 us
    all_to_all x6, waiting for transfers between devices, exchange(): lax.all_to_all(shaped, 'expert', 0, 0, axis_index_groups=sets, tiled=True)  33.5 us
    pallas_call x2, Pallas kernels, streamed_call(): pl.pallas_call(kernel, out_shape=outs, in_specs=[pl.BlockSpec(memory_spac...  28.6 us
    all_to_all x6, starting transfers between devices, exchange(): lax.all_to_all(shaped, 'expert', 0, 0, axis_index_groups=sets, tiled=True)  26.1 us
    ppermute x6, starting transfers between devices, across(): lax.ppermute(value, 'expert', [(e, (e + side) % experts) for e in range(e...  12.9 us
    pallas_call x6, Pallas kernels, local_call(): pl.pallas_call(kernel, out_shape=outs, in_specs=[SMEM] + [VMEM] * len(arg...  10.3 us
    broadcast_in_dim x1, other arithmetic, on_device(): summed[2 * units:].astype(F32)[None]  6.07 us
    unnamed x22, local copies, waits for them, and re-layouts  6.02 us
  transfers between devices with their start and end apart: 13, of which 9 were waited for; matrix products, arithmetic and copies ran while one was open for 4% of the time, Pallas kernels for 22%

profile of v19, /device:TPU:0, one launch (start us, length us, event | category | flops | bytes accessed | tf_op | source)
XLA Modules:
  0.0 207.0 jit_solution(18286778707602952428)
XLA Ops:
  7.2 4.1 %collective-permute-start = (bf16[128,2048]{1,0:T(8,128)(2,1)}, bf16[128,2048]{1,0:T(8,128)(2,1)S(1)}, u32[]{:S(2)}, u32[]{:S(2)}) collective-permute-start(bf16[128,2048]{1,0:T(8,128)(2,1)} %x_hbm.1), channel_id=1, source_target_pairs={{0,8},{1,9},{2,10},{3,11},{4,12},{5,13},{6,14},{7,15},{8,0},{9,1},... | collective-permute-start | bytes 1572872 | tf_op jit(solution)/shard_map/ppermute | solution.py:290
  13.2 3.9 %shard_map.119 = bf16[512,2048]{1,0:T(8,128)(2,1)} custom-call(s32[1]{0:T(128)} %bitcast.me_ref, f32[4,128]{1,0:T(4,128)} %copy-done.5, bf16[128,2048]{1,0:T(8,128)(2,1)} %x_hbm.1, bf16[128,2048]{1,0:T(8,128)(2,1)} %block.1), custom_call_target="tpu_custom_call" | custom-call | flops 536870912 | bytes 1 | tf_op jit(solution)/shard_map/pallas_call | solution.py:321
  17.1 4.7 %all-to-all-start = ((bf16[8,64,2048]{2,1,0:T(8,128)(2,1)}), bf16[8,64,2048]{2,1,0:T(8,128)(2,1)S(1)}, u32[]{:S(2)}, u32[]{:S(2)}) async-start(bf16[8,64,2048]{2,1,0:T(8,128)(2,1)} %bitcast.52), calls=%async_computation | async-start | bytes 4194304 | tf_op jit(solution)/shard_map/all_to_all | solution.py:294
  21.9 12.9 %collective-permute-done.1.refs_0_.meta_far.meta = f32[4,128]{1,0:T(4,128)S(1)} collective-permute-done((f32[4,128]{1,0:T(4,128)S(1)}, f32[4,128]{1,0:T(4,128)S(1)}, u32[]{:S(2)}, u32[]{:S(2)}) %collective-permute-start.1) | collective-permute-done | bytes 2080 | tf_op jit(solution)/shard_map/ppermute | solution.py:290
  36.3 20.2 %all-to-all-done = bf16[8,64,2048]{2,1,0:T(8,128)(2,1)S(1)} async-done(((bf16[8,64,2048]{2,1,0:T(8,128)(2,1)}), bf16[8,64,2048]{2,1,0:T(8,128)(2,1)S(1)}, u32[]{:S(2)}, u32[]{:S(2)}) %all-to-all-start) | async-done | bytes 2097184 | tf_op jit(solution)/shard_map/all_to_all | solution.py:294
  59.0 5.7 %all-to-all-start.1 = ((bf16[8,32,2048]{2,1,0:T(8,128)(2,1)}), bf16[8,32,2048]{2,1,0:T(8,128)(2,1)S(1)}, u32[]{:S(2)}, u32[]{:S(2)}) async-start(bf16[8,32,2048]{2,1,0:T(8,128)(2,1)} %bitcast.8), calls=%async_computation.1 | async-start | bytes 2097152 | tf_op jit(solution)/shard_map/all_to_all | solution.py:294
  64.7 18.5 %collective-permute-done.2.refs_1_.block = bf16[128,2048]{1,0:T(8,128)(2,1)S(1)} collective-permute-done((bf16[128,2048]{1,0:T(8,128)(2,1)S(1)}, bf16[128,2048]{1,0:T(8,128)(2,1)S(1)}, u32[]{:S(2)}, u32[]{:S(2)}) %collective-permute-start.2) | collective-permute-done | bytes 524320 | tf_op jit(solution)/shard_map/ppermute | solution.py:290
  84.7 4.1 %all-to-all-done.1 = bf16[8,32,2048]{2,1,0:T(8,128)(2,1)S(1)} async-done(((bf16[8,32,2048]{2,1,0:T(8,128)(2,1)}), bf16[8,32,2048]{2,1,0:T(8,128)(2,1)S(1)}, u32[]{:S(2)}, u32[]{:S(2)}) %all-to-all-start.1) | async-done | bytes 1048608 | tf_op jit(solution)/shard_map/all_to_all | solution.py:294
  88.8 4.2 %all-to-all-start.2 = ((bf16[8,32,2048]{2,1,0:T(8,128)(2,1)}), bf16[8,32,2048]{2,1,0:T(8,128)(2,1)}, u32[]{:S(2)}, u32[]{:S(2)}) async-start(bf16[8,32,2048]{2,1,0:T(8,128)(2,1)} %bitcast.12), calls=%async_computation.2 | async-start | bytes 2097152 | tf_op jit(solution)/shard_map/all_to_all | solution.py:294
  93.1 10.3 %shard_map.121 = (f32[512,704]{1,0:T(8,128)}, f32[512,704]{1,0:T(8,128)}, bf16[512,704]{1,0:T(8,128)(2,1)}, bf16[512,2048]{1,0:T(8,128)(2,1)}) custom-call(bf16[704,2048]{1,0:T(8,128)(2,1)} %bitcast.44, bf16[8,2,32,2048]{3,2,1,0:T(8,128)(2,1)} %bitcast.42, bf16[256,2048]{1,0:T(8,128)(2,1)} %bitcast.50, bf16[704,2048]{1,0:T(8,128)(2,1)} %bitcast.46, ...), custom_call_target="tpu_custom_call" | custom-call | flops 1 | bytes 1 | tf_op jit(solution)/shard_map/pallas_call | solution.py:266
  104.9 3.6 %all-to-all-start.3 = ((bf16[8,64,2048]{2,1,0:T(8,128)(2,1)}), bf16[8,64,2048]{2,1,0:T(8,128)(2,1)S(1)}, u32[]{:S(2)}, u32[]{:S(2)}) async-start(bf16[8,64,2048]{2,1,0:T(8,128)(2,1)} %bitcast.53), calls=%async_computation.3 | async-start | bytes 4194304 | tf_op jit(solution)/shard_map/all_to_all | solution.py:294
  108.8 18.3 %shard_map.122 = (bf16[256,2048]{1,0:T(8,128)(2,1)}, bf16[256,2048]{1,0:T(8,128)(2,1)}, bf16[2112,2048]{1,0:T(8,128)(2,1)}) custom-call(bf16[704,2048]{1,0:T(8,128)(2,1)} %bitcast.49, bf16[8,2,32,2048]{3,2,1,0:T(8,128)(2,1)} %bitcast.43, bf16[256,2048]{1,0:T(8,128)(2,1)} %bitcast.13.refs_2_, f32[512,704]{1,0:T(8,128)} %get-tuple-element.64.refs_3_, ...), custom_call_target="tpu_custom_call" | custom-call | flops 1 | bytes 1 | tf_op jit(solution)/shard_map/pallas_call | solution.py:266
  127.1 7.0 %all-to-all-done.3 = bf16[8,64,2048]{2,1,0:T(8,128)(2,1)S(1)} async-done(((bf16[8,64,2048]{2,1,0:T(8,128)(2,1)}), bf16[8,64,2048]{2,1,0:T(8,128)(2,1)S(1)}, u32[]{:S(2)}, u32[]{:S(2)}) %all-to-all-start.3) | async-done | bytes 2097184 | tf_op jit(solution)/shard_map/all_to_all | solution.py:294
  134.7 1.8 shard_map.123
  136.6 4.2 %all-to-all-start.4 = ((bf16[8,32,2048]{2,1,0:T(8,128)(2,1)}), bf16[8,32,2048]{2,1,0:T(8,128)(2,1)S(1)}, u32[]{:S(2)}, u32[]{:S(2)}) async-start(bf16[8,32,2048]{2,1,0:T(8,128)(2,1)} %bitcast.55), calls=%async_computation.4 | async-start | bytes 2097152 | tf_op jit(solution)/shard_map/all_to_all | solution.py:294
  140.8 21.1 %collective-permute-done.3.came.far = bf16[128,2048]{1,0:T(8,128)(2,1)} collective-permute-done((bf16[128,2048]{1,0:T(8,128)(2,1)}, bf16[128,2048]{1,0:T(8,128)(2,1)}, u32[]{:S(2)}, u32[]{:S(2)}) %collective-permute-start.3) | collective-permute-done | bytes 524320 | tf_op jit(solution)/shard_map/ppermute | solution.py:290
  161.9 1.6 shard_map.124.refs_0_
  166.1 3.6 %all-to-all-start.5 = ((bf16[8,32,2048]{2,1,0:T(8,128)(2,1)}), bf16[8,32,2048]{2,1,0:T(8,128)(2,1)S(1)}, u32[]{:S(2)}, u32[]{:S(2)}) async-start(bf16[8,32,2048]{2,1,0:T(8,128)(2,1)} %bitcast.54), calls=%async_computation.6 | async-start | bytes 2097152 | tf_op jit(solution)/shard_map/all_to_all | solution.py:294
  169.7 4.2 %collective-permute-start.4 = (bf16[128,2048]{1,0:T(8,128)(2,1)}, bf16[128,2048]{1,0:T(8,128)(2,1)}, u32[]{:S(2)}, u32[]{:S(2)}) collective-permute-start(bf16[128,2048]{1,0:T(8,128)(2,1)} %copy-done.2), channel_id=1, source_target_pairs={{0,8},{1,9},{2,10},{3,11},{4,12},{5,13},{6,14},{7,15},{8,0},{9,1},... | collective-permute-start | bytes 1572872 | tf_op jit(solution)/shard_map/ppermute | solution.py:290
  174.9 2.9 %shard_map.126 = (bf16[128,2048]{1,0:T(8,128)(2,1)}, f32[8,128]{1,0:T(8,128)S(1)}) custom-call(s32[1]{0:T(128)} %bitcast.me_ref, f32[4,128]{1,0:T(4,128)S(1)} %copy-done.6, f32[4,128]{1,0:T(4,128)S(1)} %copy-done.8, bf16[128,2048]{1,0:T(8,128)(2,1)S(1)} %copy-done.1, bf16[512,2048]{1,0:T(8,128)(2,1)S(1)} %bitcast.39, ...), custom_call_target="tpu_custom_call" | custom-call | flops 536870912 | bytes 3678208 | tf_op jit(solution)/shard_map/pallas_call | solution.py:21
  177.8 6.1 %fusion = (f32[1,704,1024]{2,1,0:T(8,128)}, f32[1,1024,704]{1,2,0:T(8,128)}, f32[1,1024,704]{1,2,0:T(8,128)}) fusion(bf16[2112,1024]{1,0:T(8,128)(2,1)} %reduce-scatter.2.cloned.1.call-done), kind=kLoop, calls=%fused_computation.3 | loop fusion | flops 2162688 | bytes 12976128 | tf_op jit(solution)/shard_map/broadcast_in_dim | solution.py:444
  183.9 7.8 %collective-permute-done.4.came.refs_2_ = bf16[128,2048]{1,0:T(8,128)(2,1)} collective-permute-done((bf16[128,2048]{1,0:T(8,128)(2,1)}, bf16[128,2048]{1,0:T(8,128)(2,1)}, u32[]{:S(2)}, u32[]{:S(2)}) %collective-permute-start.4) | collective-permute-done | bytes 524320 | tf_op jit(solution)/shard_map/ppermute | solution.py:290
  191.7 3.4 %collective-permute-start.5 = (f32[8,128]{1,0:T(8,128)S(1)}, f32[8,128]{1,0:T(8,128)S(1)}, u32[]{:S(2)}, u32[]{:S(2)}) collective-permute-start(f32[8,128]{1,0:T(8,128)S(1)} %get-tuple-element.98), channel_id=1, source_target_pairs={{0,8},{1,9},{2,10},{3,11},{4,12},{5,13},{6,14},{7,15},{8,0},{9,1},... | collective-permute-start | bytes 12296 | tf_op jit(solution)/shard_map/ppermute | solution.py:290
  197.4 2.2 %shard_map.128 = bf16[128,2048]{1,0:T(8,128)(2,1)} custom-call(s32[1]{0:T(128)} %constant.2.clone.1.me_ref, bf16[256,128]{1,0:T(8,128)(2,1)S(1)} %copy-done.3, bf16[256,2048]{1,0:T(8,128)(2,1)S(1)} %bitcast.40, bf16[128,2048]{1,0:T(8,128)(2,1)} %collective-permute-done.4.came.refs_2_), custom_call_target="tpu_custom_call" | custom-call | flops 134217728 | bytes 2162688 | tf_op jit(solution)/shard_map/pallas_call | solution.py:21
  (41 shorter events, 16.5 us)
Async XLA Ops:
  7.2 27.7 %collective-permute-start = (bf16[128,2048]{1,0:T(8,128)(2,1)}, bf16[128,2048]{1,0:T(8,128)(2,1)S(1)}, u32[]{:S(2)}, u32[]{:S(2)}) collective-permute-start(bf16[128,2048]{1,0:T(8,128)(2,1)} %x_hbm.1), channel_id=1, source_target_pairs={{0,8},{1,9},{2,10},{3,11},{4,12},{5,13},{6,14},{7,15},{8,0},{9,1},... | collective-permute-start | bytes 1572872 | tf_op jit(solution)/shard_map/ppermute | solution.py:290
  12.6 0.6 copy-start.5
  12.6 22.2 %collective-permute-start.1 = (f32[4,128]{1,0:T(4,128)S(1)}, f32[4,128]{1,0:T(4,128)S(1)}, u32[]{:S(2)}, u32[]{:S(2)}) collective-permute-start(f32[4,128]{1,0:T(4,128)S(1)} %pad_maximum_fusion.meta), channel_id=1, source_target_pairs={{0,8},{1,9},{2,10},{3,11},{4,12},{5,13},{6,14},{7,15},{8,0},{9,1},... | collective-permute-start | bytes 6152 | tf_op jit(solution)/shard_map/ppermute | solution.py:290
  17.1 39.4 %all-to-all-start = ((bf16[8,64,2048]{2,1,0:T(8,128)(2,1)}), bf16[8,64,2048]{2,1,0:T(8,128)(2,1)S(1)}, u32[]{:S(2)}, u32[]{:S(2)}) async-start(bf16[8,64,2048]{2,1,0:T(8,128)(2,1)} %bitcast.52), calls=%async_computation | async-start | bytes 4194304 | tf_op jit(solution)/shard_map/all_to_all | solution.py:294
  21.9 36.0 %copy-start = (bf16[128,2048]{1,0:T(8,128)(2,1)S(1)}, bf16[128,2048]{1,0:T(8,128)(2,1)}, u32[]{:S(2)}) copy-start(bf16[128,2048]{1,0:T(8,128)(2,1)} %block.1) | copy-start | bytes 1572868
  34.8 99.2 %copy-start.7 = (f32[4,128]{1,0:T(4,128)}, f32[4,128]{1,0:T(4,128)S(1)}, u32[]{:S(2)}) copy-start(f32[4,128]{1,0:T(4,128)S(1)} %collective-permute-done.1.refs_0_.meta_far.meta) | copy-start | bytes 6148
  56.5 1.3 copy-start.9
  57.9 25.3 %collective-permute-start.2 = (bf16[128,2048]{1,0:T(8,128)(2,1)S(1)}, bf16[128,2048]{1,0:T(8,128)(2,1)S(1)}, u32[]{:S(2)}, u32[]{:S(2)}) collective-permute-start(bf16[128,2048]{1,0:T(8,128)(2,1)S(1)} %copy-done), channel_id=1, source_target_pairs={{0,8},{1,9},{2,10},{3,11},{4,12},{5,13},{6,14},{7,15},{8,0},{9,1},... | collective-permute-start | bytes 1572872 | tf_op jit(solution)/shard_map/ppermute | solution.py:290
  59.0 29.9 %all-to-all-start.1 = ((bf16[8,32,2048]{2,1,0:T(8,128)(2,1)}), bf16[8,32,2048]{2,1,0:T(8,128)(2,1)S(1)}, u32[]{:S(2)}, u32[]{:S(2)}) async-start(bf16[8,32,2048]{2,1,0:T(8,128)(2,1)} %bitcast.8), calls=%async_computation.1 | async-start | bytes 2097152 | tf_op jit(solution)/shard_map/all_to_all | solution.py:294
  88.8 4.3 %copy-start.10 = (bf16[8,32,2048]{2,1,0:T(8,128)(2,1)}, bf16[8,32,2048]{2,1,0:T(8,128)(2,1)S(1)}, u32[]{:S(2)}) copy-start(bf16[8,32,2048]{2,1,0:T(8,128)(2,1)S(1)} %all-to-all-done.1) | copy-start | bytes 3145732
  88.8 16.1 %all-to-all-start.2 = ((bf16[8,32,2048]{2,1,0:T(8,128)(2,1)}), bf16[8,32,2048]{2,1,0:T(8,128)(2,1)}, u32[]{:S(2)}, u32[]{:S(2)}) async-start(bf16[8,32,2048]{2,1,0:T(8,128)(2,1)} %bitcast.12), calls=%async_computation.2 | async-start | bytes 2097152 | tf_op jit(solution)/shard_map/all_to_all | solution.py:294
  104.9 29.1 %all-to-all-start.3 = ((bf16[8,64,2048]{2,1,0:T(8,128)(2,1)}), bf16[8,64,2048]{2,1,0:T(8,128)(2,1)S(1)}, u32[]{:S(2)}, u32[]{:S(2)}) async-start(bf16[8,64,2048]{2,1,0:T(8,128)(2,1)} %bitcast.53), calls=%async_computation.3 | async-start | bytes 4194304 | tf_op jit(solution)/shard_map/all_to_all | solution.py:294
  108.5 69.3 %reduce-scatter.2.cloned.1.call-start = ((), (), s32[]{:S(2)}) async-start(), calls=%async_computation.7 | async-start | bytes 12976128 | tf_op jit(solution)/shard_map/reduce_scatter | solution.py:400
  134.0 0.7 copy-start.6
  136.5 25.4 %collective-permute-start.3 = (bf16[128,2048]{1,0:T(8,128)(2,1)}, bf16[128,2048]{1,0:T(8,128)(2,1)}, u32[]{:S(2)}, u32[]{:S(2)}) collective-permute-start(bf16[128,2048]{1,0:T(8,128)(2,1)} %get-tuple-element.75), channel_id=1, source_target_pairs={{0,8},{1,9},{2,10},{3,11},{4,12},{5,13},{6,14},{7,15},{8,0},{9,1},... | collective-permute-start | bytes 1572872 | tf_op jit(solution)/shard_map/ppermute | solution.py:290
  136.6 27.6 %all-to-all-start.4 = ((bf16[8,32,2048]{2,1,0:T(8,128)(2,1)}), bf16[8,32,2048]{2,1,0:T(8,128)(2,1)S(1)}, u32[]{:S(2)}, u32[]{:S(2)}) async-start(bf16[8,32,2048]{2,1,0:T(8,128)(2,1)} %bitcast.55), calls=%async_computation.4 | async-start | bytes 2097152 | tf_op jit(solution)/shard_map/all_to_all | solution.py:294
  161.9 12.0 %copy-start.8 = (f32[4,128]{1,0:T(4,128)S(1)}, f32[4,128]{1,0:T(4,128)}, u32[]{:S(2)}) copy-start(f32[4,128]{1,0:T(4,128)} %copy-done.7) | copy-start | bytes 6148
  164.2 0.8 copy-start.4
  165.3 0.8 copy-start.2
  166.1 30.4 %all-to-all-start.5 = ((bf16[8,32,2048]{2,1,0:T(8,128)(2,1)}), bf16[8,32,2048]{2,1,0:T(8,128)(2,1)S(1)}, u32[]{:S(2)}, u32[]{:S(2)}) async-start(bf16[8,32,2048]{2,1,0:T(8,128)(2,1)} %bitcast.54), calls=%async_computation.6 | async-start | bytes 2097152 | tf_op jit(solution)/shard_map/all_to_all | solution.py:294
  169.7 22.0 %collective-permute-start.4 = (bf16[128,2048]{1,0:T(8,128)(2,1)}, bf16[128,2048]{1,0:T(8,128)(2,1)}, u32[]{:S(2)}, u32[]{:S(2)}) collective-permute-start(bf16[128,2048]{1,0:T(8,128)(2,1)} %copy-done.2), channel_id=1, source_target_pairs={{0,8},{1,9},{2,10},{3,11},{4,12},{5,13},{6,14},{7,15},{8,0},{9,1},... | collective-permute-start | bytes 1572872 | tf_op jit(solution)/shard_map/ppermute | solution.py:290
  173.9 1.0 copy-start.1
  191.7 7.9 %collective-permute-start.5 = (f32[8,128]{1,0:T(8,128)S(1)}, f32[8,128]{1,0:T(8,128)S(1)}, u32[]{:S(2)}, u32[]{:S(2)}) collective-permute-start(f32[8,128]{1,0:T(8,128)S(1)} %get-tuple-element.98), channel_id=1, source_target_pairs={{0,8},{1,9},{2,10},{3,11},{4,12},{5,13},{6,14},{7,15},{8,0},{9,1},... | collective-permute-start | bytes 12296 | tf_op jit(solution)/shard_map/ppermute | solution.py:290
  196.6 0.8 copy-start.3
Sparse Core Ops, SparseCore 0:
  134.2 15.6 reduce-scatter.1

commit v20 on v19

--- a/solution.py
+++ b/solution.py
@@ -429,7 +429,9 @@
     far_table, mixed_far, dx_far_back = after(
         table(meta_far, mixed_far), mixed_far, dx_far_back
     )
-    tokens_far, dx_own, grads_far = after(total(far_table, dx_far_back), dx_own, grads_far)
+    tokens_far, dx_own, grads_far = after(
+        total(far_table, dx_far_back), dx_own, across(grads_far)
+    )
     dx_own_back = exchange(dx_own)
     mixed, grads = call(
         mix_last_kernel,
@@ -443,9 +445,8 @@
         summed[units : 2 * units].astype(F32).T[None],
         summed[2 * units :].astype(F32)[None],
     )
-    mixed, grads, grads_far, *weight_grads = after(mixed, grads, grads_far, *weight_grads)
-    grads = grads + across(grads_far)
-    tokens_far, mixed, *weight_grads = after(tokens_far, mixed, *weight_grads)
+    grads = grads + grads_far
+    tokens_far, mixed, grads, *weight_grads = after(tokens_far, mixed, grads, *weight_grads)
     own_table, tokens_far, dx_own_back = after(table(meta, tokens_far), tokens_far, dx_own_back)
     d_tokens = total(own_table, dx_own_back, tokens_far)
     return (mixed, d_tokens, grads[:top].T, *weight_grads)

time: 210 us -> 208 us (level)
  waiting for transfers between devices: 93.8 us -> 91.5 us
    ppermute x6, waiting for transfers between devices: 60.3 us -> 57.5 us  [across(): lax.ppermute(value, 'expert', [(e, (e + side) % experts) for e in range(e...]
  transfers between devices with their start and end apart: 13 -> 13, of which waited for: 9 -> 10; matrix products, arithmetic and copies ran while one was open for 4% -> 4% of each run, Pallas kernels for 22% -> 21%
where the time goes in v20:
time: 208 us; the launch traced here: 204 us
  waiting for transfers between devices  91.5 us (44%)
  Pallas kernels  45.8 us (22%)
  starting transfers between devices  38.6 us (19%)
  between operations  14.1 us (7%)
  other arithmetic  7.44 us (4%)
  local copies, waits for them, and re-layouts  6.59 us (3%)
    ppermute x6, waiting for transfers between devices, across(): lax.ppermute(value, 'expert', [(e, (e + side) % experts) for e in range(e...  57.5 us
    all_to_all x6, waiting for transfers between devices, exchange(): lax.all_to_all(shaped, 'expert', 0, 0, axis_index_groups=sets, tiled=True)  34 us
    pallas_call x2, Pallas kernels, streamed_call(): pl.pallas_call(kernel, out_shape=outs, in_specs=[pl.BlockSpec(memory_spac...  28.6 us
    all_to_all x6, starting transfers between devices, exchange(): lax.all_to_all(shaped, 'expert', 0, 0, axis_index_groups=sets, tiled=True)  26.1 us
    ppermute x6, starting transfers between devices, across(): lax.ppermute(value, 'expert', [(e, (e + side) % experts) for e in range(e...  12.3 us
    pallas_call x6, Pallas kernels, local_call(): pl.pallas_call(kernel, out_shape=outs, in_specs=[SMEM] + [VMEM] * len(arg...  10.3 us
    broadcast_in_dim x1, other arithmetic, on_device(): summed[2 * units:].astype(F32)[None]  6.07 us
    unnamed x22, local copies, waits for them, and re-layouts  6.02 us
  transfers between devices with their start and end apart: 13, of which 10 were waited for; matrix products, arithmetic and copies ran while one was open for 4% of the time, Pallas kernels for 21%

profile of v20, /device:TPU:0, one launch (start us, length us, event | category | flops | bytes accessed | tf_op | source)
XLA Modules:
  0.0 204.1 jit_solution(15079847680570844711)
XLA Ops:
  7.2 4.1 %collective-permute-start = (bf16[128,2048]{1,0:T(8,128)(2,1)}, bf16[128,2048]{1,0:T(8,128)(2,1)S(1)}, u32[]{:S(2)}, u32[]{:S(2)}) collective-permute-start(bf16[128,2048]{1,0:T(8,128)(2,1)} %x_hbm.1), channel_id=1, source_target_pairs={{0,8},{1,9},{2,10},{3,11},{4,12},{5,13},{6,14},{7,15},{8,0},{9,1},... | collective-permute-start | bytes 1572872 | tf_op jit(solution)/shard_map/ppermute | solution.py:290
  13.2 3.9 %shard_map.119 = bf16[512,2048]{1,0:T(8,128)(2,1)} custom-call(s32[1]{0:T(128)} %bitcast.me_ref, f32[4,128]{1,0:T(4,128)} %copy-done.5, bf16[128,2048]{1,0:T(8,128)(2,1)} %x_hbm.1, bf16[128,2048]{1,0:T(8,128)(2,1)} %block.1), custom_call_target="tpu_custom_call" | custom-call | flops 536870912 | bytes 1 | tf_op jit(solution)/shard_map/pallas_call | solution.py:321
  17.1 4.7 %all-to-all-start = ((bf16[8,64,2048]{2,1,0:T(8,128)(2,1)}), bf16[8,64,2048]{2,1,0:T(8,128)(2,1)S(1)}, u32[]{:S(2)}, u32[]{:S(2)}) async-start(bf16[8,64,2048]{2,1,0:T(8,128)(2,1)} %bitcast.52), calls=%async_computation | async-start | bytes 4194304 | tf_op jit(solution)/shard_map/all_to_all | solution.py:294
  21.9 12.9 %collective-permute-done.1.refs_0_.meta_far.meta = f32[4,128]{1,0:T(4,128)S(1)} collective-permute-done((f32[4,128]{1,0:T(4,128)S(1)}, f32[4,128]{1,0:T(4,128)S(1)}, u32[]{:S(2)}, u32[]{:S(2)}) %collective-permute-start.1) | collective-permute-done | bytes 2080 | tf_op jit(solution)/shard_map/ppermute | solution.py:290
  36.3 20.2 %all-to-all-done = bf16[8,64,2048]{2,1,0:T(8,128)(2,1)S(1)} async-done(((bf16[8,64,2048]{2,1,0:T(8,128)(2,1)}), bf16[8,64,2048]{2,1,0:T(8,128)(2,1)S(1)}, u32[]{:S(2)}, u32[]{:S(2)}) %all-to-all-start) | async-done | bytes 2097184 | tf_op jit(solution)/shard_map/all_to_all | solution.py:294
  59.0 5.7 %all-to-all-start.1 = ((bf16[8,32,2048]{2,1,0:T(8,128)(2,1)}), bf16[8,32,2048]{2,1,0:T(8,128)(2,1)S(1)}, u32[]{:S(2)}, u32[]{:S(2)}) async-start(bf16[8,32,2048]{2,1,0:T(8,128)(2,1)} %bitcast.8), calls=%async_computation.1 | async-start | bytes 2097152 | tf_op jit(solution)/shard_map/all_to_all | solution.py:294
  64.7 18.5 %collective-permute-done.2.refs_1_.block = bf16[128,2048]{1,0:T(8,128)(2,1)S(1)} collective-permute-done((bf16[128,2048]{1,0:T(8,128)(2,1)S(1)}, bf16[128,2048]{1,0:T(8,128)(2,1)S(1)}, u32[]{:S(2)}, u32[]{:S(2)}) %collective-permute-start.2) | collective-permute-done | bytes 524320 | tf_op jit(solution)/shard_map/ppermute | solution.py:290
  84.7 4.1 %all-to-all-done.1 = bf16[8,32,2048]{2,1,0:T(8,128)(2,1)S(1)} async-done(((bf16[8,32,2048]{2,1,0:T(8,128)(2,1)}), bf16[8,32,2048]{2,1,0:T(8,128)(2,1)S(1)}, u32[]{:S(2)}, u32[]{:S(2)}) %all-to-all-start.1) | async-done | bytes 1048608 | tf_op jit(solution)/shard_map/all_to_all | solution.py:294
  88.8 4.2 %all-to-all-start.2 = ((bf16[8,32,2048]{2,1,0:T(8,128)(2,1)}), bf16[8,32,2048]{2,1,0:T(8,128)(2,1)}, u32[]{:S(2)}, u32[]{:S(2)}) async-start(bf16[8,32,2048]{2,1,0:T(8,128)(2,1)} %bitcast.12), calls=%async_computation.2 | async-start | bytes 2097152 | tf_op jit(solution)/shard_map/all_to_all | solution.py:294
  93.1 10.3 %shard_map.121 = (f32[512,704]{1,0:T(8,128)}, f32[512,704]{1,0:T(8,128)}, bf16[512,704]{1,0:T(8,128)(2,1)}, bf16[512,2048]{1,0:T(8,128)(2,1)}) custom-call(bf16[704,2048]{1,0:T(8,128)(2,1)} %bitcast.44, bf16[8,2,32,2048]{3,2,1,0:T(8,128)(2,1)} %bitcast.42, bf16[256,2048]{1,0:T(8,128)(2,1)} %bitcast.50, bf16[704,2048]{1,0:T(8,128)(2,1)} %bitcast.46, ...), custom_call_target="tpu_custom_call" | custom-call | flops 1 | bytes 1 | tf_op jit(solution)/shard_map/pallas_call | solution.py:266
  104.9 3.6 %all-to-all-start.3 = ((bf16[8,64,2048]{2,1,0:T(8,128)(2,1)}), bf16[8,64,2048]{2,1,0:T(8,128)(2,1)S(1)}, u32[]{:S(2)}, u32[]{:S(2)}) async-start(bf16[8,64,2048]{2,1,0:T(8,128)(2,1)} %bitcast.53), calls=%async_computation.3 | async-start | bytes 4194304 | tf_op jit(solution)/shard_map/all_to_all | solution.py:294
  108.8 18.3 %shard_map.122 = (bf16[256,2048]{1,0:T(8,128)(2,1)}, bf16[256,2048]{1,0:T(8,128)(2,1)}, bf16[2112,2048]{1,0:T(8,128)(2,1)}) custom-call(bf16[704,2048]{1,0:T(8,128)(2,1)} %bitcast.49, bf16[8,2,32,2048]{3,2,1,0:T(8,128)(2,1)} %bitcast.43, bf16[256,2048]{1,0:T(8,128)(2,1)} %bitcast.13.refs_2_, f32[512,704]{1,0:T(8,128)} %get-tuple-element.59.refs_3_, ...), custom_call_target="tpu_custom_call" | custom-call | flops 1 | bytes 1 | tf_op jit(solution)/shard_map/pallas_call | solution.py:266
  127.1 7.0 %all-to-all-done.3 = bf16[8,64,2048]{2,1,0:T(8,128)(2,1)S(1)} async-done(((bf16[8,64,2048]{2,1,0:T(8,128)(2,1)}), bf16[8,64,2048]{2,1,0:T(8,128)(2,1)S(1)}, u32[]{:S(2)}, u32[]{:S(2)}) %all-to-all-start.3) | async-done | bytes 2097184 | tf_op jit(solution)/shard_map/all_to_all | solution.py:294
  134.7 1.8 shard_map.123
  136.6 4.2 %all-to-all-start.4 = ((bf16[8,32,2048]{2,1,0:T(8,128)(2,1)}), bf16[8,32,2048]{2,1,0:T(8,128)(2,1)S(1)}, u32[]{:S(2)}, u32[]{:S(2)}) async-start(bf16[8,32,2048]{2,1,0:T(8,128)(2,1)} %bitcast.55), calls=%async_computation.4 | async-start | bytes 2097152 | tf_op jit(solution)/shard_map/all_to_all | solution.py:294
  140.8 2.8 %collective-permute-start.4 = (f32[8,128]{1,0:T(8,128)S(1)}, f32[8,128]{1,0:T(8,128)S(1)}, u32[]{:S(2)}, u32[]{:S(2)}) collective-permute-start(f32[8,128]{1,0:T(8,128)S(1)} %get-tuple-element.75), channel_id=1, source_target_pairs={{0,8},{1,9},{2,10},{3,11},{4,12},{5,13},{6,14},{7,15},{8,0},{9,1},... | collective-permute-start | bytes 12296 | tf_op jit(solution)/shard_map/ppermute | solution.py:290
  143.6 18.3 %collective-permute-done.3.came.far = bf16[128,2048]{1,0:T(8,128)(2,1)} collective-permute-done((bf16[128,2048]{1,0:T(8,128)(2,1)}, bf16[128,2048]{1,0:T(8,128)(2,1)}, u32[]{:S(2)}, u32[]{:S(2)}) %collective-permute-start.3) | collective-permute-done | bytes 524320 | tf_op jit(solution)/shard_map/ppermute | solution.py:290
  161.9 1.6 shard_map.124.refs_0_
  166.2 3.6 %all-to-all-start.5 = ((bf16[8,32,2048]{2,1,0:T(8,128)(2,1)}), bf16[8,32,2048]{2,1,0:T(8,128)(2,1)S(1)}, u32[]{:S(2)}, u32[]{:S(2)}) async-start(bf16[8,32,2048]{2,1,0:T(8,128)(2,1)} %bitcast.54), calls=%async_computation.6 | async-start | bytes 2097152 | tf_op jit(solution)/shard_map/all_to_all | solution.py:294
  169.8 4.2 %collective-permute-start.5 = (bf16[128,2048]{1,0:T(8,128)(2,1)}, bf16[128,2048]{1,0:T(8,128)(2,1)}, u32[]{:S(2)}, u32[]{:S(2)}) collective-permute-start(bf16[128,2048]{1,0:T(8,128)(2,1)} %copy-done.2), channel_id=1, source_target_pairs={{0,8},{1,9},{2,10},{3,11},{4,12},{5,13},{6,14},{7,15},{8,0},{9,1},... | collective-permute-start | bytes 1572872 | tf_op jit(solution)/shard_map/ppermute | solution.py:290
  175.0 2.9 %shard_map.126 = (bf16[128,2048]{1,0:T(8,128)(2,1)}, f32[8,128]{1,0:T(8,128)S(1)}) custom-call(s32[1]{0:T(128)} %bitcast.me_ref, f32[4,128]{1,0:T(4,128)S(1)} %copy-done.6, f32[4,128]{1,0:T(4,128)S(1)} %copy-done.8, bf16[128,2048]{1,0:T(8,128)(2,1)S(1)} %copy-done.1, bf16[512,2048]{1,0:T(8,128)(2,1)S(1)} %bitcast.39, ...), custom_call_target="tpu_custom_call" | custom-call | flops 536870912 | bytes 3678208 | tf_op jit(solution)/shard_map/pallas_call | solution.py:21
  177.9 6.1 %fusion = (f32[1,704,1024]{2,1,0:T(8,128)}, f32[1,1024,704]{1,2,0:T(8,128)}, f32[1,1024,704]{1,2,0:T(8,128)}) fusion(bf16[2112,1024]{1,0:T(8,128)(2,1)} %reduce-scatter.2.cloned.1.call-done), kind=kLoop, calls=%fused_computation.3 | loop fusion | flops 2162688 | bytes 12976128 | tf_op jit(solution)/shard_map/broadcast_in_dim | solution.py:446
  184.0 7.8 %collective-permute-done.5.came.refs_2_ = bf16[128,2048]{1,0:T(8,128)(2,1)} collective-permute-done((bf16[128,2048]{1,0:T(8,128)(2,1)}, bf16[128,2048]{1,0:T(8,128)(2,1)}, u32[]{:S(2)}, u32[]{:S(2)}) %collective-permute-start.5) | collective-permute-done | bytes 524320 | tf_op jit(solution)/shard_map/ppermute | solution.py:290
  195.1 2.2 %shard_map.128 = bf16[128,2048]{1,0:T(8,128)(2,1)} custom-call(s32[1]{0:T(128)} %constant.2.clone.1.me_ref, bf16[256,128]{1,0:T(8,128)(2,1)S(1)} %copy-done.3, bf16[256,2048]{1,0:T(8,128)(2,1)S(1)} %bitcast.40, bf16[128,2048]{1,0:T(8,128)(2,1)} %collective-permute-done.5.came.refs_2_), custom_call_target="tpu_custom_call" | custom-call | flops 134217728 | bytes 2162688 | tf_op jit(solution)/shard_map/pallas_call | solution.py:21
  (41 shorter events, 16.9 us)
Async XLA Ops:
  7.2 27.7 %collective-permute-start = (bf16[128,2048]{1,0:T(8,128)(2,1)}, bf16[128,2048]{1,0:T(8,128)(2,1)S(1)}, u32[]{:S(2)}, u32[]{:S(2)}) collective-permute-start(bf16[128,2048]{1,0:T(8,128)(2,1)} %x_hbm.1), channel_id=1, source_target_pairs={{0,8},{1,9},{2,10},{3,11},{4,12},{5,13},{6,14},{7,15},{8,0},{9,1},... | collective-permute-start | bytes 1572872 | tf_op jit(solution)/shard_map/ppermute | solution.py:290
  12.6 0.6 copy-start.5
  12.6 22.2 %collective-permute-start.1 = (f32[4,128]{1,0:T(4,128)S(1)}, f32[4,128]{1,0:T(4,128)S(1)}, u32[]{:S(2)}, u32[]{:S(2)}) collective-permute-start(f32[4,128]{1,0:T(4,128)S(1)} %pad_maximum_fusion.meta), channel_id=1, source_target_pairs={{0,8},{1,9},{2,10},{3,11},{4,12},{5,13},{6,14},{7,15},{8,0},{9,1},... | collective-permute-start | bytes 6152 | tf_op jit(solution)/shard_map/ppermute | solution.py:290
  17.1 39.4 %all-to-all-start = ((bf16[8,64,2048]{2,1,0:T(8,128)(2,1)}), bf16[8,64,2048]{2,1,0:T(8,128)(2,1)S(1)}, u32[]{:S(2)}, u32[]{:S(2)}) async-start(bf16[8,64,2048]{2,1,0:T(8,128)(2,1)} %bitcast.52), calls=%async_computation | async-start | bytes 4194304 | tf_op jit(solution)/shard_map/all_to_all | solution.py:294
  21.9 36.0 %copy-start = (bf16[128,2048]{1,0:T(8,128)(2,1)S(1)}, bf16[128,2048]{1,0:T(8,128)(2,1)}, u32[]{:S(2)}) copy-start(bf16[128,2048]{1,0:T(8,128)(2,1)} %block.1) | copy-start | bytes 1572868
  34.8 99.2 %copy-start.7 = (f32[4,128]{1,0:T(4,128)}, f32[4,128]{1,0:T(4,128)S(1)}, u32[]{:S(2)}) copy-start(f32[4,128]{1,0:T(4,128)S(1)} %collective-permute-done.1.refs_0_.meta_far.meta) | copy-start | bytes 6148
  56.5 1.3 copy-start.9
  57.9 25.3 %collective-permute-start.2 = (bf16[128,2048]{1,0:T(8,128)(2,1)S(1)}, bf16[128,2048]{1,0:T(8,128)(2,1)S(1)}, u32[]{:S(2)}, u32[]{:S(2)}) collective-permute-start(bf16[128,2048]{1,0:T(8,128)(2,1)S(1)} %copy-done), channel_id=1, source_target_pairs={{0,8},{1,9},{2,10},{3,11},{4,12},{5,13},{6,14},{7,15},{8,0},{9,1},... | collective-permute-start | bytes 1572872 | tf_op jit(solution)/shard_map/ppermute | solution.py:290
  59.0 29.9 %all-to-all-start.1 = ((bf16[8,32,2048]{2,1,0:T(8,128)(2,1)}), bf16[8,32,2048]{2,1,0:T(8,128)(2,1)S(1)}, u32[]{:S(2)}, u32[]{:S(2)}) async-start(bf16[8,32,2048]{2,1,0:T(8,128)(2,1)} %bitcast.8), calls=%async_computation.1 | async-start | bytes 2097152 | tf_op jit(solution)/shard_map/all_to_all | solution.py:294
  88.8 4.3 %copy-start.10 = (bf16[8,32,2048]{2,1,0:T(8,128)(2,1)}, bf16[8,32,2048]{2,1,0:T(8,128)(2,1)S(1)}, u32[]{:S(2)}) copy-start(bf16[8,32,2048]{2,1,0:T(8,128)(2,1)S(1)} %all-to-all-done.1) | copy-start | bytes 3145732
  88.8 16.1 %all-to-all-start.2 = ((bf16[8,32,2048]{2,1,0:T(8,128)(2,1)}), bf16[8,32,2048]{2,1,0:T(8,128)(2,1)}, u32[]{:S(2)}, u32[]{:S(2)}) async-start(bf16[8,32,2048]{2,1,0:T(8,128)(2,1)} %bitcast.12), calls=%async_computation.2 | async-start | bytes 2097152 | tf_op jit(solution)/shard_map/all_to_all | solution.py:294
  104.9 29.1 %all-to-all-start.3 = ((bf16[8,64,2048]{2,1,0:T(8,128)(2,1)}), bf16[8,64,2048]{2,1,0:T(8,128)(2,1)S(1)}, u32[]{:S(2)}, u32[]{:S(2)}) async-start(bf16[8,64,2048]{2,1,0:T(8,128)(2,1)} %bitcast.53), calls=%async_computation.3 | async-start | bytes 4194304 | tf_op jit(solution)/shard_map/all_to_all | solution.py:294
  108.5 69.4 %reduce-scatter.2.cloned.1.call-start = ((), (), s32[]{:S(2)}) async-start(), calls=%async_computation.7 | async-start | bytes 12976128 | tf_op jit(solution)/shard_map/reduce_scatter | solution.py:400
  134.0 0.7 copy-start.6
  136.5 25.4 %collective-permute-start.3 = (bf16[128,2048]{1,0:T(8,128)(2,1)}, bf16[128,2048]{1,0:T(8,128)(2,1)}, u32[]{:S(2)}, u32[]{:S(2)}) collective-permute-start(bf16[128,2048]{1,0:T(8,128)(2,1)} %get-tuple-element.70), channel_id=1, source_target_pairs={{0,8},{1,9},{2,10},{3,11},{4,12},{5,13},{6,14},{7,15},{8,0},{9,1},... | collective-permute-start | bytes 1572872 | tf_op jit(solution)/shard_map/ppermute | solution.py:290
  136.6 27.7 %all-to-all-start.4 = ((bf16[8,32,2048]{2,1,0:T(8,128)(2,1)}), bf16[8,32,2048]{2,1,0:T(8,128)(2,1)S(1)}, u32[]{:S(2)}, u32[]{:S(2)}) async-start(bf16[8,32,2048]{2,1,0:T(8,128)(2,1)} %bitcast.55), calls=%async_computation.4 | async-start | bytes 2097152 | tf_op jit(solution)/shard_map/all_to_all | solution.py:294
  140.8 25.4 %collective-permute-start.4 = (f32[8,128]{1,0:T(8,128)S(1)}, f32[8,128]{1,0:T(8,128)S(1)}, u32[]{:S(2)}, u32[]{:S(2)}) collective-permute-start(f32[8,128]{1,0:T(8,128)S(1)} %get-tuple-element.75), channel_id=1, source_target_pairs={{0,8},{1,9},{2,10},{3,11},{4,12},{5,13},{6,14},{7,15},{8,0},{9,1},... | collective-permute-start | bytes 12296 | tf_op jit(solution)/shard_map/ppermute | solution.py:290
  161.9 12.0 %copy-start.8 = (f32[4,128]{1,0:T(4,128)S(1)}, f32[4,128]{1,0:T(4,128)}, u32[]{:S(2)}) copy-start(f32[4,128]{1,0:T(4,128)} %copy-done.7) | copy-start | bytes 6148
  164.3 0.8 copy-start.4
  165.4 0.8 copy-start.2
  166.2 28.0 %all-to-all-start.5 = ((bf16[8,32,2048]{2,1,0:T(8,128)(2,1)}), bf16[8,32,2048]{2,1,0:T(8,128)(2,1)S(1)}, u32[]{:S(2)}, u32[]{:S(2)}) async-start(bf16[8,32,2048]{2,1,0:T(8,128)(2,1)} %bitcast.54), calls=%async_computation.6 | async-start | bytes 2097152 | tf_op jit(solution)/shard_map/all_to_all | solution.py:294
  169.8 22.0 %collective-permute-start.5 = (bf16[128,2048]{1,0:T(8,128)(2,1)}, bf16[128,2048]{1,0:T(8,128)(2,1)}, u32[]{:S(2)}, u32[]{:S(2)}) collective-permute-start(bf16[128,2048]{1,0:T(8,128)(2,1)} %copy-done.2), channel_id=1, source_target_pairs={{0,8},{1,9},{2,10},{3,11},{4,12},{5,13},{6,14},{7,15},{8,0},{9,1},... | collective-permute-start | bytes 1572872 | tf_op jit(solution)/shard_map/ppermute | solution.py:290
  174.0 1.0 copy-start.1
  194.2 0.8 copy-start.3
Sparse Core Ops, SparseCore 0:
  134.2 15.6 reduce-scatter.1

commit v21 on v20

--- a/solution.py
+++ b/solution.py
@@ -23,7 +23,7 @@
         out_shape=outs,
         in_specs=[SMEM] + [VMEM] * len(args),
         out_specs=[VMEM] * len(outs),
-        compiler_params=pltpu.CompilerParams(vmem_limit_bytes=6 * 1024 * 1024),
+        compiler_params=pltpu.CompilerParams(vmem_limit_bytes=60 * 1024 * 1024),
         cost_estimate=pl.CostEstimate(flops=flops, bytes_accessed=size, transcendentals=0),
     )(me, *args)
 

time: 208 us -> 212 us (1.019)
  Pallas kernels: 45.8 us -> 53 us
  starting transfers between devices: 38.6 us -> 36.2 us
    pallas_call x6, Pallas kernels: 10.3 us -> 17.3 us  [local_call(): pl.pallas_call(kernel, out_shape=outs, in_specs=[SMEM] + [VMEM] * len(arg...]
    all_to_all x6, waiting for transfers between devices: 34 us -> 31.1 us  [exchange(): lax.all_to_all(shaped, 'expert', 0, 0, axis_index_groups=sets, tiled=True)]
  transfers between devices with their start and end apart: 13 -> 13, of which waited for: 10 -> 9; matrix products, arithmetic and copies ran while one was open for 4% -> 4% of each run, Pallas kernels for 21% -> 24%
where the time goes in v21:
time: 212 us; the launch traced here: 210 us
  waiting for transfers between devices  90 us (42%)
  Pallas kernels  53 us (25%)
  starting transfers between devices  36.2 us (17%)
  between operations  14.1 us (7%)
  local copies, waits for them, and re-layouts  8.33 us (4%)
  other arithmetic  8.12 us (4%)
    ppermute x6, waiting for transfers between devices, across(): lax.ppermute(value, 'expert', [(e, (e + side) % experts) for e in range(e...  58.9 us
    all_to_all x6, waiting for transfers between devices, exchange(): lax.all_to_all(shaped, 'expert', 0, 0, axis_index_groups=sets, tiled=True)  31.1 us
    pallas_call x2, Pallas kernels, streamed_call(): pl.pallas_call(kernel, out_shape=outs, in_specs=[pl.BlockSpec(memory_spac...  28.8 us
    all_to_all x6, starting transfers between devices, exchange(): lax.all_to_all(shaped, 'expert', 0, 0, axis_index_groups=sets, tiled=True)  25.4 us
    pallas_call x6, Pallas kernels, local_call(): pl.pallas_call(kernel, out_shape=outs, in_specs=[SMEM] + [VMEM] * len(arg...  17.3 us
    ppermute x6, starting transfers between devices, across(): lax.ppermute(value, 'expert', [(e, (e + side) % experts) for e in range(e...  10.5 us
    unnamed x22, local copies, waits for them, and re-layouts  7.77 us
    broadcast_in_dim x1, other arithmetic, on_device(): summed[2 * units:].astype(F32)[None]  6.07 us
  transfers between devices with their start and end apart: 13, of which 9 were waited for; matrix products, arithmetic and copies ran while one was open for 4% of the time, Pallas kernels for 24%

profile of v21, /device:TPU:0, one launch (start us, length us, event | category | flops | bytes accessed | tf_op | source)
XLA Modules:
  0.0 209.7 jit_solution(14689391622528311118)
XLA Ops:
  7.2 4.1 %collective-permute-start = (bf16[128,2048]{1,0:T(8,128)(2,1)}, bf16[128,2048]{1,0:T(8,128)(2,1)S(1)}, u32[]{:S(2)}, u32[]{:S(2)}) collective-permute-start(bf16[128,2048]{1,0:T(8,128)(2,1)} %x_hbm.1), channel_id=1, source_target_pairs={{0,8},{1,9},{2,10},{3,11},{4,12},{5,13},{6,14},{7,15},{8,0},{9,1},... | collective-permute-start | bytes 1572872 | tf_op jit(solution)/shard_map/ppermute | solution.py:290
  13.2 3.9 %shard_map.119 = bf16[512,2048]{1,0:T(8,128)(2,1)} custom-call(s32[1]{0:T(128)} %bitcast.me_ref, f32[4,128]{1,0:T(4,128)} %copy-done.8, bf16[128,2048]{1,0:T(8,128)(2,1)} %x_hbm.1, bf16[128,2048]{1,0:T(8,128)(2,1)} %block.1), custom_call_target="tpu_custom_call" | custom-call | flops 536870912 | bytes 1 | tf_op jit(solution)/shard_map/pallas_call | solution.py:321
  17.1 4.7 %all-to-all-start = ((bf16[8,64,2048]{2,1,0:T(8,128)(2,1)}), bf16[8,64,2048]{2,1,0:T(8,128)(2,1)S(1)}, u32[]{:S(2)}, u32[]{:S(2)}) async-start(bf16[8,64,2048]{2,1,0:T(8,128)(2,1)} %bitcast.50), calls=%async_computation | async-start | bytes 4194304 | tf_op jit(solution)/shard_map/all_to_all | solution.py:294
  21.9 13.0 %collective-permute-done.1.refs_0_.meta_far.meta = f32[4,128]{1,0:T(4,128)S(1)} collective-permute-done((f32[4,128]{1,0:T(4,128)S(1)}, f32[4,128]{1,0:T(4,128)S(1)}, u32[]{:S(2)}, u32[]{:S(2)}) %collective-permute-start.1) | collective-permute-done | bytes 2080 | tf_op jit(solution)/shard_map/ppermute | solution.py:290
  36.2 2.6 %shard_map.118 = bf16[256,2048]{1,0:T(8,128)(2,1)} custom-call(s32[1]{0:T(128)} %bitcast.me_ref, f32[4,128]{1,0:T(4,128)} %copy-done.9, bf16[128,2048]{1,0:T(8,128)(2,1)} %copy-done.10), custom_call_target="tpu_custom_call" | custom-call | flops 99999997952 | bytes 1574912 | tf_op jit(solution)/shard_map/pallas_call | solution.py:21
  38.8 17.8 %all-to-all-done = bf16[8,64,2048]{2,1,0:T(8,128)(2,1)S(1)} async-done(((bf16[8,64,2048]{2,1,0:T(8,128)(2,1)}), bf16[8,64,2048]{2,1,0:T(8,128)(2,1)S(1)}, u32[]{:S(2)}, u32[]{:S(2)}) %all-to-all-start) | async-done | bytes 2097184 | tf_op jit(solution)/shard_map/all_to_all | solution.py:294
  57.6 5.7 %all-to-all-start.1 = ((bf16[8,32,2048]{2,1,0:T(8,128)(2,1)}), bf16[8,32,2048]{2,1,0:T(8,128)(2,1)S(1)}, u32[]{:S(2)}, u32[]{:S(2)}) async-start(bf16[8,32,2048]{2,1,0:T(8,128)(2,1)} %bitcast.55), calls=%async_computation.1 | async-start | bytes 2097152 | tf_op jit(solution)/shard_map/all_to_all | solution.py:294
  63.4 18.8 %collective-permute-done.2.refs_1_.block = bf16[128,2048]{1,0:T(8,128)(2,1)} collective-permute-done((bf16[128,2048]{1,0:T(8,128)(2,1)}, bf16[128,2048]{1,0:T(8,128)(2,1)}, u32[]{:S(2)}, u32[]{:S(2)}) %collective-permute-start.2) | collective-permute-done | bytes 524320 | tf_op jit(solution)/shard_map/ppermute | solution.py:290
  82.2 2.6 %shard_map.120 = bf16[256,2048]{1,0:T(8,128)(2,1)} custom-call(s32[1]{0:T(128)} %bitcast.me_ref, f32[4,128]{1,0:T(4,128)} %copy-done.9, bf16[128,2048]{1,0:T(8,128)(2,1)} %collective-permute-done.2.refs_1_.block), custom_call_target="tpu_custom_call" | custom-call | flops 99999997952 | bytes 1574912 | tf_op jit(solution)/shard_map/pallas_call | solution.py:21
  84.7 2.8 %all-to-all-done.1 = bf16[8,32,2048]{2,1,0:T(8,128)(2,1)S(1)} async-done(((bf16[8,32,2048]{2,1,0:T(8,128)(2,1)}), bf16[8,32,2048]{2,1,0:T(8,128)(2,1)S(1)}, u32[]{:S(2)}, u32[]{:S(2)}) %all-to-all-start.1) | async-done | bytes 1048608 | tf_op jit(solution)/shard_map/all_to_all | solution.py:294
  87.5 3.6 %all-to-all-start.2 = ((bf16[8,32,2048]{2,1,0:T(8,128)(2,1)}), bf16[8,32,2048]{2,1,0:T(8,128)(2,1)S(1)}, u32[]{:S(2)}, u32[]{:S(2)}) async-start(bf16[8,32,2048]{2,1,0:T(8,128)(2,1)} %bitcast.56), calls=%async_computation.2 | async-start | bytes 2097152 | tf_op jit(solution)/shard_map/all_to_all | solution.py:294
  91.1 10.3 %shard_map.121 = (f32[512,704]{1,0:T(8,128)}, f32[512,704]{1,0:T(8,128)}, bf16[512,704]{1,0:T(8,128)(2,1)}, bf16[512,2048]{1,0:T(8,128)(2,1)}) custom-call(bf16[704,2048]{1,0:T(8,128)(2,1)} %bitcast.42, bf16[8,2,32,2048]{3,2,1,0:T(8,128)(2,1)} %bitcast.40, bf16[256,2048]{1,0:T(8,128)(2,1)} %bitcast.48, bf16[704,2048]{1,0:T(8,128)(2,1)} %bitcast.44, ...), custom_call_target="tpu_custom_call" | custom-call | flops 1 | bytes 1 | tf_op jit(solution)/shard_map/pallas_call | solution.py:266
  104.2 3.6 %all-to-all-start.3 = ((bf16[8,64,2048]{2,1,0:T(8,128)(2,1)}), bf16[8,64,2048]{2,1,0:T(8,128)(2,1)S(1)}, u32[]{:S(2)}, u32[]{:S(2)}) async-start(bf16[8,64,2048]{2,1,0:T(8,128)(2,1)} %bitcast.54), calls=%async_computation.3 | async-start | bytes 4194304 | tf_op jit(solution)/shard_map/all_to_all | solution.py:294
  108.1 18.4 %shard_map.122 = (bf16[256,2048]{1,0:T(8,128)(2,1)}, bf16[256,2048]{1,0:T(8,128)(2,1)}, bf16[2112,2048]{1,0:T(8,128)(2,1)}) custom-call(bf16[704,2048]{1,0:T(8,128)(2,1)} %bitcast.47, bf16[8,2,32,2048]{3,2,1,0:T(8,128)(2,1)} %bitcast.41, bf16[256,2048]{1,0:T(8,128)(2,1)} %bitcast.51, f32[512,704]{1,0:T(8,128)} %get-tuple-element.59.refs_3_, ...), custom_call_target="tpu_custom_call" | custom-call | flops 1 | bytes 1 | tf_op jit(solution)/shard_map/pallas_call | solution.py:266
  126.5 6.8 %all-to-all-done.3 = bf16[8,64,2048]{2,1,0:T(8,128)(2,1)S(1)} async-done(((bf16[8,64,2048]{2,1,0:T(8,128)(2,1)}), bf16[8,64,2048]{2,1,0:T(8,128)(2,1)S(1)}, u32[]{:S(2)}, u32[]{:S(2)}) %all-to-all-start.3) | async-done | bytes 2097184 | tf_op jit(solution)/shard_map/all_to_all | solution.py:294
  134.7 3.6 %shard_map.123 = (bf16[128,2048]{1,0:T(8,128)(2,1)}, f32[8,128]{1,0:T(8,128)}) custom-call(s32[1]{0:T(128)} %bitcast.me_ref, f32[4,128]{1,0:T(4,128)} %copy-done.8, f32[4,128]{1,0:T(4,128)} %copy-done.9, bf16[128,2048]{1,0:T(8,128)(2,1)} %collective-permute-done.2.refs_1_.block, bf16[512,2048]{1,0:T(8,128)(2,1)} %bitcast.38), custom_call_target="tpu_custom_call" | custom-call | flops 536870912 | bytes 3153920 | tf_op jit(solution)/shard_map/pallas_call | solution.py:21
  140.2 4.2 %all-to-all-start.4 = ((bf16[8,32,2048]{2,1,0:T(8,128)(2,1)}), bf16[8,32,2048]{2,1,0:T(8,128)(2,1)S(1)}, u32[]{:S(2)}, u32[]{:S(2)}) async-start(bf16[8,32,2048]{2,1,0:T(8,128)(2,1)} %bitcast.16), calls=%async_computation.4 | async-start | bytes 2097152 | tf_op jit(solution)/shard_map/all_to_all | solution.py:294
  145.4 18.2 %collective-permute-done.3.came.far = bf16[128,2048]{1,0:T(8,128)(2,1)S(1)} collective-permute-done((bf16[128,2048]{1,0:T(8,128)(2,1)}, bf16[128,2048]{1,0:T(8,128)(2,1)S(1)}, u32[]{:S(2)}, u32[]{:S(2)}) %collective-permute-start.3) | collective-permute-done | bytes 524320 | tf_op jit(solution)/shard_map/ppermute | solution.py:290
  171.1 3.6 %all-to-all-start.5 = ((bf16[8,32,2048]{2,1,0:T(8,128)(2,1)}), bf16[8,32,2048]{2,1,0:T(8,128)(2,1)S(1)}, u32[]{:S(2)}, u32[]{:S(2)}) async-start(bf16[8,32,2048]{2,1,0:T(8,128)(2,1)} %bitcast.23), calls=%async_computation.6 | async-start | bytes 2097152 | tf_op jit(solution)/shard_map/all_to_all | solution.py:294
  174.7 2.4 %collective-permute-start.5 = (bf16[128,2048]{1,0:T(8,128)(2,1)}, bf16[128,2048]{1,0:T(8,128)(2,1)S(1)}, u32[]{:S(2)}, u32[]{:S(2)}) collective-permute-start(bf16[128,2048]{1,0:T(8,128)(2,1)} %shard_map.125), channel_id=1, source_target_pairs={{0,8},{1,9},{2,10},{3,11},{4,12},{5,13},{6,14},{7,15},{8,0},{9,1},... | collective-permute-start | bytes 1572872 | tf_op jit(solution)/shard_map/ppermute | solution.py:290
  177.1 3.7 %shard_map.126 = (bf16[128,2048]{1,0:T(8,128)(2,1)}, f32[8,128]{1,0:T(8,128)}) custom-call(s32[1]{0:T(128)} %bitcast.me_ref, f32[4,128]{1,0:T(4,128)} %copy-done.8, f32[4,128]{1,0:T(4,128)} %copy-done.9, bf16[128,2048]{1,0:T(8,128)(2,1)} %block.1, bf16[512,2048]{1,0:T(8,128)(2,1)} %bitcast.39, bf16[128,2048]{1,0:T(8,128)(2,1)} %copy-done.7), custom_call_target="tpu_custom_call" | custom-call | flops 536870912 | bytes 3678208 | tf_op jit(solution)/shard_map/pallas_call | solution.py:21
  181.5 6.1 %fusion = (f32[1,704,1024]{2,1,0:T(8,128)}, f32[1,1024,704]{1,2,0:T(8,128)}, f32[1,1024,704]{1,2,0:T(8,128)}) fusion(bf16[2112,1024]{1,0:T(8,128)(2,1)} %reduce-scatter.2.cloned.1.call-done), kind=kLoop, calls=%fused_computation.3 | loop fusion | flops 2162688 | bytes 12976128 | tf_op jit(solution)/shard_map/broadcast_in_dim | solution.py:446
  187.5 9.0 %collective-permute-done.5.came.refs_2_ = bf16[128,2048]{1,0:T(8,128)(2,1)S(1)} collective-permute-done((bf16[128,2048]{1,0:T(8,128)(2,1)}, bf16[128,2048]{1,0:T(8,128)(2,1)S(1)}, u32[]{:S(2)}, u32[]{:S(2)}) %collective-permute-start.5) | collective-permute-done | bytes 524320 | tf_op jit(solution)/shard_map/ppermute | solution.py:290
  200.3 2.5 %shard_map.128 = bf16[128,2048]{1,0:T(8,128)(2,1)} custom-call(s32[1]{0:T(128)} %constant.2.clone.1.me_ref, bf16[256,128]{1,0:T(8,128)(2,1)} %shard_map.127.refs_0_, bf16[256,2048]{1,0:T(8,128)(2,1)} %bitcast.52, bf16[128,2048]{1,0:T(8,128)(2,1)} %copy-done.6), custom_call_target="tpu_custom_call" | custom-call | flops 134217728 | bytes 2162688 | tf_op jit(solution)/shard_map/pallas_call | solution.py:21
  (41 shorter events, 23.7 us)
Async XLA Ops:
  7.2 27.7 %collective-permute-start = (bf16[128,2048]{1,0:T(8,128)(2,1)}, bf16[128,2048]{1,0:T(8,128)(2,1)S(1)}, u32[]{:S(2)}, u32[]{:S(2)}) collective-permute-start(bf16[128,2048]{1,0:T(8,128)(2,1)} %x_hbm.1), channel_id=1, source_target_pairs={{0,8},{1,9},{2,10},{3,11},{4,12},{5,13},{6,14},{7,15},{8,0},{9,1},... | collective-permute-start | bytes 1572872 | tf_op jit(solution)/shard_map/ppermute | solution.py:290
  12.6 0.6 copy-start.8
  12.6 22.2 %collective-permute-start.1 = (f32[4,128]{1,0:T(4,128)S(1)}, f32[4,128]{1,0:T(4,128)S(1)}, u32[]{:S(2)}, u32[]{:S(2)}) collective-permute-start(f32[4,128]{1,0:T(4,128)S(1)} %pad_maximum_fusion.meta), channel_id=1, source_target_pairs={{0,8},{1,9},{2,10},{3,11},{4,12},{5,13},{6,14},{7,15},{8,0},{9,1},... | collective-permute-start | bytes 6152 | tf_op jit(solution)/shard_map/ppermute | solution.py:290
  17.1 39.4 %all-to-all-start = ((bf16[8,64,2048]{2,1,0:T(8,128)(2,1)}), bf16[8,64,2048]{2,1,0:T(8,128)(2,1)S(1)}, u32[]{:S(2)}, u32[]{:S(2)}) async-start(bf16[8,64,2048]{2,1,0:T(8,128)(2,1)} %bitcast.50), calls=%async_computation | async-start | bytes 4194304 | tf_op jit(solution)/shard_map/all_to_all | solution.py:294
  34.8 0.6 copy-start.9
  35.4 0.8 copy-start.10
  56.5 28.2 %copy-start.1 = (bf16[8,64,2048]{2,1,0:T(8,128)(2,1)}, bf16[8,64,2048]{2,1,0:T(8,128)(2,1)S(1)}, u32[]{:S(2)}) copy-start(bf16[8,64,2048]{2,1,0:T(8,128)(2,1)S(1)} %all-to-all-done) | copy-start | bytes 6291460
  56.5 25.6 %collective-permute-start.2 = (bf16[128,2048]{1,0:T(8,128)(2,1)}, bf16[128,2048]{1,0:T(8,128)(2,1)}, u32[]{:S(2)}, u32[]{:S(2)}) collective-permute-start(bf16[128,2048]{1,0:T(8,128)(2,1)} %block.1), channel_id=1, source_target_pairs={{0,8},{1,9},{2,10},{3,11},{4,12},{5,13},{6,14},{7,15},{8,0},{9,1},... | collective-permute-start | bytes 1572872 | tf_op jit(solution)/shard_map/ppermute | solution.py:290
  57.6 29.9 %all-to-all-start.1 = ((bf16[8,32,2048]{2,1,0:T(8,128)(2,1)}), bf16[8,32,2048]{2,1,0:T(8,128)(2,1)S(1)}, u32[]{:S(2)}, u32[]{:S(2)}) async-start(bf16[8,32,2048]{2,1,0:T(8,128)(2,1)} %bitcast.55), calls=%async_computation.1 | async-start | bytes 2097152 | tf_op jit(solution)/shard_map/all_to_all | solution.py:294
  87.5 3.6 %copy-start.2 = (bf16[8,32,2048]{2,1,0:T(8,128)(2,1)}, bf16[8,32,2048]{2,1,0:T(8,128)(2,1)S(1)}, u32[]{:S(2)}) copy-start(bf16[8,32,2048]{2,1,0:T(8,128)(2,1)S(1)} %all-to-all-done.1) | copy-start | bytes 3145732
  87.5 15.7 %all-to-all-start.2 = ((bf16[8,32,2048]{2,1,0:T(8,128)(2,1)}), bf16[8,32,2048]{2,1,0:T(8,128)(2,1)S(1)}, u32[]{:S(2)}, u32[]{:S(2)}) async-start(bf16[8,32,2048]{2,1,0:T(8,128)(2,1)} %bitcast.56), calls=%async_computation.2 | async-start | bytes 2097152 | tf_op jit(solution)/shard_map/all_to_all | solution.py:294
  103.2 1.0 copy-start.3
  104.2 29.1 %all-to-all-start.3 = ((bf16[8,64,2048]{2,1,0:T(8,128)(2,1)}), bf16[8,64,2048]{2,1,0:T(8,128)(2,1)S(1)}, u32[]{:S(2)}, u32[]{:S(2)}) async-start(bf16[8,64,2048]{2,1,0:T(8,128)(2,1)} %bitcast.54), calls=%async_computation.3 | async-start | bytes 4194304 | tf_op jit(solution)/shard_map/all_to_all | solution.py:294
  107.8 73.6 %reduce-scatter.2.cloned.1.call-start = ((), (), s32[]{:S(2)}) async-start(), calls=%async_computation.7 | async-start | bytes 12976128 | tf_op jit(solution)/shard_map/reduce_scatter | solution.py:400
  133.3 1.3 copy-start
  138.3 25.3 %collective-permute-start.3 = (bf16[128,2048]{1,0:T(8,128)(2,1)}, bf16[128,2048]{1,0:T(8,128)(2,1)S(1)}, u32[]{:S(2)}, u32[]{:S(2)}) collective-permute-start(bf16[128,2048]{1,0:T(8,128)(2,1)} %get-tuple-element.70), channel_id=1, source_target_pairs={{0,8},{1,9},{2,10},{3,11},{4,12},{5,13},{6,14},{7,15},{8,0},{9,1},... | collective-permute-start | bytes 1572872 | tf_op jit(solution)/shard_map/ppermute | solution.py:290
  140.2 27.5 %all-to-all-start.4 = ((bf16[8,32,2048]{2,1,0:T(8,128)(2,1)}), bf16[8,32,2048]{2,1,0:T(8,128)(2,1)S(1)}, u32[]{:S(2)}, u32[]{:S(2)}) async-start(bf16[8,32,2048]{2,1,0:T(8,128)(2,1)} %bitcast.16), calls=%async_computation.4 | async-start | bytes 2097152 | tf_op jit(solution)/shard_map/all_to_all | solution.py:294
  144.4 26.7 %collective-permute-start.4 = (f32[8,128]{1,0:T(8,128)}, f32[8,128]{1,0:T(8,128)S(1)}, u32[]{:S(2)}, u32[]{:S(2)}) collective-permute-start(f32[8,128]{1,0:T(8,128)} %get-tuple-element.75), channel_id=1, source_target_pairs={{0,8},{1,9},{2,10},{3,11},{4,12},{5,13},{6,14},{7,15},{8,0},{9,1},... | collective-permute-start | bytes 12296 | tf_op jit(solution)/shard_map/ppermute | solution.py:290
  163.6 0.8 copy-start.7
  167.7 1.0 copy-start.5
  171.1 28.3 %all-to-all-start.5 = ((bf16[8,32,2048]{2,1,0:T(8,128)(2,1)}), bf16[8,32,2048]{2,1,0:T(8,128)(2,1)S(1)}, u32[]{:S(2)}, u32[]{:S(2)}) async-start(bf16[8,32,2048]{2,1,0:T(8,128)(2,1)} %bitcast.23), calls=%async_computation.6 | async-start | bytes 2097152 | tf_op jit(solution)/shard_map/all_to_all | solution.py:294
  174.7 21.9 %collective-permute-start.5 = (bf16[128,2048]{1,0:T(8,128)(2,1)}, bf16[128,2048]{1,0:T(8,128)(2,1)S(1)}, u32[]{:S(2)}, u32[]{:S(2)}) collective-permute-start(bf16[128,2048]{1,0:T(8,128)(2,1)} %shard_map.125), channel_id=1, source_target_pairs={{0,8},{1,9},{2,10},{3,11},{4,12},{5,13},{6,14},{7,15},{8,0},{9,1},... | collective-permute-start | bytes 1572872 | tf_op jit(solution)/shard_map/ppermute | solution.py:290
  196.5 0.8 copy-start.6
  199.4 1.0 copy-start.4
Sparse Core Ops, SparseCore 0:
  133.5 17.1 reduce-scatter.1
